TPU v7x, 256 devices: a whole 4x4x8 slice. The times are simulated.
256 devices in a mesh: dp: 16 (over z, x_lo), fsdp: 16 (over y, x_hi, core).
Axes of the slice: x: 4 (x_hi: 2, x_lo: 2; x = x_hi * 2 + x_lo), y: 4, z: 8, core: 2. Of those that a mesh axis runs over, the one named last changes fastest.
Arguments:
- residual: bfloat16 [73728, 2048], P(('dp', 'fsdp')), may hold values from -6 to 6
- student_mix: bfloat16 [73728, 2048], P(('dp', 'fsdp')), may hold values from -6 to 6
- teacher_mix: bfloat16 [73728, 2048], P(('dp', 'fsdp')), may hold values from -6 to 6
- positions: int32 [512, 144], P(('dp', 'fsdp')), may hold values from 0 to 143
- layer_scale: float32 [2048], replicated, may hold values from 0.3 to 3
- student_weight: float32 [2048, 2048], P('fsdp'), may hold values from -6 to 6
- teacher_weight: float32 [2048, 2048], P('fsdp'), may hold values from -6 to 6
- moment: float32 [2048, 2048], P('fsdp'), may hold values from -0.00036621094 to 0.00036621094
- second: float32 [2048, 2048], P('fsdp'), may hold values from 1.9868216e-09 to 1.9868216e-08
Outputs:
- student_new: float32 [2048, 2048], P('fsdp')
- teacher_new: float32 [2048, 2048], P('fsdp')
- moment_new: float32 [2048, 2048], P('fsdp')
- second_new: float32 [2048, 2048], P('fsdp')
- student_tokens: bfloat16 [73728, 2048], P(('dp', 'fsdp'))
All inputs are finite; a program needn't handle non-finite values.
Results may differ from a plain program's by a relative error of at most 0.01.
Values may be sent and summed in bfloat16 or wider, within the bound.
No kernel may reach another device: no remote copies, remote signals or barrier semaphores. Data moves between devices by JAX's collectives and lax.ppermute only.
A program may use at most 128 MiB of HBM per device.

v0:
```python
import jax
import jax.numpy as jnp
from jax import lax
from jax.sharding import PartitionSpec as P

KIN = 2048
DOUT = 2048
PATCHES = 144


def normalize(values):
    inverse_rms = lax.rsqrt(jnp.mean(values * values, axis=-1, keepdims=True) + 1e-06)
    return (values * inverse_rms, inverse_rms)


def add_rows(mixture, piece):
    return jnp.dot(mixture, piece, preferred_element_type=jnp.float32)


def adamw_update(grad, weight, teacher, first, squares):
    first_next = 0.9 * first + 0.1 * grad
    squares_next = 0.95 * squares + 0.05 * grad * grad
    weight_next = weight - 0.1 * (first_next / (jnp.sqrt(squares_next) + 1e-08) + 0.04 * weight)
    teacher_next = 0.96 * teacher + 0.04 * weight_next
    return (weight_next, teacher_next, first_next, squares_next)


def shards(
    residual,
    student_mix,
    teacher_mix,
    positions,
    layer_scale,
    student_weight,
    teacher_weight,
    moment,
    second,
):
    inverse_root = KIN ** (-0.5)
    token_count = student_mix.shape[0]
    total_tokens = token_count * lax.axis_size("dp") * lax.axis_size("fsdp")
    student_copy = student_weight.astype(jnp.bfloat16)
    teacher_copy = teacher_weight.astype(jnp.bfloat16)
    student_prod = add_rows(student_mix, lax.all_gather(student_copy, "fsdp", axis=0, tiled=True))
    teacher_prod = add_rows(teacher_mix, lax.all_gather(teacher_copy, "fsdp", axis=0, tiled=True))
    base = residual.astype(jnp.float32)
    student_out = base + layer_scale * (student_prod * inverse_root)
    teacher_out = base + layer_scale * (teacher_prod * inverse_root)
    student_norm, inverse_rms = normalize(student_out)
    student_tokens = student_norm.astype(jnp.bfloat16)
    teacher_norm, unused = normalize(teacher_out)
    crop_count = positions.shape[0]
    matched = jnp.take_along_axis(
        teacher_norm.reshape(crop_count, PATCHES, DOUT), positions[:, :, None], axis=1
    )
    matched = matched.reshape(token_count, DOUT)
    mismatch = (student_norm - matched) / total_tokens
    out_grad = inverse_rms * (
        mismatch - student_norm * jnp.mean(mismatch * student_norm, axis=-1, keepdims=True)
    )
    mix_grad = (layer_scale * out_grad * inverse_root).astype(jnp.bfloat16)
    shard_grad = lax.psum_scatter(
        lax.dot_general(
            student_mix, mix_grad, (((0,), (0,)), ((), ())), preferred_element_type=jnp.float32
        ).astype(jnp.bfloat16),
        "fsdp",
        scatter_dimension=0,
        tiled=True,
    )
    grad = lax.psum(shard_grad, "dp").astype(jnp.float32)
    weight_next, teacher_next, first_next, squares_next = adamw_update(
        grad, student_weight, teacher_weight, moment, second
    )
    return (weight_next, teacher_next, first_next, squares_next, student_tokens)


def solution(mesh):
    placed = (
        P(("dp", "fsdp"), None),
        P(("dp", "fsdp"), None),
        P(("dp", "fsdp"), None),
        P(("dp", "fsdp"), None),
        P(),
        P("fsdp", None),
        P("fsdp", None),
        P("fsdp", None),
        P("fsdp", None),
    )
    return jax.shard_map(
        shards,
        mesh=mesh,
        in_specs=placed,
        out_specs=(
            P("fsdp", None),
            P("fsdp", None),
            P("fsdp", None),
            P("fsdp", None),
            P(("dp", "fsdp"), None),
        ),
        check_vma=False,
    )
```

profile of v0, /device:TPU:4, one launch (start us, length us, event | category | flops | bytes accessed | tf_op | source)
XLA Modules:
  0.0 479.1 jit_solution(15726961534862599385)
XLA Ops:
  7.3 2.2 convert_element_type.26
  9.6 0.9 convert_element_type.25
  10.7 79.2 %all-gather.5.cloned.1.call-done = bf16[2048,2048]{1,0:T(8,128)(2,1)} async-done(((bf16[128,2048]{1,0:T(8,128)(2,1)}), bf16[2048,2048]{1,0:T(8,128)(2,1)}) %all-gather.5.cloned.1.call-update) | async-done | bytes 8388624 | tf_op jit(solution)/shard_map/all_gather | solution.py:45
  89.9 7.8 %multiply_reduce_fusion.1 = (f32[288]{0:T(512)S(1)}, f32[288,2048]{1,0:T(8,128)}) fusion(f32[2048]{0:T(1024)S(1)} %broadcast_multiply_fusion.1, bf16[288,2048]{1,0:T(8,128)(2,1)S(1)} %copy-done.13, bf16[2048,2048]{1,0:T(8,128)(2,1)} %all-gather.5.cloned.1.call-done, bf16[288,2048]{1,0:T(8,128)(2,1)} %param.9), kind=kOutput, calls=%fused_computation.9 | convolution fusion | flops 2418867968 | bytes 13116544 | tf_op jit(solution)/shard_map/dot_general | solution.py:17
  97.7 71.4 %all-gather.3.cloned.1.call-done = bf16[2048,2048]{1,0:T(8,128)(2,1)} async-done(((bf16[128,2048]{1,0:T(8,128)(2,1)}), bf16[2048,2048]{1,0:T(8,128)(2,1)}) %all-gather.3.cloned.1.call-update) | async-done | bytes 8388624 | tf_op jit(solution)/shard_map/all_gather | solution.py:44
  169.2 8.0 %multiply_reduce_fusion.2 = (f32[288]{0:T(512)S(1)}, f32[288,2048]{1,0:T(8,128)}) fusion(f32[2048]{0:T(1024)S(1)} %broadcast_multiply_fusion.1, bf16[288,2048]{1,0:T(8,128)(2,1)S(1)} %copy-done, bf16[2048,2048]{1,0:T(8,128)(2,1)} %all-gather.3.cloned.1.call-done, bf16[288,2048]{1,0:T(8,128)(2,1)} %param.9), kind=kOutput, calls=%fused_computation.10 | convolution fusion | flops 2418867968 | bytes 13116544 | tf_op jit(solution)/shard_map/dot_general | solution.py:17
  177.2 0.2 broadcast_multiply_fusion
  177.4 10.0 %gather_fusion = f32[288,2048]{1,0:T(8,128)} fusion(f32[2,144,2048]{2,1,0:T(8,128)S(1)} %bitcast.13, s32[288]{0:T(512)S(1)} %reshape.47), kind=kCustom, calls=%fused_computation | custom fusion | bytes 4720896 | tf_op jit(solution)/shard_map/jit(take_along_axis)/gather | solution.py:53
  187.4 4.1 multiply_convert_fusion.1
  191.6 7.3 %convert_bitcast_fusion = bf16[2048,2048]{0,1:T(8,128)(2,1)} fusion(bf16[288,2048]{1,0:T(8,128)(2,1)S(1)} %copy-done, f32[288,2048]{1,0:T(8,128)S(1)} %copy-done.2, f32[288,2048]{1,0:T(8,128)S(1)} %copy-done.9, f32[288]{0:T(512)S(1)} %broadcast_multiply_fusion.2, f32[288]{0:T(512)S(1)} %add_rsqrt_fusion.1, f32[2048]{0:T(1024)S(1)} %copy-done.11, ...), kind=kOutput, calls=%fused_computation.1 | convolution fusion | flops 2426011648 | bytes 14297632 | tf_op jit(solution)/shard_map/dot_general | solution.py:63
  198.8 12.4 %copy.32 = bf16[2048,2048]{1,0:T(8,128)(2,1)} copy(bf16[2048,2048]{0,1:T(8,128)(2,1)} %convert_bitcast_fusion) | data formatting | bytes 16777216
  211.2 0.2 all-reduce.2.cloned.1.call-start
  211.5 107.8 %reduce-scatter.4.cloned.1.call-done = bf16[128,2048]{1,0:T(8,128)(2,1)} async-done(((bf16[2048,2048]{1,0:T(8,128)(2,1)}), bf16[128,2048]{1,0:T(8,128)(2,1)}) %reduce-scatter.4.cloned.1.call-update) | async-done | bytes 524304
  319.3 2.0 copy.33
  321.3 0.3 copy.26
  321.7 0.3 copy.27
  322.0 1.6 copy.23
  323.6 2.5 copy.24
  326.1 134.6 %all-reduce.2.cloned.1.call-done = bf16[128,2048]{0,1:T(8,128)(2,1)} async-done(((bf16[128,2048]{0,1:T(8,128)(2,1)}), bf16[128,2048]{0,1:T(8,128)(2,1)}) %all-reduce.2.cloned.1.call-update) | async-done | bytes 524304 | tf_op jit(solution)/shard_map/psum | solution.py:70
  460.7 3.9 multiply_add_fusion
  464.6 2.6 copy.28
  467.2 2.7 copy.29
  469.9 1.3 copy.30
  471.2 1.3 copy.31
  (43 shorter events, 0.5 us)
Async XLA Ops:
  7.2 162.0 %copy-start = (bf16[288,2048]{1,0:T(8,128)(2,1)S(1)}, bf16[288,2048]{1,0:T(8,128)(2,1)}, u32[]{:S(2)}) copy-start(bf16[288,2048]{1,0:T(8,128)(2,1)} %param.10) | copy-start | bytes 3538948
  7.2 2.4 copy-start.5
  7.2 3.3 copy-start.12
  7.2 3.5 copy-start.10
  7.2 82.7 %copy-start.13 = (bf16[288,2048]{1,0:T(8,128)(2,1)S(1)}, bf16[288,2048]{1,0:T(8,128)(2,1)}, u32[]{:S(2)}) copy-start(bf16[288,2048]{1,0:T(8,128)(2,1)} %param.11) | copy-start | bytes 3538948
  7.2 82.7 %all-gather.5.cloned.1.call-start = ((), (), s32[]{:S(2)}) async-start(), calls=%async_computation.2 | async-start | bytes 8912896 | tf_op jit(solution)/shard_map/all_gather | solution.py:45
  9.5 159.6 %all-gather.3.cloned.1.call-start = ((), (), s32[]{:S(2)}) async-start(), calls=%async_computation.1 | async-start | bytes 8912896 | tf_op jit(solution)/shard_map/all_gather | solution.py:44
  10.5 308.8 %reduce-scatter.4.cloned.1.call-start = ((), (), s32[]{:S(2)}) async-start(), calls=%async_computation.4 | async-start | bytes 8912896
  169.2 8.0 %copy-start.8 = (f32[288,2048]{1,0:T(8,128)S(1)}, f32[288,2048]{1,0:T(8,128)}, u32[]{:S(2)}) copy-start(f32[288,2048]{1,0:T(8,128)} %get-tuple-element.22) | copy-start | bytes 7077892
  187.4 4.1 copy-start.2
  187.4 4.1 copy-start.9
  187.4 4.1 copy-start.11
  211.2 110.2 %copy-start.6 = (f32[128,2048]{1,0:T(8,128)S(1)}, f32[128,2048]{1,0:T(8,128)}, u32[]{:S(2)}) copy-start(f32[128,2048]{1,0:T(8,128)} %param.14) | copy-start | bytes 3145732
  211.2 110.5 %copy-start.7 = (f32[128,2048]{1,0:T(8,128)S(1)}, f32[128,2048]{1,0:T(8,128)}, u32[]{:S(2)}) copy-start(f32[128,2048]{1,0:T(8,128)} %param.15) | copy-start | bytes 3145732
  211.2 249.4 %all-reduce.2.cloned.1.call-start = ((), (), s32[]{:S(2)}) async-start(), calls=%async_computation.3 | async-start | bytes 1048576 | tf_op jit(solution)/shard_map/psum | solution.py:70
  464.6 5.3 %copy-start.4 = (f32[128,2048]{0,1:T(8,128)S(1)}, f32[128,2048]{0,1:T(8,128)}, u32[]{:S(2)}) copy-start(f32[128,2048]{0,1:T(8,128)} %get-tuple-element.18) | copy-start | bytes 3145732
  467.2 4.0 copy-start.3
  467.2 5.3 %copy-start.1 = (bf16[288,2048]{1,0:T(8,128)(2,1)S(1)}, bf16[288,2048]{1,0:T(8,128)(2,1)}, u32[]{:S(2)}) copy-start(bf16[288,2048]{1,0:T(8,128)(2,1)} %param.10) | copy-start | bytes 3538948
Sparse Core Ops, SparseCore 0:
  11.4 78.4 all-gather.4
  93.3 75.8 all-gather.2
  211.3 107.8 reduce-scatter.3
  322.3 138.3 all-reduce.1
where the time goes:
time: 480 us; the launch traced here: 479 us
  waiting for transfers between devices  393 us (82%)
  local copies, waits for them, and re-layouts  37.3 us (8%)
  matrix products  23 us (5%)
  between operations  13.9 us (3%)
  other arithmetic  11.4 us (2%)
    psum x1, waiting for transfers between devices, shards(): grad = lax.psum(shard_grad, 'dp').astype(jnp.float32)  135 us
    unnamed x5, waiting for transfers between devices  108 us
    all_gather x1, waiting for transfers between devices, shards(): lax.all_gather(teacher_copy, 'fsdp', axis=0, tiled=True)  79.2 us
    all_gather x1, waiting for transfers between devices, shards(): lax.all_gather(student_copy, 'fsdp', axis=0, tiled=True)  71.4 us
    unnamed x38, local copies, waits for them, and re-layouts  27.1 us
    dot_general x2, matrix products, add_rows(): return jnp.dot(mixture, piece, preferred_element_type=jnp.float32)  15.8 us
    gather x2, local copies, waits for them, and re-layouts, shards(): jnp.take_along_axis(teacher_norm.reshape(crop_count, PATCHES, DOUT), posi...  10.1 us
  transfers between devices with their start and end apart: 4, of which 4 were waited for; matrix products, arithmetic and copies ran while one was open for 3% of the time, Pallas kernels for 0%

commit v1 on v0

v1 whole, which is shorter than its diff:
```python
import functools

import jax
import jax.numpy as jnp
from jax import lax
from jax.experimental import pallas as pl
from jax.experimental.pallas import tpu as pltpu
from jax.sharding import Mesh, PartitionSpec as P

KIN = 2048
DOUT = 2048
PATCHES = 144
EPS = 1e-06
AXES = ("z", "xlo", "y", "xhi", "core")
VMEM_LIMIT = 44 * 1024 * 1024

X_INDEX = (0, 2, 1, 3)
CORE_SWAP = ((0, 1), (1, 0))
X_NEAR = tuple((X_INDEX[a], X_INDEX[b]) for a, b in ((1, 2), (2, 1), (0, 3), (3, 0)))


def from_next(size):
    return tuple(((i + 1) % size, i) for i in range(size))


def from_previous(size):
    return tuple((i, (i + 1) % size) for i in range(size))


def swap_cores(value):
    return lax.ppermute(value, "core", CORE_SWAP)


def from_y_next(value):
    return lax.ppermute(value, "y", from_next(4))


def from_y_previous(value):
    return lax.ppermute(value, "y", from_previous(4))


def from_x_near(value):
    return lax.ppermute(value, ("xlo", "xhi"), X_NEAR)


def from_z_next(value):
    return lax.ppermute(value, "z", from_next(8))


def from_z_previous(value):
    return lax.ppermute(value, "z", from_previous(8))


def from_x_twin(value):
    return lax.ppermute(value, "xlo", CORE_SWAP)


def gather_rows(own, other):
    first = {(0, 0): own}
    first[1, 0] = from_y_next(own)
    first[3, 0] = from_y_previous(own)
    first[0, 1] = from_x_near(own)
    first[2, 0] = from_y_next(first[1, 0])
    first[3, 1] = from_y_previous(first[0, 1])
    first[1, 1] = from_x_near(first[1, 0])
    last_student = from_y_next(first[1, 1][0])
    last_teacher = from_y_previous(first[3, 1][1])

    second = {(0, 0): other}
    second[1, 0] = from_z_next(first[1, 0])
    second[3, 0] = from_z_previous(first[3, 0])
    second[0, 1] = from_x_twin(first[0, 1])
    second[2, 0] = from_z_next(first[2, 0])
    second[3, 1] = from_x_twin(first[3, 1])
    second[1, 1] = from_z_previous(first[1, 1])
    other_student = from_z_next(last_student)
    other_teacher = from_z_previous(last_teacher)

    pieces = []
    for group, student, teacher in ((first, last_student, last_teacher), (second, other_student, other_teacher)):
        for dy in range(4):
            for dx in range(2):
                if (dy, dx) == (2, 1):
                    pieces.append((student, teacher))
                else:
                    pieces.append(group[dy, dx])
    return pieces


def forward_kernel(layout, order, student_mix, teacher_mix, residual, scale, positions, *refs):
    count = sum(2 if split else 1 for split in layout)
    weights, (student_out, matched_out, sums_out, held) = refs[:count], refs[count:]
    at = 0
    for block, split in enumerate(layout):
        rows = pl.ds(pl.multiple_of(order[block] * 128, 128), 128)
        if split:
            held[0, rows, :] = weights[at][...]
            held[1, rows, :] = weights[at + 1][...]
            at += 2
        else:
            held[0, rows, :] = weights[at][0]
            held[1, rows, :] = weights[at][1]
            at += 1
    inverse_root = KIN ** (-0.5)
    base = residual[...].astype(jnp.float32)
    factor = scale[...]
    student = base + factor * (
        jnp.dot(student_mix[...], held[0], preferred_element_type=jnp.float32) * inverse_root
    )
    teacher = base + factor * (
        jnp.dot(teacher_mix[...], held[1], preferred_element_type=jnp.float32) * inverse_root
    )
    high = teacher.astype(jnp.bfloat16)
    low = (teacher - high.astype(jnp.float32)).astype(jnp.bfloat16)
    lane = lax.broadcasted_iota(jnp.int32, (PATCHES, PATCHES), 1)
    parts = []
    for crop in range(student.shape[0] // PATCHES):
        rows = slice(crop * PATCHES, (crop + 1) * PATCHES)
        pick = (positions[rows, :] == lane).astype(jnp.float32).astype(jnp.bfloat16)
        parts.append(
            jnp.dot(pick, high[rows], preferred_element_type=jnp.float32)
            + jnp.dot(pick, low[rows], preferred_element_type=jnp.float32)
        )
    matched = jnp.concatenate(parts, axis=0)
    student_out[...] = student
    matched_out[...] = matched
    spot = lax.broadcasted_iota(jnp.int32, sums_out.shape, 1)
    sums = jnp.where(
        spot == 0,
        jnp.sum(student * student, axis=-1, keepdims=True),
        jnp.where(
            spot == 1,
            jnp.sum(matched * matched, axis=-1, keepdims=True),
            jnp.where(spot == 2, jnp.sum(student * matched, axis=-1, keepdims=True), 0.0),
        ),
    )

    @pl.when(pl.program_id(0) == 0)
    def _():
        sums_out[...] = sums

    @pl.when(pl.program_id(0) != 0)
    def _():
        sums_out[...] += sums


def forward(order, pieces, student_mix, teacher_mix, residual, scale, positions):
    rows, columns, width = student_mix.shape[0], scale.shape[1], 256
    layout, weights, weight_specs = [], [], []
    for piece in pieces:
        if isinstance(piece, tuple):
            layout.append(True)
            weights.extend(piece)
            weight_specs.extend([pl.BlockSpec((128, width), lambda j, order: (0, j))] * 2)
        else:
            layout.append(False)
            weights.append(piece)
            weight_specs.append(pl.BlockSpec((2, 128, width), lambda j, order: (0, 0, j)))
    whole = pl.BlockSpec((rows, KIN), lambda j, order: (0, 0))
    column = pl.BlockSpec((rows, width), lambda j, order: (0, j))
    return pl.pallas_call(
        functools.partial(forward_kernel, tuple(layout)),
        grid_spec=pltpu.PrefetchScalarGridSpec(
            num_scalar_prefetch=1,
            grid=(columns // width,),
            in_specs=[
                whole,
                whole,
                column,
                pl.BlockSpec((1, width), lambda j, order: (0, j)),
                pl.BlockSpec((rows, 1), lambda j, order: (0, 0)),
            ]
            + weight_specs,
            out_specs=[column, column, pl.BlockSpec((rows, 128), lambda j, order: (0, 0))],
            scratch_shapes=[pltpu.VMEM((2, KIN, width), jnp.bfloat16)],
        ),
        out_shape=[
            jax.ShapeDtypeStruct((rows, columns), jnp.float32),
            jax.ShapeDtypeStruct((rows, columns), jnp.float32),
            jax.ShapeDtypeStruct((rows, 128), jnp.float32),
        ],
        compiler_params=pltpu.CompilerParams(vmem_limit_bytes=VMEM_LIMIT),
        cost_estimate=pl.CostEstimate(
            flops=4 * rows * KIN * columns, bytes_accessed=20 * 1024 * 1024, transcendentals=0
        ),
    )(order, student_mix, teacher_mix, residual, scale, positions, *weights)


def backward_kernel(total_tokens, student, matched, sums, more_sums, scale, mix, grad_out, tokens_out, held):
    @pl.when(pl.program_id(0) == 0)
    def _():
        own = more_sums.shape[0] // 2
        swapped = jnp.concatenate([more_sums[own:, :], more_sums[:own, :]], axis=0)
        total = (sums[...] + swapped) * (1.0 / DOUT)
        inverse_rms = lax.rsqrt(total[:, 0:1] + EPS)
        inverse_matched = lax.rsqrt(total[:, 1:2] + EPS)
        overlap = inverse_rms * inverse_matched * total[:, 2:3]
        shared = inverse_rms * (1.0 / total_tokens)
        student_part = shared * inverse_rms * (EPS * inverse_rms * inverse_rms + overlap)
        matched_part = shared * inverse_matched
        values = student[...]
        tokens_out[...] = (values * inverse_rms).astype(jnp.bfloat16)
        factor = scale[...] * (KIN ** (-0.5))
        held[...] = (factor * (values * student_part - matched[...] * matched_part)).astype(jnp.bfloat16)

    grad_out[...] = jnp.dot(mix[...], held[...], preferred_element_type=jnp.float32).astype(jnp.bfloat16)


def backward(total_tokens, student, matched, sums, more_sums, scale, mix):
    rows, columns = student.shape
    depth = 256
    whole = pl.BlockSpec((rows, columns), lambda i: (0, 0))
    narrow = pl.BlockSpec((rows, 128), lambda i: (0, 0))
    return pl.pallas_call(
        functools.partial(backward_kernel, total_tokens),
        grid=(KIN // depth,),
        in_specs=[
            whole,
            whole,
            narrow,
            narrow,
            pl.BlockSpec((1, columns), lambda i: (0, 0)),
            pl.BlockSpec((depth, rows), lambda i: (i, 0)),
        ],
        out_specs=[pl.BlockSpec((depth, columns), lambda i: (i, 0)), whole],
        out_shape=[
            jax.ShapeDtypeStruct((KIN, columns), jnp.bfloat16),
            jax.ShapeDtypeStruct((rows, columns), jnp.bfloat16),
        ],
        scratch_shapes=[pltpu.VMEM((rows, columns), jnp.bfloat16)],
        compiler_params=pltpu.CompilerParams(vmem_limit_bytes=VMEM_LIMIT),
        cost_estimate=pl.CostEstimate(
            flops=2 * rows * KIN * columns, bytes_accessed=12 * 1024 * 1024, transcendentals=0
        ),
    )(student, matched, sums, more_sums, scale, mix)


def adamw_update(grad, weight, teacher, first, squares):
    first_next = 0.9 * first + 0.1 * grad
    squares_next = 0.95 * squares + 0.05 * grad * grad
    weight_next = weight - 0.1 * (first_next / (jnp.sqrt(squares_next) + 1e-08) + 0.04 * weight)
    teacher_next = 0.96 * teacher + 0.04 * weight_next
    return (weight_next, teacher_next, first_next, squares_next)


def join_columns(core, own, other):
    return jnp.where(
        core == 0, jnp.concatenate([own, other], axis=-1), jnp.concatenate([other, own], axis=-1)
    )


def shards(
    residual,
    student_mix,
    teacher_mix,
    positions,
    layer_scale,
    student_weight,
    teacher_weight,
    moment,
    second,
):
    half = DOUT // 2
    token_count = student_mix.shape[0]
    total_tokens = token_count * 256
    z, xlo, y, xhi, core = (lax.axis_index(name) for name in AXES)
    parity = (z + (xhi ^ xlo)) & 1

    def columns_of(value, which):
        return lax.dynamic_slice_in_dim(value, which * half, half, axis=-1)

    copies = jnp.stack([student_weight, teacher_weight]).astype(jnp.bfloat16)
    mine = columns_of(copies, core)
    theirs = swap_cores(columns_of(copies, 1 - core))
    fetched = jnp.where(core == parity, mine, theirs)
    passed = jnp.where(core == parity, theirs, mine)
    pieces = gather_rows(fetched, passed)
    order = jnp.stack(
        [
            (((y + dy) & 3) * 2 + (xhi ^ dx)) * 2 + (parity ^ side)
            for side in range(2)
            for dy in range(4)
            for dx in range(2)
        ]
    ).astype(jnp.int32)

    student_rows = jnp.concatenate([student_mix, swap_cores(student_mix)], axis=0)
    teacher_rows = jnp.concatenate([teacher_mix, swap_cores(teacher_mix)], axis=0)
    residual_rows = jnp.concatenate(
        [columns_of(residual, core), swap_cores(columns_of(residual, 1 - core))], axis=0
    )
    places = jnp.concatenate([positions, swap_cores(positions)], axis=0).reshape(2 * token_count, 1)
    scale = columns_of(layer_scale, core).reshape(1, half)

    student_out, matched, sums = forward(
        order, pieces, student_rows, teacher_rows, residual_rows, scale, places
    )
    grads, tokens = backward(
        total_tokens, student_out, matched, sums, swap_cores(sums), scale, student_rows.T
    )

    student_tokens = join_columns(core, tokens[:token_count], swap_cores(tokens[token_count:]))

    by_chip = lax.all_to_all(grads.reshape(8, 256, half), ("y", "xhi"), 0, 0)
    chip_rows = jnp.sum(by_chip.astype(jnp.float32), axis=0).astype(jnp.bfloat16)
    by_copy = lax.all_to_all(chip_rows.reshape(16, 16, half), ("z", "xlo"), 0, 0)
    copy_rows = jnp.sum(by_copy.astype(jnp.float32), axis=0).astype(jnp.bfloat16)
    full = lax.all_to_all(
        jnp.broadcast_to(copy_rows[None], (16, 16, half)), ("z", "xlo"), 0, 0
    ).reshape(256, half)
    own_rows = lax.dynamic_slice_in_dim(full, core * 128, 128, axis=0)
    other_rows = lax.dynamic_slice_in_dim(full, (1 - core) * 128, 128, axis=0)
    grad = join_columns(core, own_rows, swap_cores(other_rows)).astype(jnp.float32)
    weight_next, teacher_next, first_next, squares_next = adamw_update(
        grad, student_weight, teacher_weight, moment, second
    )
    return (weight_next, teacher_next, first_next, squares_next, student_tokens)


def solution(mesh):
    split = Mesh(mesh.devices.reshape(8, 2, 4, 2, 2), AXES)
    tokens = P(AXES, None)
    owned = P(("y", "xhi", "core"), None)
    return jax.shard_map(
        shards,
        mesh=split,
        in_specs=(tokens, tokens, tokens, tokens, P(), owned, owned, owned, owned),
        out_specs=(owned, owned, owned, owned, tokens),
        check_vma=False,
    )
```

time: 480 us -> 210 us (0.44)
  waiting for transfers between devices: 393 us -> 37.3 us
  blocking collectives: 0 us -> 77.7 us
  starting transfers between devices: 0.34 us -> 31.1 us
  matrix products: 23 us -> 0 us
  local copies, waits for them, and re-layouts: 37.3 us -> 16.9 us
  Pallas kernels: 0 us -> 20.1 us
  between operations: 13.9 us -> 0.92 us
  other arithmetic: 11.4 us -> 21.8 us
    all_gather x2 -> x0, waiting for transfers between devices: 151 us -> none  [the longest x1 79.2 us: shards(): lax.all_gather(teacher_copy, 'fsdp', axis=0, tiled=True)]
    psum x1 -> x0, waiting for transfers between devices: 135 us -> none  [shards(): grad = lax.psum(shard_grad, 'dp').astype(jnp.float32)]
    unnamed x5 -> x0, waiting for transfers between devices: 108 us -> none
    all_to_all x0 -> x2, blocking collectives: none -> 77.7 us  [the longest x1 55.4 us: shards(): by_chip = lax.all_to_all(grads.reshape(8, 256, half), ('y', 'xhi'), 0, 0)]
    ppermute x0 -> x24, starting transfers between devices: none -> 26.9 us  [the longest x3 9.52 us: from_z_next(): return lax.ppermute(value, 'z', from_next(8))]
    ppermute x0 -> x24, waiting for transfers between devices: none -> 23.9 us  [the longest x3 9.61 us: from_y_next(): return lax.ppermute(value, 'y', from_next(4))]
    unnamed x38 -> x29, local copies, waits for them, and re-layouts: 27.1 us -> 3.27 us
    dot_general x3 -> x0, matrix products: 23 us -> none  [the longest x2 15.8 us: add_rows(): return jnp.dot(mixture, piece, preferred_element_type=jnp.float32)]
  transfers between devices with their start and end apart: 4 -> 25, of which waited for: 4 -> 11; matrix products, arithmetic and copies ran while one was open for 3% -> 14% of each run, Pallas kernels for 0% -> 0%
where the time goes in v1:
time: 210 us; the launch traced here: 206 us
  blocking collectives  77.7 us (37%)
  waiting for transfers between devices  37.3 us (18%)
  starting transfers between devices  31.1 us (15%)
  other arithmetic  21.8 us (10%)
  Pallas kernels  20.1 us (10%)
  local copies, waits for them, and re-layouts  16.9 us (8%)
    all_to_all x1, blocking collectives, shards(): by_chip = lax.all_to_all(grads.reshape(8, 256, half), ('y', 'xhi'), 0, 0)  55.4 us
    all_to_all x1, blocking collectives, shards(): lax.all_to_all(chip_rows.reshape(16, 16, half), ('z', 'xlo'), 0, 0)  22.3 us
    all_to_all x1, waiting for transfers between devices, shards(): lax.all_to_all(jnp.broadcast_to(copy_rows[None], (16, 16, half)), ('z', '...  13.4 us
    pallas_call x1, Pallas kernels, forward(): pl.pallas_call(functools.partial(forward_kernel, tuple(layout)), grid_spe...  13.1 us
    ppermute x3, waiting for transfers between devices, from_y_next(): return lax.ppermute(value, 'y', from_next(4))  9.61 us
    ppermute x3, starting transfers between devices, from_z_next(): return lax.ppermute(value, 'z', from_next(8))  9.52 us
    ppermute x3, waiting for transfers between devices, from_z_previous(): return lax.ppermute(value, 'z', from_previous(8))  8.04 us
    ppermute x3, starting transfers between devices, from_y_next(): return lax.ppermute(value, 'y', from_next(4))  7.89 us
  transfers between devices with their start and end apart: 25, of which 11 were waited for; matrix products, arithmetic and copies ran while one was open for 14% of the time, Pallas kernels for 0%

profile of v1, /device:TPU:4, one launch (start us, length us, event | category | flops | bytes accessed | tf_op | source)
XLA Modules:
  0.0 205.8 jit_solution(10936377332310378645)
XLA Ops:
  5.9 3.1 %collective-permute-start.6 = (bf16[2,128,1024]{2,1,0:T(8,128)(2,1)S(1)}, bf16[2,128,1024]{2,1,0:T(8,128)(2,1)}, u32[]{:S(2)}, u32[]{:S(2)}) collective-permute-start(bf16[2,128,1024]{2,1,0:T(8,128)(2,1)S(1)} %get-tuple-element.20.refs_0_), channel_id=1, source_target_pairs={{4,0},{8,4},{12,8},{0,12},{5,1},{9,5},{13,9},{1,13},{6,2},{10,6},{... | collective-permute-start | bytes 1572872 | tf_op jit(solution)/shard_map/ppermute | solution.py:35
  10.9 9.6 %collective-permute-done.6.refs_2_ = bf16[2,128,1024]{2,1,0:T(8,128)(2,1)} collective-permute-done((bf16[2,128,1024]{2,1,0:T(8,128)(2,1)S(1)}, bf16[2,128,1024]{2,1,0:T(8,128)(2,1)}, u32[]{:S(2)}, u32[]{:S(2)}) %collective-permute-start.6) | collective-permute-done | bytes 524320 | tf_op jit(solution)/shard_map/ppermute | solution.py:35
  22.8 2.5 %copy.25 = bf16[288,2048]{0,1:T(8,128)(2,1)} copy(bf16[288,2048]{1,0:T(8,128)(2,1)} %param.10) | data formatting | bytes 2359296 | tf_op args[1]
  26.8 5.9 %collective-permute-start.14 = (bf16[2,128,1024]{2,1,0:T(8,128)(2,1)}, bf16[2,128,1024]{2,1,0:T(8,128)(2,1)}, u32[]{:S(2)}, u32[]{:S(2)}) collective-permute-start(bf16[2,128,1024]{2,1,0:T(8,128)(2,1)} %collective-permute-done.6.refs_2_), channel_id=1, source_target_pairs={{32,0},{64,32},{96,64},{128,96},{160,128},{192,160},{224,192},{0,2... | collective-permute-start | bytes 1572872 | tf_op jit(solution)/shard_map/ppermute | solution.py:47
  32.6 2.2 %collective-permute-start.8 = (bf16[2,128,1024]{2,1,0:T(8,128)(2,1)}, bf16[2,128,1024]{2,1,0:T(8,128)(2,1)}, u32[]{:S(2)}, u32[]{:S(2)}) collective-permute-start(bf16[2,128,1024]{2,1,0:T(8,128)(2,1)} %collective-permute-done.6.refs_2_), channel_id=1, source_target_pairs={{4,0},{8,4},{12,8},{0,12},{5,1},{9,5},{13,9},{1,13},{6,2},{10,6},{... | collective-permute-start | bytes 1572872 | tf_op jit(solution)/shard_map/ppermute | solution.py:35
  34.9 2.4 %collective-permute-start.13 = (bf16[2,128,1024]{2,1,0:T(8,128)(2,1)}, bf16[2,128,1024]{2,1,0:T(8,128)(2,1)}, u32[]{:S(2)}, u32[]{:S(2)}) collective-permute-start(bf16[2,128,1024]{2,1,0:T(8,128)(2,1)} %collective-permute-done.5.refs_1_), channel_id=1, source_target_pairs={{0,16},{16,0},{1,17},{17,1},{2,18},{18,2},{3,19},{19,3},{4,20},{20... | collective-permute-start | bytes 1572872 | tf_op jit(solution)/shard_map/ppermute | solution.py:55
  37.5 1.9 collective-permute-start.19
  40.8 2.6 %copy.26 = bf16[288,2048]{0,1:T(8,128)(2,1)} copy(bf16[288,2048]{1,0:T(8,128)(2,1)} %collective-permute-done) | data formatting | bytes 2359296 | tf_op jit(solution)/shard_map/ppermute | solution.py:31
  45.7 2.6 %collective-permute-start.9 = (bf16[128,1024]{1,0:T(8,128)(2,1)}, bf16[128,1024]{1,0:T(8,128)(2,1)S(1)}, u32[]{:S(2)}, u32[]{:S(2)}) collective-permute-start(bf16[128,1024]{1,0:T(8,128)(2,1)} %slice_bitcast_fusion.1), channel_id=1, source_target_pairs={{4,0},{8,4},{12,8},{0,12},{5,1},{9,5},{13,9},{1,13},{6,2},{10,6},{... | collective-permute-start | bytes 786440 | tf_op jit(solution)/shard_map/ppermute | solution.py:35
  48.3 6.1 %collective-permute-done.19.refs_16_ = bf16[2,128,1024]{2,1,0:T(8,128)(2,1)} collective-permute-done((bf16[2,128,1024]{2,1,0:T(8,128)(2,1)}, bf16[2,128,1024]{2,1,0:T(8,128)(2,1)}, u32[]{:S(2)}, u32[]{:S(2)}) %collective-permute-start.19) | collective-permute-done | bytes 524320 | tf_op jit(solution)/shard_map/ppermute | solution.py:51
  56.0 3.1 %collective-permute-start.16 = (bf16[2,128,1024]{2,1,0:T(8,128)(2,1)}, bf16[2,128,1024]{2,1,0:T(8,128)(2,1)}, u32[]{:S(2)}, u32[]{:S(2)}) collective-permute-start(bf16[2,128,1024]{2,1,0:T(8,128)(2,1)} %collective-permute-done.8.refs_4_), channel_id=1, source_target_pairs={{32,0},{64,32},{96,64},{128,96},{160,128},{192,160},{224,192},{0,2... | collective-permute-start | bytes 1572872 | tf_op jit(solution)/shard_map/ppermute | solution.py:47
  59.1 4.3 %pad_maximum_fusion = bf16[576,2048]{0,1:T(8,128)(2,1)} fusion(bf16[288,2048]{0,1:T(8,128)(2,1)} %copy.26, bf16[288,2048]{0,1:T(8,128)(2,1)} %copy.25), kind=kLoop, calls=%fused_computation | loop fusion | flops 4718592 | bytes 4718592 | tf_op jit(solution)/shard_map/concatenate | solution.py:287
  63.5 4.4 %copy.27.student_mix = bf16[576,2048]{1,0:T(8,128)(2,1)} copy(bf16[576,2048]{0,1:T(8,128)(2,1)} %pad_maximum_fusion) | data formatting | bytes 4718592 | tf_op jit(solution)/shard_map/concatenate | solution.py:287
  69.9 3.4 %pad_maximum_fusion.1.teacher_mix = bf16[576,2048]{1,0:T(8,128)(2,1)} fusion(bf16[288,2048]{1,0:T(8,128)(2,1)} %collective-permute-done.1, bf16[288,2048]{1,0:T(8,128)(2,1)} %param.11), kind=kLoop, calls=%fused_computation.1 | loop fusion | flops 4718592 | bytes 4718592 | tf_op jit(solution)/shard_map/concatenate | solution.py:288
  74.3 2.0 collective-permute-done.18.refs_15_
  76.3 13.1 %shard_map.128 = (f32[576,1024]{1,0:T(8,128)}, f32[576,1024]{1,0:T(8,128)}, f32[576,128]{1,0:T(8,128)S(1)}) custom-call(s32[16]{0:T(128)S(1)} %stack.79.order, bf16[576,2048]{1,0:T(8,128)(2,1)} %copy.27.student_mix, bf16[576,2048]{1,0:T(8,128)(2,1)} %pad_maximum_fusion.1.teacher_mix, bf16[576,1024]{1,0:T(8,128)(2,1)S(1)} %pad_maximum_fusion.2.residual, ...), custom_call_target="tpu_custom_call" | custom-call | flops 4831838208 | bytes 20971520 | tf_op jit(solution)/shard_map/pallas_call | solution.py:161
  91.8 7.0 %shard_map.129 = (bf16[2048,1024]{1,0:T(8,128)(2,1)}, bf16[576,1024]{1,0:T(8,128)(2,1)S(1)}) custom-call(f32[576,1024]{1,0:T(8,128)S(1)} %copy-done.2, f32[576,1024]{1,0:T(8,128)S(1)} %copy-done.3, f32[576,128]{1,0:T(8,128)S(1)} %get-tuple-element.12.sums, f32[576,128]{1,0:T(8,128)S(1)} %collective-permute-done.21.more_sums, f32[1,1024]{1,0:T(1,128)S(1)} %bitcast.31, ...), custom_call_target="tpu_custom_call" | custom-call | flops 2415919104 | bytes 12582912 | tf_op jit(solution)/shard_map/pallas_call | solution.py:214
  98.7 55.4 %all_to_all.15 = bf16[8,256,1024]{2,1,0:T(8,128)(2,1)} all-to-all(bf16[8,256,1024]{2,1,0:T(8,128)(2,1)} %bitcast.32), channel_id=1, replica_groups=mesh['z'=8,'xlo'=2,'y'=4,'xhi'=2,'core'=2] {'y','xhi'}, dimensions={0} | all-to-all | bytes 8388608 | tf_op jit(solution)/shard_map/all_to_all | solution.py:304
  154.2 3.1 %reduce_sum.24 = bf16[256,1024]{1,0:T(8,128)(2,1)S(1)} reduce(bf16[8,256,1024]{2,1,0:T(8,128)(2,1)} %all_to_all.15, bf16[]{:T(256)} %constant.46.clone.1), dimensions={0}, to_apply=%region_0.1 | reduce | flops 1835008 | bytes 4718594 | tf_op jit(solution)/shard_map/reduce_sum | solution.py:305
  157.3 22.3 %all_to_all.16 = bf16[16,16,1024]{2,1,0:T(8,128)(2,1)S(1)} all-to-all(bf16[16,16,1024]{2,1,0:T(8,128)(2,1)S(1)} %bitcast.33), channel_id=1, replica_groups=mesh['z'=8,'xlo'=2,'y'=4,'xhi'=2,'core'=2] {'z','xlo'}, dimensions={0} | all-to-all | bytes 1048576 | tf_op jit(solution)/shard_map/all_to_all | solution.py:306
  180.5 4.2 %all-to-all-start.2 = ((bf16[16,16,1024]{2,1,0:T(8,128)(2,1)}), bf16[16,16,1024]{2,1,0:T(8,128)(2,1)}, u32[]{:S(2)}, u32[]{:S(2)}) async-start(bf16[16,16,1024]{2,1,0:T(8,128)(2,1)} %broadcast_in_dim.2), calls=%async_computation.2 | async-start | bytes 1048576 | tf_op jit(solution)/shard_map/all_to_all | solution.py:308
  185.6 13.4 %all-to-all-done.2 = bf16[16,16,1024]{2,1,0:T(8,128)(2,1)} async-done(((bf16[16,16,1024]{2,1,0:T(8,128)(2,1)}), bf16[16,16,1024]{2,1,0:T(8,128)(2,1)}, u32[]{:S(2)}, u32[]{:S(2)}) %all-to-all-start.2) | async-done | bytes 524320 | tf_op jit(solution)/shard_map/all_to_all | solution.py:308
  200.3 2.9 %maximum_select_fusion = bf16[288,2048]{1,0:T(8,128)(2,1)} fusion(bf16[288,1024]{1,0:T(8,128)(2,1)} %collective-permute-done.23, bf16[288,1024]{1,0:T(8,128)(2,1)S(1)} %get-tuple-element.21, pred[]{:T(512)S(6)} %eq.8), kind=kLoop, calls=%fused_computation.9 | loop fusion | flops 5308416 | bytes 2359297 | tf_op jit(solution)/shard_map/jit(_where)/select_n | solution.py:247
  203.1 2.7 %multiply_add_fusion = (f32[128,2048]{1,0:T(8,128)}, f32[128,2048]{1,0:T(8,128)}, f32[128,2048]{1,0:T(8,128)}, f32[128,2048]{1,0:T(8,128)}) fusion(f32[128,2048]{1,0:T(8,128)S(1)} %copy-done.6, f32[128,2048]{1,0:T(8,128)S(1)} %copy-done.7, bf16[128,1024]{1,0:T(8,128)(2,1)S(1)} %get-tuple-element.26, bf16[128,1024]{1,0:T(8,128)(2,1)S(1)} %collective-permute-done.22, ...), kind=kLoop, calls=%fused_computation.12 | loop fusion | flops 6815744 | bytes 8912897 | tf_op jit(solution)/shard_map/add | solution.py:242
  (82 shorter events, 24.7 us)
Async XLA Ops:
  2.5 2.1 %collective-permute-start.4 = (bf16[2,128,1024]{2,1,0:T(8,128)(2,1)S(1)}, bf16[2,128,1024]{2,1,0:T(8,128)(2,1)}, u32[]{:S(2)}, u32[]{:S(2)}) collective-permute-start(bf16[2,128,1024]{2,1,0:T(8,128)(2,1)S(1)} %fusion.2), channel_id=1, source_target_pairs={{0,1},{1,0},{2,3},{3,2},{4,5},{5,4},{6,7},{7,6},{8,9},{9,8},{10,11... | collective-permute-start | bytes 1572872 | tf_op jit(solution)/shard_map/ppermute | solution.py:31
  3.7 7.2 %collective-permute-start.2 = (bf16[288,1024]{1,0:T(8,128)(2,1)}, bf16[288,1024]{1,0:T(8,128)(2,1)S(1)}, u32[]{:S(2)}, u32[]{:S(2)}) collective-permute-start(bf16[288,1024]{1,0:T(8,128)(2,1)} %get-tuple-element.24), channel_id=1, source_target_pairs={{0,1},{1,0},{2,3},{3,2},{4,5},{5,4},{6,7},{7,6},{8,9},{9,8},{10,11... | collective-permute-start | bytes 1769480 | tf_op jit(solution)/shard_map/ppermute | solution.py:31
  4.2 28.4 %collective-permute-start = (bf16[288,2048]{1,0:T(8,128)(2,1)}, bf16[288,2048]{1,0:T(8,128)(2,1)}, u32[]{:S(2)}, u32[]{:S(2)}) collective-permute-start(bf16[288,2048]{1,0:T(8,128)(2,1)} %param.10), channel_id=1, source_target_pairs={{0,1},{1,0},{2,3},{3,2},{4,5},{5,4},{6,7},{7,6},{8,9},{9,8},{10,11... | collective-permute-start | bytes 3538952 | tf_op jit(solution)/shard_map/ppermute | solution.py:31
  5.9 14.6 %collective-permute-start.6 = (bf16[2,128,1024]{2,1,0:T(8,128)(2,1)S(1)}, bf16[2,128,1024]{2,1,0:T(8,128)(2,1)}, u32[]{:S(2)}, u32[]{:S(2)}) collective-permute-start(bf16[2,128,1024]{2,1,0:T(8,128)(2,1)S(1)} %get-tuple-element.20.refs_0_), channel_id=1, source_target_pairs={{4,0},{8,4},{12,8},{0,12},{5,1},{9,5},{13,9},{1,13},{6,2},{10,6},{... | collective-permute-start | bytes 1572872 | tf_op jit(solution)/shard_map/ppermute | solution.py:35
  9.0 13.8 %collective-permute-start.5 = (bf16[2,128,1024]{2,1,0:T(8,128)(2,1)S(1)}, bf16[2,128,1024]{2,1,0:T(8,128)(2,1)}, u32[]{:S(2)}, u32[]{:S(2)}) collective-permute-start(bf16[2,128,1024]{2,1,0:T(8,128)(2,1)S(1)} %get-tuple-element.20.refs_0_), channel_id=1, source_target_pairs={{16,2},{2,16},{0,18},{18,0},{17,3},{3,17},{1,19},{19,1},{20,6},{6,... | collective-permute-start | bytes 1572872 | tf_op jit(solution)/shard_map/ppermute | solution.py:43
  10.7 35.0 %collective-permute-start.1 = (bf16[288,2048]{1,0:T(8,128)(2,1)}, bf16[288,2048]{1,0:T(8,128)(2,1)}, u32[]{:S(2)}, u32[]{:S(2)}) collective-permute-start(bf16[288,2048]{1,0:T(8,128)(2,1)} %param.11), channel_id=1, source_target_pairs={{0,1},{1,0},{2,3},{3,2},{4,5},{5,4},{6,7},{7,6},{8,9},{9,8},{10,11... | collective-permute-start | bytes 3538952 | tf_op jit(solution)/shard_map/ppermute | solution.py:31
  10.9 15.9 %collective-permute-start.12 = (bf16[2,128,1024]{2,1,0:T(8,128)(2,1)S(1)}, bf16[2,128,1024]{2,1,0:T(8,128)(2,1)}, u32[]{:S(2)}, u32[]{:S(2)}) collective-permute-start(bf16[2,128,1024]{2,1,0:T(8,128)(2,1)S(1)} %get-tuple-element.20.refs_0_), channel_id=1, source_target_pairs={{0,4},{4,8},{8,12},{12,0},{1,5},{5,9},{9,13},{13,1},{2,6},{6,10},{... | collective-permute-start | bytes 1572872 | tf_op jit(solution)/shard_map/ppermute | solution.py:39
  20.5 14.4 %collective-permute-start.7 = (bf16[2,128,1024]{2,1,0:T(8,128)(2,1)}, bf16[2,128,1024]{2,1,0:T(8,128)(2,1)S(1)}, u32[]{:S(2)}, u32[]{:S(2)}) collective-permute-start(bf16[2,128,1024]{2,1,0:T(8,128)(2,1)} %collective-permute-done.6.refs_2_), channel_id=1, source_target_pairs={{16,2},{2,16},{0,18},{18,0},{17,3},{3,17},{1,19},{19,1},{20,6},{6,... | collective-permute-start | bytes 1572872 | tf_op jit(solution)/shard_map/ppermute | solution.py:43
  22.8 14.7 %collective-permute-start.10 = (bf16[2,128,1024]{2,1,0:T(8,128)(2,1)}, bf16[2,128,1024]{2,1,0:T(8,128)(2,1)S(1)}, u32[]{:S(2)}, u32[]{:S(2)}) collective-permute-start(bf16[2,128,1024]{2,1,0:T(8,128)(2,1)} %collective-permute-done.5.refs_1_), channel_id=1, source_target_pairs={{0,4},{4,8},{8,12},{12,0},{1,5},{5,9},{9,13},{13,1},{2,6},{6,10},{... | collective-permute-start | bytes 1572872 | tf_op jit(solution)/shard_map/ppermute | solution.py:39
  26.8 27.6 %collective-permute-start.14 = (bf16[2,128,1024]{2,1,0:T(8,128)(2,1)}, bf16[2,128,1024]{2,1,0:T(8,128)(2,1)}, u32[]{:S(2)}, u32[]{:S(2)}) collective-permute-start(bf16[2,128,1024]{2,1,0:T(8,128)(2,1)} %collective-permute-done.6.refs_2_), channel_id=1, source_target_pairs={{32,0},{64,32},{96,64},{128,96},{160,128},{192,160},{224,192},{0,2... | collective-permute-start | bytes 1572872 | tf_op jit(solution)/shard_map/ppermute | solution.py:47
  32.6 21.8 %collective-permute-start.8 = (bf16[2,128,1024]{2,1,0:T(8,128)(2,1)}, bf16[2,128,1024]{2,1,0:T(8,128)(2,1)}, u32[]{:S(2)}, u32[]{:S(2)}) collective-permute-start(bf16[2,128,1024]{2,1,0:T(8,128)(2,1)} %collective-permute-done.6.refs_2_), channel_id=1, source_target_pairs={{4,0},{8,4},{12,8},{0,12},{5,1},{9,5},{13,9},{1,13},{6,2},{10,6},{... | collective-permute-start | bytes 1572872 | tf_op jit(solution)/shard_map/ppermute | solution.py:35
  34.9 21.1 %collective-permute-start.13 = (bf16[2,128,1024]{2,1,0:T(8,128)(2,1)}, bf16[2,128,1024]{2,1,0:T(8,128)(2,1)}, u32[]{:S(2)}, u32[]{:S(2)}) collective-permute-start(bf16[2,128,1024]{2,1,0:T(8,128)(2,1)} %collective-permute-done.5.refs_1_), channel_id=1, source_target_pairs={{0,16},{16,0},{1,17},{17,1},{2,18},{18,2},{3,19},{19,3},{4,20},{20... | collective-permute-start | bytes 1572872 | tf_op jit(solution)/shard_map/ppermute | solution.py:55
  37.5 16.9 %collective-permute-start.19 = (bf16[2,128,1024]{2,1,0:T(8,128)(2,1)}, bf16[2,128,1024]{2,1,0:T(8,128)(2,1)}, u32[]{:S(2)}, u32[]{:S(2)}) collective-permute-start(bf16[2,128,1024]{2,1,0:T(8,128)(2,1)} %collective-permute-done.12.refs_7_), channel_id=1, source_target_pairs={{0,32},{32,64},{64,96},{96,128},{128,160},{160,192},{192,224},{224... | collective-permute-start | bytes 1572872 | tf_op jit(solution)/shard_map/ppermute | solution.py:51
  45.7 22.1 %collective-permute-start.9 = (bf16[128,1024]{1,0:T(8,128)(2,1)}, bf16[128,1024]{1,0:T(8,128)(2,1)S(1)}, u32[]{:S(2)}, u32[]{:S(2)}) collective-permute-start(bf16[128,1024]{1,0:T(8,128)(2,1)} %slice_bitcast_fusion.1), channel_id=1, source_target_pairs={{4,0},{8,4},{12,8},{0,12},{5,1},{9,5},{13,9},{1,13},{6,2},{10,6},{... | collective-permute-start | bytes 786440 | tf_op jit(solution)/shard_map/ppermute | solution.py:35
  54.4 14.0 %collective-permute-start.11 = (bf16[128,1024]{1,0:T(8,128)(2,1)}, bf16[128,1024]{1,0:T(8,128)(2,1)}, u32[]{:S(2)}, u32[]{:S(2)}) collective-permute-start(bf16[128,1024]{1,0:T(8,128)(2,1)} %slice_bitcast_fusion), channel_id=1, source_target_pairs={{0,4},{4,8},{8,12},{12,0},{1,5},{5,9},{9,13},{13,1},{2,6},{6,10},{... | collective-permute-start | bytes 786440 | tf_op jit(solution)/shard_map/ppermute | solution.py:39
  54.4 21.8 %collective-permute-start.15 = (bf16[2,128,1024]{2,1,0:T(8,128)(2,1)S(1)}, bf16[2,128,1024]{2,1,0:T(8,128)(2,1)}, u32[]{:S(2)}, u32[]{:S(2)}) collective-permute-start(bf16[2,128,1024]{2,1,0:T(8,128)(2,1)S(1)} %collective-permute-done.7.refs_3_), channel_id=1, source_target_pairs={{0,32},{32,64},{64,96},{96,128},{128,160},{160,192},{192,224},{224... | collective-permute-start | bytes 1572872 | tf_op jit(solution)/shard_map/ppermute | solution.py:51
  54.4 21.8 %collective-permute-start.20 = (bf16[2,128,1024]{2,1,0:T(8,128)(2,1)}, bf16[2,128,1024]{2,1,0:T(8,128)(2,1)}, u32[]{:S(2)}, u32[]{:S(2)}) collective-permute-start(bf16[2,128,1024]{2,1,0:T(8,128)(2,1)} %copy-done), channel_id=1, source_target_pairs={{0,16},{16,0},{1,17},{17,1},{2,18},{18,2},{3,19},{19,3},{4,20},{20... | collective-permute-start | bytes 1572872 | tf_op jit(solution)/shard_map/ppermute | solution.py:55
  56.0 20.2 %collective-permute-start.16 = (bf16[2,128,1024]{2,1,0:T(8,128)(2,1)}, bf16[2,128,1024]{2,1,0:T(8,128)(2,1)}, u32[]{:S(2)}, u32[]{:S(2)}) collective-permute-start(bf16[2,128,1024]{2,1,0:T(8,128)(2,1)} %collective-permute-done.8.refs_4_), channel_id=1, source_target_pairs={{32,0},{64,32},{96,64},{128,96},{160,128},{192,160},{224,192},{0,2... | collective-permute-start | bytes 1572872 | tf_op jit(solution)/shard_map/ppermute | solution.py:47
  67.9 6.4 %collective-permute-start.17 = (bf16[128,1024]{1,0:T(8,128)(2,1)S(1)}, bf16[128,1024]{1,0:T(8,128)(2,1)S(1)}, u32[]{:S(2)}, u32[]{:S(2)}) collective-permute-start(bf16[128,1024]{1,0:T(8,128)(2,1)S(1)} %collective-permute-done.9.refs_5_), channel_id=1, source_target_pairs={{32,0},{64,32},{96,64},{128,96},{160,128},{192,160},{224,192},{0,2... | collective-permute-start | bytes 786440 | tf_op jit(solution)/shard_map/ppermute | solution.py:47
  68.4 7.8 %collective-permute-start.18 = (bf16[128,1024]{1,0:T(8,128)(2,1)}, bf16[128,1024]{1,0:T(8,128)(2,1)S(1)}, u32[]{:S(2)}, u32[]{:S(2)}) collective-permute-start(bf16[128,1024]{1,0:T(8,128)(2,1)} %collective-permute-done.11.refs_6_), channel_id=1, source_target_pairs={{0,32},{32,64},{64,96},{96,128},{128,160},{160,192},{192,224},{224... | collective-permute-start | bytes 786440 | tf_op jit(solution)/shard_map/ppermute | solution.py:51
  89.4 1.7 collective-permute-start.21
  180.5 18.6 %all-to-all-start.2 = ((bf16[16,16,1024]{2,1,0:T(8,128)(2,1)}), bf16[16,16,1024]{2,1,0:T(8,128)(2,1)}, u32[]{:S(2)}, u32[]{:S(2)}) async-start(bf16[16,16,1024]{2,1,0:T(8,128)(2,1)} %broadcast_in_dim.2), calls=%async_computation.2 | async-start | bytes 1048576 | tf_op jit(solution)/shard_map/all_to_all | solution.py:308
  185.6 14.6 %collective-permute-start.23 = (bf16[288,1024]{1,0:T(8,128)(2,1)}, bf16[288,1024]{1,0:T(8,128)(2,1)}, u32[]{:S(2)}, u32[]{:S(2)}) collective-permute-start(bf16[288,1024]{1,0:T(8,128)(2,1)} %get-tuple-element.22), channel_id=1, source_target_pairs={{0,1},{1,0},{2,3},{3,2},{4,5},{5,4},{6,7},{7,6},{8,9},{9,8},{10,11... | collective-permute-start | bytes 1769480 | tf_op jit(solution)/shard_map/ppermute | solution.py:31
  200.1 3.0 %collective-permute-start.22 = (bf16[128,1024]{1,0:T(8,128)(2,1)S(1)}, bf16[128,1024]{1,0:T(8,128)(2,1)S(1)}, u32[]{:S(2)}, u32[]{:S(2)}) collective-permute-start(bf16[128,1024]{1,0:T(8,128)(2,1)S(1)} %get-tuple-element.25), channel_id=1, source_target_pairs={{0,1},{1,0},{2,3},{3,2},{4,5},{5,4},{6,7},{7,6},{8,9},{9,8},{10,11... | collective-permute-start | bytes 786440 | tf_op jit(solution)/shard_map/ppermute | solution.py:31
  (15 other events, 123.9 us)

commit v2 on v1

v2 whole, which is shorter than its diff:
```python
import functools

import jax
import jax.numpy as jnp
from jax import lax
from jax.experimental import pallas as pl
from jax.experimental.pallas import tpu as pltpu
from jax.sharding import Mesh, PartitionSpec as P

KIN = 2048
DOUT = 2048
PATCHES = 144
EPS = 1e-06
AXES = ("z", "xlo", "y", "xhi", "core")
VMEM_LIMIT = 44 * 1024 * 1024

X_INDEX = (0, 2, 1, 3)
CORE_SWAP = ((0, 1), (1, 0))
X_NEAR = tuple((X_INDEX[a], X_INDEX[b]) for a, b in ((1, 2), (2, 1), (0, 3), (3, 0)))


def from_next(size):
    return tuple(((i + 1) % size, i) for i in range(size))


def from_previous(size):
    return tuple((i, (i + 1) % size) for i in range(size))


def with_core_flip(pairs):
    return tuple((2 * a + 1 - core, 2 * b + core) for a, b in pairs for core in range(2))


FSDP_GROUPS = tuple(
    tuple((xhi ^ side) * 8 + y * 2 + xhi for y in range(4) for xhi in range(2)) for side in range(2)
)
DP_GROUPS = tuple(
    tuple((z * 2 + xlo) * 2 + (side ^ ((z + xlo) & 1)) for z in range(8) for xlo in range(2)) for side in range(2)
)


def swap_cores(value):
    return lax.ppermute(value, "core", CORE_SWAP)


def from_y_next(value):
    return lax.ppermute(value, "y", from_next(4))


def from_y_previous(value):
    return lax.ppermute(value, "y", from_previous(4))


def from_x_near(value):
    return lax.ppermute(value, ("xlo", "xhi"), X_NEAR)


def from_z_next(value):
    return lax.ppermute(value, ("z", "core"), with_core_flip(from_next(8)))


def from_z_previous(value):
    return lax.ppermute(value, ("z", "core"), with_core_flip(from_previous(8)))


def from_x_twin(value):
    return lax.ppermute(value, ("xlo", "core"), with_core_flip(CORE_SWAP))


def fsdp_exchange(value):
    return lax.all_to_all(value, ("xlo", "y", "xhi"), 0, 0, axis_index_groups=FSDP_GROUPS)


def dp_exchange(value):
    return lax.all_to_all(value, ("z", "xlo", "core"), 0, 0, axis_index_groups=DP_GROUPS)


EARLY = (
    (0, 0, 0), (1, 0, 0), (0, 1, 0), (0, 3, 0), (0, 0, 1), (0, 2, 0), (0, 3, 1), (0, 1, 1), (1, 1, 0), (1, 3, 0),
    (1, 0, 1),
)
LATE = ((0, 2, 1), (1, 2, 0), (1, 3, 1), (1, 1, 1), (1, 2, 1))


def gather_rows(own, other):
    up, down, across = lax.optimization_barrier((from_y_next(own), from_y_previous(own), from_x_near(own)))
    up_two = from_y_next(up)
    across_up = from_x_near(up)
    across_down = from_y_previous(across)
    passed_up, passed_down, passed_across = from_z_next(up), from_z_previous(down), from_x_twin(across)
    up_two, across_up, across_down = lax.optimization_barrier((up_two, across_up, across_down))
    student = from_y_next(across_up[0])
    teacher = from_y_previous(across_down[1])
    passed_two = from_z_next(up_two)
    passed_across_up = from_z_previous(across_up)
    passed_across_down = from_x_twin(across_down)
    student, teacher = lax.optimization_barrier((student, teacher))
    passed_student = from_z_next(student)
    passed_teacher = from_z_previous(teacher)
    early = (
        own, other, up, down, across, up_two, across_down, across_up, passed_up, passed_down, passed_across,
    )
    late = (
        student, teacher, passed_two, passed_across_down, passed_across_up, passed_student, passed_teacher,
    )
    return early, late


def early_kernel(order, student_own, student_other, teacher_own, teacher_other, *refs):
    count = len(EARLY)
    weights = refs[:count]
    student_out, teacher_out, student_late, teacher_late, turned, mix, held = refs[count:]
    step, own = pl.program_id(0), student_own.shape[0]

    @pl.when(step == 0)
    def _():
        for block in range(count + len(LATE)):
            columns = pl.ds(pl.multiple_of(order[block] * 128, 128), 128)
            at = block if block < count else block - count
            spot = slice(at * 128, (at + 1) * 128)
            to_student = mix.at[0] if block < count else student_late
            to_teacher = mix.at[1] if block < count else teacher_late
            to_student[:own, spot] = student_own[:, columns]
            to_student[own:, spot] = student_other[:, columns]
            to_teacher[:own, spot] = teacher_own[:, columns]
            to_teacher[own:, spot] = teacher_other[:, columns]

    for block in range(count):
        rows = slice(block * 128, (block + 1) * 128)
        held[0, rows, :] = weights[block][0]
        held[1, rows, :] = weights[block][1]
    student_out[...] = jnp.dot(mix[0], held[0], preferred_element_type=jnp.float32)
    teacher_out[...] = jnp.dot(mix[1], held[1], preferred_element_type=jnp.float32)
    width = turned.shape[0]
    columns = pl.ds(pl.multiple_of(step * width, width), width)
    turned[...] = jnp.concatenate([student_own[:, columns], student_other[:, columns]], axis=0).T


def early_forward(order, weights, student_own, student_other, teacher_own, teacher_other):
    own, columns, width = student_own.shape[0], weights[0].shape[-1], 256
    rows, steps, count = 2 * own, columns // width, len(EARLY)
    whole = pl.BlockSpec((own, KIN), lambda j, order: (0, 0))
    column = pl.BlockSpec((rows, width), lambda j, order: (0, j))
    late = pl.BlockSpec((rows, len(LATE) * 128), lambda j, order: (0, 0))
    return pl.pallas_call(
        early_kernel,
        grid_spec=pltpu.PrefetchScalarGridSpec(
            num_scalar_prefetch=1,
            grid=(steps,),
            in_specs=[whole] * 4 + [pl.BlockSpec((2, 128, width), lambda j, order: (0, 0, j))] * count,
            out_specs=[column, column, late, late, pl.BlockSpec((KIN // steps, rows), lambda j, order: (j, 0))],
            scratch_shapes=[
                pltpu.VMEM((2, rows, count * 128), jnp.bfloat16),
                pltpu.VMEM((2, count * 128, width), jnp.bfloat16),
            ],
        ),
        out_shape=[
            jax.ShapeDtypeStruct((rows, columns), jnp.float32),
            jax.ShapeDtypeStruct((rows, columns), jnp.float32),
            jax.ShapeDtypeStruct((rows, len(LATE) * 128), jnp.bfloat16),
            jax.ShapeDtypeStruct((rows, len(LATE) * 128), jnp.bfloat16),
            jax.ShapeDtypeStruct((KIN, rows), jnp.bfloat16),
        ],
        compiler_params=pltpu.CompilerParams(vmem_limit_bytes=VMEM_LIMIT),
        cost_estimate=pl.CostEstimate(
            flops=4 * rows * count * 128 * columns, bytes_accessed=18 * 1024 * 1024, transcendentals=0
        ),
    )(order, student_own, student_other, teacher_own, teacher_other, *weights)


def late_kernel(
    order, student_mix, teacher_mix, student_part, teacher_part, residual_own, residual_other, scale, places_own,
    places_other, *refs
):
    weights = refs[:7]
    student_out, matched_out, sums_out, held = refs[7:]
    depth = held.shape[1]
    held[0, :128, :] = weights[0][...]
    held[1, :128, :] = weights[1][...]
    for block in range(1, 4):
        rows = slice(block * 128, (block + 1) * 128)
        held[0, rows, :] = weights[block + 1][0]
        held[1, rows, :] = weights[block + 1][1]
    held[0, depth - 128 :, :] = weights[5][...]
    held[1, depth - 128 :, :] = weights[6][...]
    factor = scale[...] * (KIN ** (-0.5))
    student_sum = student_part[...] + jnp.dot(student_mix[...], held[0], preferred_element_type=jnp.float32)
    teacher_sum = teacher_part[...] + jnp.dot(teacher_mix[...], held[1], preferred_element_type=jnp.float32)
    own = residual_own.shape[0]
    lane = lax.broadcasted_iota(jnp.int32, (PATCHES, PATCHES), 1)
    students, parts = [], []
    for side, (residual, places) in enumerate(((residual_own, places_own), (residual_other, places_other))):
        tokens = slice(side * own, (side + 1) * own)
        base = residual[...].astype(jnp.float32)
        students.append(base + factor * student_sum[tokens])
        teacher = base + factor * teacher_sum[tokens]
        high = teacher.astype(jnp.bfloat16)
        low = (teacher - high.astype(jnp.float32)).astype(jnp.bfloat16)
        for crop in range(own // PATCHES):
            rows = slice(crop * PATCHES, (crop + 1) * PATCHES)
            pick = (places[rows, :] == lane).astype(jnp.float32).astype(jnp.bfloat16)
            parts.append(
                jnp.dot(pick, high[rows], preferred_element_type=jnp.float32)
                + jnp.dot(pick, low[rows], preferred_element_type=jnp.float32)
            )
    student = jnp.concatenate(students, axis=0)
    matched = jnp.concatenate(parts, axis=0)
    student_out[...] = student
    matched_out[...] = matched
    spot = lax.broadcasted_iota(jnp.int32, sums_out.shape, 1)
    sums = jnp.where(
        spot == 0,
        jnp.sum(student * student, axis=-1, keepdims=True),
        jnp.where(
            spot == 1,
            jnp.sum(matched * matched, axis=-1, keepdims=True),
            jnp.where(spot == 2, jnp.sum(student * matched, axis=-1, keepdims=True), 0.0),
        ),
    )

    @pl.when(pl.program_id(0) == 0)
    def _():
        sums_out[...] = sums

    @pl.when(pl.program_id(0) != 0)
    def _():
        sums_out[...] += sums


def late_forward(
    order, weights, student_mix, teacher_mix, student_part, teacher_part, residual_own, residual_other, scale,
    places_own, places_other
):
    (rows, columns), own, width, depth = student_part.shape, residual_own.shape[0], 256, student_mix.shape[1]
    steps = columns // width
    half_at = len(EARLY) + len(LATE)
    mix = pl.BlockSpec((rows, depth), lambda j, order: (0, 0))
    column = pl.BlockSpec((rows, width), lambda j, order: (0, j))
    places = pl.BlockSpec((own, 1), lambda j, order: (0, 0))
    pair = pl.BlockSpec((2, 128, width), lambda j, order: (0, 0, j))
    single = pl.BlockSpec((128, width), lambda j, order: (0, j))
    return pl.pallas_call(
        late_kernel,
        grid_spec=pltpu.PrefetchScalarGridSpec(
            num_scalar_prefetch=1,
            grid=(steps,),
            in_specs=[
                mix,
                mix,
                column,
                column,
                pl.BlockSpec((own, width), lambda j, order: (0, order[half_at] * steps + j)),
                pl.BlockSpec((own, width), lambda j, order: (0, j)),
                pl.BlockSpec((1, width), lambda j, order: (0, order[half_at] * steps + j)),
                places,
                places,
                single,
                single,
                pair,
                pair,
                pair,
                single,
                single,
            ],
            out_specs=[column, column, pl.BlockSpec((rows, 128), lambda j, order: (0, 0))],
            scratch_shapes=[pltpu.VMEM((2, depth, width), jnp.bfloat16)],
        ),
        out_shape=[
            jax.ShapeDtypeStruct((rows, columns), jnp.float32),
            jax.ShapeDtypeStruct((rows, columns), jnp.float32),
            jax.ShapeDtypeStruct((rows, 128), jnp.float32),
        ],
        compiler_params=pltpu.CompilerParams(vmem_limit_bytes=VMEM_LIMIT),
        cost_estimate=pl.CostEstimate(
            flops=4 * rows * depth * columns, bytes_accessed=16 * 1024 * 1024, transcendentals=0
        ),
    )(
        order, student_mix, teacher_mix, student_part, teacher_part, residual_own, residual_other, scale, places_own,
        places_other, *weights
    )


def backward_kernel(total_tokens, order, student, matched, sums, more_sums, scale, mix, grad_out, tokens_out, held):
    @pl.when(pl.program_id(0) == 0)
    def _():
        own = more_sums.shape[0] // 2
        swapped = jnp.concatenate([more_sums[own:, :], more_sums[:own, :]], axis=0)
        total = (sums[...] + swapped) * (1.0 / DOUT)
        inverse_rms = lax.rsqrt(total[:, 0:1] + EPS)
        inverse_matched = lax.rsqrt(total[:, 1:2] + EPS)
        overlap = inverse_rms * inverse_matched * total[:, 2:3]
        shared = inverse_rms * (1.0 / total_tokens)
        student_part = shared * inverse_rms * (EPS * inverse_rms * inverse_rms + overlap)
        matched_part = shared * inverse_matched
        values = student[...]
        tokens_out[...] = (values * inverse_rms).astype(jnp.bfloat16)
        factor = scale[...] * (KIN ** (-0.5))
        held[...] = (factor * (values * student_part - matched[...] * matched_part)).astype(jnp.bfloat16)

    width = grad_out.shape[-1]
    for part in range(grad_out.shape[1]):
        grad_out[0, part] = jnp.dot(
            mix[...], held[:, part * width : (part + 1) * width], preferred_element_type=jnp.float32
        ).astype(jnp.bfloat16)


def backward(total_tokens, order, student, matched, sums, more_sums, scale, mix):
    rows, columns = student.shape
    depth = 256
    half_at = len(EARLY) + len(LATE)
    whole = pl.BlockSpec((rows, columns), lambda i, order: (0, 0))
    narrow = pl.BlockSpec((rows, 128), lambda i, order: (0, 0))
    return pl.pallas_call(
        functools.partial(backward_kernel, total_tokens),
        grid_spec=pltpu.PrefetchScalarGridSpec(
            num_scalar_prefetch=1,
            grid=(KIN // depth,),
            in_specs=[
                whole,
                whole,
                narrow,
                narrow,
                pl.BlockSpec((1, columns), lambda i, order: (0, order[half_at])),
                pl.BlockSpec((depth, rows), lambda i, order: (i, 0)),
            ],
            out_specs=[pl.BlockSpec((1, 2, depth, columns // 2), lambda i, order: (i, 0, 0, 0)), whole],
            scratch_shapes=[pltpu.VMEM((rows, columns), jnp.bfloat16)],
        ),
        out_shape=[
            jax.ShapeDtypeStruct((KIN // depth, 2, depth, columns // 2), jnp.bfloat16),
            jax.ShapeDtypeStruct((rows, columns), jnp.bfloat16),
        ],
        compiler_params=pltpu.CompilerParams(vmem_limit_bytes=VMEM_LIMIT),
        cost_estimate=pl.CostEstimate(
            flops=2 * rows * KIN * columns, bytes_accessed=12 * 1024 * 1024, transcendentals=0
        ),
    )(order, student, matched, sums, more_sums, scale, mix)


def adamw_update(grad, weight, teacher, first, squares):
    first_next = 0.9 * first + 0.1 * grad
    squares_next = 0.95 * squares + 0.05 * grad * grad
    weight_next = weight - 0.1 * (first_next / (jnp.sqrt(squares_next) + 1e-08) + 0.04 * weight)
    teacher_next = 0.96 * teacher + 0.04 * weight_next
    return (weight_next, teacher_next, first_next, squares_next)


def join_columns(which, own, other):
    return jnp.where(
        which == 0, jnp.concatenate([own, other], axis=-1), jnp.concatenate([other, own], axis=-1)
    )


def shards(
    residual,
    student_mix,
    teacher_mix,
    positions,
    layer_scale,
    student_weight,
    teacher_weight,
    moment,
    second,
):
    half = DOUT // 2
    token_count = student_mix.shape[0]
    total_tokens = token_count * 256
    z, xlo, y, xhi, core = (lax.axis_index(name) for name in AXES)
    which = (core + z + xhi + xlo) & 1

    def columns_of(value, index):
        return lax.dynamic_slice_in_dim(value, index * half, half, axis=-1)

    def both_weights(index):
        return jnp.stack([columns_of(student_weight, index), columns_of(teacher_weight, index)]).astype(jnp.bfloat16)

    own = both_weights(which)
    order = jnp.stack(
        [
            (((y + dy) & 3) * 2 + (xhi ^ dx)) * 2 + (core ^ side)
            for side, dy, dx in EARLY + LATE
        ]
        + [which]
    ).astype(jnp.int32)
    own, student_sent, teacher_sent, residual_sent, positions_sent, student_held, teacher_held = (
        lax.optimization_barrier(
            (own, student_mix, teacher_mix, residual, positions, student_weight, teacher_weight)
        )
    )
    student_weight, teacher_weight = student_held, teacher_held
    other = swap_cores(both_weights(1 - which))
    student_other = swap_cores(student_sent)
    teacher_other = swap_cores(teacher_sent)
    residual_other = swap_cores(columns_of(residual_sent, 1 - which))
    places_other = swap_cores(positions_sent).reshape(token_count, 1)
    places = positions.reshape(token_count, 1)
    scale = layer_scale.reshape(1, DOUT)

    early, late = gather_rows(own, other)
    student_part, teacher_part, student_late, teacher_late, turned = early_forward(
        order, early, student_mix, student_other, teacher_mix, teacher_other
    )
    student_out, matched, sums = late_forward(
        order, late, student_late, teacher_late, student_part, teacher_part, residual, residual_other, scale, places,
        places_other
    )
    grads, tokens = backward(
        total_tokens, order, student_out, matched, sums, swap_cores(sums), scale, turned
    )

    student_tokens = join_columns(which, tokens[:token_count], swap_cores(tokens[token_count:]))

    by_chip = fsdp_exchange(grads)
    chip_rows = jnp.sum(by_chip.astype(jnp.float32), axis=0).astype(jnp.bfloat16)
    by_copy = dp_exchange(chip_rows.reshape(2, 16, 16, half // 2).transpose(1, 0, 2, 3))
    copy_rows = jnp.sum(by_copy.astype(jnp.float32), axis=0).astype(jnp.bfloat16)
    full = dp_exchange(jnp.broadcast_to(copy_rows[None], (16, 2, 16, half // 2)))

    def rows_of(index):
        return (
            lax.dynamic_slice_in_dim(full, index * 8, 8, axis=0).transpose(0, 2, 1, 3).reshape(128, half)
        )

    grad = join_columns(which, rows_of(core), swap_cores(rows_of(1 - core))).astype(jnp.float32)
    weight_next, teacher_next, first_next, squares_next = adamw_update(
        grad, student_weight, teacher_weight, moment, second
    )
    return (weight_next, teacher_next, first_next, squares_next, student_tokens)


def solution(mesh):
    split = Mesh(mesh.devices.reshape(8, 2, 4, 2, 2), AXES)
    tokens = P(AXES, None)
    owned = P(("y", "xhi", "core"), None)
    return jax.shard_map(
        shards,
        mesh=split,
        in_specs=(tokens, tokens, tokens, tokens, P(), owned, owned, owned, owned),
        out_specs=(owned, owned, owned, owned, tokens),
        check_vma=False,
    )
```

time: 210 us -> 228 us (1.086)
  waiting for transfers between devices: 37.3 us -> 53.1 us
  other arithmetic: 21.8 us -> 10 us
  Pallas kernels: 20.1 us -> 26.4 us
  local copies, waits for them, and re-layouts: 16.9 us -> 21.5 us
  blocking collectives: 77.7 us -> 81.2 us
    concatenate x4 -> x0, other arithmetic: 9.04 us -> none  [the longest x1 4.32 us: shards(): jnp.concatenate([student_mix, swap_cores(student_mix)], axis=0)]
    unnamed x29 -> x50, local copies, waits for them, and re-layouts: 3.27 us -> 12.2 us
    ppermute x3, waiting for transfers between devices: 1.32 us -> 9.99 us  [from_y_previous(): return lax.ppermute(value, 'y', from_previous(4))]
    pallas_call x2 -> x3, Pallas kernels: 20.1 us -> 26.4 us  [the longest x1 11.1 us: early_forward(): pl.pallas_call(early_kernel, grid_spec=pltpu.PrefetchScalarGridSpec(num_s...]
    ppermute x3, waiting for transfers between devices: 9.61 us -> 14.6 us  [from_y_next(): return lax.ppermute(value, 'y', from_next(4))]
    concatenate x1 -> x0, local copies, waits for them, and re-layouts: 4.41 us -> none  [shards(): jnp.concatenate([student_mix, swap_cores(student_mix)], axis=0)]
    all_to_all x2, blocking collectives: 77.7 us -> 81.2 us  [the longest x1 55.3 us: fsdp_exchange(): lax.all_to_all(value, ('xlo', 'y', 'xhi'), 0, 0, axis_index_groups=FSDP_G...]
    another operation x1 -> x4, local copies, waits for them, and re-layouts: 0.09 us -> 3.52 us  [the longest x3 3.42 us: both_weights(): jnp.stack([columns_of(student_weight, index), columns_of(teacher_weight,...]
  transfers between devices with their start and end apart: 25 -> 25, of which waited for: 11 -> 11; matrix products, arithmetic and copies ran while one was open for 14% -> 5% of each run, Pallas kernels for 0% -> 5%
where the time goes in v2:
time: 228 us; the launch traced here: 224 us
  blocking collectives  81.2 us (36%)
  waiting for transfers between devices  53.1 us (23%)
  starting transfers between devices  30.8 us (14%)
  Pallas kernels  26.4 us (12%)
  local copies, waits for them, and re-layouts  21.5 us (9%)
  other arithmetic  10 us (4%)
    all_to_all x1, blocking collectives, fsdp_exchange(): lax.all_to_all(value, ('xlo', 'y', 'xhi'), 0, 0, axis_index_groups=FSDP_G...  55.3 us
    all_to_all x1, blocking collectives, dp_exchange(): lax.all_to_all(value, ('z', 'xlo', 'core'), 0, 0, axis_index_groups=DP_GR...  25.9 us
    all_to_all x1, waiting for transfers between devices, dp_exchange(): lax.all_to_all(value, ('z', 'xlo', 'core'), 0, 0, axis_index_groups=DP_GR...  16.5 us
    ppermute x3, waiting for transfers between devices, from_y_next(): return lax.ppermute(value, 'y', from_next(4))  14.6 us
    ppermute x3, starting transfers between devices, from_z_next(): return lax.ppermute(value, ('z', 'core'), with_core_flip(from_next(8)))  14.6 us
    unnamed x50, local copies, waits for them, and re-layouts  12.2 us
    pallas_call x1, Pallas kernels, early_forward(): pl.pallas_call(early_kernel, grid_spec=pltpu.PrefetchScalarGridSpec(num_s...  11.1 us
    ppermute x3, waiting for transfers between devices, from_y_previous(): return lax.ppermute(value, 'y', from_previous(4))  9.99 us
  transfers between devices with their start and end apart: 25, of which 11 were waited for; matrix products, arithmetic and copies ran while one was open for 5% of the time, Pallas kernels for 5%

profile of v2, /device:TPU:4, one launch (start us, length us, event | category | flops | bytes accessed | tf_op | source)
XLA Modules:
  0.0 224.0 jit_solution(12402902050862688259)
XLA Ops:
  2.0 3.1 %collective-permute-start.3 = (bf16[2,128,1024]{2,1,0:T(8,128)(2,1)S(1)}, bf16[2,128,1024]{2,1,0:T(8,128)(2,1)S(1)}, u32[]{:S(2)}, u32[]{:S(2)}) collective-permute-start(bf16[2,128,1024]{2,1,0:T(8,128)(2,1)S(1)} %pad_maximum_fusion.refs_0_), channel_id=1, source_target_pairs={{4,0},{8,4},{12,8},{0,12},{5,1},{9,5},{13,9},{1,13},{6,2},{10,6},{... | collective-permute-start | bytes 1572872 | tf_op jit(solution)/shard_map/ppermute | solution.py:47
  8.0 8.3 %collective-permute-done.3.refs_2_ = bf16[2,128,1024]{2,1,0:T(8,128)(2,1)S(1)} collective-permute-done((bf16[2,128,1024]{2,1,0:T(8,128)(2,1)S(1)}, bf16[2,128,1024]{2,1,0:T(8,128)(2,1)S(1)}, u32[]{:S(2)}, u32[]{:S(2)}) %collective-permute-start.3) | collective-permute-done | bytes 524320 | tf_op jit(solution)/shard_map/ppermute | solution.py:47
  16.3 3.4 %collective-permute-done.4.refs_3_ = bf16[2,128,1024]{2,1,0:T(8,128)(2,1)S(1)} collective-permute-done((bf16[2,128,1024]{2,1,0:T(8,128)(2,1)S(1)}, bf16[2,128,1024]{2,1,0:T(8,128)(2,1)S(1)}, u32[]{:S(2)}, u32[]{:S(2)}) %collective-permute-start.4) | collective-permute-done | bytes 524320 | tf_op jit(solution)/shard_map/ppermute | solution.py:51
  19.7 1.8 collective-permute-start.6
  24.4 1.6 collective-permute-start.10
  26.0 6.3 %collective-permute-done.6.refs_5_ = bf16[2,128,1024]{2,1,0:T(8,128)(2,1)} collective-permute-done((bf16[2,128,1024]{2,1,0:T(8,128)(2,1)S(1)}, bf16[2,128,1024]{2,1,0:T(8,128)(2,1)}, u32[]{:S(2)}, u32[]{:S(2)}) %collective-permute-start.6) | collective-permute-done | bytes 524320 | tf_op jit(solution)/shard_map/ppermute | solution.py:47
  33.6 6.2 %collective-permute-done.8.refs_6_ = bf16[2,128,1024]{2,1,0:T(8,128)(2,1)} collective-permute-done((bf16[2,128,1024]{2,1,0:T(8,128)(2,1)}, bf16[2,128,1024]{2,1,0:T(8,128)(2,1)}, u32[]{:S(2)}, u32[]{:S(2)}) %collective-permute-start.8) | collective-permute-done | bytes 524320 | tf_op jit(solution)/shard_map/ppermute | solution.py:51
  41.0 6.7 %collective-permute-start.9 = (bf16[2,128,1024]{2,1,0:T(8,128)(2,1)S(1)}, bf16[2,128,1024]{2,1,0:T(8,128)(2,1)S(1)}, u32[]{:S(2)}, u32[]{:S(2)}) collective-permute-start(bf16[2,128,1024]{2,1,0:T(8,128)(2,1)S(1)} %collective-permute-done.3.refs_2_), channel_id=1, source_target_pairs={{33,0},{32,1},{65,32},{64,33},{97,64},{96,65},{129,96},{128,97},{1... | collective-permute-start | bytes 1572872 | tf_op jit(solution)/shard_map/ppermute | solution.py:59
  49.8 3.5 %collective-permute-done.11.refs_10_ = bf16[2,128,1024]{2,1,0:T(8,128)(2,1)S(1)} collective-permute-done((bf16[2,128,1024]{2,1,0:T(8,128)(2,1)}, bf16[2,128,1024]{2,1,0:T(8,128)(2,1)S(1)}, u32[]{:S(2)}, u32[]{:S(2)}) %collective-permute-start.11) | collective-permute-done | bytes 524320 | tf_op jit(solution)/shard_map/ppermute | solution.py:67
  54.1 4.5 %collective-permute-done.9.refs_8_ = bf16[2,128,1024]{2,1,0:T(8,128)(2,1)S(1)} collective-permute-done((bf16[2,128,1024]{2,1,0:T(8,128)(2,1)S(1)}, bf16[2,128,1024]{2,1,0:T(8,128)(2,1)S(1)}, u32[]{:S(2)}, u32[]{:S(2)}) %collective-permute-start.9) | collective-permute-done | bytes 524320 | tf_op jit(solution)/shard_map/ppermute | solution.py:59
  60.2 3.9 %collective-permute-start.16 = (bf16[2,128,1024]{2,1,0:T(8,128)(2,1)}, bf16[2,128,1024]{2,1,0:T(8,128)(2,1)S(1)}, u32[]{:S(2)}, u32[]{:S(2)}) collective-permute-start(bf16[2,128,1024]{2,1,0:T(8,128)(2,1)} %collective-permute-done.6.refs_5_), channel_id=1, source_target_pairs={{33,0},{32,1},{65,32},{64,33},{97,64},{96,65},{129,96},{128,97},{1... | collective-permute-start | bytes 1572872 | tf_op jit(solution)/shard_map/ppermute | solution.py:59
  64.5 1.6 collective-permute-start.18
  66.7 4.0 %collective-permute-start.19 = (bf16[128,1024]{1,0:T(8,128)(2,1)S(1)}, bf16[128,1024]{1,0:T(8,128)(2,1)S(1)}, u32[]{:S(2)}, u32[]{:S(2)}) collective-permute-start(bf16[128,1024]{1,0:T(8,128)(2,1)S(1)} %collective-permute-done.14.refs_0_), channel_id=1, source_target_pairs={{33,0},{32,1},{65,32},{64,33},{97,64},{96,65},{129,96},{128,97},{1... | collective-permute-start | bytes 786440 | tf_op jit(solution)/shard_map/ppermute | solution.py:59
  78.0 11.1 %shard_map.128 = (f32[576,1024]{1,0:T(8,128)}, f32[576,1024]{1,0:T(8,128)}, bf16[576,640]{1,0:T(8,128)(2,1)S(1)}, bf16[576,640]{1,0:T(8,128)(2,1)S(1)}, bf16[2048,576]{1,0:T(8,128)(2,1)}) custom-call(s32[17]{0:T(128)S(1)} %stack.98.order, bf16[288,2048]{1,0:T(8,128)(2,1)} %student_own.1, bf16[288,2048]{1,0:T(8,128)(2,1)} %collective-permute-done.student_other, ...), custom_call_target="tpu_custom_call" | custom-call | flops 3321888768 | bytes 18874368 | tf_op jit(solution)/shard_map/pallas_call | solution.py:145
  89.2 7.9 %shard_map.129 = (f32[576,1024]{1,0:T(8,128)S(1)}, f32[576,1024]{1,0:T(8,128)}, f32[576,128]{1,0:T(8,128)S(1)}) custom-call(s32[17]{0:T(128)S(1)} %stack.98.order, bf16[576,640]{1,0:T(8,128)(2,1)S(1)} %get-tuple-element.41.student_mix, bf16[576,640]{1,0:T(8,128)(2,1)S(1)} %get-tuple-element.42.teacher_mix, f32[576,1024]{1,0:T(8,128)} %get-tuple-element.43.student_part, ...), custom_call_target="tpu_custom_call" | custom-call | flops 1509949440 | bytes 16777216 | tf_op jit(solution)/shard_map/pallas_call | solution.py:242
  98.6 1.7 copy-done.4
  100.3 7.5 %shard_map.130 = (bf16[8,2,256,512]{3,2,1,0:T(8,128)(2,1)}, bf16[576,1024]{1,0:T(8,128)(2,1)S(1)}) custom-call(s32[17]{0:T(128)S(1)} %stack.98.order, f32[576,1024]{1,0:T(8,128)S(1)} %get-tuple-element.49.student, f32[576,1024]{1,0:T(8,128)S(1)} %copy-done.4, f32[576,128]{1,0:T(8,128)S(1)} %get-tuple-element.51.sums, ...), custom_call_target="tpu_custom_call" | custom-call | flops 2415919104 | bytes 12582912 | tf_op jit(solution)/shard_map/pallas_call | solution.py:313
  107.8 55.3 %all_to_all.15 = bf16[8,2,256,512]{3,2,1,0:T(8,128)(2,1)} all-to-all(bf16[8,2,256,512]{3,2,1,0:T(8,128)(2,1)} %get-tuple-element.53), channel_id=1, replica_groups={{0,18,4,22,8,26,12,30},{16,2,20,6,24,10,28,14},{1,19,5,23,9,27,13,31},{..., dimensions={0} | all-to-all | bytes 8388608 | tf_op jit(solution)/shard_map/all_to_all | solution.py:71
  163.1 3.0 %reduce_sum.24 = bf16[2,256,512]{2,1,0:T(8,128)(2,1)S(1)} reduce(bf16[8,2,256,512]{3,2,1,0:T(8,128)(2,1)} %all_to_all.15, bf16[]{:T(256)} %constant.46.clone.1), dimensions={0}, to_apply=%region_0.1 | reduce | flops 1835008 | bytes 4718594 | tf_op jit(solution)/shard_map/reduce_sum | solution.py:414
  166.1 25.9 %all_to_all.16 = bf16[16,2,16,512]{3,2,1,0:T(8,128)(2,1)S(1)} all-to-all(bf16[16,2,16,512]{3,2,1,0:T(8,128)(2,1)S(1)} %copy.23), channel_id=1, replica_groups={{0,17,33,48,64,81,97,112,128,145,161,176,192,209,225,240},{1,16,32,49,6..., dimensions={0} | all-to-all | bytes 1048576 | tf_op jit(solution)/shard_map/all_to_all | solution.py:75
  193.3 3.6 %all-to-all-start.2 = ((bf16[16,2,16,512]{3,1,2,0:T(2,128)(2,1)}), bf16[16,2,16,512]{3,1,2,0:T(2,128)(2,1)S(1)}, u32[]{:S(2)}, u32[]{:S(2)}) async-start(bf16[16,2,16,512]{3,1,2,0:T(2,128)(2,1)} %broadcast_in_dim.2), calls=%async_computation.2 | async-start | bytes 1048576 | tf_op jit(solution)/shard_map/all_to_all | solution.py:75
  197.8 16.5 %all-to-all-done.2 = bf16[16,2,16,512]{3,1,2,0:T(2,128)(2,1)S(1)} async-done(((bf16[16,2,16,512]{3,1,2,0:T(2,128)(2,1)}), bf16[16,2,16,512]{3,1,2,0:T(2,128)(2,1)S(1)}, u32[]{:S(2)}, u32[]{:S(2)}) %all-to-all-start.2) | async-done | bytes 524320 | tf_op jit(solution)/shard_map/all_to_all | solution.py:75
  217.0 2.9 %maximum_select_fusion = bf16[288,2048]{1,0:T(8,128)(2,1)} fusion(bf16[288,1024]{1,0:T(8,128)(2,1)} %copy-done.22, bf16[288,1024]{1,0:T(8,128)(2,1)S(1)} %get-tuple-element.59, pred[]{:T(512)S(6)} %eq.4), kind=kLoop, calls=%fused_computation.2 | loop fusion | flops 5308416 | bytes 2359297 | tf_op jit(solution)/shard_map/jit(_where)/select_n | solution.py:349
  219.9 4.0 %multiply_add_fusion = (f32[128,2048]{1,0:T(8,128)}, f32[128,2048]{1,0:T(8,128)}, f32[128,2048]{1,0:T(8,128)}, f32[128,2048]{1,0:T(8,128)}) fusion(f32[128,2048]{1,0:T(8,128)S(1)} %copy-done.18, f32[128,2048]{1,0:T(8,128)S(1)} %copy-done.19, bf16[128,1024]{1,0:T(8,128)(2,1)S(1)} %bitcast.45, bf16[128,1024]{1,0:T(8,128)(2,1)} %collective-permute-done.22, ...), kind=kLoop, calls=%fused_computation.5 | loop fusion | flops 6815744 | bytes 8912897 | tf_op jit(solution)/shard_map/add | solution.py:344
  (101 shorter events, 28.9 us)
Async XLA Ops:
  2.0 14.3 %collective-permute-start.3 = (bf16[2,128,1024]{2,1,0:T(8,128)(2,1)S(1)}, bf16[2,128,1024]{2,1,0:T(8,128)(2,1)S(1)}, u32[]{:S(2)}, u32[]{:S(2)}) collective-permute-start(bf16[2,128,1024]{2,1,0:T(8,128)(2,1)S(1)} %pad_maximum_fusion.refs_0_), channel_id=1, source_target_pairs={{4,0},{8,4},{12,8},{0,12},{5,1},{9,5},{13,9},{1,13},{6,2},{10,6},{... | collective-permute-start | bytes 1572872 | tf_op jit(solution)/shard_map/ppermute | solution.py:47
  5.1 14.6 %collective-permute-start.4 = (bf16[2,128,1024]{2,1,0:T(8,128)(2,1)S(1)}, bf16[2,128,1024]{2,1,0:T(8,128)(2,1)S(1)}, u32[]{:S(2)}, u32[]{:S(2)}) collective-permute-start(bf16[2,128,1024]{2,1,0:T(8,128)(2,1)S(1)} %pad_maximum_fusion.refs_0_), channel_id=1, source_target_pairs={{0,4},{4,8},{8,12},{12,0},{1,5},{5,9},{9,13},{13,1},{2,6},{6,10},{... | collective-permute-start | bytes 1572872 | tf_op jit(solution)/shard_map/ppermute | solution.py:51
  5.1 14.6 %collective-permute-start.5 = (bf16[2,128,1024]{2,1,0:T(8,128)(2,1)S(1)}, bf16[2,128,1024]{2,1,0:T(8,128)(2,1)}, u32[]{:S(2)}, u32[]{:S(2)}) collective-permute-start(bf16[2,128,1024]{2,1,0:T(8,128)(2,1)S(1)} %pad_maximum_fusion.refs_0_), channel_id=1, source_target_pairs={{16,2},{2,16},{0,18},{18,0},{17,3},{3,17},{1,19},{19,1},{20,6},{6,... | collective-permute-start | bytes 1572872 | tf_op jit(solution)/shard_map/ppermute | solution.py:55
  7.9 16.5 %collective-permute-start.2 = (bf16[2,128,1024]{2,1,0:T(8,128)(2,1)S(1)}, bf16[2,128,1024]{2,1,0:T(8,128)(2,1)S(1)}, u32[]{:S(2)}, u32[]{:S(2)}) collective-permute-start(bf16[2,128,1024]{2,1,0:T(8,128)(2,1)S(1)} %pad_maximum_fusion.1), channel_id=1, source_target_pairs={{0,1},{1,0},{2,3},{3,2},{4,5},{5,4},{6,7},{7,6},{8,9},{9,8},{10,11... | collective-permute-start | bytes 1572872 | tf_op jit(solution)/shard_map/ppermute | solution.py:43
  19.7 12.6 %collective-permute-start.6 = (bf16[2,128,1024]{2,1,0:T(8,128)(2,1)S(1)}, bf16[2,128,1024]{2,1,0:T(8,128)(2,1)}, u32[]{:S(2)}, u32[]{:S(2)}) collective-permute-start(bf16[2,128,1024]{2,1,0:T(8,128)(2,1)S(1)} %collective-permute-done.3.refs_2_), channel_id=1, source_target_pairs={{4,0},{8,4},{12,8},{0,12},{5,1},{9,5},{13,9},{1,13},{6,2},{10,6},{... | collective-permute-start | bytes 1572872 | tf_op jit(solution)/shard_map/ppermute | solution.py:47
  21.5 12.0 %collective-permute-start.7 = (bf16[2,128,1024]{2,1,0:T(8,128)(2,1)S(1)}, bf16[2,128,1024]{2,1,0:T(8,128)(2,1)}, u32[]{:S(2)}, u32[]{:S(2)}) collective-permute-start(bf16[2,128,1024]{2,1,0:T(8,128)(2,1)S(1)} %collective-permute-done.3.refs_2_), channel_id=1, source_target_pairs={{16,2},{2,16},{0,18},{18,0},{17,3},{3,17},{1,19},{19,1},{20,6},{6,... | collective-permute-start | bytes 1572872 | tf_op jit(solution)/shard_map/ppermute | solution.py:55
  22.1 18.9 %collective-permute-start.12 = (bf16[288,1024]{1,0:T(8,128)(2,1)S(1)}, bf16[288,1024]{1,0:T(8,128)(2,1)S(1)}, u32[]{:S(2)}, u32[]{:S(2)}) collective-permute-start(bf16[288,1024]{1,0:T(8,128)(2,1)S(1)} %constant_dynamic-slice_fusion.2), channel_id=1, source_target_pairs={{0,1},{1,0},{2,3},{3,2},{4,5},{5,4},{6,7},{7,6},{8,9},{9,8},{10,11... | collective-permute-start | bytes 1769480 | tf_op jit(solution)/shard_map/ppermute | solution.py:43
  22.2 2.0 collective-permute-start.13
  24.2 15.5 %collective-permute-start.8 = (bf16[2,128,1024]{2,1,0:T(8,128)(2,1)}, bf16[2,128,1024]{2,1,0:T(8,128)(2,1)}, u32[]{:S(2)}, u32[]{:S(2)}) collective-permute-start(bf16[2,128,1024]{2,1,0:T(8,128)(2,1)} %collective-permute-done.5.refs_4_), channel_id=1, source_target_pairs={{0,4},{4,8},{8,12},{12,0},{1,5},{5,9},{9,13},{13,1},{2,6},{6,10},{... | collective-permute-start | bytes 1572872 | tf_op jit(solution)/shard_map/ppermute | solution.py:51
  24.4 24.2 %collective-permute-start.10 = (bf16[2,128,1024]{2,1,0:T(8,128)(2,1)S(1)}, bf16[2,128,1024]{2,1,0:T(8,128)(2,1)S(1)}, u32[]{:S(2)}, u32[]{:S(2)}) collective-permute-start(bf16[2,128,1024]{2,1,0:T(8,128)(2,1)S(1)} %collective-permute-done.4.refs_3_), channel_id=1, source_target_pairs={{1,32},{0,33},{33,64},{32,65},{65,96},{64,97},{97,128},{96,129},{1... | collective-permute-start | bytes 1572872 | tf_op jit(solution)/shard_map/ppermute | solution.py:63
  32.3 34.4 %collective-permute-start = (bf16[288,2048]{1,0:T(8,128)(2,1)}, bf16[288,2048]{1,0:T(8,128)(2,1)}, u32[]{:S(2)}, u32[]{:S(2)}) collective-permute-start(bf16[288,2048]{1,0:T(8,128)(2,1)} %student_own.1), channel_id=1, source_target_pairs={{0,1},{1,0},{2,3},{3,2},{4,5},{5,4},{6,7},{7,6},{8,9},{9,8},{10,11... | collective-permute-start | bytes 3538952 | tf_op jit(solution)/shard_map/ppermute | solution.py:43
  33.5 37.2 %collective-permute-start.1 = (bf16[288,2048]{1,0:T(8,128)(2,1)}, bf16[288,2048]{1,0:T(8,128)(2,1)}, u32[]{:S(2)}, u32[]{:S(2)}) collective-permute-start(bf16[288,2048]{1,0:T(8,128)(2,1)} %teacher_own.1), channel_id=1, source_target_pairs={{0,1},{1,0},{2,3},{3,2},{4,5},{5,4},{6,7},{7,6},{8,9},{9,8},{10,11... | collective-permute-start | bytes 3538952 | tf_op jit(solution)/shard_map/ppermute | solution.py:43
  39.7 13.5 %collective-permute-start.11 = (bf16[2,128,1024]{2,1,0:T(8,128)(2,1)}, bf16[2,128,1024]{2,1,0:T(8,128)(2,1)S(1)}, u32[]{:S(2)}, u32[]{:S(2)}) collective-permute-start(bf16[2,128,1024]{2,1,0:T(8,128)(2,1)} %collective-permute-done.5.refs_4_), channel_id=1, source_target_pairs={{1,16},{0,17},{17,0},{16,1},{3,18},{2,19},{19,2},{18,3},{5,20},{4,... | collective-permute-start | bytes 1572872 | tf_op jit(solution)/shard_map/ppermute | solution.py:67
  41.0 17.6 %collective-permute-start.9 = (bf16[2,128,1024]{2,1,0:T(8,128)(2,1)S(1)}, bf16[2,128,1024]{2,1,0:T(8,128)(2,1)S(1)}, u32[]{:S(2)}, u32[]{:S(2)}) collective-permute-start(bf16[2,128,1024]{2,1,0:T(8,128)(2,1)S(1)} %collective-permute-done.3.refs_2_), channel_id=1, source_target_pairs={{33,0},{32,1},{65,32},{64,33},{97,64},{96,65},{129,96},{128,97},{1... | collective-permute-start | bytes 1572872 | tf_op jit(solution)/shard_map/ppermute | solution.py:59
  48.6 11.6 %collective-permute-start.14 = (bf16[128,1024]{1,0:T(8,128)(2,1)S(1)}, bf16[128,1024]{1,0:T(8,128)(2,1)S(1)}, u32[]{:S(2)}, u32[]{:S(2)}) collective-permute-start(bf16[128,1024]{1,0:T(8,128)(2,1)S(1)} %slice_bitcast_fusion.1), channel_id=1, source_target_pairs={{4,0},{8,4},{12,8},{0,12},{5,1},{9,5},{13,9},{1,13},{6,2},{10,6},{... | collective-permute-start | bytes 786440 | tf_op jit(solution)/shard_map/ppermute | solution.py:47
  54.1 10.5 %collective-permute-start.15 = (bf16[128,1024]{1,0:T(8,128)(2,1)S(1)}, bf16[128,1024]{1,0:T(8,128)(2,1)}, u32[]{:S(2)}, u32[]{:S(2)}) collective-permute-start(bf16[128,1024]{1,0:T(8,128)(2,1)S(1)} %slice_bitcast_fusion), channel_id=1, source_target_pairs={{0,4},{4,8},{8,12},{12,0},{1,5},{5,9},{9,13},{13,1},{2,6},{6,10},{... | collective-permute-start | bytes 786440 | tf_op jit(solution)/shard_map/ppermute | solution.py:51
  59.4 29.7 %collective-permute-start.17 = (bf16[2,128,1024]{2,1,0:T(8,128)(2,1)}, bf16[2,128,1024]{2,1,0:T(8,128)(2,1)S(1)}, u32[]{:S(2)}, u32[]{:S(2)}) collective-permute-start(bf16[2,128,1024]{2,1,0:T(8,128)(2,1)} %collective-permute-done.8.refs_6_), channel_id=1, source_target_pairs={{1,16},{0,17},{17,0},{16,1},{3,18},{2,19},{19,2},{18,3},{5,20},{4,... | collective-permute-start | bytes 1572872 | tf_op jit(solution)/shard_map/ppermute | solution.py:67
  60.2 28.9 %collective-permute-start.16 = (bf16[2,128,1024]{2,1,0:T(8,128)(2,1)}, bf16[2,128,1024]{2,1,0:T(8,128)(2,1)S(1)}, u32[]{:S(2)}, u32[]{:S(2)}) collective-permute-start(bf16[2,128,1024]{2,1,0:T(8,128)(2,1)} %collective-permute-done.6.refs_5_), channel_id=1, source_target_pairs={{33,0},{32,1},{65,32},{64,33},{97,64},{96,65},{129,96},{128,97},{1... | collective-permute-start | bytes 1572872 | tf_op jit(solution)/shard_map/ppermute | solution.py:59
  64.5 24.6 %collective-permute-start.18 = (bf16[2,128,1024]{2,1,0:T(8,128)(2,1)}, bf16[2,128,1024]{2,1,0:T(8,128)(2,1)}, u32[]{:S(2)}, u32[]{:S(2)}) collective-permute-start(bf16[2,128,1024]{2,1,0:T(8,128)(2,1)} %collective-permute-done.7.refs_7_), channel_id=1, source_target_pairs={{1,32},{0,33},{33,64},{32,65},{65,96},{64,97},{97,128},{96,129},{1... | collective-permute-start | bytes 1572872 | tf_op jit(solution)/shard_map/ppermute | solution.py:63
  66.7 22.4 %collective-permute-start.19 = (bf16[128,1024]{1,0:T(8,128)(2,1)S(1)}, bf16[128,1024]{1,0:T(8,128)(2,1)S(1)}, u32[]{:S(2)}, u32[]{:S(2)}) collective-permute-start(bf16[128,1024]{1,0:T(8,128)(2,1)S(1)} %collective-permute-done.14.refs_0_), channel_id=1, source_target_pairs={{33,0},{32,1},{65,32},{64,33},{97,64},{96,65},{129,96},{128,97},{1... | collective-permute-start | bytes 786440 | tf_op jit(solution)/shard_map/ppermute | solution.py:59
  70.7 18.4 %collective-permute-start.20 = (bf16[128,1024]{1,0:T(8,128)(2,1)}, bf16[128,1024]{1,0:T(8,128)(2,1)S(1)}, u32[]{:S(2)}, u32[]{:S(2)}) collective-permute-start(bf16[128,1024]{1,0:T(8,128)(2,1)} %collective-permute-done.15.refs_1_), channel_id=1, source_target_pairs={{1,32},{0,33},{33,64},{32,65},{65,96},{64,97},{97,128},{96,129},{1... | collective-permute-start | bytes 786440 | tf_op jit(solution)/shard_map/ppermute | solution.py:63
  193.3 21.0 %all-to-all-start.2 = ((bf16[16,2,16,512]{3,1,2,0:T(2,128)(2,1)}), bf16[16,2,16,512]{3,1,2,0:T(2,128)(2,1)S(1)}, u32[]{:S(2)}, u32[]{:S(2)}) async-start(bf16[16,2,16,512]{3,1,2,0:T(2,128)(2,1)} %broadcast_in_dim.2), calls=%async_computation.2 | async-start | bytes 1048576 | tf_op jit(solution)/shard_map/all_to_all | solution.py:75
  197.8 18.3 %collective-permute-start.23 = (bf16[288,1024]{1,0:T(8,128)(2,1)}, bf16[288,1024]{1,0:T(8,128)(2,1)S(1)}, u32[]{:S(2)}, u32[]{:S(2)}) collective-permute-start(bf16[288,1024]{1,0:T(8,128)(2,1)} %get-tuple-element.60), channel_id=1, source_target_pairs={{0,1},{1,0},{2,3},{3,2},{4,5},{5,4},{6,7},{7,6},{8,9},{9,8},{10,11... | collective-permute-start | bytes 1769480 | tf_op jit(solution)/shard_map/ppermute | solution.py:43
  216.2 3.7 %collective-permute-start.22 = (bf16[128,1024]{1,0:T(8,128)(2,1)}, bf16[128,1024]{1,0:T(8,128)(2,1)}, u32[]{:S(2)}, u32[]{:S(2)}) collective-permute-start(bf16[128,1024]{1,0:T(8,128)(2,1)} %bitcast.34), channel_id=1, source_target_pairs={{0,1},{1,0},{2,3},{3,2},{4,5},{5,4},{6,7},{7,6},{8,9},{9,8},{10,11... | collective-permute-start | bytes 786440 | tf_op jit(solution)/shard_map/ppermute | solution.py:43
  (25 other events, 243.7 us)

commit v3 on v2

--- a/solution.py
+++ b/solution.py
@@ -12,7 +12,7 @@
 PATCHES = 144
 EPS = 1e-06
 AXES = ("z", "xlo", "y", "xhi", "core")
-VMEM_LIMIT = 44 * 1024 * 1024
+VMEM_LIMIT = 60 * 1024 * 1024
 
 X_INDEX = (0, 2, 1, 3)
 CORE_SWAP = ((0, 1), (1, 0))
@@ -31,12 +31,7 @@
     return tuple((2 * a + 1 - core, 2 * b + core) for a, b in pairs for core in range(2))
 
 
-FSDP_GROUPS = tuple(
-    tuple((xhi ^ side) * 8 + y * 2 + xhi for y in range(4) for xhi in range(2)) for side in range(2)
-)
-DP_GROUPS = tuple(
-    tuple((z * 2 + xlo) * 2 + (side ^ ((z + xlo) & 1)) for z in range(8) for xlo in range(2)) for side in range(2)
-)
+DP_GROUPS = tuple(tuple(z * 2 + ((z + side) & 1) for z in range(8)) for side in range(2))
 
 
 def swap_cores(value):
@@ -67,12 +62,12 @@
     return lax.ppermute(value, ("xlo", "core"), with_core_flip(CORE_SWAP))
 
 
-def fsdp_exchange(value):
-    return lax.all_to_all(value, ("xlo", "y", "xhi"), 0, 0, axis_index_groups=FSDP_GROUPS)
-
-
-def dp_exchange(value):
-    return lax.all_to_all(value, ("z", "xlo", "core"), 0, 0, axis_index_groups=DP_GROUPS)
+def to_y_next(value):
+    return from_y_previous(value)
+
+
+def to_y_previous(value):
+    return from_y_next(value)
 
 
 EARLY = (
@@ -80,15 +75,22 @@
     (1, 0, 1),
 )
 LATE = ((0, 2, 1), (1, 2, 0), (1, 3, 1), (1, 1, 1), (1, 2, 1))
-
-
-def gather_rows(own, other):
-    up, down, across = lax.optimization_barrier((from_y_next(own), from_y_previous(own), from_x_near(own)))
+SENT = ((1, 2, 1), (1, 2, 0), (1, 1, 1), (1, 3, 0), (1, 3, 1), (1, 1, 0), (1, 0, 1), (1, 0, 0))
+KEPT = tuple((0, dy, dx) for side, dy, dx in SENT)
+HALF_AT = len(EARLY) + len(LATE)
+TURNED_AT = HALF_AT + 1
+
+
+def gather_rows(own, other, swapped):
+    up, down, across = from_y_next(own), from_y_previous(own), from_x_near(own)
+    up, down, across, other, *swapped = lax.optimization_barrier((up, down, across, other, *swapped))
     up_two = from_y_next(up)
     across_up = from_x_near(up)
     across_down = from_y_previous(across)
     passed_up, passed_down, passed_across = from_z_next(up), from_z_previous(down), from_x_twin(across)
-    up_two, across_up, across_down = lax.optimization_barrier((up_two, across_up, across_down))
+    up_two, across_up, across_down, passed_up, passed_down, passed_across = lax.optimization_barrier(
+        (up_two, across_up, across_down, passed_up, passed_down, passed_across)
+    )
     student = from_y_next(across_up[0])
     teacher = from_y_previous(across_down[1])
     passed_two = from_z_next(up_two)
@@ -103,7 +105,7 @@
     late = (
         student, teacher, passed_two, passed_across_down, passed_across_up, passed_student, passed_teacher,
     )
-    return early, late
+    return early, late, swapped
 
 
 def early_kernel(order, student_own, student_other, teacher_own, teacher_other, *refs):
@@ -131,9 +133,10 @@
         held[1, rows, :] = weights[block][1]
     student_out[...] = jnp.dot(mix[0], held[0], preferred_element_type=jnp.float32)
     teacher_out[...] = jnp.dot(mix[1], held[1], preferred_element_type=jnp.float32)
-    width = turned.shape[0]
-    columns = pl.ds(pl.multiple_of(step * width, width), width)
-    turned[...] = jnp.concatenate([student_own[:, columns], student_other[:, columns]], axis=0).T
+    for block in range(turned.shape[0]):
+        spot = order[TURNED_AT + step * turned.shape[0] + block]
+        columns = pl.ds(pl.multiple_of(spot * 128, 128), 128)
+        turned[block] = jnp.concatenate([student_own[:, columns], student_other[:, columns]], axis=0).T
 
 
 def early_forward(order, weights, student_own, student_other, teacher_own, teacher_other):
@@ -148,7 +151,7 @@
             num_scalar_prefetch=1,
             grid=(steps,),
             in_specs=[whole] * 4 + [pl.BlockSpec((2, 128, width), lambda j, order: (0, 0, j))] * count,
-            out_specs=[column, column, late, late, pl.BlockSpec((KIN // steps, rows), lambda j, order: (j, 0))],
+            out_specs=[column, column, late, late, pl.BlockSpec((16 // steps, 128, rows), lambda j, order: (j, 0, 0))],
             scratch_shapes=[
                 pltpu.VMEM((2, rows, count * 128), jnp.bfloat16),
                 pltpu.VMEM((2, count * 128, width), jnp.bfloat16),
@@ -159,7 +162,7 @@
             jax.ShapeDtypeStruct((rows, columns), jnp.float32),
             jax.ShapeDtypeStruct((rows, len(LATE) * 128), jnp.bfloat16),
             jax.ShapeDtypeStruct((rows, len(LATE) * 128), jnp.bfloat16),
-            jax.ShapeDtypeStruct((KIN, rows), jnp.bfloat16),
+            jax.ShapeDtypeStruct((16, 128, rows), jnp.bfloat16),
         ],
         compiler_params=pltpu.CompilerParams(vmem_limit_bytes=VMEM_LIMIT),
         cost_estimate=pl.CostEstimate(
@@ -233,7 +236,6 @@
 ):
     (rows, columns), own, width, depth = student_part.shape, residual_own.shape[0], 256, student_mix.shape[1]
     steps = columns // width
-    half_at = len(EARLY) + len(LATE)
     mix = pl.BlockSpec((rows, depth), lambda j, order: (0, 0))
     column = pl.BlockSpec((rows, width), lambda j, order: (0, j))
     places = pl.BlockSpec((own, 1), lambda j, order: (0, 0))
@@ -249,9 +251,9 @@
                 mix,
                 column,
                 column,
-                pl.BlockSpec((own, width), lambda j, order: (0, order[half_at] * steps + j)),
+                pl.BlockSpec((own, width), lambda j, order: (0, order[HALF_AT] * steps + j)),
                 pl.BlockSpec((own, width), lambda j, order: (0, j)),
-                pl.BlockSpec((1, width), lambda j, order: (0, order[half_at] * steps + j)),
+                pl.BlockSpec((1, width), lambda j, order: (0, order[HALF_AT] * steps + j)),
                 places,
                 places,
                 single,
@@ -280,69 +282,199 @@
     )
 
 
-def backward_kernel(total_tokens, order, student, matched, sums, more_sums, scale, mix, grad_out, tokens_out, held):
-    @pl.when(pl.program_id(0) == 0)
-    def _():
-        own = more_sums.shape[0] // 2
-        swapped = jnp.concatenate([more_sums[own:, :], more_sums[:own, :]], axis=0)
-        total = (sums[...] + swapped) * (1.0 / DOUT)
-        inverse_rms = lax.rsqrt(total[:, 0:1] + EPS)
-        inverse_matched = lax.rsqrt(total[:, 1:2] + EPS)
-        overlap = inverse_rms * inverse_matched * total[:, 2:3]
-        shared = inverse_rms * (1.0 / total_tokens)
-        student_part = shared * inverse_rms * (EPS * inverse_rms * inverse_rms + overlap)
-        matched_part = shared * inverse_matched
-        values = student[...]
-        tokens_out[...] = (values * inverse_rms).astype(jnp.bfloat16)
-        factor = scale[...] * (KIN ** (-0.5))
-        held[...] = (factor * (values * student_part - matched[...] * matched_part)).astype(jnp.bfloat16)
-
-    width = grad_out.shape[-1]
-    for part in range(grad_out.shape[1]):
-        grad_out[0, part] = jnp.dot(
-            mix[...], held[:, part * width : (part + 1) * width], preferred_element_type=jnp.float32
-        ).astype(jnp.bfloat16)
-
-
-def backward(total_tokens, order, student, matched, sums, more_sums, scale, mix):
-    rows, columns = student.shape
-    depth = 256
-    half_at = len(EARLY) + len(LATE)
-    whole = pl.BlockSpec((rows, columns), lambda i, order: (0, 0))
-    narrow = pl.BlockSpec((rows, 128), lambda i, order: (0, 0))
+def send_kernel(
+    total_tokens, order, student, matched, sums, more_sums, scale, mix, next_out, previous_out, twin_out, held_out,
+    tokens_out
+):
+    own = more_sums.shape[0] // 2
+    swapped = jnp.concatenate([more_sums[own:, :], more_sums[:own, :]], axis=0)
+    total = (sums[...] + swapped) * (1.0 / DOUT)
+    inverse_rms = lax.rsqrt(total[:, 0:1] + EPS)
+    inverse_matched = lax.rsqrt(total[:, 1:2] + EPS)
+    overlap = inverse_rms * inverse_matched * total[:, 2:3]
+    shared = inverse_rms * (1.0 / total_tokens)
+    student_part = shared * inverse_rms * (EPS * inverse_rms * inverse_rms + overlap)
+    matched_part = shared * inverse_matched
+    values = student[...]
+    tokens_out[...] = (values * inverse_rms).astype(jnp.bfloat16)
+    factor = scale[...] * (KIN ** (-0.5))
+    held_out[...] = (factor * (values * student_part - matched[...] * matched_part)).astype(jnp.bfloat16)
+    at = 0
+    for out in (next_out, previous_out, twin_out):
+        count = out.shape[0]
+        grad = jnp.dot(
+            mix[at : at + count].reshape(count * 128, mix.shape[-1]),
+            held_out[...],
+            preferred_element_type=jnp.float32,
+        )
+        out[...] = grad.astype(jnp.bfloat16).reshape(out.shape)
+        at += count
+
+
+def send_grads(total_tokens, order, student, matched, sums, more_sums, scale, turned):
+    (rows, columns), width = student.shape, 256
+    steps = columns // width
+    column = pl.BlockSpec((rows, width), lambda j, order: (0, j))
+    narrow = pl.BlockSpec((rows, 128), lambda j, order: (0, 0))
+
+    def blocks(count):
+        return pl.BlockSpec((count, 128, width), lambda j, order: (0, 0, j))
+
     return pl.pallas_call(
-        functools.partial(backward_kernel, total_tokens),
+        functools.partial(send_kernel, total_tokens),
         grid_spec=pltpu.PrefetchScalarGridSpec(
             num_scalar_prefetch=1,
-            grid=(KIN // depth,),
+            grid=(steps,),
             in_specs=[
-                whole,
-                whole,
+                column,
+                column,
                 narrow,
                 narrow,
-                pl.BlockSpec((1, columns), lambda i, order: (0, order[half_at])),
-                pl.BlockSpec((depth, rows), lambda i, order: (i, 0)),
+                pl.BlockSpec((1, width), lambda j, order: (0, order[HALF_AT] * steps + j)),
+                pl.BlockSpec((8, 128, rows), lambda j, order: (0, 0, 0)),
             ],
-            out_specs=[pl.BlockSpec((1, 2, depth, columns // 2), lambda i, order: (i, 0, 0, 0)), whole],
-            scratch_shapes=[pltpu.VMEM((rows, columns), jnp.bfloat16)],
+            out_specs=[blocks(3), blocks(3), blocks(2), column, column],
         ),
         out_shape=[
-            jax.ShapeDtypeStruct((KIN // depth, 2, depth, columns // 2), jnp.bfloat16),
+            jax.ShapeDtypeStruct((3, 128, columns), jnp.bfloat16),
+            jax.ShapeDtypeStruct((3, 128, columns), jnp.bfloat16),
+            jax.ShapeDtypeStruct((2, 128, columns), jnp.bfloat16),
+            jax.ShapeDtypeStruct((rows, columns), jnp.bfloat16),
             jax.ShapeDtypeStruct((rows, columns), jnp.bfloat16),
         ],
         compiler_params=pltpu.CompilerParams(vmem_limit_bytes=VMEM_LIMIT),
         cost_estimate=pl.CostEstimate(
-            flops=2 * rows * KIN * columns, bytes_accessed=12 * 1024 * 1024, transcendentals=0
-        ),
-    )(order, student, matched, sums, more_sums, scale, mix)
-
-
-def adamw_update(grad, weight, teacher, first, squares):
-    first_next = 0.9 * first + 0.1 * grad
-    squares_next = 0.95 * squares + 0.05 * grad * grad
-    weight_next = weight - 0.1 * (first_next / (jnp.sqrt(squares_next) + 1e-08) + 0.04 * weight)
-    teacher_next = 0.96 * teacher + 0.04 * weight_next
-    return (weight_next, teacher_next, first_next, squares_next)
+            flops=rows * KIN * columns, bytes_accessed=12 * 1024 * 1024, transcendentals=0
+        ),
+    )(order, student, matched, sums, more_sums, scale, turned)
+
+
+def keep_kernel(held, mix, out):
+    grad = jnp.dot(
+        mix[...].reshape(8 * 128, mix.shape[-1]), held[...], preferred_element_type=jnp.float32
+    )
+    out[...] = grad.reshape(out.shape)
+
+
+def keep_grads(held, turned):
+    (rows, columns), width = held.shape, 256
+    return pl.pallas_call(
+        keep_kernel,
+        grid=(columns // width,),
+        in_specs=[
+            pl.BlockSpec((rows, width), lambda j: (0, j)),
+            pl.BlockSpec((8, 128, rows), lambda j: (1, 0, 0)),
+        ],
+        out_specs=pl.BlockSpec((8, 128, width), lambda j: (0, 0, j)),
+        out_shape=jax.ShapeDtypeStruct((8, 128, columns), jnp.float32),
+        compiler_params=pltpu.CompilerParams(vmem_limit_bytes=VMEM_LIMIT),
+        cost_estimate=pl.CostEstimate(
+            flops=rows * KIN * columns, bytes_accessed=7 * 1024 * 1024, transcendentals=0
+        ),
+    )(held, turned)
+
+
+def add_kernel(plan, count, *refs):
+    inputs, outs = refs[:count], refs[count:]
+    at = 0
+    for out, (rows, terms) in zip(outs, plan):
+        total = None
+        for skip in terms:
+            ref = inputs[at]
+            value = (ref[0] if len(ref.shape) == 3 else ref[...]).astype(jnp.float32)
+            if value.shape[0] < rows.stop - rows.start:
+                gap = jnp.zeros_like(value)
+                value = jnp.concatenate([gap, value] if skip else [value, gap], axis=0)
+            else:
+                value = value[rows]
+            total = value if total is None else total + value
+            at += 1
+        out[...] = total.astype(jnp.bfloat16)
+
+
+def add_blocks(*outs):
+    width, operands, specs, plan = 512, [], [], []
+    for rows, terms in outs:
+        skips = []
+        for array, index in terms:
+            operands.append(array)
+            skips.append(index == "second")
+            if array.ndim == 3:
+                specs.append(pl.BlockSpec((1, 128, width), functools.partial(lambda at, j: (at, 0, j), index)))
+            else:
+                specs.append(pl.BlockSpec((array.shape[0], width), lambda j: (0, j)))
+        plan.append((rows, tuple(skips)))
+    columns = operands[0].shape[-1]
+    sizes = [rows.stop - rows.start for rows, _ in plan]
+    return pl.pallas_call(
+        functools.partial(add_kernel, tuple(plan), len(operands)),
+        grid=(columns // width,),
+        in_specs=specs,
+        out_specs=[pl.BlockSpec((size, width), lambda j: (0, j)) for size in sizes],
+        out_shape=[jax.ShapeDtypeStruct((size, columns), jnp.bfloat16) for size in sizes],
+        compiler_params=pltpu.CompilerParams(vmem_limit_bytes=VMEM_LIMIT),
+    )(*operands)
+
+
+def reduce_rows(kept, next_sent, previous_sent, twin_sent):
+    passed = (from_z_previous(next_sent), from_z_next(previous_sent), from_x_twin(twin_sent))
+    passed = lax.optimization_barrier(passed)
+    places = {}
+    for number, (_, dy, dx) in enumerate(SENT):
+        group = 0 if number < 3 else 1 if number < 6 else 2
+        places[dy, dx] = ((kept, number), (passed[group], number - 3 * group))
+    whole = slice(0, 128)
+    first, last, up_two, down = add_blocks(
+        (slice(0, 64), places[2, 1]), (slice(64, 128), places[2, 1]), (whole, places[2, 0]), (whole, places[3, 0])
+    )
+    first, last = to_y_next(first), to_y_previous(last)
+    up_two, down = to_y_next(up_two), to_y_previous(down)
+    first, last = lax.optimization_barrier((first, last))
+    across_up, across_down = add_blocks(
+        (whole, places[1, 1] + ((first, None),)), (whole, places[3, 1] + ((last, "second"),))
+    )
+    across_up, across_down, up_two = lax.optimization_barrier(
+        (from_x_near(across_up), to_y_previous(across_down), up_two)
+    )
+    up, across = add_blocks(
+        (whole, places[1, 0] + ((up_two, None), (across_up, None))), (whole, places[0, 1] + ((across_down, None),))
+    )
+    up, across, down = lax.optimization_barrier((to_y_next(up), from_x_near(across), down))
+    (total,) = add_blocks((whole, places[0, 0] + ((up, None), (down, None), (across, None))))
+    return total
+
+
+def update_kernel(flip, grads, weight, teacher, first, squares, weight_out, teacher_out, first_out, squares_out):
+    rows = []
+    for index in range(grads.shape[0]):
+        swap = ((flip[0] + index) & 1) == 1
+        left = jnp.where(swap, grads[index, 1], grads[index, 0])
+        right = jnp.where(swap, grads[index, 0], grads[index, 1])
+        rows.append(jnp.concatenate([left, right], axis=1))
+    grad = jnp.concatenate(rows, axis=0).astype(jnp.float32)
+    first_next = 0.9 * first[...] + 0.1 * grad
+    squares_next = 0.95 * squares[...] + 0.05 * grad * grad
+    held = weight[...]
+    weight_next = held - 0.1 * (first_next / (jnp.sqrt(squares_next) + 1e-08) + 0.04 * held)
+    weight_out[...] = weight_next
+    teacher_out[...] = 0.96 * teacher[...] + 0.04 * weight_next
+    first_out[...] = first_next
+    squares_out[...] = squares_next
+
+
+def adamw_update(flip, grads, weight, teacher, first, squares):
+    rows = pl.BlockSpec((32, DOUT), lambda i, flip: (i, 0))
+    return pl.pallas_call(
+        update_kernel,
+        grid_spec=pltpu.PrefetchScalarGridSpec(
+            num_scalar_prefetch=1,
+            grid=(4,),
+            in_specs=[pl.BlockSpec((2, 2, 16, DOUT // 2), lambda i, flip: (i, 0, 0, 0))] + [rows] * 4,
+            out_specs=[rows] * 4,
+        ),
+        out_shape=[jax.ShapeDtypeStruct(weight.shape, jnp.float32)] * 4,
+        compiler_params=pltpu.CompilerParams(vmem_limit_bytes=VMEM_LIMIT),
+    )(flip, grads, weight, teacher, first, squares)
 
 
 def join_columns(which, own, other):
@@ -381,6 +513,7 @@
             for side, dy, dx in EARLY + LATE
         ]
         + [which]
+        + [(((y + dy) & 3) * 2 + (xhi ^ dx)) * 2 + (core ^ side) for side, dy, dx in SENT + KEPT]
     ).astype(jnp.int32)
     own, student_sent, teacher_sent, residual_sent, positions_sent, student_held, teacher_held = (
         lax.optimization_barrier(
@@ -392,11 +525,14 @@
     student_other = swap_cores(student_sent)
     teacher_other = swap_cores(teacher_sent)
     residual_other = swap_cores(columns_of(residual_sent, 1 - which))
-    places_other = swap_cores(positions_sent).reshape(token_count, 1)
+    places_other = swap_cores(positions_sent)
     places = positions.reshape(token_count, 1)
     scale = layer_scale.reshape(1, DOUT)
 
-    early, late = gather_rows(own, other)
+    early, late, (student_other, teacher_other, residual_other, places_other) = gather_rows(
+        own, other, (student_other, teacher_other, residual_other, places_other)
+    )
+    places_other = places_other.reshape(token_count, 1)
     student_part, teacher_part, student_late, teacher_late, turned = early_forward(
         order, early, student_mix, student_other, teacher_mix, teacher_other
     )
@@ -404,26 +540,21 @@
         order, late, student_late, teacher_late, student_part, teacher_part, residual, residual_other, scale, places,
         places_other
     )
-    grads, tokens = backward(
+    next_sent, previous_sent, twin_sent, held, tokens = send_grads(
         total_tokens, order, student_out, matched, sums, swap_cores(sums), scale, turned
     )
-
+    kept = keep_grads(held, turned)
     student_tokens = join_columns(which, tokens[:token_count], swap_cores(tokens[token_count:]))
-
-    by_chip = fsdp_exchange(grads)
-    chip_rows = jnp.sum(by_chip.astype(jnp.float32), axis=0).astype(jnp.bfloat16)
-    by_copy = dp_exchange(chip_rows.reshape(2, 16, 16, half // 2).transpose(1, 0, 2, 3))
+    total = reduce_rows(kept, next_sent, previous_sent, twin_sent)
+    total, student_tokens = lax.optimization_barrier((total, student_tokens))
+    by_copy = lax.all_to_all(
+        total.reshape(8, 16, half), ("z", "xlo"), 0, 0, axis_index_groups=DP_GROUPS
+    )
     copy_rows = jnp.sum(by_copy.astype(jnp.float32), axis=0).astype(jnp.bfloat16)
-    full = dp_exchange(jnp.broadcast_to(copy_rows[None], (16, 2, 16, half // 2)))
-
-    def rows_of(index):
-        return (
-            lax.dynamic_slice_in_dim(full, index * 8, 8, axis=0).transpose(0, 2, 1, 3).reshape(128, half)
-        )
-
-    grad = join_columns(which, rows_of(core), swap_cores(rows_of(1 - core))).astype(jnp.float32)
+    full = lax.all_to_all(jnp.broadcast_to(copy_rows[None], (16, 16, half)), ("z", "xlo"), 0, 0)
+    flip = ((core + xhi) & 1).astype(jnp.int32).reshape(1)
     weight_next, teacher_next, first_next, squares_next = adamw_update(
-        grad, student_weight, teacher_weight, moment, second
+        flip, full.reshape(8, 2, 16, half), student_weight, teacher_weight, moment, second
     )
     return (weight_next, teacher_next, first_next, squares_next, student_tokens)
 

time: 228 us -> 215 us (0.943)
  blocking collectives: 81.2 us -> 15 us
  waiting for transfers between devices: 53.1 us -> 80.8 us
  Pallas kernels: 26.4 us -> 49.5 us
  starting transfers between devices: 30.8 us -> 45.3 us
  other arithmetic: 10 us -> 1.61 us
    all_to_all x2 -> x1, blocking collectives: 81.2 us -> 15 us  [shards(): lax.all_to_all(total.reshape(8, 16, half), ('z', 'xlo'), 0, 0, axis_index...]
    pallas_call x1 -> x7, Pallas kernels: 7.51 us -> 27.9 us  [the longest x4 9.53 us: add_blocks(): pl.pallas_call(functools.partial(add_kernel, tuple(plan), len(operands)),...]
    ppermute x2 -> x4, waiting for transfers between devices: 1.27 us -> 15.7 us  [from_x_near(): return lax.ppermute(value, ('xlo', 'xhi'), X_NEAR)]
    ppermute x3 -> x6, starting transfers between devices: 5.02 us -> 16.9 us  [from_y_next(): return lax.ppermute(value, 'y', from_next(4))]
    ppermute x3 -> x6, waiting for transfers between devices: 9.99 us -> 18.3 us  [from_y_previous(): return lax.ppermute(value, 'y', from_previous(4))]
    ppermute x2 -> x3, waiting for transfers between devices: 3.46 us -> 9.97 us  [from_x_twin(): return lax.ppermute(value, ('xlo', 'core'), with_core_flip(CORE_SWAP))]
    ppermute x3 -> x4, waiting for transfers between devices: 4.5 us -> 0.18 us  [from_z_next(): return lax.ppermute(value, ('z', 'core'), with_core_flip(from_next(8)))]
    ppermute x3 -> x4, waiting for transfers between devices: 0.01 us -> 4.13 us  [from_z_previous(): return lax.ppermute(value, ('z', 'core'), with_core_flip(from_previous(8)))]
  transfers between devices with their start and end apart: 25 -> 35, of which waited for: 11 -> 18; matrix products, arithmetic and copies ran while one was open for 5% -> 4% of each run, Pallas kernels for 5% -> 12%
where the time goes in v3:
time: 215 us; the launch traced here: 213 us
  waiting for transfers between devices  80.8 us (38%)
  Pallas kernels  49.5 us (23%)
  starting transfers between devices  45.3 us (21%)
  local copies, waits for them, and re-layouts  19.6 us (9%)
  blocking collectives  15 us (7%)
    ppermute x6, waiting for transfers between devices, from_y_previous(): return lax.ppermute(value, 'y', from_previous(4))  18.3 us
    ppermute x6, waiting for transfers between devices, from_y_next(): return lax.ppermute(value, 'y', from_next(4))  17.7 us
    ppermute x4, starting transfers between devices, from_z_next(): return lax.ppermute(value, ('z', 'core'), with_core_flip(from_next(8)))  17.5 us
    ppermute x6, starting transfers between devices, from_y_next(): return lax.ppermute(value, 'y', from_next(4))  16.9 us
    ppermute x4, waiting for transfers between devices, from_x_near(): return lax.ppermute(value, ('xlo', 'xhi'), X_NEAR)  15.7 us
    all_to_all x1, blocking collectives, shards(): lax.all_to_all(total.reshape(8, 16, half), ('z', 'xlo'), 0, 0, axis_index...  15 us
    all_to_all x1, waiting for transfers between devices, shards(): lax.all_to_all(jnp.broadcast_to(copy_rows[None], (16, 16, half)), ('z', '...  13.3 us
    pallas_call x1, Pallas kernels, early_forward(): pl.pallas_call(early_kernel, grid_spec=pltpu.PrefetchScalarGridSpec(num_s...  12.1 us
  transfers between devices with their start and end apart: 35, of which 18 were waited for; matrix products, arithmetic and copies ran while one was open for 4% of the time, Pallas kernels for 12%

profile of v3, /device:TPU:4, one launch (start us, length us, event | category | flops | bytes accessed | tf_op | source)
XLA Modules:
  0.0 212.9 jit_solution(5714339573288340115)
XLA Ops:
  8.7 8.5 %collective-permute-done.refs_2_ = bf16[2,128,1024]{2,1,0:T(8,128)(2,1)} collective-permute-done((bf16[2,128,1024]{2,1,0:T(8,128)(2,1)S(1)}, bf16[2,128,1024]{2,1,0:T(8,128)(2,1)}, u32[]{:S(2)}, u32[]{:S(2)}) %collective-permute-start) | collective-permute-done | bytes 524320 | tf_op jit(solution)/shard_map/ppermute | solution.py:42
  20.8 9.6 %collective-permute-done.2.refs_4_ = bf16[2,128,1024]{2,1,0:T(8,128)(2,1)S(1)} collective-permute-done((bf16[2,128,1024]{2,1,0:T(8,128)(2,1)S(1)}, bf16[2,128,1024]{2,1,0:T(8,128)(2,1)S(1)}, u32[]{:S(2)}, u32[]{:S(2)}) %collective-permute-start.2) | collective-permute-done | bytes 524320 | tf_op jit(solution)/shard_map/ppermute | solution.py:50
  30.4 3.9 %collective-permute-start.8 = (bf16[2,128,1024]{2,1,0:T(8,128)(2,1)}, bf16[2,128,1024]{2,1,0:T(8,128)(2,1)}, u32[]{:S(2)}, u32[]{:S(2)}) collective-permute-start(bf16[2,128,1024]{2,1,0:T(8,128)(2,1)} %collective-permute-done.refs_2_), channel_id=1, source_target_pairs={{4,0},{8,4},{12,8},{0,12},{5,1},{9,5},{13,9},{1,13},{6,2},{10,6},{... | collective-permute-start | bytes 1572872 | tf_op jit(solution)/shard_map/ppermute | solution.py:42
  34.8 3.2 %collective-permute-start.11 = (bf16[2,128,1024]{2,1,0:T(8,128)(2,1)}, bf16[2,128,1024]{2,1,0:T(8,128)(2,1)S(1)}, u32[]{:S(2)}, u32[]{:S(2)}) collective-permute-start(bf16[2,128,1024]{2,1,0:T(8,128)(2,1)} %collective-permute-done.refs_2_), channel_id=1, source_target_pairs={{33,0},{32,1},{65,32},{64,33},{97,64},{96,65},{129,96},{128,97},{1... | collective-permute-start | bytes 1572872 | tf_op jit(solution)/shard_map/ppermute | solution.py:54
  38.1 6.2 %collective-permute-done.8.refs_5_ = bf16[2,128,1024]{2,1,0:T(8,128)(2,1)} collective-permute-done((bf16[2,128,1024]{2,1,0:T(8,128)(2,1)}, bf16[2,128,1024]{2,1,0:T(8,128)(2,1)}, u32[]{:S(2)}, u32[]{:S(2)}) %collective-permute-start.8) | collective-permute-done | bytes 524320 | tf_op jit(solution)/shard_map/ppermute | solution.py:42
  46.5 5.9 %collective-permute-done.10.refs_6_ = bf16[2,128,1024]{2,1,0:T(8,128)(2,1)} collective-permute-done((bf16[2,128,1024]{2,1,0:T(8,128)(2,1)S(1)}, bf16[2,128,1024]{2,1,0:T(8,128)(2,1)}, u32[]{:S(2)}, u32[]{:S(2)}) %collective-permute-start.10) | collective-permute-done | bytes 524320 | tf_op jit(solution)/shard_map/ppermute | solution.py:46
  53.9 3.7 %collective-permute-done.13.refs_10_ = bf16[2,128,1024]{2,1,0:T(8,128)(2,1)} collective-permute-done((bf16[2,128,1024]{2,1,0:T(8,128)(2,1)S(1)}, bf16[2,128,1024]{2,1,0:T(8,128)(2,1)}, u32[]{:S(2)}, u32[]{:S(2)}) %collective-permute-start.13) | collective-permute-done | bytes 524320 | tf_op jit(solution)/shard_map/ppermute | solution.py:62
  58.6 3.8 %collective-permute-start.14 = (bf16[128,1024]{1,0:T(8,128)(2,1)S(1)}, bf16[128,1024]{1,0:T(8,128)(2,1)S(1)}, u32[]{:S(2)}, u32[]{:S(2)}) collective-permute-start(bf16[128,1024]{1,0:T(8,128)(2,1)S(1)} %slice_bitcast_fusion.1), channel_id=1, source_target_pairs={{4,0},{8,4},{12,8},{0,12},{5,1},{9,5},{13,9},{1,13},{6,2},{10,6},{... | collective-permute-start | bytes 786440 | tf_op jit(solution)/shard_map/ppermute | solution.py:42
  63.5 6.0 %collective-permute-start.16 = (bf16[2,128,1024]{2,1,0:T(8,128)(2,1)}, bf16[2,128,1024]{2,1,0:T(8,128)(2,1)S(1)}, u32[]{:S(2)}, u32[]{:S(2)}) collective-permute-start(bf16[2,128,1024]{2,1,0:T(8,128)(2,1)} %collective-permute-done.8.refs_5_), channel_id=1, source_target_pairs={{33,0},{32,1},{65,32},{64,33},{97,64},{96,65},{129,96},{128,97},{1... | collective-permute-start | bytes 1572872 | tf_op jit(solution)/shard_map/ppermute | solution.py:54
  73.4 5.2 %collective-permute-start.19 = (bf16[128,1024]{1,0:T(8,128)(2,1)S(1)}, bf16[128,1024]{1,0:T(8,128)(2,1)S(1)}, u32[]{:S(2)}, u32[]{:S(2)}) collective-permute-start(bf16[128,1024]{1,0:T(8,128)(2,1)S(1)} %collective-permute-done.14.refs_0_), channel_id=1, source_target_pairs={{33,0},{32,1},{65,32},{64,33},{97,64},{96,65},{129,96},{128,97},{1... | collective-permute-start | bytes 786440 | tf_op jit(solution)/shard_map/ppermute | solution.py:54
  78.5 12.1 %shard_map.128 = (f32[576,1024]{1,0:T(8,128)}, f32[576,1024]{1,0:T(8,128)}, bf16[576,640]{1,0:T(8,128)(2,1)}, bf16[576,640]{1,0:T(8,128)(2,1)}, bf16[16,128,576]{2,1,0:T(8,128)(2,1)}) custom-call(s32[33]{0:T(128)} %stack.111.order, bf16[288,2048]{1,0:T(8,128)(2,1)} %student_own.1, bf16[288,2048]{1,0:T(8,128)(2,1)} %collective-permute-done.4.student_other, ...), custom_call_target="tpu_custom_call" | custom-call | flops 3321888768 | bytes 18874368 | tf_op jit(solution)/shard_map/pallas_call | solution.py:148
  92.3 9.6 %shard_map.129 = (f32[576,1024]{1,0:T(8,128)}, f32[576,1024]{1,0:T(8,128)}, f32[576,128]{1,0:T(8,128)}) custom-call(s32[33]{0:T(128)} %stack.111.order, bf16[576,640]{1,0:T(8,128)(2,1)} %get-tuple-element.85.student_mix, bf16[576,640]{1,0:T(8,128)(2,1)} %get-tuple-element.86.teacher_mix, f32[576,1024]{1,0:T(8,128)} %get-tuple-element.87.student_part, ...), custom_call_target="tpu_custom_call" | custom-call | flops 1509949440 | bytes 16777216 | tf_op jit(solution)/shard_map/pallas_call | solution.py:244
  104.6 7.7 %shard_map.130 = (bf16[3,128,1024]{2,1,0:T(8,128)(2,1)}, bf16[3,128,1024]{2,1,0:T(8,128)(2,1)}, bf16[2,128,1024]{2,1,0:T(8,128)(2,1)}, bf16[576,1024]{1,0:T(8,128)(2,1)}, bf16[576,1024]{1,0:T(8,128)(2,1)}) custom-call(s32[33]{0:T(128)} %stack.111.order, f32[576,1024]{1,0:T(8,128)} %get-tuple-element.93.student, f32[576,1024]{1,0:T(8,128)} %get-tuple-element.94.matched, ...), custom_call_target="tpu_custom_call" | custom-call | flops 1207959552 | bytes 12582912 | tf_op jit(solution)/shard_map/pallas_call | solution.py:323
  117.5 5.6 %shard_map.131.refs_0_.refs_2_.refs_4_.refs_6_.refs_3_ = f32[8,128,1024]{2,1,0:T(8,128)} custom-call(bf16[576,1024]{1,0:T(8,128)(2,1)} %get-tuple-element.97.held, bf16[16,128,576]{2,1,0:T(8,128)(2,1)} %get-tuple-element.96.mix), custom_call_target="tpu_custom_call" | custom-call | flops 1207959552 | bytes 7340032 | tf_op jit(solution)/shard_map/pallas_call | solution.py:361
  123.1 6.3 %collective-permute-done.24.refs_5_.refs_1_ = bf16[2,128,1024]{2,1,0:T(8,128)(2,1)S(1)} collective-permute-done((bf16[2,128,1024]{2,1,0:T(8,128)(2,1)}, bf16[2,128,1024]{2,1,0:T(8,128)(2,1)S(1)}, u32[]{:S(2)}, u32[]{:S(2)}) %collective-permute-start.24) | collective-permute-done | bytes 524320 | tf_op jit(solution)/shard_map/ppermute | solution.py:62
  129.4 3.8 %collective-permute-done.22.refs_1_.refs_3_.refs_5_ = bf16[3,128,1024]{2,1,0:T(8,128)(2,1)S(1)} collective-permute-done((bf16[3,128,1024]{2,1,0:T(8,128)(2,1)}, bf16[3,128,1024]{2,1,0:T(8,128)(2,1)S(1)}, u32[]{:S(2)}, u32[]{:S(2)}) %collective-permute-start.22) | collective-permute-done | bytes 786464 | tf_op jit(solution)/shard_map/ppermute | solution.py:58
  137.7 3.4 %collective-permute-start.26 = (bf16[64,1024]{1,0:T(8,128)(2,1)}, bf16[64,1024]{1,0:T(8,128)(2,1)S(1)}, u32[]{:S(2)}, u32[]{:S(2)}) collective-permute-start(bf16[64,1024]{1,0:T(8,128)(2,1)} %get-tuple-element.105), channel_id=1, source_target_pairs={{4,0},{8,4},{12,8},{0,12},{5,1},{9,5},{13,9},{1,13},{6,2},{10,6},{... | collective-permute-start | bytes 393224 | tf_op jit(solution)/shard_map/ppermute | solution.py:42
  141.2 3.7 %collective-permute-done.25.refs_2_ = bf16[64,1024]{1,0:T(8,128)(2,1)S(1)} collective-permute-done((bf16[64,1024]{1,0:T(8,128)(2,1)}, bf16[64,1024]{1,0:T(8,128)(2,1)S(1)}, u32[]{:S(2)}, u32[]{:S(2)}) %collective-permute-start.25) | collective-permute-done | bytes 131104 | tf_op jit(solution)/shard_map/ppermute | solution.py:46
  152.4 3.9 %collective-permute-done.27.refs_3_ = bf16[128,1024]{1,0:T(8,128)(2,1)S(1)} collective-permute-done((bf16[128,1024]{1,0:T(8,128)(2,1)}, bf16[128,1024]{1,0:T(8,128)(2,1)S(1)}, u32[]{:S(2)}, u32[]{:S(2)}) %collective-permute-start.27) | collective-permute-done | bytes 262176 | tf_op jit(solution)/shard_map/ppermute | solution.py:50
  165.0 5.6 %collective-permute-done.30.refs_2_ = bf16[128,1024]{1,0:T(8,128)(2,1)S(1)} collective-permute-done((bf16[128,1024]{1,0:T(8,128)(2,1)}, bf16[128,1024]{1,0:T(8,128)(2,1)S(1)}, u32[]{:S(2)}, u32[]{:S(2)}) %collective-permute-start.30) | collective-permute-done | bytes 262176 | tf_op jit(solution)/shard_map/ppermute | solution.py:46
  174.1 15.0 %all_to_all.10 = bf16[8,16,1024]{2,1,0:T(8,128)(2,1)S(1)} all-to-all(bf16[8,16,1024]{2,1,0:T(8,128)(2,1)} %bitcast.34), channel_id=1, replica_groups={{0,48,64,112,128,176,192,240},{16,32,80,96,144,160,208,224},{1,49,65,11..., dimensions={0} | all-to-all | bytes 524288 | tf_op jit(solution)/shard_map/all_to_all | solution.py:550
  190.0 3.6 %all-to-all-start.1 = ((bf16[16,16,1024]{2,1,0:T(8,128)(2,1)}), bf16[16,16,1024]{2,1,0:T(8,128)(2,1)S(1)}, u32[]{:S(2)}, u32[]{:S(2)}) async-start(bf16[16,16,1024]{2,1,0:T(8,128)(2,1)} %broadcast_in_dim.2), calls=%async_computation.1 | async-start | bytes 1048576 | tf_op jit(solution)/shard_map/all_to_all | solution.py:554
  193.6 13.3 %all-to-all-done.1 = bf16[16,16,1024]{2,1,0:T(8,128)(2,1)S(1)} async-done(((bf16[16,16,1024]{2,1,0:T(8,128)(2,1)}), bf16[16,16,1024]{2,1,0:T(8,128)(2,1)S(1)}, u32[]{:S(2)}, u32[]{:S(2)}) %all-to-all-start.1) | async-done | bytes 524320 | tf_op jit(solution)/shard_map/all_to_all | solution.py:554
  207.7 5.1 %shard_map.136 = (f32[128,2048]{1,0:T(8,128)}, f32[128,2048]{1,0:T(8,128)}, f32[128,2048]{1,0:T(8,128)}, f32[128,2048]{1,0:T(8,128)}) custom-call(s32[1]{0:T(128)} %bitcast.flip, bf16[8,2,16,1024]{3,2,1,0:T(8,128)(2,1)} %bitcast.33, f32[128,2048]{1,0:T(8,128)} %weight, f32[128,2048]{1,0:T(8,128)} %teacher, f32[128,2048]{1,0:T(8,128)} %first.1, ...), custom_call_target="tpu_custom_call" | custom-call | tf_op jit(solution)/shard_map/pallas_call | solution.py:467
  (131 shorter events, 57.3 us)
Async XLA Ops:
  2.2 28.2 %collective-permute-start.4 = (bf16[288,2048]{1,0:T(8,128)(2,1)S(1)}, bf16[288,2048]{1,0:T(8,128)(2,1)}, u32[]{:S(2)}, u32[]{:S(2)}) collective-permute-start(bf16[288,2048]{1,0:T(8,128)(2,1)S(1)} %copy-done.24), channel_id=1, source_target_pairs={{0,1},{1,0},{2,3},{3,2},{4,5},{5,4},{6,7},{7,6},{8,9},{9,8},{10,11... | collective-permute-start | bytes 3538952 | tf_op jit(solution)/shard_map/ppermute | solution.py:38
  2.3 28.1 %collective-permute-start.5 = (bf16[288,2048]{1,0:T(8,128)(2,1)}, bf16[288,2048]{1,0:T(8,128)(2,1)}, u32[]{:S(2)}, u32[]{:S(2)}) collective-permute-start(bf16[288,2048]{1,0:T(8,128)(2,1)} %teacher_own.1), channel_id=1, source_target_pairs={{0,1},{1,0},{2,3},{3,2},{4,5},{5,4},{6,7},{7,6},{8,9},{9,8},{10,11... | collective-permute-start | bytes 3538952 | tf_op jit(solution)/shard_map/ppermute | solution.py:38
  2.8 14.5 %collective-permute-start = (bf16[2,128,1024]{2,1,0:T(8,128)(2,1)S(1)}, bf16[2,128,1024]{2,1,0:T(8,128)(2,1)}, u32[]{:S(2)}, u32[]{:S(2)}) collective-permute-start(bf16[2,128,1024]{2,1,0:T(8,128)(2,1)S(1)} %pad_maximum_fusion.refs_0_), channel_id=1, source_target_pairs={{4,0},{8,4},{12,8},{0,12},{5,1},{9,5},{13,9},{1,13},{6,2},{10,6},{... | collective-permute-start | bytes 1572872 | tf_op jit(solution)/shard_map/ppermute | solution.py:42
  5.8 15.0 %collective-permute-start.1 = (bf16[2,128,1024]{2,1,0:T(8,128)(2,1)S(1)}, bf16[2,128,1024]{2,1,0:T(8,128)(2,1)}, u32[]{:S(2)}, u32[]{:S(2)}) collective-permute-start(bf16[2,128,1024]{2,1,0:T(8,128)(2,1)S(1)} %pad_maximum_fusion.refs_0_), channel_id=1, source_target_pairs={{0,4},{4,8},{8,12},{12,0},{1,5},{5,9},{9,13},{13,1},{2,6},{6,10},{... | collective-permute-start | bytes 1572872 | tf_op jit(solution)/shard_map/ppermute | solution.py:46
  8.1 22.3 %collective-permute-start.6 = (bf16[288,1024]{1,0:T(8,128)(2,1)S(1)}, bf16[288,1024]{1,0:T(8,128)(2,1)S(1)}, u32[]{:S(2)}, u32[]{:S(2)}) collective-permute-start(bf16[288,1024]{1,0:T(8,128)(2,1)S(1)} %constant_dynamic-slice_fusion), channel_id=1, source_target_pairs={{0,1},{1,0},{2,3},{3,2},{4,5},{5,4},{6,7},{7,6},{8,9},{9,8},{10,11... | collective-permute-start | bytes 1769480 | tf_op jit(solution)/shard_map/ppermute | solution.py:38
  17.3 13.1 %collective-permute-start.2 = (bf16[2,128,1024]{2,1,0:T(8,128)(2,1)S(1)}, bf16[2,128,1024]{2,1,0:T(8,128)(2,1)S(1)}, u32[]{:S(2)}, u32[]{:S(2)}) collective-permute-start(bf16[2,128,1024]{2,1,0:T(8,128)(2,1)S(1)} %pad_maximum_fusion.refs_0_), channel_id=1, source_target_pairs={{16,2},{2,16},{0,18},{18,0},{17,3},{3,17},{1,19},{19,1},{20,6},{6,... | collective-permute-start | bytes 1572872 | tf_op jit(solution)/shard_map/ppermute | solution.py:50
  30.4 13.9 %collective-permute-start.8 = (bf16[2,128,1024]{2,1,0:T(8,128)(2,1)}, bf16[2,128,1024]{2,1,0:T(8,128)(2,1)}, u32[]{:S(2)}, u32[]{:S(2)}) collective-permute-start(bf16[2,128,1024]{2,1,0:T(8,128)(2,1)} %collective-permute-done.refs_2_), channel_id=1, source_target_pairs={{4,0},{8,4},{12,8},{0,12},{5,1},{9,5},{13,9},{1,13},{6,2},{10,6},{... | collective-permute-start | bytes 1572872 | tf_op jit(solution)/shard_map/ppermute | solution.py:42
  34.3 12.2 %collective-permute-start.9 = (bf16[2,128,1024]{2,1,0:T(8,128)(2,1)}, bf16[2,128,1024]{2,1,0:T(8,128)(2,1)}, u32[]{:S(2)}, u32[]{:S(2)}) collective-permute-start(bf16[2,128,1024]{2,1,0:T(8,128)(2,1)} %collective-permute-done.refs_2_), channel_id=1, source_target_pairs={{16,2},{2,16},{0,18},{18,0},{17,3},{3,17},{1,19},{19,1},{20,6},{6,... | collective-permute-start | bytes 1572872 | tf_op jit(solution)/shard_map/ppermute | solution.py:50
  34.8 17.5 %collective-permute-start.11 = (bf16[2,128,1024]{2,1,0:T(8,128)(2,1)}, bf16[2,128,1024]{2,1,0:T(8,128)(2,1)S(1)}, u32[]{:S(2)}, u32[]{:S(2)}) collective-permute-start(bf16[2,128,1024]{2,1,0:T(8,128)(2,1)} %collective-permute-done.refs_2_), channel_id=1, source_target_pairs={{33,0},{32,1},{65,32},{64,33},{97,64},{96,65},{129,96},{128,97},{1... | collective-permute-start | bytes 1572872 | tf_op jit(solution)/shard_map/ppermute | solution.py:54
  38.0 14.3 %collective-permute-start.10 = (bf16[2,128,1024]{2,1,0:T(8,128)(2,1)S(1)}, bf16[2,128,1024]{2,1,0:T(8,128)(2,1)}, u32[]{:S(2)}, u32[]{:S(2)}) collective-permute-start(bf16[2,128,1024]{2,1,0:T(8,128)(2,1)S(1)} %collective-permute-done.2.refs_4_), channel_id=1, source_target_pairs={{0,4},{4,8},{8,12},{12,0},{1,5},{5,9},{9,13},{13,1},{2,6},{6,10},{... | collective-permute-start | bytes 1572872 | tf_op jit(solution)/shard_map/ppermute | solution.py:46
  38.1 14.3 %collective-permute-start.12 = (bf16[2,128,1024]{2,1,0:T(8,128)(2,1)}, bf16[2,128,1024]{2,1,0:T(8,128)(2,1)S(1)}, u32[]{:S(2)}, u32[]{:S(2)}) collective-permute-start(bf16[2,128,1024]{2,1,0:T(8,128)(2,1)} %collective-permute-done.1.refs_3_), channel_id=1, source_target_pairs={{1,32},{0,33},{33,64},{32,65},{65,96},{64,97},{97,128},{96,129},{1... | collective-permute-start | bytes 1572872 | tf_op jit(solution)/shard_map/ppermute | solution.py:58
  44.3 13.4 %collective-permute-start.13 = (bf16[2,128,1024]{2,1,0:T(8,128)(2,1)S(1)}, bf16[2,128,1024]{2,1,0:T(8,128)(2,1)}, u32[]{:S(2)}, u32[]{:S(2)}) collective-permute-start(bf16[2,128,1024]{2,1,0:T(8,128)(2,1)S(1)} %collective-permute-done.2.refs_4_), channel_id=1, source_target_pairs={{1,16},{0,17},{17,0},{16,1},{3,18},{2,19},{19,2},{18,3},{5,20},{4,... | collective-permute-start | bytes 1572872 | tf_op jit(solution)/shard_map/ppermute | solution.py:62
  58.6 14.5 %collective-permute-start.14 = (bf16[128,1024]{1,0:T(8,128)(2,1)S(1)}, bf16[128,1024]{1,0:T(8,128)(2,1)S(1)}, u32[]{:S(2)}, u32[]{:S(2)}) collective-permute-start(bf16[128,1024]{1,0:T(8,128)(2,1)S(1)} %slice_bitcast_fusion.1), channel_id=1, source_target_pairs={{4,0},{8,4},{12,8},{0,12},{5,1},{9,5},{13,9},{1,13},{6,2},{10,6},{... | collective-permute-start | bytes 786440 | tf_op jit(solution)/shard_map/ppermute | solution.py:42
  63.5 27.6 %collective-permute-start.16 = (bf16[2,128,1024]{2,1,0:T(8,128)(2,1)}, bf16[2,128,1024]{2,1,0:T(8,128)(2,1)S(1)}, u32[]{:S(2)}, u32[]{:S(2)}) collective-permute-start(bf16[2,128,1024]{2,1,0:T(8,128)(2,1)} %collective-permute-done.8.refs_5_), channel_id=1, source_target_pairs={{33,0},{32,1},{65,32},{64,33},{97,64},{96,65},{129,96},{128,97},{1... | collective-permute-start | bytes 1572872 | tf_op jit(solution)/shard_map/ppermute | solution.py:54
  69.5 21.6 %collective-permute-start.17 = (bf16[2,128,1024]{2,1,0:T(8,128)(2,1)}, bf16[2,128,1024]{2,1,0:T(8,128)(2,1)S(1)}, u32[]{:S(2)}, u32[]{:S(2)}) collective-permute-start(bf16[2,128,1024]{2,1,0:T(8,128)(2,1)} %collective-permute-done.10.refs_6_), channel_id=1, source_target_pairs={{1,16},{0,17},{17,0},{16,1},{3,18},{2,19},{19,2},{18,3},{5,20},{4,... | collective-permute-start | bytes 1572872 | tf_op jit(solution)/shard_map/ppermute | solution.py:62
  70.6 20.4 %collective-permute-start.18 = (bf16[2,128,1024]{2,1,0:T(8,128)(2,1)}, bf16[2,128,1024]{2,1,0:T(8,128)(2,1)S(1)}, u32[]{:S(2)}, u32[]{:S(2)}) collective-permute-start(bf16[2,128,1024]{2,1,0:T(8,128)(2,1)} %collective-permute-done.9.refs_7_), channel_id=1, source_target_pairs={{1,32},{0,33},{33,64},{32,65},{65,96},{64,97},{97,128},{96,129},{1... | collective-permute-start | bytes 1572872 | tf_op jit(solution)/shard_map/ppermute | solution.py:58
  73.4 17.3 %collective-permute-start.19 = (bf16[128,1024]{1,0:T(8,128)(2,1)S(1)}, bf16[128,1024]{1,0:T(8,128)(2,1)S(1)}, u32[]{:S(2)}, u32[]{:S(2)}) collective-permute-start(bf16[128,1024]{1,0:T(8,128)(2,1)S(1)} %collective-permute-done.14.refs_0_), channel_id=1, source_target_pairs={{33,0},{32,1},{65,32},{64,33},{97,64},{96,65},{129,96},{128,97},{1... | collective-permute-start | bytes 786440 | tf_op jit(solution)/shard_map/ppermute | solution.py:54
  78.5 12.5 %collective-permute-start.20 = (bf16[128,1024]{1,0:T(8,128)(2,1)S(1)}, bf16[128,1024]{1,0:T(8,128)(2,1)S(1)}, u32[]{:S(2)}, u32[]{:S(2)}) collective-permute-start(bf16[128,1024]{1,0:T(8,128)(2,1)S(1)} %collective-permute-done.15.refs_1_), channel_id=1, source_target_pairs={{1,32},{0,33},{33,64},{32,65},{65,96},{64,97},{97,128},{96,129},{1... | collective-permute-start | bytes 786440 | tf_op jit(solution)/shard_map/ppermute | solution.py:58
  112.3 20.9 %collective-permute-start.22 = (bf16[3,128,1024]{2,1,0:T(8,128)(2,1)}, bf16[3,128,1024]{2,1,0:T(8,128)(2,1)S(1)}, u32[]{:S(2)}, u32[]{:S(2)}) collective-permute-start(bf16[3,128,1024]{2,1,0:T(8,128)(2,1)} %get-tuple-element.98), channel_id=1, source_target_pairs={{1,32},{0,33},{33,64},{32,65},{65,96},{64,97},{97,128},{96,129},{1... | collective-permute-start | bytes 2359304 | tf_op jit(solution)/shard_map/ppermute | solution.py:58
  112.4 21.0 %collective-permute-start.23 = (bf16[3,128,1024]{2,1,0:T(8,128)(2,1)}, bf16[3,128,1024]{2,1,0:T(8,128)(2,1)S(1)}, u32[]{:S(2)}, u32[]{:S(2)}) collective-permute-start(bf16[3,128,1024]{2,1,0:T(8,128)(2,1)} %get-tuple-element.99), channel_id=1, source_target_pairs={{33,0},{32,1},{65,32},{64,33},{97,64},{96,65},{129,96},{128,97},{1... | collective-permute-start | bytes 2359304 | tf_op jit(solution)/shard_map/ppermute | solution.py:54
  115.4 14.0 %collective-permute-start.24 = (bf16[2,128,1024]{2,1,0:T(8,128)(2,1)}, bf16[2,128,1024]{2,1,0:T(8,128)(2,1)S(1)}, u32[]{:S(2)}, u32[]{:S(2)}) collective-permute-start(bf16[2,128,1024]{2,1,0:T(8,128)(2,1)} %get-tuple-element.100), channel_id=1, source_target_pairs={{1,16},{0,17},{17,0},{16,1},{3,18},{2,19},{19,2},{18,3},{5,20},{4,... | collective-permute-start | bytes 1572872 | tf_op jit(solution)/shard_map/ppermute | solution.py:62
  117.3 46.3 %collective-permute-start.33 = (bf16[288,1024]{1,0:T(8,128)(2,1)S(1)}, bf16[288,1024]{1,0:T(8,128)(2,1)S(1)}, u32[]{:S(2)}, u32[]{:S(2)}) collective-permute-start(bf16[288,1024]{1,0:T(8,128)(2,1)S(1)} %get-tuple-element.128), channel_id=1, source_target_pairs={{0,1},{1,0},{2,3},{3,2},{4,5},{5,4},{6,7},{7,6},{8,9},{9,8},{10,11... | collective-permute-start | bytes 1769480 | tf_op jit(solution)/shard_map/ppermute | solution.py:38
  152.2 12.8 %collective-permute-start.32 = (bf16[128,1024]{1,0:T(8,128)(2,1)S(1)}, bf16[128,1024]{1,0:T(8,128)(2,1)S(1)}, u32[]{:S(2)}, u32[]{:S(2)}) collective-permute-start(bf16[128,1024]{1,0:T(8,128)(2,1)S(1)} %copy-done.29), channel_id=1, source_target_pairs={{4,0},{8,4},{12,8},{0,12},{5,1},{9,5},{13,9},{1,13},{6,2},{10,6},{... | collective-permute-start | bytes 786440 | tf_op jit(solution)/shard_map/ppermute | solution.py:42
  190.0 16.9 %all-to-all-start.1 = ((bf16[16,16,1024]{2,1,0:T(8,128)(2,1)}), bf16[16,16,1024]{2,1,0:T(8,128)(2,1)S(1)}, u32[]{:S(2)}, u32[]{:S(2)}) async-start(bf16[16,16,1024]{2,1,0:T(8,128)(2,1)} %broadcast_in_dim.2), calls=%async_computation.1 | async-start | bytes 1048576 | tf_op jit(solution)/shard_map/all_to_all | solution.py:554
  (41 other events, 333.2 us)

commit v4 on v3

--- a/solution.py
+++ b/solution.py
@@ -70,144 +70,128 @@
     return from_y_next(value)
 
 
-EARLY = (
+ORDER = (
     (0, 0, 0), (1, 0, 0), (0, 1, 0), (0, 3, 0), (0, 0, 1), (0, 2, 0), (0, 3, 1), (0, 1, 1), (1, 1, 0), (1, 3, 0),
-    (1, 0, 1),
+    (1, 0, 1), (1, 2, 0), (1, 1, 1), (1, 3, 1), (0, 2, 1), (1, 2, 1),
 )
-LATE = ((0, 2, 1), (1, 2, 0), (1, 3, 1), (1, 1, 1), (1, 2, 1))
-SENT = ((1, 2, 1), (1, 2, 0), (1, 1, 1), (1, 3, 0), (1, 3, 1), (1, 1, 0), (1, 0, 1), (1, 0, 0))
-KEPT = tuple((0, dy, dx) for side, dy, dx in SENT)
-HALF_AT = len(EARLY) + len(LATE)
-TURNED_AT = HALF_AT + 1
-
-
-def gather_rows(own, other, swapped):
+SPLIT = 14
+SENT = ((2, 1), (2, 0), (1, 1), (3, 0), (3, 1), (1, 0), (0, 1), (0, 0))
+HALF_AT = len(ORDER)
+CORE_AT = HALF_AT + 1
+PLACE_AT = CORE_AT + 1
+
+
+def gather_rows(own, ready_other, swapped, prepare):
     up, down, across = from_y_next(own), from_y_previous(own), from_x_near(own)
-    up, down, across, other, *swapped = lax.optimization_barrier((up, down, across, other, *swapped))
+    up, down, across, swapped = lax.optimization_barrier((up, down, across, swapped))
     up_two = from_y_next(up)
+    across_down = from_y_previous(across)
     across_up = from_x_near(up)
-    across_down = from_y_previous(across)
-    passed_up, passed_down, passed_across = from_z_next(up), from_z_previous(down), from_x_twin(across)
-    up_two, across_up, across_down, passed_up, passed_down, passed_across = lax.optimization_barrier(
-        (up_two, across_up, across_down, passed_up, passed_down, passed_across)
+    passed_up, passed_down = from_z_next(up), from_z_previous(down)
+    up_two, across_up, across_down, passed_up, passed_down, prepared = lax.optimization_barrier(
+        (up_two, across_up, across_down, passed_up, passed_down, prepare(*swapped))
     )
     student = from_y_next(across_up[0])
     teacher = from_y_previous(across_down[1])
     passed_two = from_z_next(up_two)
     passed_across_up = from_z_previous(across_up)
-    passed_across_down = from_x_twin(across_down)
-    student, teacher = lax.optimization_barrier((student, teacher))
+    passed_across = from_x_twin(across)
+    (student, teacher), other = ready_other((student, teacher))
     passed_student = from_z_next(student)
     passed_teacher = from_z_previous(teacher)
-    early = (
+    passed_student, passed_teacher, other = lax.optimization_barrier((passed_student, passed_teacher, other))
+    other = swap_cores(other)
+    passed_across_down = from_x_twin(lax.optimization_barrier((across_down, passed_across))[0])
+    pieces = (
         own, other, up, down, across, up_two, across_down, across_up, passed_up, passed_down, passed_across,
-    )
-    late = (
-        student, teacher, passed_two, passed_across_down, passed_across_up, passed_student, passed_teacher,
-    )
-    return early, late, swapped
-
-
-def early_kernel(order, student_own, student_other, teacher_own, teacher_other, *refs):
-    count = len(EARLY)
-    weights = refs[:count]
-    student_out, teacher_out, student_late, teacher_late, turned, mix, held = refs[count:]
-    step, own = pl.program_id(0), student_own.shape[0]
-
-    @pl.when(step == 0)
-    def _():
-        for block in range(count + len(LATE)):
-            columns = pl.ds(pl.multiple_of(order[block] * 128, 128), 128)
-            at = block if block < count else block - count
-            spot = slice(at * 128, (at + 1) * 128)
-            to_student = mix.at[0] if block < count else student_late
-            to_teacher = mix.at[1] if block < count else teacher_late
-            to_student[:own, spot] = student_own[:, columns]
-            to_student[own:, spot] = student_other[:, columns]
-            to_teacher[:own, spot] = teacher_own[:, columns]
-            to_teacher[own:, spot] = teacher_other[:, columns]
-
-    for block in range(count):
-        rows = slice(block * 128, (block + 1) * 128)
-        held[0, rows, :] = weights[block][0]
-        held[1, rows, :] = weights[block][1]
-    student_out[...] = jnp.dot(mix[0], held[0], preferred_element_type=jnp.float32)
-    teacher_out[...] = jnp.dot(mix[1], held[1], preferred_element_type=jnp.float32)
-    for block in range(turned.shape[0]):
-        spot = order[TURNED_AT + step * turned.shape[0] + block]
-        columns = pl.ds(pl.multiple_of(spot * 128, 128), 128)
-        turned[block] = jnp.concatenate([student_own[:, columns], student_other[:, columns]], axis=0).T
-
-
-def early_forward(order, weights, student_own, student_other, teacher_own, teacher_other):
-    own, columns, width = student_own.shape[0], weights[0].shape[-1], 256
-    rows, steps, count = 2 * own, columns // width, len(EARLY)
-    whole = pl.BlockSpec((own, KIN), lambda j, order: (0, 0))
-    column = pl.BlockSpec((rows, width), lambda j, order: (0, j))
-    late = pl.BlockSpec((rows, len(LATE) * 128), lambda j, order: (0, 0))
+        passed_two, passed_across_up, passed_across_down, student, teacher, passed_student, passed_teacher,
+    )
+    return pieces, prepared
+
+
+def prepare_kernel(
+    order, student_own, student_other, teacher_own, teacher_other, residual_own, residual_other, places_own, places_other,
+    student_out, teacher_out, residual_out, picked_out, sent_out, kept_out
+):
+    own = student_own.shape[0]
+    lane = lax.broadcasted_iota(jnp.int32, (PATCHES, PATCHES), 1)
+    sides = ((teacher_own, residual_own, places_own), (teacher_other, residual_other, places_other))
+    for side, (teacher, residual, places) in enumerate(sides):
+        for crop in range(own // PATCHES):
+            rows = slice(crop * PATCHES, (crop + 1) * PATCHES)
+            out_rows = slice(side * own + crop * PATCHES, side * own + (crop + 1) * PATCHES)
+            pick = (places[rows, :] == lane).astype(jnp.float32).astype(jnp.bfloat16)
+            teacher_out[out_rows, :] = jnp.dot(
+                pick, teacher[rows, :], preferred_element_type=jnp.float32
+            ).astype(jnp.bfloat16)
+            picked_out[out_rows, :] = jnp.dot(
+                pick, residual[rows, :], preferred_element_type=jnp.float32
+            ).astype(jnp.bfloat16)
+        residual_out[side * own : (side + 1) * own, :] = residual[...]
+    student_out[:own, :] = student_own[...]
+    student_out[own:, :] = student_other[...]
+    turned = student_out[...].T
+    first = order[CORE_AT] == 0
+    kept_out[0] = jnp.where(first, turned[:128], turned[128:])
+    sent_out[0] = jnp.where(first, turned[128:], turned[:128])
+
+
+def prepare_rows(order, student_own, student_other, teacher_own, teacher_other, residual, residual_other, places, places_other):
+    own, steps = student_own.shape[0], 8
+    rows, columns = 2 * own, DOUT // 2
+    width, narrow = KIN // steps, columns // steps
+    mix = pl.BlockSpec((own, width), lambda i, order: (0, i))
+    place = pl.BlockSpec((own, 1), lambda i, order: (0, 0))
+    packed = pl.BlockSpec((rows, width), lambda i, order: (0, i))
+    slim = pl.BlockSpec((rows, narrow), lambda i, order: (0, i))
+    turned = pl.BlockSpec((1, 128, rows), lambda i, order: (order[PLACE_AT + i], 0, 0))
     return pl.pallas_call(
-        early_kernel,
+        prepare_kernel,
         grid_spec=pltpu.PrefetchScalarGridSpec(
             num_scalar_prefetch=1,
             grid=(steps,),
-            in_specs=[whole] * 4 + [pl.BlockSpec((2, 128, width), lambda j, order: (0, 0, j))] * count,
-            out_specs=[column, column, late, late, pl.BlockSpec((16 // steps, 128, rows), lambda j, order: (j, 0, 0))],
-            scratch_shapes=[
-                pltpu.VMEM((2, rows, count * 128), jnp.bfloat16),
-                pltpu.VMEM((2, count * 128, width), jnp.bfloat16),
+            in_specs=[mix] * 4
+            + [
+                pl.BlockSpec((own, narrow), lambda i, order: (0, order[HALF_AT] * steps + i)),
+                pl.BlockSpec((own, narrow), lambda i, order: (0, order[HALF_AT] * steps + i)),
+                place,
+                place,
             ],
+            out_specs=[packed, packed, slim, slim, turned, turned],
         ),
         out_shape=[
-            jax.ShapeDtypeStruct((rows, columns), jnp.float32),
-            jax.ShapeDtypeStruct((rows, columns), jnp.float32),
-            jax.ShapeDtypeStruct((rows, len(LATE) * 128), jnp.bfloat16),
-            jax.ShapeDtypeStruct((rows, len(LATE) * 128), jnp.bfloat16),
-            jax.ShapeDtypeStruct((16, 128, rows), jnp.bfloat16),
+            jax.ShapeDtypeStruct((rows, KIN), jnp.bfloat16),
+            jax.ShapeDtypeStruct((rows, KIN), jnp.bfloat16),
+            jax.ShapeDtypeStruct((rows, columns), jnp.bfloat16),
+            jax.ShapeDtypeStruct((rows, columns), jnp.bfloat16),
+            jax.ShapeDtypeStruct((8, 128, rows), jnp.bfloat16),
+            jax.ShapeDtypeStruct((8, 128, rows), jnp.bfloat16),
         ],
         compiler_params=pltpu.CompilerParams(vmem_limit_bytes=VMEM_LIMIT),
         cost_estimate=pl.CostEstimate(
-            flops=4 * rows * count * 128 * columns, bytes_accessed=18 * 1024 * 1024, transcendentals=0
-        ),
-    )(order, student_own, student_other, teacher_own, teacher_other, *weights)
-
-
-def late_kernel(
-    order, student_mix, teacher_mix, student_part, teacher_part, residual_own, residual_other, scale, places_own,
-    places_other, *refs
-):
-    weights = refs[:7]
-    student_out, matched_out, sums_out, held = refs[7:]
-    depth = held.shape[1]
-    held[0, :128, :] = weights[0][...]
-    held[1, :128, :] = weights[1][...]
-    for block in range(1, 4):
-        rows = slice(block * 128, (block + 1) * 128)
-        held[0, rows, :] = weights[block + 1][0]
-        held[1, rows, :] = weights[block + 1][1]
-    held[0, depth - 128 :, :] = weights[5][...]
-    held[1, depth - 128 :, :] = weights[6][...]
+            flops=4 * rows * PATCHES * KIN, bytes_accessed=16 * 1024 * 1024, transcendentals=0
+        ),
+    )(order, student_own, student_other, teacher_own, teacher_other, residual, residual_other, places, places_other)
+
+
+def forward_kernel(order, student_mix, teacher_mix, residual, picked, scale, *refs):
+    count = SPLIT + 2 * (len(ORDER) - SPLIT)
+    weights, (student_out, matched_out, sums_out, held) = refs[:count], refs[count:]
+    for block in range(len(ORDER)):
+        rows = pl.ds(pl.multiple_of(order[block] * 128, 128), 128)
+        if block < SPLIT:
+            held[0, rows, :] = weights[block][0]
+            held[1, rows, :] = weights[block][1]
+        else:
+            held[0, rows, :] = weights[2 * block - SPLIT][...]
+            held[1, rows, :] = weights[2 * block - SPLIT + 1][...]
     factor = scale[...] * (KIN ** (-0.5))
-    student_sum = student_part[...] + jnp.dot(student_mix[...], held[0], preferred_element_type=jnp.float32)
-    teacher_sum = teacher_part[...] + jnp.dot(teacher_mix[...], held[1], preferred_element_type=jnp.float32)
-    own = residual_own.shape[0]
-    lane = lax.broadcasted_iota(jnp.int32, (PATCHES, PATCHES), 1)
-    students, parts = [], []
-    for side, (residual, places) in enumerate(((residual_own, places_own), (residual_other, places_other))):
-        tokens = slice(side * own, (side + 1) * own)
-        base = residual[...].astype(jnp.float32)
-        students.append(base + factor * student_sum[tokens])
-        teacher = base + factor * teacher_sum[tokens]
-        high = teacher.astype(jnp.bfloat16)
-        low = (teacher - high.astype(jnp.float32)).astype(jnp.bfloat16)
-        for crop in range(own // PATCHES):
-            rows = slice(crop * PATCHES, (crop + 1) * PATCHES)
-            pick = (places[rows, :] == lane).astype(jnp.float32).astype(jnp.bfloat16)
-            parts.append(
-                jnp.dot(pick, high[rows], preferred_element_type=jnp.float32)
-                + jnp.dot(pick, low[rows], preferred_element_type=jnp.float32)
-            )
-    student = jnp.concatenate(students, axis=0)
-    matched = jnp.concatenate(parts, axis=0)
+    student = residual[...].astype(jnp.float32) + factor * jnp.dot(
+        student_mix[...], held[0], preferred_element_type=jnp.float32
+    )
+    matched = picked[...].astype(jnp.float32) + factor * jnp.dot(
+        teacher_mix[...], held[1], preferred_element_type=jnp.float32
+    )
     student_out[...] = student
     matched_out[...] = matched
     spot = lax.broadcasted_iota(jnp.int32, sums_out.shape, 1)
@@ -230,42 +214,29 @@
         sums_out[...] += sums
 
 
-def late_forward(
-    order, weights, student_mix, teacher_mix, student_part, teacher_part, residual_own, residual_other, scale,
-    places_own, places_other
-):
-    (rows, columns), own, width, depth = student_part.shape, residual_own.shape[0], 256, student_mix.shape[1]
+def forward(order, pieces, student_mix, teacher_mix, residual, picked, scale):
+    rows, columns, width = student_mix.shape[0], residual.shape[1], 256
     steps = columns // width
-    mix = pl.BlockSpec((rows, depth), lambda j, order: (0, 0))
+    whole = pl.BlockSpec((rows, KIN), lambda j, order: (0, 0))
     column = pl.BlockSpec((rows, width), lambda j, order: (0, j))
-    places = pl.BlockSpec((own, 1), lambda j, order: (0, 0))
     pair = pl.BlockSpec((2, 128, width), lambda j, order: (0, 0, j))
     single = pl.BlockSpec((128, width), lambda j, order: (0, j))
     return pl.pallas_call(
-        late_kernel,
+        forward_kernel,
         grid_spec=pltpu.PrefetchScalarGridSpec(
             num_scalar_prefetch=1,
             grid=(steps,),
             in_specs=[
-                mix,
-                mix,
+                whole,
+                whole,
                 column,
                 column,
-                pl.BlockSpec((own, width), lambda j, order: (0, order[HALF_AT] * steps + j)),
-                pl.BlockSpec((own, width), lambda j, order: (0, j)),
                 pl.BlockSpec((1, width), lambda j, order: (0, order[HALF_AT] * steps + j)),
-                places,
-                places,
-                single,
-                single,
-                pair,
-                pair,
-                pair,
-                single,
-                single,
-            ],
+            ]
+            + [pair] * SPLIT
+            + [single] * (2 * (len(ORDER) - SPLIT)),
             out_specs=[column, column, pl.BlockSpec((rows, 128), lambda j, order: (0, 0))],
-            scratch_shapes=[pltpu.VMEM((2, depth, width), jnp.bfloat16)],
+            scratch_shapes=[pltpu.VMEM((2, KIN, width), jnp.bfloat16)],
         ),
         out_shape=[
             jax.ShapeDtypeStruct((rows, columns), jnp.float32),
@@ -274,12 +245,9 @@
         ],
         compiler_params=pltpu.CompilerParams(vmem_limit_bytes=VMEM_LIMIT),
         cost_estimate=pl.CostEstimate(
-            flops=4 * rows * depth * columns, bytes_accessed=16 * 1024 * 1024, transcendentals=0
-        ),
-    )(
-        order, student_mix, teacher_mix, student_part, teacher_part, residual_own, residual_other, scale, places_own,
-        places_other, *weights
-    )
+            flops=4 * rows * KIN * columns, bytes_accessed=20 * 1024 * 1024, transcendentals=0
+        ),
+    )(order, student_mix, teacher_mix, residual, picked, scale, *pieces)
 
 
 def send_kernel(
@@ -356,14 +324,14 @@
     out[...] = grad.reshape(out.shape)
 
 
-def keep_grads(held, turned):
+def keep_grads(held, kept):
     (rows, columns), width = held.shape, 256
     return pl.pallas_call(
         keep_kernel,
         grid=(columns // width,),
         in_specs=[
             pl.BlockSpec((rows, width), lambda j: (0, j)),
-            pl.BlockSpec((8, 128, rows), lambda j: (1, 0, 0)),
+            pl.BlockSpec((8, 128, rows), lambda j: (0, 0, 0)),
         ],
         out_specs=pl.BlockSpec((8, 128, width), lambda j: (0, 0, j)),
         out_shape=jax.ShapeDtypeStruct((8, 128, columns), jnp.float32),
@@ -371,7 +339,7 @@
         cost_estimate=pl.CostEstimate(
             flops=rows * KIN * columns, bytes_accessed=7 * 1024 * 1024, transcendentals=0
         ),
-    )(held, turned)
+    )(held, kept)
 
 
 def add_kernel(plan, count, *refs):
@@ -420,7 +388,7 @@
     passed = (from_z_previous(next_sent), from_z_next(previous_sent), from_x_twin(twin_sent))
     passed = lax.optimization_barrier(passed)
     places = {}
-    for number, (_, dy, dx) in enumerate(SENT):
+    for number, (dy, dx) in enumerate(SENT):
         group = 0 if number < 3 else 1 if number < 6 else 2
         places[dy, dx] = ((kept, number), (passed[group], number - 3 * group))
     whole = slice(0, 128)
@@ -440,8 +408,10 @@
         (whole, places[1, 0] + ((up_two, None), (across_up, None))), (whole, places[0, 1] + ((across_down, None),))
     )
     up, across, down = lax.optimization_barrier((to_y_next(up), from_x_near(across), down))
-    (total,) = add_blocks((whole, places[0, 0] + ((up, None), (down, None), (across, None))))
-    return total
+    total = up.astype(jnp.float32) + down.astype(jnp.float32) + across.astype(jnp.float32)
+    for array, index in places[0, 0]:
+        total = total + array[index].astype(jnp.float32)
+    return total.astype(jnp.bfloat16)
 
 
 def update_kernel(flip, grads, weight, teacher, first, squares, weight_out, teacher_out, first_out, squares_out):
@@ -507,43 +477,52 @@
         return jnp.stack([columns_of(student_weight, index), columns_of(teacher_weight, index)]).astype(jnp.bfloat16)
 
     own = both_weights(which)
-    order = jnp.stack(
+    chips = jnp.stack([((y + dy) & 3) * 2 + (xhi ^ dx) for dy, dx in SENT])
+    number = jnp.arange(8, dtype=jnp.int32)
+    place = jnp.sum(jnp.where(chips[:, None] == number[None, :], number[:, None], 0), axis=0)
+    order = jnp.concatenate(
         [
-            (((y + dy) & 3) * 2 + (xhi ^ dx)) * 2 + (core ^ side)
-            for side, dy, dx in EARLY + LATE
+            jnp.stack(
+                [(((y + dy) & 3) * 2 + (xhi ^ dx)) * 2 + (core ^ side) for side, dy, dx in ORDER] + [which, core]
+            ).astype(jnp.int32),
+            place.astype(jnp.int32),
         ]
-        + [which]
-        + [(((y + dy) & 3) * 2 + (xhi ^ dx)) * 2 + (core ^ side) for side, dy, dx in SENT + KEPT]
-    ).astype(jnp.int32)
+    )
     own, student_sent, teacher_sent, residual_sent, positions_sent, student_held, teacher_held = (
         lax.optimization_barrier(
             (own, student_mix, teacher_mix, residual, positions, student_weight, teacher_weight)
         )
     )
     student_weight, teacher_weight = student_held, teacher_held
-    other = swap_cores(both_weights(1 - which))
-    student_other = swap_cores(student_sent)
-    teacher_other = swap_cores(teacher_sent)
-    residual_other = swap_cores(columns_of(residual_sent, 1 - which))
+    student_other, residual_sent = lax.optimization_barrier((swap_cores(student_sent), residual_sent))
+    residual_other = swap_cores(residual_sent)
+    teacher_other, positions_sent = lax.optimization_barrier((swap_cores(teacher_sent), positions_sent))
     places_other = swap_cores(positions_sent)
-    places = positions.reshape(token_count, 1)
+
+    def ready_other(ready):
+        ready, student_late, teacher_late = lax.optimization_barrier((ready, student_held, teacher_held))
+        return ready, jnp.stack(
+            [columns_of(student_late, 1 - which), columns_of(teacher_late, 1 - which)]
+        ).astype(jnp.bfloat16)
+
     scale = layer_scale.reshape(1, DOUT)
 
-    early, late, (student_other, teacher_other, residual_other, places_other) = gather_rows(
-        own, other, (student_other, teacher_other, residual_other, places_other)
-    )
-    places_other = places_other.reshape(token_count, 1)
-    student_part, teacher_part, student_late, teacher_late, turned = early_forward(
-        order, early, student_mix, student_other, teacher_mix, teacher_other
-    )
-    student_out, matched, sums = late_forward(
-        order, late, student_late, teacher_late, student_part, teacher_part, residual, residual_other, scale, places,
-        places_other
+    def prepare(student_other, teacher_other, residual_other, places_other):
+        return prepare_rows(
+            order, student_mix, student_other, teacher_mix, teacher_other, residual, residual_other,
+            positions.reshape(token_count, 1), places_other.reshape(token_count, 1)
+        )
+
+    pieces, (student_rows, teacher_rows, residual_rows, picked_rows, sent_mix, kept_mix) = gather_rows(
+        own, ready_other, (student_other, teacher_other, residual_other, places_other), prepare
+    )
+    student_out, matched, sums = forward(
+        order, pieces, student_rows, teacher_rows, residual_rows, picked_rows, scale
     )
     next_sent, previous_sent, twin_sent, held, tokens = send_grads(
-        total_tokens, order, student_out, matched, sums, swap_cores(sums), scale, turned
-    )
-    kept = keep_grads(held, turned)
+        total_tokens, order, student_out, matched, sums, swap_cores(sums), scale, sent_mix
+    )
+    kept = keep_grads(held, kept_mix)
     student_tokens = join_columns(which, tokens[:token_count], swap_cores(tokens[token_count:]))
     total = reduce_rows(kept, next_sent, previous_sent, twin_sent)
     total, student_tokens = lax.optimization_barrier((total, student_tokens))

time: 215 us -> 209 us (0.972)
  starting transfers between devices: 45.3 us -> 40.9 us
  local copies, waits for them, and re-layouts: 19.6 us -> 16.3 us
  waiting for transfers between devices: 80.8 us -> 78.2 us
    ppermute x6, waiting for transfers between devices: 17.7 us -> 2.02 us  [from_y_next(): return lax.ppermute(value, 'y', from_next(4))]
    ppermute x4, waiting for transfers between devices: 0.18 us -> 13.3 us  [from_z_next(): return lax.ppermute(value, ('z', 'core'), with_core_flip(from_next(8)))]
    ppermute x4, starting transfers between devices: 17.5 us -> 9.04 us  [from_z_next(): return lax.ppermute(value, ('z', 'core'), with_core_flip(from_next(8)))]
    ppermute x6, waiting for transfers between devices: 18.3 us -> 9.93 us  [from_y_previous(): return lax.ppermute(value, 'y', from_previous(4))]
    ppermute x7, waiting for transfers between devices: 1.44 us -> 6.8 us  [swap_cores(): return lax.ppermute(value, 'core', CORE_SWAP)]
    ppermute x6, starting transfers between devices: 16.9 us -> 11.9 us  [from_y_next(): return lax.ppermute(value, 'y', from_next(4))]
    ppermute x3, waiting for transfers between devices: 9.97 us -> 13.5 us  [from_x_twin(): return lax.ppermute(value, ('xlo', 'core'), with_core_flip(CORE_SWAP))]
    unnamed x60 -> x54, local copies, waits for them, and re-layouts: 9.4 us -> 6.25 us
  transfers between devices with their start and end apart: 35 -> 35, of which waited for: 18 -> 14; matrix products, arithmetic and copies ran while one was open for 4% -> 5% of each run, Pallas kernels for 12% -> 12%
where the time goes in v4:
time: 209 us; the launch traced here: 205 us
  waiting for transfers between devices  78.2 us (37%)
  Pallas kernels  49.4 us (24%)
  starting transfers between devices  40.9 us (20%)
  blocking collectives  16.6 us (8%)
  local copies, waits for them, and re-layouts  16.3 us (8%)
  other arithmetic  2.93 us (1%)
    all_to_all x1, blocking collectives, shards(): lax.all_to_all(total.reshape(8, 16, half), ('z', 'xlo'), 0, 0, axis_index...  16.6 us
    ppermute x4, waiting for transfers between devices, from_x_near(): return lax.ppermute(value, ('xlo', 'xhi'), X_NEAR)  15.6 us
    ppermute x3, waiting for transfers between devices, from_x_twin(): return lax.ppermute(value, ('xlo', 'core'), with_core_flip(CORE_SWAP))  13.5 us
    ppermute x4, waiting for transfers between devices, from_z_next(): return lax.ppermute(value, ('z', 'core'), with_core_flip(from_next(8)))  13.3 us
    all_to_all x1, waiting for transfers between devices, shards(): lax.all_to_all(jnp.broadcast_to(copy_rows[None], (16, 16, half)), ('z', '...  13.1 us
    pallas_call x1, Pallas kernels, forward(): pl.pallas_call(forward_kernel, grid_spec=pltpu.PrefetchScalarGridSpec(num...  12.7 us
    ppermute x6, starting transfers between devices, from_y_next(): return lax.ppermute(value, 'y', from_next(4))  11.9 us
    pallas_call x1, Pallas kernels, prepare_rows(): pl.pallas_call(prepare_kernel, grid_spec=pltpu.PrefetchScalarGridSpec(num...  10.8 us
  transfers between devices with their start and end apart: 35, of which 14 were waited for; matrix products, arithmetic and copies ran while one was open for 5% of the time, Pallas kernels for 12%

profile of v4, /device:TPU:4, one launch (start us, length us, event | category | flops | bytes accessed | tf_op | source)
XLA Modules:
  0.0 205.3 jit_solution(9783812504970171572)
XLA Ops:
  2.7 3.3 %collective-permute-done.3.student_other = bf16[288,2048]{1,0:T(8,128)(2,1)S(1)} collective-permute-done((bf16[288,2048]{1,0:T(8,128)(2,1)S(1)}, bf16[288,2048]{1,0:T(8,128)(2,1)S(1)}, u32[]{:S(2)}, u32[]{:S(2)}) %collective-permute-start.3) | collective-permute-done | bytes 1179680 | tf_op jit(solution)/shard_map/ppermute | solution.py:38
  10.1 10.4 %collective-permute-done.2.refs_4_ = bf16[2,128,1024]{2,1,0:T(8,128)(2,1)} collective-permute-done((bf16[2,128,1024]{2,1,0:T(8,128)(2,1)S(1)}, bf16[2,128,1024]{2,1,0:T(8,128)(2,1)}, u32[]{:S(2)}, u32[]{:S(2)}) %collective-permute-start.2) | collective-permute-done | bytes 524320 | tf_op jit(solution)/shard_map/ppermute | solution.py:50
  24.2 3.8 %collective-permute-start.10 = (bf16[2,128,1024]{2,1,0:T(8,128)(2,1)}, bf16[2,128,1024]{2,1,0:T(8,128)(2,1)}, u32[]{:S(2)}, u32[]{:S(2)}) collective-permute-start(bf16[2,128,1024]{2,1,0:T(8,128)(2,1)} %collective-permute-done.refs_2_), channel_id=1, source_target_pairs={{33,0},{32,1},{65,32},{64,33},{97,64},{96,65},{129,96},{128,97},{1... | collective-permute-start | bytes 1572872 | tf_op jit(solution)/shard_map/ppermute | solution.py:54
  34.0 10.8 %shard_map.128 = (bf16[576,2048]{1,0:T(8,128)(2,1)}, bf16[576,2048]{1,0:T(8,128)(2,1)}, bf16[576,1024]{1,0:T(8,128)(2,1)}, bf16[576,1024]{1,0:T(8,128)(2,1)}, bf...) custom-call(s32[26]{0:T(128)} %concatenate.9.order, bf16[288,2048]{1,0:T(8,128)(2,1)} %student_own.1, ...), custom_call_target="tpu_custom_call" | custom-call | flops 679477248 | bytes 16777216 | tf_op jit(solution)/shard_map/pallas_call | solution.py:148
  44.8 3.0 %collective-permute-start.17 = (bf16[2,128,1024]{2,1,0:T(8,128)(2,1)}, bf16[2,128,1024]{2,1,0:T(8,128)(2,1)S(1)}, u32[]{:S(2)}, u32[]{:S(2)}) collective-permute-start(bf16[2,128,1024]{2,1,0:T(8,128)(2,1)} %collective-permute-done.2.refs_4_), channel_id=1, source_target_pairs={{1,16},{0,17},{17,0},{16,1},{3,18},{2,19},{19,2},{18,3},{5,20},{4,... | collective-permute-start | bytes 1572872 | tf_op jit(solution)/shard_map/ppermute | solution.py:62
  50.3 2.8 %collective-permute-start.12 = (bf16[128,1024]{1,0:T(8,128)(2,1)S(1)}, bf16[128,1024]{1,0:T(8,128)(2,1)S(1)}, u32[]{:S(2)}, u32[]{:S(2)}) collective-permute-start(bf16[128,1024]{1,0:T(8,128)(2,1)S(1)} %slice_bitcast_fusion.2), channel_id=1, source_target_pairs={{4,0},{8,4},{12,8},{0,12},{5,1},{9,5},{13,9},{1,13},{6,2},{10,6},{... | collective-permute-start | bytes 786440 | tf_op jit(solution)/shard_map/ppermute | solution.py:42
  53.2 7.3 %collective-permute-done.17.refs_10_ = bf16[2,128,1024]{2,1,0:T(8,128)(2,1)S(1)} collective-permute-done((bf16[2,128,1024]{2,1,0:T(8,128)(2,1)}, bf16[2,128,1024]{2,1,0:T(8,128)(2,1)S(1)}, u32[]{:S(2)}, u32[]{:S(2)}) %collective-permute-start.17) | collective-permute-done | bytes 524320 | tf_op jit(solution)/shard_map/ppermute | solution.py:62
  67.7 13.3 %collective-permute-done.14.refs_16_ = bf16[128,1024]{1,0:T(8,128)(2,1)S(1)} collective-permute-done((bf16[128,1024]{1,0:T(8,128)(2,1)S(1)}, bf16[128,1024]{1,0:T(8,128)(2,1)S(1)}, u32[]{:S(2)}, u32[]{:S(2)}) %collective-permute-start.14) | collective-permute-done | bytes 262176 | tf_op jit(solution)/shard_map/ppermute | solution.py:54
  83.8 12.7 %shard_map.129 = (f32[576,1024]{1,0:T(8,128)}, f32[576,1024]{1,0:T(8,128)}, f32[576,128]{1,0:T(8,128)}) custom-call(s32[26]{0:T(128)} %concatenate.9.order, bf16[576,2048]{1,0:T(8,128)(2,1)} %get-tuple-element.103.student_mix, bf16[576,2048]{1,0:T(8,128)(2,1)} %get-tuple-element.104.teacher_mix, bf16[576,1024]{1,0:T(8,128)(2,1)} %get-tuple-element.105.residual, ...), custom_call_target="tpu_custom_call" | custom-call | flops 4831838208 | bytes 20971520 | tf_op jit(solution)/shard_map/pallas_call | solution.py:224
  99.1 7.7 %shard_map.130 = (bf16[3,128,1024]{2,1,0:T(8,128)(2,1)}, bf16[3,128,1024]{2,1,0:T(8,128)(2,1)}, bf16[2,128,1024]{2,1,0:T(8,128)(2,1)}, bf16[576,1024]{1,0:T(8,128)(2,1)}, bf16[576,1024]{1,0:T(8,128)(2,1)}) custom-call(s32[26]{0:T(128)} %concatenate.9.order, f32[576,1024]{1,0:T(8,128)} %get-tuple-element.122.student, f32[576,1024]{1,0:T(8,128)} %get-tuple-element.123.matched, ...), custom_call_target="tpu_custom_call" | custom-call | flops 1207959552 | bytes 12582912 | tf_op jit(solution)/shard_map/pallas_call | solution.py:291
  106.9 2.9 %collective-permute-start.23 = (bf16[3,128,1024]{2,1,0:T(8,128)(2,1)}, bf16[3,128,1024]{2,1,0:T(8,128)(2,1)S(1)}, u32[]{:S(2)}, u32[]{:S(2)}) collective-permute-start(bf16[3,128,1024]{2,1,0:T(8,128)(2,1)} %get-tuple-element.129), channel_id=1, source_target_pairs={{33,0},{32,1},{65,32},{64,33},{97,64},{96,65},{129,96},{128,97},{1... | collective-permute-start | bytes 2359304 | tf_op jit(solution)/shard_map/ppermute | solution.py:54
  112.1 5.7 %shard_map.131.refs_0_.refs_2_.refs_4_.refs_6_.refs_3_ = f32[8,128,1024]{2,1,0:T(8,128)} custom-call(bf16[576,1024]{1,0:T(8,128)(2,1)} %get-tuple-element.126.held, bf16[8,128,576]{2,1,0:T(8,128)(2,1)} %get-tuple-element.127.mix), custom_call_target="tpu_custom_call" | custom-call | flops 1207959552 | bytes 7340032 | tf_op jit(solution)/shard_map/pallas_call | solution.py:329
  117.8 6.2 %collective-permute-done.24.refs_5_ = bf16[2,128,1024]{2,1,0:T(8,128)(2,1)S(1)} collective-permute-done((bf16[2,128,1024]{2,1,0:T(8,128)(2,1)}, bf16[2,128,1024]{2,1,0:T(8,128)(2,1)S(1)}, u32[]{:S(2)}, u32[]{:S(2)}) %collective-permute-start.24) | collective-permute-done | bytes 524320 | tf_op jit(solution)/shard_map/ppermute | solution.py:62
  123.9 3.9 %collective-permute-done.22.refs_1_.refs_3_.refs_5_ = bf16[3,128,1024]{2,1,0:T(8,128)(2,1)S(1)} collective-permute-done((bf16[3,128,1024]{2,1,0:T(8,128)(2,1)}, bf16[3,128,1024]{2,1,0:T(8,128)(2,1)S(1)}, u32[]{:S(2)}, u32[]{:S(2)}) %collective-permute-start.22) | collective-permute-done | bytes 786464 | tf_op jit(solution)/shard_map/ppermute | solution.py:58
  129.6 2.7 %shard_map.132 = (bf16[64,1024]{1,0:T(8,128)(2,1)}, bf16[64,1024]{1,0:T(8,128)(2,1)}, bf16[128,1024]{1,0:T(8,128)(2,1)}, bf16[128,1024]{1,0:T(8,128)(2,1)}) custom-call(f32[8,128,1024]{2,1,0:T(8,128)} %shard_map.131.refs_0_.refs_2_.refs_4_.refs_6_.refs_3_, bf16[3,128,1024]{2,1,0:T(8,128)(2,1)} %copy-done, ...), custom_call_target="tpu_custom_call" | custom-call | tf_op jit(solution)/shard_map/pallas_call | solution.py:377
  132.5 3.1 %collective-permute-start.26 = (bf16[64,1024]{1,0:T(8,128)(2,1)}, bf16[64,1024]{1,0:T(8,128)(2,1)S(1)}, u32[]{:S(2)}, u32[]{:S(2)}) collective-permute-start(bf16[64,1024]{1,0:T(8,128)(2,1)} %get-tuple-element.134), channel_id=1, source_target_pairs={{4,0},{8,4},{12,8},{0,12},{5,1},{9,5},{13,9},{1,13},{6,2},{10,6},{... | collective-permute-start | bytes 393224 | tf_op jit(solution)/shard_map/ppermute | solution.py:42
  135.6 3.8 %collective-permute-done.25.refs_2_ = bf16[64,1024]{1,0:T(8,128)(2,1)S(1)} collective-permute-done((bf16[64,1024]{1,0:T(8,128)(2,1)}, bf16[64,1024]{1,0:T(8,128)(2,1)S(1)}, u32[]{:S(2)}, u32[]{:S(2)}) %collective-permute-start.25) | collective-permute-done | bytes 131104 | tf_op jit(solution)/shard_map/ppermute | solution.py:46
  145.6 5.2 %collective-permute-done.27.refs_3_ = bf16[128,1024]{1,0:T(8,128)(2,1)S(1)} collective-permute-done((bf16[128,1024]{1,0:T(8,128)(2,1)}, bf16[128,1024]{1,0:T(8,128)(2,1)S(1)}, u32[]{:S(2)}, u32[]{:S(2)}) %collective-permute-start.27) | collective-permute-done | bytes 262176 | tf_op jit(solution)/shard_map/ppermute | solution.py:50
  153.5 2.5 %shard_map.134 = (bf16[128,1024]{1,0:T(8,128)(2,1)}, bf16[128,1024]{1,0:T(8,128)(2,1)}) custom-call(f32[8,128,1024]{2,1,0:T(8,128)} %shard_map.131.refs_0_.refs_2_.refs_4_.refs_6_.refs_3_, bf16[3,128,1024]{2,1,0:T(8,128)(2,1)} %copy-done.1, bf16[128,1024]{1,0:T(8,128)(2,1)} %copy-done.11, bf16[128,1024]{1,0:T(8,128)(2,1)} %copy-done.12, ...), custom_call_target="tpu_custom_call" | custom-call | tf_op jit(solution)/shard_map/pallas_call | solution.py:377
  159.3 4.6 %collective-permute-done.30 = bf16[128,1024]{1,0:T(8,128)(2,1)S(1)} collective-permute-done((bf16[128,1024]{1,0:T(8,128)(2,1)}, bf16[128,1024]{1,0:T(8,128)(2,1)S(1)}, u32[]{:S(2)}, u32[]{:S(2)}) %collective-permute-start.30) | collective-permute-done | bytes 262176 | tf_op jit(solution)/shard_map/ppermute | solution.py:46
  165.2 16.6 %all_to_all.10 = bf16[8,16,1024]{2,1,0:T(8,128)(2,1)S(1)} all-to-all(bf16[8,16,1024]{2,1,0:T(8,128)(2,1)S(1)} %bitcast.54), channel_id=1, replica_groups={{0,48,64,112,128,176,192,240},{16,32,80,96,144,160,208,224},{1,49,65,11..., dimensions={0} | all-to-all | bytes 524288 | tf_op jit(solution)/shard_map/all_to_all | solution.py:529
  182.7 3.6 %all-to-all-start.1 = ((bf16[16,16,1024]{2,1,0:T(8,128)(2,1)}), bf16[16,16,1024]{2,1,0:T(8,128)(2,1)S(1)}, u32[]{:S(2)}, u32[]{:S(2)}) async-start(bf16[16,16,1024]{2,1,0:T(8,128)(2,1)} %broadcast_in_dim.23), calls=%async_computation.1 | async-start | bytes 1048576 | tf_op jit(solution)/shard_map/all_to_all | solution.py:533
  186.2 13.1 %all-to-all-done.1 = bf16[16,16,1024]{2,1,0:T(8,128)(2,1)S(1)} async-done(((bf16[16,16,1024]{2,1,0:T(8,128)(2,1)}), bf16[16,16,1024]{2,1,0:T(8,128)(2,1)S(1)}, u32[]{:S(2)}, u32[]{:S(2)}) %all-to-all-start.1) | async-done | bytes 524320 | tf_op jit(solution)/shard_map/all_to_all | solution.py:533
  200.2 5.1 %shard_map.135 = (f32[128,2048]{1,0:T(8,128)}, f32[128,2048]{1,0:T(8,128)}, f32[128,2048]{1,0:T(8,128)}, f32[128,2048]{1,0:T(8,128)}) custom-call(s32[1]{0:T(128)} %bitcast.flip, bf16[8,2,16,1024]{3,2,1,0:T(8,128)(2,1)} %bitcast.53, f32[128,2048]{1,0:T(8,128)} %weight, f32[128,2048]{1,0:T(8,128)} %teacher, f32[128,2048]{1,0:T(8,128)} %first.1, ...), custom_call_target="tpu_custom_call" | custom-call | tf_op jit(solution)/shard_map/pallas_call | solution.py:437
  (126 shorter events, 50.2 us)
Async XLA Ops:
  6.0 16.0 %collective-permute-start.5 = (bf16[288,2048]{1,0:T(8,128)(2,1)}, bf16[288,2048]{1,0:T(8,128)(2,1)S(1)}, u32[]{:S(2)}, u32[]{:S(2)}) collective-permute-start(bf16[288,2048]{1,0:T(8,128)(2,1)} %residual_own.1), channel_id=1, source_target_pairs={{0,1},{1,0},{2,3},{3,2},{4,5},{5,4},{6,7},{7,6},{8,9},{9,8},{10,11... | collective-permute-start | bytes 3538952 | tf_op jit(solution)/shard_map/ppermute | solution.py:38
  6.2 14.3 %collective-permute-start.2 = (bf16[2,128,1024]{2,1,0:T(8,128)(2,1)S(1)}, bf16[2,128,1024]{2,1,0:T(8,128)(2,1)}, u32[]{:S(2)}, u32[]{:S(2)}) collective-permute-start(bf16[2,128,1024]{2,1,0:T(8,128)(2,1)S(1)} %pad_maximum_fusion.refs_0_), channel_id=1, source_target_pairs={{16,2},{2,16},{0,18},{18,0},{17,3},{3,17},{1,19},{19,1},{20,6},{6,... | collective-permute-start | bytes 1572872 | tf_op jit(solution)/shard_map/ppermute | solution.py:50
  6.7 15.3 %collective-permute-start.1 = (bf16[2,128,1024]{2,1,0:T(8,128)(2,1)S(1)}, bf16[2,128,1024]{2,1,0:T(8,128)(2,1)}, u32[]{:S(2)}, u32[]{:S(2)}) collective-permute-start(bf16[2,128,1024]{2,1,0:T(8,128)(2,1)S(1)} %pad_maximum_fusion.refs_0_), channel_id=1, source_target_pairs={{0,4},{4,8},{8,12},{12,0},{1,5},{5,9},{9,13},{13,1},{2,6},{6,10},{... | collective-permute-start | bytes 1572872 | tf_op jit(solution)/shard_map/ppermute | solution.py:46
  8.3 13.7 %collective-permute-start = (bf16[2,128,1024]{2,1,0:T(8,128)(2,1)S(1)}, bf16[2,128,1024]{2,1,0:T(8,128)(2,1)}, u32[]{:S(2)}, u32[]{:S(2)}) collective-permute-start(bf16[2,128,1024]{2,1,0:T(8,128)(2,1)S(1)} %pad_maximum_fusion.refs_0_), channel_id=1, source_target_pairs={{4,0},{8,4},{12,8},{0,12},{5,1},{9,5},{13,9},{1,13},{6,2},{10,6},{... | collective-permute-start | bytes 1572872 | tf_op jit(solution)/shard_map/ppermute | solution.py:42
  10.0 12.1 %collective-permute-start.6 = (s32[2,144]{1,0:T(2,128)S(1)}, s32[2,144]{1,0:T(2,128)S(1)}, u32[]{:S(2)}, u32[]{:S(2)}) collective-permute-start(s32[2,144]{1,0:T(2,128)S(1)} %copy-done.16), channel_id=1, source_target_pairs={{0,1},{1,0},{2,3},{3,2},{4,5},{5,4},{6,7},{7,6},{8,9},{9,8},{10,11... | collective-permute-start | bytes 3464 | tf_op jit(solution)/shard_map/ppermute | solution.py:38
  22.1 22.8 %collective-permute-start.11 = (bf16[2,128,1024]{2,1,0:T(8,128)(2,1)}, bf16[2,128,1024]{2,1,0:T(8,128)(2,1)}, u32[]{:S(2)}, u32[]{:S(2)}) collective-permute-start(bf16[2,128,1024]{2,1,0:T(8,128)(2,1)} %collective-permute-done.1.refs_3_), channel_id=1, source_target_pairs={{1,32},{0,33},{33,64},{32,65},{65,96},{64,97},{97,128},{96,129},{1... | collective-permute-start | bytes 1572872 | tf_op jit(solution)/shard_map/ppermute | solution.py:58
  23.0 24.9 %collective-permute-start.9 = (bf16[2,128,1024]{2,1,0:T(8,128)(2,1)}, bf16[2,128,1024]{2,1,0:T(8,128)(2,1)}, u32[]{:S(2)}, u32[]{:S(2)}) collective-permute-start(bf16[2,128,1024]{2,1,0:T(8,128)(2,1)} %collective-permute-done.2.refs_4_), channel_id=1, source_target_pairs={{0,4},{4,8},{8,12},{12,0},{1,5},{5,9},{9,13},{13,1},{2,6},{6,10},{... | collective-permute-start | bytes 1572872 | tf_op jit(solution)/shard_map/ppermute | solution.py:46
  24.2 23.7 %collective-permute-start.10 = (bf16[2,128,1024]{2,1,0:T(8,128)(2,1)}, bf16[2,128,1024]{2,1,0:T(8,128)(2,1)}, u32[]{:S(2)}, u32[]{:S(2)}) collective-permute-start(bf16[2,128,1024]{2,1,0:T(8,128)(2,1)} %collective-permute-done.refs_2_), channel_id=1, source_target_pairs={{33,0},{32,1},{65,32},{64,33},{97,64},{96,65},{129,96},{128,97},{1... | collective-permute-start | bytes 1572872 | tf_op jit(solution)/shard_map/ppermute | solution.py:54
  27.9 20.0 %collective-permute-start.8 = (bf16[2,128,1024]{2,1,0:T(8,128)(2,1)}, bf16[2,128,1024]{2,1,0:T(8,128)(2,1)}, u32[]{:S(2)}, u32[]{:S(2)}) collective-permute-start(bf16[2,128,1024]{2,1,0:T(8,128)(2,1)} %collective-permute-done.refs_2_), channel_id=1, source_target_pairs={{16,2},{2,16},{0,18},{18,0},{17,3},{3,17},{1,19},{19,1},{20,6},{6,... | collective-permute-start | bytes 1572872 | tf_op jit(solution)/shard_map/ppermute | solution.py:50
  29.4 18.5 %collective-permute-start.7 = (bf16[2,128,1024]{2,1,0:T(8,128)(2,1)}, bf16[2,128,1024]{2,1,0:T(8,128)(2,1)}, u32[]{:S(2)}, u32[]{:S(2)}) collective-permute-start(bf16[2,128,1024]{2,1,0:T(8,128)(2,1)} %collective-permute-done.refs_2_), channel_id=1, source_target_pairs={{4,0},{8,4},{12,8},{0,12},{5,1},{9,5},{13,9},{1,13},{6,2},{10,6},{... | collective-permute-start | bytes 1572872 | tf_op jit(solution)/shard_map/ppermute | solution.py:42
  44.8 15.6 %collective-permute-start.17 = (bf16[2,128,1024]{2,1,0:T(8,128)(2,1)}, bf16[2,128,1024]{2,1,0:T(8,128)(2,1)S(1)}, u32[]{:S(2)}, u32[]{:S(2)}) collective-permute-start(bf16[2,128,1024]{2,1,0:T(8,128)(2,1)} %collective-permute-done.2.refs_4_), channel_id=1, source_target_pairs={{1,16},{0,17},{17,0},{16,1},{3,18},{2,19},{19,2},{18,3},{5,20},{4,... | collective-permute-start | bytes 1572872 | tf_op jit(solution)/shard_map/ppermute | solution.py:62
  49.8 13.8 %collective-permute-start.13 = (bf16[128,1024]{1,0:T(8,128)(2,1)S(1)}, bf16[128,1024]{1,0:T(8,128)(2,1)S(1)}, u32[]{:S(2)}, u32[]{:S(2)}) collective-permute-start(bf16[128,1024]{1,0:T(8,128)(2,1)S(1)} %slice_bitcast_fusion.1), channel_id=1, source_target_pairs={{0,4},{4,8},{8,12},{12,0},{1,5},{5,9},{9,13},{13,1},{2,6},{6,10},{... | collective-permute-start | bytes 786440 | tf_op jit(solution)/shard_map/ppermute | solution.py:46
  50.3 13.3 %collective-permute-start.12 = (bf16[128,1024]{1,0:T(8,128)(2,1)S(1)}, bf16[128,1024]{1,0:T(8,128)(2,1)S(1)}, u32[]{:S(2)}, u32[]{:S(2)}) collective-permute-start(bf16[128,1024]{1,0:T(8,128)(2,1)S(1)} %slice_bitcast_fusion.2), channel_id=1, source_target_pairs={{4,0},{8,4},{12,8},{0,12},{5,1},{9,5},{13,9},{1,13},{6,2},{10,6},{... | collective-permute-start | bytes 786440 | tf_op jit(solution)/shard_map/ppermute | solution.py:42
  53.2 28.0 %collective-permute-start.19 = (bf16[2,128,1024]{2,1,0:T(8,128)(2,1)}, bf16[2,128,1024]{2,1,0:T(8,128)(2,1)S(1)}, u32[]{:S(2)}, u32[]{:S(2)}) collective-permute-start(bf16[2,128,1024]{2,1,0:T(8,128)(2,1)} %collective-permute-done.8.refs_7_), channel_id=1, source_target_pairs={{1,32},{0,33},{33,64},{32,65},{65,96},{64,97},{97,128},{96,129},{1... | collective-permute-start | bytes 1572872 | tf_op jit(solution)/shard_map/ppermute | solution.py:58
  60.5 20.6 %collective-permute-start.20 = (bf16[2,128,1024]{2,1,0:T(8,128)(2,1)}, bf16[2,128,1024]{2,1,0:T(8,128)(2,1)S(1)}, u32[]{:S(2)}, u32[]{:S(2)}) collective-permute-start(bf16[2,128,1024]{2,1,0:T(8,128)(2,1)} %collective-permute-done.9.refs_6_), channel_id=1, source_target_pairs={{1,16},{0,17},{17,0},{16,1},{3,18},{2,19},{19,2},{18,3},{5,20},{4,... | collective-permute-start | bytes 1572872 | tf_op jit(solution)/shard_map/ppermute | solution.py:62
  61.5 19.6 %collective-permute-start.18 = (bf16[2,128,1024]{2,1,0:T(8,128)(2,1)}, bf16[2,128,1024]{2,1,0:T(8,128)(2,1)S(1)}, u32[]{:S(2)}, u32[]{:S(2)}) collective-permute-start(bf16[2,128,1024]{2,1,0:T(8,128)(2,1)} %collective-permute-done.7.refs_5_), channel_id=1, source_target_pairs={{33,0},{32,1},{65,32},{64,33},{97,64},{96,65},{129,96},{128,97},{1... | collective-permute-start | bytes 1572872 | tf_op jit(solution)/shard_map/ppermute | solution.py:54
  63.6 17.4 %collective-permute-start.14 = (bf16[128,1024]{1,0:T(8,128)(2,1)S(1)}, bf16[128,1024]{1,0:T(8,128)(2,1)S(1)}, u32[]{:S(2)}, u32[]{:S(2)}) collective-permute-start(bf16[128,1024]{1,0:T(8,128)(2,1)S(1)} %collective-permute-done.12.refs_14_), channel_id=1, source_target_pairs={{33,0},{32,1},{65,32},{64,33},{97,64},{96,65},{129,96},{128,97},{1... | collective-permute-start | bytes 786440 | tf_op jit(solution)/shard_map/ppermute | solution.py:54
  63.9 17.1 %collective-permute-start.15 = (bf16[128,1024]{1,0:T(8,128)(2,1)S(1)}, bf16[128,1024]{1,0:T(8,128)(2,1)S(1)}, u32[]{:S(2)}, u32[]{:S(2)}) collective-permute-start(bf16[128,1024]{1,0:T(8,128)(2,1)S(1)} %collective-permute-done.13.refs_15_), channel_id=1, source_target_pairs={{1,32},{0,33},{33,64},{32,65},{65,96},{64,97},{97,128},{96,129},{1... | collective-permute-start | bytes 786440 | tf_op jit(solution)/shard_map/ppermute | solution.py:58
  106.8 21.0 %collective-permute-start.22 = (bf16[3,128,1024]{2,1,0:T(8,128)(2,1)}, bf16[3,128,1024]{2,1,0:T(8,128)(2,1)S(1)}, u32[]{:S(2)}, u32[]{:S(2)}) collective-permute-start(bf16[3,128,1024]{2,1,0:T(8,128)(2,1)} %get-tuple-element.128), channel_id=1, source_target_pairs={{1,32},{0,33},{33,64},{32,65},{65,96},{64,97},{97,128},{96,129},{1... | collective-permute-start | bytes 2359304 | tf_op jit(solution)/shard_map/ppermute | solution.py:58
  106.9 20.9 %collective-permute-start.23 = (bf16[3,128,1024]{2,1,0:T(8,128)(2,1)}, bf16[3,128,1024]{2,1,0:T(8,128)(2,1)S(1)}, u32[]{:S(2)}, u32[]{:S(2)}) collective-permute-start(bf16[3,128,1024]{2,1,0:T(8,128)(2,1)} %get-tuple-element.129), channel_id=1, source_target_pairs={{33,0},{32,1},{65,32},{64,33},{97,64},{96,65},{129,96},{128,97},{1... | collective-permute-start | bytes 2359304 | tf_op jit(solution)/shard_map/ppermute | solution.py:54
  109.8 14.1 %collective-permute-start.24 = (bf16[2,128,1024]{2,1,0:T(8,128)(2,1)}, bf16[2,128,1024]{2,1,0:T(8,128)(2,1)S(1)}, u32[]{:S(2)}, u32[]{:S(2)}) collective-permute-start(bf16[2,128,1024]{2,1,0:T(8,128)(2,1)} %get-tuple-element.130), channel_id=1, source_target_pairs={{1,16},{0,17},{17,0},{16,1},{3,18},{2,19},{19,2},{18,3},{5,20},{4,... | collective-permute-start | bytes 1572872 | tf_op jit(solution)/shard_map/ppermute | solution.py:62
  111.9 46.0 %collective-permute-start.33 = (bf16[288,1024]{1,0:T(8,128)(2,1)S(1)}, bf16[288,1024]{1,0:T(8,128)(2,1)S(1)}, u32[]{:S(2)}, u32[]{:S(2)}) collective-permute-start(bf16[288,1024]{1,0:T(8,128)(2,1)S(1)} %get-tuple-element.158), channel_id=1, source_target_pairs={{0,1},{1,0},{2,3},{3,2},{4,5},{5,4},{6,7},{7,6},{8,9},{9,8},{10,11... | collective-permute-start | bytes 1769480 | tf_op jit(solution)/shard_map/ppermute | solution.py:38
  145.5 13.8 %collective-permute-start.32 = (bf16[128,1024]{1,0:T(8,128)(2,1)S(1)}, bf16[128,1024]{1,0:T(8,128)(2,1)S(1)}, u32[]{:S(2)}, u32[]{:S(2)}) collective-permute-start(bf16[128,1024]{1,0:T(8,128)(2,1)S(1)} %copy-done.24), channel_id=1, source_target_pairs={{4,0},{8,4},{12,8},{0,12},{5,1},{9,5},{13,9},{1,13},{6,2},{10,6},{... | collective-permute-start | bytes 786440 | tf_op jit(solution)/shard_map/ppermute | solution.py:42
  182.7 16.7 %all-to-all-start.1 = ((bf16[16,16,1024]{2,1,0:T(8,128)(2,1)}), bf16[16,16,1024]{2,1,0:T(8,128)(2,1)S(1)}, u32[]{:S(2)}, u32[]{:S(2)}) async-start(bf16[16,16,1024]{2,1,0:T(8,128)(2,1)} %broadcast_in_dim.23), calls=%async_computation.1 | async-start | bytes 1048576 | tf_op jit(solution)/shard_map/all_to_all | solution.py:533
  (38 other events, 278.0 us)

commit v5 on v4

v5 whole, which is shorter than its diff:
```python
import functools

import jax
import jax.numpy as jnp
from jax import lax
from jax.experimental import pallas as pl
from jax.experimental.pallas import tpu as pltpu
from jax.sharding import Mesh, PartitionSpec as P

KIN = 2048
DOUT = 2048
PATCHES = 144
EPS = 1e-06
AXES = ("z", "xlo", "y", "xhi", "core")
VMEM_LIMIT = 60 * 1024 * 1024

X_INDEX = (0, 2, 1, 3)
CORE_SWAP = ((0, 1), (1, 0))
X_NEAR = tuple((X_INDEX[a], X_INDEX[b]) for a, b in ((1, 2), (2, 1), (0, 3), (3, 0)))


def from_next(size):
    return tuple(((i + 1) % size, i) for i in range(size))


def from_previous(size):
    return tuple((i, (i + 1) % size) for i in range(size))


def with_core_flip(pairs):
    return tuple((2 * a + 1 - core, 2 * b + core) for a, b in pairs for core in range(2))


FSDP_GROUPS = tuple(
    tuple((xhi ^ side) * 8 + y * 2 + xhi for y in range(4) for xhi in range(2)) for side in range(2)
)
DP_GROUPS = tuple(tuple(z * 2 + ((z + side) & 1) for z in range(8)) for side in range(2))


def swap_cores(value):
    return lax.ppermute(value, "core", CORE_SWAP)


def from_y_next(value):
    return lax.ppermute(value, "y", from_next(4))


def from_y_previous(value):
    return lax.ppermute(value, "y", from_previous(4))


def from_x_near(value):
    return lax.ppermute(value, ("xlo", "xhi"), X_NEAR)


def from_z_next(value):
    return lax.ppermute(value, ("z", "core"), with_core_flip(from_next(8)))


def from_z_previous(value):
    return lax.ppermute(value, ("z", "core"), with_core_flip(from_previous(8)))


def from_x_twin(value):
    return lax.ppermute(value, ("xlo", "core"), with_core_flip(CORE_SWAP))


ORDER = (
    (0, 0, 0), (0, 1, 0), (0, 3, 0), (0, 0, 1), (0, 2, 0), (0, 3, 1), (0, 1, 1), (1, 1, 0), (1, 3, 0), (0, 2, 1),
    (1, 2, 0), (1, 1, 1), (1, 3, 1), (1, 0, 1), (1, 0, 0), (1, 2, 1),
)
EARLY = 14
LATE = len(ORDER) - EARLY
HALF_AT = len(ORDER)
CORE_AT = HALF_AT + 1
SENT = (3, 3, 2)


def prepare_kernel(
    order, student_own, student_other, teacher_own, teacher_other, residual, places_own, places_other, student_early,
    teacher_early, student_late, teacher_late, picked_out, sent_out, kept_out, turned, packed, gathered
):
    own, step = student_own.shape[0], pl.program_id(0)
    lane = lax.broadcasted_iota(jnp.int32, (PATCHES, PATCHES), 1)
    for side, (teacher, places) in enumerate(((teacher_own, places_own), (teacher_other, places_other))):
        for crop in range(own // PATCHES):
            rows = slice(crop * PATCHES, (crop + 1) * PATCHES)
            out_rows = slice(side * own + crop * PATCHES, side * own + (crop + 1) * PATCHES)
            pick = (places[rows, :] == lane).astype(jnp.float32).astype(jnp.bfloat16)
            gathered[out_rows, :] = jnp.dot(
                pick, teacher[rows, :], preferred_element_type=jnp.float32
            ).astype(jnp.bfloat16)
            if side == 0:
                picked_out[rows, :] = jnp.dot(
                    pick, residual[rows, :], preferred_element_type=jnp.float32
                ).astype(jnp.bfloat16)
    packed[:own, :] = student_own[...]
    packed[own:, :] = student_other[...]
    turned[...] = packed[...].T
    core = order[CORE_AT]
    kept_out[0] = turned[pl.ds(pl.multiple_of(core * 128, 128), 128), :]
    sent_out[0] = turned[pl.ds(pl.multiple_of((1 - core) * 128, 128), 128), :]
    for part in range(2):
        columns = slice(part * 128, (part + 1) * 128)
        for block in range(len(ORDER)):
            @pl.when(order[block] == 2 * step + part)
            def _():
                at = block if block < EARLY else block - EARLY
                spot = slice(at * 128, (at + 1) * 128)
                if block < EARLY:
                    student_early[:, spot] = packed[:, columns]
                    teacher_early[:, spot] = gathered[:, columns]
                else:
                    student_late[:, spot] = packed[:, columns]
                    teacher_late[:, spot] = gathered[:, columns]


def prepare_rows(order, student_own, student_other, teacher_own, teacher_other, residual, places, places_other):
    own, steps = student_own.shape[0], 8
    rows, width = 2 * own, KIN // steps
    mix = pl.BlockSpec((own, width), lambda i, order: (0, i))
    place = pl.BlockSpec((own, 1), lambda i, order: (0, 0))
    early = pl.BlockSpec((rows, EARLY * 128), lambda i, order: (0, 0))
    late = pl.BlockSpec((rows, LATE * 128), lambda i, order: (0, 0))
    turned = pl.BlockSpec((1, 128, rows), lambda i, order: (i, 0, 0))
    return pl.pallas_call(
        prepare_kernel,
        grid_spec=pltpu.PrefetchScalarGridSpec(
            num_scalar_prefetch=1,
            grid=(steps,),
            in_specs=[mix] * 5 + [place] * 2,
            out_specs=[early, early, late, late, mix, turned, turned],
            scratch_shapes=[
                pltpu.VMEM((width, rows), jnp.bfloat16),
                pltpu.VMEM((rows, width), jnp.bfloat16),
                pltpu.VMEM((rows, width), jnp.bfloat16),
            ],
        ),
        out_shape=[
            jax.ShapeDtypeStruct((rows, EARLY * 128), jnp.bfloat16),
            jax.ShapeDtypeStruct((rows, EARLY * 128), jnp.bfloat16),
            jax.ShapeDtypeStruct((rows, LATE * 128), jnp.bfloat16),
            jax.ShapeDtypeStruct((rows, LATE * 128), jnp.bfloat16),
            jax.ShapeDtypeStruct((own, DOUT), jnp.bfloat16),
            jax.ShapeDtypeStruct((8, 128, rows), jnp.bfloat16),
            jax.ShapeDtypeStruct((8, 128, rows), jnp.bfloat16),
        ],
        compiler_params=pltpu.CompilerParams(vmem_limit_bytes=VMEM_LIMIT),
        cost_estimate=pl.CostEstimate(
            flops=4 * rows * PATCHES * KIN, bytes_accessed=16 * 1024 * 1024, transcendentals=0
        ),
    )(order, student_own, student_other, teacher_own, teacher_other, residual, places, places_other)


def early_kernel(student_mix, teacher_mix, *refs):
    weights, (student_out, teacher_out, held) = refs[:EARLY], refs[EARLY:]
    for block in range(EARLY):
        rows = slice(block * 128, (block + 1) * 128)
        held[0, rows, :] = weights[block][0]
        held[1, rows, :] = weights[block][1]
    student_out[...] = jnp.dot(student_mix[...], held[0], preferred_element_type=jnp.float32)
    teacher_out[...] = jnp.dot(teacher_mix[...], held[1], preferred_element_type=jnp.float32)


def early_forward(pieces, student_mix, teacher_mix):
    rows, depth = student_mix.shape
    columns, width = pieces[0].shape[-1], 256
    whole = pl.BlockSpec((rows, depth), lambda j: (0, 0))
    column = pl.BlockSpec((rows, width), lambda j: (0, j))
    return pl.pallas_call(
        early_kernel,
        grid=(columns // width,),
        in_specs=[whole, whole] + [pl.BlockSpec((2, 128, width), lambda j: (0, 0, j))] * EARLY,
        out_specs=[column, column],
        out_shape=[jax.ShapeDtypeStruct((rows, columns), jnp.float32)] * 2,
        scratch_shapes=[pltpu.VMEM((2, depth, width), jnp.bfloat16)],
        compiler_params=pltpu.CompilerParams(vmem_limit_bytes=VMEM_LIMIT),
        cost_estimate=pl.CostEstimate(
            flops=4 * rows * depth * columns, bytes_accessed=17 * 1024 * 1024, transcendentals=0
        ),
    )(student_mix, teacher_mix, *pieces)


def late_kernel(
    order, student_mix, teacher_mix, student_part, teacher_part, residual_own, residual_other, picked_own, picked_other,
    scale, *refs
):
    weights, (student_out, matched_out, sums_out, held) = refs[:LATE], refs[LATE:]
    for block in range(LATE):
        rows = slice(block * 128, (block + 1) * 128)
        held[0, rows, :] = weights[block][0]
        held[1, rows, :] = weights[block][1]
    factor = scale[...] * (KIN ** (-0.5))
    student_sum = student_part[...] + jnp.dot(student_mix[...], held[0], preferred_element_type=jnp.float32)
    teacher_sum = teacher_part[...] + jnp.dot(teacher_mix[...], held[1], preferred_element_type=jnp.float32)
    own = residual_own.shape[0]
    first = pl.program_id(0) == 0
    for side, (residual, picked) in enumerate(((residual_own, picked_own), (residual_other, picked_other))):
        tokens = slice(side * own, (side + 1) * own)
        student = residual[...].astype(jnp.float32) + factor * student_sum[tokens]
        matched = picked[...].astype(jnp.float32) + factor * teacher_sum[tokens]
        student_out[tokens, :] = student
        matched_out[tokens, :] = matched
        spot = lax.broadcasted_iota(jnp.int32, (own, 128), 1)
        sums = jnp.where(
            spot == 0,
            jnp.sum(student * student, axis=-1, keepdims=True),
            jnp.where(
                spot == 1,
                jnp.sum(matched * matched, axis=-1, keepdims=True),
                jnp.where(spot == 2, jnp.sum(student * matched, axis=-1, keepdims=True), 0.0),
            ),
        )
        sums_out[tokens, :] = sums + jnp.where(first, 0.0, sums_out[tokens, :])


def late_forward(
    order, pieces, student_mix, teacher_mix, student_part, teacher_part, residual, residual_other, picked, picked_other,
    scale
):
    (rows, columns), own, width = student_part.shape, residual.shape[0], 256
    steps = columns // width
    whole = pl.BlockSpec((rows, LATE * 128), lambda j, order: (0, 0))
    column = pl.BlockSpec((rows, width), lambda j, order: (0, j))
    tokens = pl.BlockSpec((own, width), lambda j, order: (0, order[HALF_AT] * steps + j))
    return pl.pallas_call(
        late_kernel,
        grid_spec=pltpu.PrefetchScalarGridSpec(
            num_scalar_prefetch=1,
            grid=(steps,),
            in_specs=[whole, whole, column, column]
            + [tokens] * 4
            + [pl.BlockSpec((1, width), lambda j, order: (0, order[HALF_AT] * steps + j))]
            + [pl.BlockSpec((2, 128, width), lambda j, order: (0, 0, j))] * LATE,
            out_specs=[column, column, pl.BlockSpec((rows, 128), lambda j, order: (0, 0))],
            scratch_shapes=[pltpu.VMEM((2, LATE * 128, width), jnp.bfloat16)],
        ),
        out_shape=[
            jax.ShapeDtypeStruct((rows, columns), jnp.float32),
            jax.ShapeDtypeStruct((rows, columns), jnp.float32),
            jax.ShapeDtypeStruct((rows, 128), jnp.float32),
        ],
        compiler_params=pltpu.CompilerParams(vmem_limit_bytes=VMEM_LIMIT),
        cost_estimate=pl.CostEstimate(
            flops=4 * rows * LATE * 128 * columns, bytes_accessed=13 * 1024 * 1024, transcendentals=0
        ),
    )(
        order, student_mix, teacher_mix, student_part, teacher_part, residual, residual_other, picked, picked_other,
        scale, *pieces
    )


def send_kernel(
    total_tokens, order, student, matched, sums, more_sums, scale, mix, next_out, previous_out, twin_out, held_out,
    tokens_own, tokens_other
):
    own = more_sums.shape[0] // 2
    swapped = jnp.concatenate([more_sums[own:, :], more_sums[:own, :]], axis=0)
    total = (sums[...] + swapped) * (1.0 / DOUT)
    inverse_rms = lax.rsqrt(total[:, 0:1] + EPS)
    inverse_matched = lax.rsqrt(total[:, 1:2] + EPS)
    overlap = inverse_rms * inverse_matched * total[:, 2:3]
    shared = inverse_rms * (1.0 / total_tokens)
    student_part = shared * inverse_rms * (EPS * inverse_rms * inverse_rms + overlap)
    matched_part = shared * inverse_matched
    values = student[...]
    tokens = (values * inverse_rms).astype(jnp.bfloat16)
    tokens_own[...] = tokens[:own]
    tokens_other[...] = tokens[own:]
    factor = scale[...] * (KIN ** (-0.5))
    held_out[...] = (factor * (values * student_part - matched[...] * matched_part)).astype(jnp.bfloat16)
    at = 0
    for out in (next_out, previous_out, twin_out):
        count = out.shape[0]
        grad = jnp.dot(
            mix[at : at + count].reshape(count * 128, mix.shape[-1]),
            held_out[...],
            preferred_element_type=jnp.float32,
        )
        out[...] = grad.astype(jnp.bfloat16).reshape(out.shape)
        at += count


def send_grads(total_tokens, order, student, matched, sums, more_sums, scale, turned):
    (rows, columns), width = student.shape, 256
    steps = columns // width
    column = pl.BlockSpec((rows, width), lambda j, order: (0, j))
    narrow = pl.BlockSpec((rows, 128), lambda j, order: (0, 0))
    half = pl.BlockSpec((rows // 2, width), lambda j, order: (0, j))

    def blocks(count):
        return pl.BlockSpec((count, 128, width), lambda j, order: (0, 0, j))

    return pl.pallas_call(
        functools.partial(send_kernel, total_tokens),
        grid_spec=pltpu.PrefetchScalarGridSpec(
            num_scalar_prefetch=1,
            grid=(steps,),
            in_specs=[
                column,
                column,
                narrow,
                narrow,
                pl.BlockSpec((1, width), lambda j, order: (0, order[HALF_AT] * steps + j)),
                pl.BlockSpec((8, 128, rows), lambda j, order: (0, 0, 0)),
            ],
            out_specs=[blocks(count) for count in SENT] + [column, half, half],
        ),
        out_shape=[
            jax.ShapeDtypeStruct((count, 128, columns), jnp.bfloat16) for count in SENT
        ]
        + [
            jax.ShapeDtypeStruct((rows, columns), jnp.bfloat16),
            jax.ShapeDtypeStruct((rows // 2, columns), jnp.bfloat16),
            jax.ShapeDtypeStruct((rows // 2, columns), jnp.bfloat16),
        ],
        compiler_params=pltpu.CompilerParams(vmem_limit_bytes=VMEM_LIMIT),
        cost_estimate=pl.CostEstimate(
            flops=rows * KIN * columns, bytes_accessed=12 * 1024 * 1024, transcendentals=0
        ),
    )(order, student, matched, sums, more_sums, scale, turned)


def keep_kernel(held, mix, out):
    grad = jnp.dot(
        mix[...].reshape(8 * 128, mix.shape[-1]), held[...], preferred_element_type=jnp.float32
    )
    out[...] = grad.reshape(out.shape)


def keep_grads(held, kept):
    (rows, columns), width = held.shape, 256
    return pl.pallas_call(
        keep_kernel,
        grid=(columns // width,),
        in_specs=[
            pl.BlockSpec((rows, width), lambda j: (0, j)),
            pl.BlockSpec((8, 128, rows), lambda j: (0, 0, 0)),
        ],
        out_specs=pl.BlockSpec((8, 128, width), lambda j: (0, 0, j)),
        out_shape=jax.ShapeDtypeStruct((8, 128, columns), jnp.float32),
        compiler_params=pltpu.CompilerParams(vmem_limit_bytes=VMEM_LIMIT),
        cost_estimate=pl.CostEstimate(
            flops=rows * KIN * columns, bytes_accessed=7 * 1024 * 1024, transcendentals=0
        ),
    )(held, kept)


def add_kernel(kept, *refs):
    passed, out = refs[:-1], refs[-1]
    at = 0
    for part in passed:
        spot = slice(at, at + part.shape[0])
        out[spot] = (kept[spot] + part[...].astype(jnp.float32)).astype(jnp.bfloat16)
        at += part.shape[0]


def add_passed(kept, passed):
    width = 256

    def blocks(count):
        return pl.BlockSpec((count, 128, width), lambda j: (0, 0, j))

    return pl.pallas_call(
        add_kernel,
        grid=(kept.shape[-1] // width,),
        in_specs=[blocks(8)] + [blocks(count) for count in SENT],
        out_specs=blocks(8),
        out_shape=jax.ShapeDtypeStruct(kept.shape, jnp.bfloat16),
        compiler_params=pltpu.CompilerParams(vmem_limit_bytes=VMEM_LIMIT),
    )(kept, *passed)


def update_kernel(flip, grads, weight, teacher, first, squares, weight_out, teacher_out, first_out, squares_out):
    rows = []
    for index in range(grads.shape[0]):
        swap = ((flip[0] + index) & 1) == 1
        left = jnp.where(swap, grads[index, 1], grads[index, 0])
        right = jnp.where(swap, grads[index, 0], grads[index, 1])
        rows.append(jnp.concatenate([left, right], axis=1))
    grad = jnp.concatenate(rows, axis=0).astype(jnp.float32)
    first_next = 0.9 * first[...] + 0.1 * grad
    squares_next = 0.95 * squares[...] + 0.05 * grad * grad
    held = weight[...]
    weight_next = held - 0.1 * (first_next / (jnp.sqrt(squares_next) + 1e-08) + 0.04 * held)
    weight_out[...] = weight_next
    teacher_out[...] = 0.96 * teacher[...] + 0.04 * weight_next
    first_out[...] = first_next
    squares_out[...] = squares_next


def adamw_update(flip, grads, weight, teacher, first, squares):
    rows = pl.BlockSpec((32, DOUT), lambda i, flip: (i, 0))
    return pl.pallas_call(
        update_kernel,
        grid_spec=pltpu.PrefetchScalarGridSpec(
            num_scalar_prefetch=1,
            grid=(4,),
            in_specs=[pl.BlockSpec((2, 2, 16, DOUT // 2), lambda i, flip: (i, 0, 0, 0))] + [rows] * 4,
            out_specs=[rows] * 4,
        ),
        out_shape=[jax.ShapeDtypeStruct(weight.shape, jnp.float32)] * 4,
        compiler_params=pltpu.CompilerParams(vmem_limit_bytes=VMEM_LIMIT),
    )(flip, grads, weight, teacher, first, squares)


def join_columns(which, own, other):
    return jnp.where(
        which == 0, jnp.concatenate([own, other], axis=-1), jnp.concatenate([other, own], axis=-1)
    )


def shards(
    residual,
    student_mix,
    teacher_mix,
    positions,
    layer_scale,
    student_weight,
    teacher_weight,
    moment,
    second,
):
    half = DOUT // 2
    token_count = student_mix.shape[0]
    total_tokens = token_count * 256
    z, xlo, y, xhi, core = (lax.axis_index(name) for name in AXES)
    which = (core + z + xhi + xlo) & 1

    def columns_of(value, index):
        return lax.dynamic_slice_in_dim(value, index * half, half, axis=-1)

    def both_weights(index):
        return jnp.stack([columns_of(student_weight, index), columns_of(teacher_weight, index)]).astype(jnp.bfloat16)

    own = both_weights(which)
    order = jnp.stack(
        [(((y + dy) & 3) * 2 + (xhi ^ dx)) * 2 + (core ^ side) for side, dy, dx in ORDER] + [which, core]
    ).astype(jnp.int32)
    scale = layer_scale.reshape(1, DOUT)

    own, student_sent, teacher_sent, positions_sent, student_held, teacher_held, residual = lax.optimization_barrier(
        (own, student_mix, teacher_mix, positions, student_weight, teacher_weight, residual)
    )
    student_weight, teacher_weight = student_held, teacher_held
    student_other, positions_sent = lax.optimization_barrier((swap_cores(student_sent), positions_sent))
    teacher_other, places_other = swap_cores(teacher_sent), swap_cores(positions_sent)
    up, down, across, student_other, teacher_other, places, places_other, student_held, teacher_held = (
        lax.optimization_barrier(
            (
                from_y_next(own), from_y_previous(own), from_x_near(own), student_other, teacher_other, positions,
                places_other, student_held, teacher_held,
            )
        )
    )
    other_sent = jnp.stack(
        [columns_of(student_held, 1 - which), columns_of(teacher_held, 1 - which)]
    ).astype(jnp.bfloat16)
    (
        up_two, across_down, across_up, passed_up, passed_down, across, other_sent, places, places_other, student_other,
        teacher_other, residual,
    ) = lax.optimization_barrier(
        (
            from_y_next(up), from_y_previous(across), from_x_near(up), from_z_next(up), from_z_previous(down), across,
            other_sent, places.reshape(token_count, 1), places_other.reshape(token_count, 1), student_other,
            teacher_other, residual,
        )
    )
    prepared = prepare_rows(
        order, student_mix, student_other, teacher_mix, teacher_other, residual, places, places_other
    )
    (
        across_two, passed_two, passed_across_up, passed_across_down, passed_across, prepared, other_sent, residual_sent
    ) = lax.optimization_barrier(
        (
            from_y_next(across_up), from_z_next(up_two), from_z_previous(across_up), from_x_near(passed_down),
            from_x_twin(across), prepared, other_sent, residual,
        )
    )
    student_early, teacher_early, student_late, teacher_late, picked, sent_mix, kept_mix = prepared
    passed_across_two = from_z_next(across_two)
    residual_other, picked_other, other = swap_cores(residual_sent), swap_cores(picked), swap_cores(other_sent)
    student_part, teacher_part = early_forward(
        (
            own, up, down, across, up_two, across_down, across_up, passed_up, passed_down, across_two, passed_two,
            passed_across_up, passed_across_down, passed_across,
        ),
        student_early,
        teacher_early,
    )
    student_out, matched, sums = late_forward(
        order, (other, passed_across_two), student_late, teacher_late, student_part, teacher_part, residual,
        residual_other, picked, picked_other, scale
    )
    *sent, held, tokens_own, tokens_other = send_grads(
        total_tokens, order, student_out, matched, sums, swap_cores(sums), scale, sent_mix
    )
    kept = keep_grads(held, kept_mix)
    student_tokens = join_columns(which, tokens_own, swap_cores(tokens_other))
    passed = lax.optimization_barrier((from_z_previous(sent[0]), from_z_next(sent[1]), from_x_twin(sent[2])))
    by_chip = lax.all_to_all(
        add_passed(kept, passed), ("xlo", "y", "xhi"), 0, 0, axis_index_groups=FSDP_GROUPS
    )
    by_chip, student_tokens = lax.optimization_barrier((by_chip, student_tokens))
    total = jnp.sum(by_chip.astype(jnp.float32), axis=0).astype(jnp.bfloat16)
    by_copy = lax.all_to_all(
        total.reshape(8, 16, half), ("z", "xlo"), 0, 0, axis_index_groups=DP_GROUPS
    )
    copy_rows = jnp.sum(by_copy.astype(jnp.float32), axis=0).astype(jnp.bfloat16)
    full = lax.all_to_all(jnp.broadcast_to(copy_rows[None], (16, 16, half)), ("z", "xlo"), 0, 0)
    flip = ((core + xhi) & 1).astype(jnp.int32).reshape(1)
    weight_next, teacher_next, first_next, squares_next = adamw_update(
        flip, full.reshape(8, 2, 16, half), student_weight, teacher_weight, moment, second
    )
    return (weight_next, teacher_next, first_next, squares_next, student_tokens)


def solution(mesh):
    split = Mesh(mesh.devices.reshape(8, 2, 4, 2, 2), AXES)
    tokens = P(AXES, None)
    owned = P(("y", "xhi", "core"), None)
    return jax.shard_map(
        shards,
        mesh=split,
        in_specs=(tokens, tokens, tokens, tokens, P(), owned, owned, owned, owned),
        out_specs=(owned, owned, owned, owned, tokens),
        check_vma=False,
    )
```

time: 209 us -> 201 us (0.962)
  local copies, waits for them, and re-layouts: 16.3 us -> 11.5 us
  Pallas kernels: 49.4 us -> 53 us
  starting transfers between devices: 40.9 us -> 37.5 us
    all_to_all x0 -> x1, waiting for transfers between devices: none -> 22.9 us  [shards(): lax.all_to_all(add_passed(kept, passed), ('xlo', 'y', 'xhi'), 0, 0, axis_...]
    ppermute x4, waiting for transfers between devices: 13.3 us -> 4.76 us  [from_z_next(): return lax.ppermute(value, ('z', 'core'), with_core_flip(from_next(8)))]
    ppermute x6 -> x2, waiting for transfers between devices: 9.93 us -> 3.47 us  [from_y_previous(): return lax.ppermute(value, 'y', from_previous(4))]
    all_to_all x0 -> x1, starting transfers between devices: none -> 5.79 us  [shards(): lax.all_to_all(add_passed(kept, passed), ('xlo', 'y', 'xhi'), 0, 0, axis_...]
    ppermute x6 -> x3, starting transfers between devices: 11.9 us -> 6.25 us  [from_y_next(): return lax.ppermute(value, 'y', from_next(4))]
    ppermute x3 -> x2, waiting for transfers between devices: 13.5 us -> 8.42 us  [from_x_twin(): return lax.ppermute(value, ('xlo', 'core'), with_core_flip(CORE_SWAP))]
    ppermute x4 -> x3, waiting for transfers between devices: 15.6 us -> 11.7 us  [from_x_near(): return lax.ppermute(value, ('xlo', 'xhi'), X_NEAR)]
    ppermute x7 -> x8, waiting for transfers between devices: 6.8 us -> 3.94 us  [swap_cores(): return lax.ppermute(value, 'core', CORE_SWAP)]
  transfers between devices with their start and end apart: 35 -> 27, of which waited for: 14 -> 16; matrix products, arithmetic and copies ran while one was open for 5% -> 3% of each run, Pallas kernels for 12% -> 14%
where the time goes in v5:
time: 201 us; the launch traced here: 199 us
  waiting for transfers between devices  77.8 us (39%)
  Pallas kernels  53 us (26%)
  starting transfers between devices  37.5 us (19%)
  blocking collectives  15.7 us (8%)
  local copies, waits for them, and re-layouts  11.5 us (6%)
  other arithmetic  2.78 us (1%)
    all_to_all x1, waiting for transfers between devices, shards(): lax.all_to_all(add_passed(kept, passed), ('xlo', 'y', 'xhi'), 0, 0, axis_...  22.9 us
    all_to_all x1, blocking collectives, shards(): lax.all_to_all(total.reshape(8, 16, half), ('z', 'xlo'), 0, 0, axis_index...  15.7 us
    all_to_all x1, waiting for transfers between devices, shards(): lax.all_to_all(jnp.broadcast_to(copy_rows[None], (16, 16, half)), ('z', '...  15.4 us
    pallas_call x1, Pallas kernels, prepare_rows(): pl.pallas_call(prepare_kernel, grid_spec=pltpu.PrefetchScalarGridSpec(num...  12.2 us
    ppermute x3, waiting for transfers between devices, from_x_near(): return lax.ppermute(value, ('xlo', 'xhi'), X_NEAR)  11.7 us
    pallas_call x1, Pallas kernels, early_forward(): pl.pallas_call(early_kernel, grid=(columns // width,), in_specs=[whole, w...  9.78 us
    ppermute x4, starting transfers between devices, from_z_next(): return lax.ppermute(value, ('z', 'core'), with_core_flip(from_next(8)))  9.63 us
    ppermute x2, waiting for transfers between devices, from_x_twin(): return lax.ppermute(value, ('xlo', 'core'), with_core_flip(CORE_SWAP))  8.42 us
  transfers between devices with their start and end apart: 27, of which 16 were waited for; matrix products, arithmetic and copies ran while one was open for 3% of the time, Pallas kernels for 14%

profile of v5, /device:TPU:4, one launch (start us, length us, event | category | flops | bytes accessed | tf_op | source)
XLA Modules:
  0.0 199.2 jit_solution(11100738813357715780)
XLA Ops:
  6.6 10.0 %collective-permute-done.2.refs_3_ = bf16[2,128,1024]{2,1,0:T(8,128)(2,1)S(1)} collective-permute-done((bf16[2,128,1024]{2,1,0:T(8,128)(2,1)S(1)}, bf16[2,128,1024]{2,1,0:T(8,128)(2,1)S(1)}, u32[]{:S(2)}, u32[]{:S(2)}) %collective-permute-start.2) | collective-permute-done | bytes 524320 | tf_op jit(solution)/shard_map/ppermute | solution.py:53
  19.9 3.8 %collective-permute-start.9 = (bf16[2,128,1024]{2,1,0:T(8,128)(2,1)}, bf16[2,128,1024]{2,1,0:T(8,128)(2,1)S(1)}, u32[]{:S(2)}, u32[]{:S(2)}) collective-permute-start(bf16[2,128,1024]{2,1,0:T(8,128)(2,1)} %collective-permute-done.refs_1_), channel_id=1, source_target_pairs={{33,0},{32,1},{65,32},{64,33},{97,64},{96,65},{129,96},{128,97},{1... | collective-permute-start | bytes 1572872 | tf_op jit(solution)/shard_map/ppermute | solution.py:57
  25.2 2.0 %collective-permute-start.6 = (bf16[2,128,1024]{2,1,0:T(8,128)(2,1)}, bf16[2,128,1024]{2,1,0:T(8,128)(2,1)}, u32[]{:S(2)}, u32[]{:S(2)}) collective-permute-start(bf16[2,128,1024]{2,1,0:T(8,128)(2,1)} %collective-permute-done.refs_1_), channel_id=1, source_target_pairs={{4,0},{8,4},{12,8},{0,12},{5,1},{9,5},{13,9},{1,13},{6,2},{10,6},{... | collective-permute-start | bytes 1572872 | tf_op jit(solution)/shard_map/ppermute | solution.py:45
  33.8 2.0 %collective-permute-done.9.refs_7_ = bf16[2,128,1024]{2,1,0:T(8,128)(2,1)S(1)} collective-permute-done((bf16[2,128,1024]{2,1,0:T(8,128)(2,1)}, bf16[2,128,1024]{2,1,0:T(8,128)(2,1)S(1)}, u32[]{:S(2)}, u32[]{:S(2)}) %collective-permute-start.9) | collective-permute-done | bytes 524320 | tf_op jit(solution)/shard_map/ppermute | solution.py:57
  40.6 5.0 %collective-permute-start.15 = (bf16[2,128,1024]{2,1,0:T(8,128)(2,1)S(1)}, bf16[2,128,1024]{2,1,0:T(8,128)(2,1)}, u32[]{:S(2)}, u32[]{:S(2)}) collective-permute-start(bf16[2,128,1024]{2,1,0:T(8,128)(2,1)S(1)} %collective-permute-done.2.refs_3_), channel_id=1, source_target_pairs={{1,16},{0,17},{17,0},{16,1},{3,18},{2,19},{19,2},{18,3},{5,20},{4,... | collective-permute-start | bytes 1572872 | tf_op jit(solution)/shard_map/ppermute | solution.py:65
  45.6 2.6 %collective-permute-start.11 = (bf16[2,128,1024]{2,1,0:T(8,128)(2,1)}, bf16[2,128,1024]{2,1,0:T(8,128)(2,1)}, u32[]{:S(2)}, u32[]{:S(2)}) collective-permute-start(bf16[2,128,1024]{2,1,0:T(8,128)(2,1)} %collective-permute-done.8.refs_6_), channel_id=1, source_target_pairs={{4,0},{8,4},{12,8},{0,12},{5,1},{9,5},{13,9},{1,13},{6,2},{10,6},{... | collective-permute-start | bytes 1572872 | tf_op jit(solution)/shard_map/ppermute | solution.py:45
  50.5 12.2 %shard_map.128 = (bf16[576,1792]{1,0:T(8,128)(2,1)}, bf16[576,1792]{1,0:T(8,128)(2,1)}, bf16[576,256]{1,0:T(8,128)(2,1)}, bf16[576,256]{1,0:T(8,128)(2,1)}, bf16...) custom-call(s32[18]{0:T(128)} %stack.99.order, bf16[288,2048]{1,0:T(8,128)(2,1)} %student_own.1, ...), custom_call_target="tpu_custom_call" | custom-call | flops 679477248 | bytes 16777216 | tf_op jit(solution)/shard_map/pallas_call | solution.py:126
  63.4 2.0 collective-permute-start.19
  65.4 9.8 %shard_map.129 = (f32[576,1024]{1,0:T(8,128)}, f32[576,1024]{1,0:T(8,128)}) custom-call(bf16[576,1792]{1,0:T(8,128)(2,1)} %get-tuple-element.113.student_mix, bf16[576,1792]{1,0:T(8,128)(2,1)} %get-tuple-element.114.teacher_mix, bf16[2,128,1024]{2,1,0:T(8,128)(2,1)} %copy-done.11, bf16[2,128,1024]{2,1,0:T(8,128)(2,1)} %collective-permute-done.refs_1_, ...), custom_call_target="tpu_custom_call" | custom-call | flops 4227858432 | bytes 17825792 | tf_op jit(solution)/shard_map/pallas_call | solution.py:170
  75.2 2.5 %collective-permute-done.19.refs_1_ = bf16[2,128,1024]{2,1,0:T(8,128)(2,1)} collective-permute-done((bf16[2,128,1024]{2,1,0:T(8,128)(2,1)}, bf16[2,128,1024]{2,1,0:T(8,128)(2,1)}, u32[]{:S(2)}, u32[]{:S(2)}) %collective-permute-start.19) | collective-permute-done | bytes 524320 | tf_op jit(solution)/shard_map/ppermute | solution.py:57
  79.2 7.9 %shard_map.130 = (f32[576,1024]{1,0:T(8,128)}, f32[576,1024]{1,0:T(8,128)}, f32[576,128]{1,0:T(8,128)}) custom-call(s32[18]{0:T(128)} %stack.99.order, bf16[576,256]{1,0:T(8,128)(2,1)} %get-tuple-element.111.student_mix, bf16[576,256]{1,0:T(8,128)(2,1)} %get-tuple-element.112.teacher_mix, f32[576,1024]{1,0:T(8,128)} %get-tuple-element.122.student_part, ...), custom_call_target="tpu_custom_call" | custom-call | flops 603979776 | bytes 13631488 | tf_op jit(solution)/shard_map/pallas_call | solution.py:226
  89.7 7.7 %shard_map.131 = (bf16[3,128,1024]{2,1,0:T(8,128)(2,1)}, bf16[3,128,1024]{2,1,0:T(8,128)(2,1)}, bf16[2,128,1024]{2,1,0:T(8,128)(2,1)}, bf16[576,1024]{1,0:T(8,12...) custom-call(s32[18]{0:T(128)} %stack.99.order, f32[576,1024]{1,0:T(8,128)} %get-tuple-element.127.student, ...), custom_call_target="tpu_custom_call" | custom-call | flops 1207959552 | bytes 12582912 | tf_op jit(solution)/shard_map/pallas_call | solution.py:294
  97.5 3.2 %collective-permute-start.22 = (bf16[3,128,1024]{2,1,0:T(8,128)(2,1)}, bf16[3,128,1024]{2,1,0:T(8,128)(2,1)S(1)}, u32[]{:S(2)}, u32[]{:S(2)}) collective-permute-start(bf16[3,128,1024]{2,1,0:T(8,128)(2,1)} %get-tuple-element.134), channel_id=1, source_target_pairs={{33,0},{32,1},{65,32},{64,33},{97,64},{96,65},{129,96},{128,97},{1... | collective-permute-start | bytes 2359304 | tf_op jit(solution)/shard_map/ppermute | solution.py:57
  100.8 5.6 %shard_map.132.kept = f32[8,128,1024]{2,1,0:T(8,128)} custom-call(bf16[576,1024]{1,0:T(8,128)(2,1)} %get-tuple-element.131.held, bf16[8,128,576]{2,1,0:T(8,128)(2,1)} %get-tuple-element.132.mix), custom_call_target="tpu_custom_call" | custom-call | flops 1207959552 | bytes 7340032 | tf_op jit(solution)/shard_map/pallas_call | solution.py:333
  106.3 8.4 %collective-permute-done.23.refs_2_ = bf16[2,128,1024]{2,1,0:T(8,128)(2,1)S(1)} collective-permute-done((bf16[2,128,1024]{2,1,0:T(8,128)(2,1)}, bf16[2,128,1024]{2,1,0:T(8,128)(2,1)S(1)}, u32[]{:S(2)}, u32[]{:S(2)}) %collective-permute-start.23) | collective-permute-done | bytes 524320 | tf_op jit(solution)/shard_map/ppermute | solution.py:65
  114.7 3.8 %collective-permute-done.21.refs_0_ = bf16[3,128,1024]{2,1,0:T(8,128)(2,1)S(1)} collective-permute-done((bf16[3,128,1024]{2,1,0:T(8,128)(2,1)}, bf16[3,128,1024]{2,1,0:T(8,128)(2,1)S(1)}, u32[]{:S(2)}, u32[]{:S(2)}) %collective-permute-start.21) | collective-permute-done | bytes 786464 | tf_op jit(solution)/shard_map/ppermute | solution.py:61
  120.2 4.7 %shard_map.133 = bf16[8,128,1024]{2,1,0:T(8,128)(2,1)} custom-call(f32[8,128,1024]{2,1,0:T(8,128)} %shard_map.132.kept, bf16[3,128,1024]{2,1,0:T(8,128)(2,1)} %copy-done.6, bf16[3,128,1024]{2,1,0:T(8,128)(2,1)} %copy-done.7, bf16[2,128,1024]{2,1,0:T(8,128)(2,1)} %copy-done.10), custom_call_target="tpu_custom_call" | custom-call | tf_op jit(solution)/shard_map/pallas_call | solution.py:364
  125.0 5.8 %all-to-all-start = ((bf16[8,128,1024]{2,1,0:T(8,128)(2,1)}), bf16[8,128,1024]{2,1,0:T(8,128)(2,1)S(1)}, u32[]{:S(2)}, u32[]{:S(2)}) async-start(bf16[8,128,1024]{2,1,0:T(8,128)(2,1)} %shard_map.133), calls=%async_computation | async-start | bytes 4194304 | tf_op jit(solution)/shard_map/all_to_all | solution.py:501
  130.8 2.2 %collective-permute-done.24 = bf16[288,1024]{1,0:T(8,128)(2,1)S(1)} collective-permute-done((bf16[288,1024]{1,0:T(8,128)(2,1)}, bf16[288,1024]{1,0:T(8,128)(2,1)S(1)}, u32[]{:S(2)}, u32[]{:S(2)}) %collective-permute-start.24) | collective-permute-done | bytes 589856 | tf_op jit(solution)/shard_map/ppermute | solution.py:41
  134.4 22.9 %all-to-all-done = bf16[8,128,1024]{2,1,0:T(8,128)(2,1)S(1)} async-done(((bf16[8,128,1024]{2,1,0:T(8,128)(2,1)}), bf16[8,128,1024]{2,1,0:T(8,128)(2,1)S(1)}, u32[]{:S(2)}, u32[]{:S(2)}) %all-to-all-start) | async-done | bytes 2097184 | tf_op jit(solution)/shard_map/all_to_all | solution.py:501
  157.7 15.7 %all_to_all.15 = bf16[8,16,1024]{2,1,0:T(8,128)(2,1)S(1)} all-to-all(bf16[8,16,1024]{2,1,0:T(8,128)(2,1)S(1)} %bitcast.31), channel_id=1, replica_groups={{0,48,64,112,128,176,192,240},{16,32,80,96,144,160,208,224},{1,49,65,11..., dimensions={0} | all-to-all | bytes 524288 | tf_op jit(solution)/shard_map/all_to_all | solution.py:506
  174.3 3.6 %all-to-all-start.2 = ((bf16[16,16,1024]{2,1,0:T(8,128)(2,1)}), bf16[16,16,1024]{2,1,0:T(8,128)(2,1)S(1)}, u32[]{:S(2)}, u32[]{:S(2)}) async-start(bf16[16,16,1024]{2,1,0:T(8,128)(2,1)} %broadcast_in_dim.2), calls=%async_computation.2 | async-start | bytes 1048576 | tf_op jit(solution)/shard_map/all_to_all | solution.py:510
  177.9 15.4 %all-to-all-done.2 = bf16[16,16,1024]{2,1,0:T(8,128)(2,1)S(1)} async-done(((bf16[16,16,1024]{2,1,0:T(8,128)(2,1)}), bf16[16,16,1024]{2,1,0:T(8,128)(2,1)S(1)}, u32[]{:S(2)}, u32[]{:S(2)}) %all-to-all-start.2) | async-done | bytes 524320 | tf_op jit(solution)/shard_map/all_to_all | solution.py:510
  194.1 5.1 %shard_map.134 = (f32[128,2048]{1,0:T(8,128)}, f32[128,2048]{1,0:T(8,128)}, f32[128,2048]{1,0:T(8,128)}, f32[128,2048]{1,0:T(8,128)}) custom-call(s32[1]{0:T(128)} %bitcast.flip, bf16[8,2,16,1024]{3,2,1,0:T(8,128)(2,1)} %bitcast.30, f32[128,2048]{1,0:T(8,128)} %weight, f32[128,2048]{1,0:T(8,128)} %teacher, f32[128,2048]{1,0:T(8,128)} %first.1, ...), custom_call_target="tpu_custom_call" | custom-call | tf_op jit(solution)/shard_map/pallas_call | solution.py:394
  (88 shorter events, 34.5 us)
Async XLA Ops:
  2.2 16.1 %collective-permute-start.4 = (bf16[288,2048]{1,0:T(8,128)(2,1)}, bf16[288,2048]{1,0:T(8,128)(2,1)}, u32[]{:S(2)}, u32[]{:S(2)}) collective-permute-start(bf16[288,2048]{1,0:T(8,128)(2,1)} %teacher_own.1), channel_id=1, source_target_pairs={{0,1},{1,0},{2,3},{3,2},{4,5},{5,4},{6,7},{7,6},{8,9},{9,8},{10,11... | collective-permute-start | bytes 3538952 | tf_op jit(solution)/shard_map/ppermute | solution.py:41
  2.7 13.9 %collective-permute-start.2 = (bf16[2,128,1024]{2,1,0:T(8,128)(2,1)S(1)}, bf16[2,128,1024]{2,1,0:T(8,128)(2,1)S(1)}, u32[]{:S(2)}, u32[]{:S(2)}) collective-permute-start(bf16[2,128,1024]{2,1,0:T(8,128)(2,1)S(1)} %pad_maximum_fusion.refs_0_), channel_id=1, source_target_pairs={{16,2},{2,16},{0,18},{18,0},{17,3},{3,17},{1,19},{19,1},{20,6},{6,... | collective-permute-start | bytes 1572872 | tf_op jit(solution)/shard_map/ppermute | solution.py:53
  3.3 14.9 %collective-permute-start.1 = (bf16[2,128,1024]{2,1,0:T(8,128)(2,1)S(1)}, bf16[2,128,1024]{2,1,0:T(8,128)(2,1)S(1)}, u32[]{:S(2)}, u32[]{:S(2)}) collective-permute-start(bf16[2,128,1024]{2,1,0:T(8,128)(2,1)S(1)} %pad_maximum_fusion.refs_0_), channel_id=1, source_target_pairs={{0,4},{4,8},{8,12},{12,0},{1,5},{5,9},{9,13},{13,1},{2,6},{6,10},{... | collective-permute-start | bytes 1572872 | tf_op jit(solution)/shard_map/ppermute | solution.py:49
  4.9 13.4 %collective-permute-start = (bf16[2,128,1024]{2,1,0:T(8,128)(2,1)S(1)}, bf16[2,128,1024]{2,1,0:T(8,128)(2,1)}, u32[]{:S(2)}, u32[]{:S(2)}) collective-permute-start(bf16[2,128,1024]{2,1,0:T(8,128)(2,1)S(1)} %pad_maximum_fusion.refs_0_), channel_id=1, source_target_pairs={{4,0},{8,4},{12,8},{0,12},{5,1},{9,5},{13,9},{1,13},{6,2},{10,6},{... | collective-permute-start | bytes 1572872 | tf_op jit(solution)/shard_map/ppermute | solution.py:45
  6.5 11.8 %collective-permute-start.5 = (s32[2,144]{1,0:T(2,128)S(1)}, s32[2,144]{1,0:T(2,128)S(1)}, u32[]{:S(2)}, u32[]{:S(2)}) collective-permute-start(s32[2,144]{1,0:T(2,128)S(1)} %copy-done.13), channel_id=1, source_target_pairs={{0,1},{1,0},{2,3},{3,2},{4,5},{5,4},{6,7},{7,6},{8,9},{9,8},{10,11... | collective-permute-start | bytes 3464 | tf_op jit(solution)/shard_map/ppermute | solution.py:41
  18.3 14.0 %collective-permute-start.7 = (bf16[2,128,1024]{2,1,0:T(8,128)(2,1)S(1)}, bf16[2,128,1024]{2,1,0:T(8,128)(2,1)S(1)}, u32[]{:S(2)}, u32[]{:S(2)}) collective-permute-start(bf16[2,128,1024]{2,1,0:T(8,128)(2,1)S(1)} %collective-permute-done.2.refs_3_), channel_id=1, source_target_pairs={{0,4},{4,8},{8,12},{12,0},{1,5},{5,9},{9,13},{13,1},{2,6},{6,10},{... | collective-permute-start | bytes 1572872 | tf_op jit(solution)/shard_map/ppermute | solution.py:49
  19.9 13.9 %collective-permute-start.10 = (bf16[2,128,1024]{2,1,0:T(8,128)(2,1)S(1)}, bf16[2,128,1024]{2,1,0:T(8,128)(2,1)}, u32[]{:S(2)}, u32[]{:S(2)}) collective-permute-start(bf16[2,128,1024]{2,1,0:T(8,128)(2,1)S(1)} %collective-permute-done.1.refs_2_), channel_id=1, source_target_pairs={{1,32},{0,33},{33,64},{32,65},{65,96},{64,97},{97,128},{96,129},{1... | collective-permute-start | bytes 1572872 | tf_op jit(solution)/shard_map/ppermute | solution.py:61
  19.9 15.9 %collective-permute-start.9 = (bf16[2,128,1024]{2,1,0:T(8,128)(2,1)}, bf16[2,128,1024]{2,1,0:T(8,128)(2,1)S(1)}, u32[]{:S(2)}, u32[]{:S(2)}) collective-permute-start(bf16[2,128,1024]{2,1,0:T(8,128)(2,1)} %collective-permute-done.refs_1_), channel_id=1, source_target_pairs={{33,0},{32,1},{65,32},{64,33},{97,64},{96,65},{129,96},{128,97},{1... | collective-permute-start | bytes 1572872 | tf_op jit(solution)/shard_map/ppermute | solution.py:57
  23.7 13.9 %collective-permute-start.8 = (bf16[2,128,1024]{2,1,0:T(8,128)(2,1)}, bf16[2,128,1024]{2,1,0:T(8,128)(2,1)}, u32[]{:S(2)}, u32[]{:S(2)}) collective-permute-start(bf16[2,128,1024]{2,1,0:T(8,128)(2,1)} %collective-permute-done.refs_1_), channel_id=1, source_target_pairs={{16,2},{2,16},{0,18},{18,0},{17,3},{3,17},{1,19},{19,1},{20,6},{6,... | collective-permute-start | bytes 1572872 | tf_op jit(solution)/shard_map/ppermute | solution.py:53
  25.2 14.2 %collective-permute-start.6 = (bf16[2,128,1024]{2,1,0:T(8,128)(2,1)}, bf16[2,128,1024]{2,1,0:T(8,128)(2,1)}, u32[]{:S(2)}, u32[]{:S(2)}) collective-permute-start(bf16[2,128,1024]{2,1,0:T(8,128)(2,1)} %collective-permute-done.refs_1_), channel_id=1, source_target_pairs={{4,0},{8,4},{12,8},{0,12},{5,1},{9,5},{13,9},{1,13},{6,2},{10,6},{... | collective-permute-start | bytes 1572872 | tf_op jit(solution)/shard_map/ppermute | solution.py:45
  39.3 23.3 %collective-permute-start.12 = (bf16[2,128,1024]{2,1,0:T(8,128)(2,1)}, bf16[2,128,1024]{2,1,0:T(8,128)(2,1)}, u32[]{:S(2)}, u32[]{:S(2)}) collective-permute-start(bf16[2,128,1024]{2,1,0:T(8,128)(2,1)} %collective-permute-done.6.refs_4_), channel_id=1, source_target_pairs={{33,0},{32,1},{65,32},{64,33},{97,64},{96,65},{129,96},{128,97},{1... | collective-permute-start | bytes 1572872 | tf_op jit(solution)/shard_map/ppermute | solution.py:57
  40.0 22.7 %collective-permute-start.14 = (bf16[2,128,1024]{2,1,0:T(8,128)(2,1)}, bf16[2,128,1024]{2,1,0:T(8,128)(2,1)}, u32[]{:S(2)}, u32[]{:S(2)}) collective-permute-start(bf16[2,128,1024]{2,1,0:T(8,128)(2,1)} %collective-permute-done.10.refs_8_), channel_id=1, source_target_pairs={{16,2},{2,16},{0,18},{18,0},{17,3},{3,17},{1,19},{19,1},{20,6},{6,... | collective-permute-start | bytes 1572872 | tf_op jit(solution)/shard_map/ppermute | solution.py:53
  40.6 22.1 %collective-permute-start.15 = (bf16[2,128,1024]{2,1,0:T(8,128)(2,1)S(1)}, bf16[2,128,1024]{2,1,0:T(8,128)(2,1)}, u32[]{:S(2)}, u32[]{:S(2)}) collective-permute-start(bf16[2,128,1024]{2,1,0:T(8,128)(2,1)S(1)} %collective-permute-done.2.refs_3_), channel_id=1, source_target_pairs={{1,16},{0,17},{17,0},{16,1},{3,18},{2,19},{19,2},{18,3},{5,20},{4,... | collective-permute-start | bytes 1572872 | tf_op jit(solution)/shard_map/ppermute | solution.py:65
  45.6 17.1 %collective-permute-start.13 = (bf16[2,128,1024]{2,1,0:T(8,128)(2,1)}, bf16[2,128,1024]{2,1,0:T(8,128)(2,1)}, u32[]{:S(2)}, u32[]{:S(2)}) collective-permute-start(bf16[2,128,1024]{2,1,0:T(8,128)(2,1)} %collective-permute-done.8.refs_6_), channel_id=1, source_target_pairs={{1,32},{0,33},{33,64},{32,65},{65,96},{64,97},{97,128},{96,129},{1... | collective-permute-start | bytes 1572872 | tf_op jit(solution)/shard_map/ppermute | solution.py:61
  45.6 17.1 %collective-permute-start.11 = (bf16[2,128,1024]{2,1,0:T(8,128)(2,1)}, bf16[2,128,1024]{2,1,0:T(8,128)(2,1)}, u32[]{:S(2)}, u32[]{:S(2)}) collective-permute-start(bf16[2,128,1024]{2,1,0:T(8,128)(2,1)} %collective-permute-done.8.refs_6_), channel_id=1, source_target_pairs={{4,0},{8,4},{12,8},{0,12},{5,1},{9,5},{13,9},{1,13},{6,2},{10,6},{... | collective-permute-start | bytes 1572872 | tf_op jit(solution)/shard_map/ppermute | solution.py:45
  62.7 15.0 %collective-permute-start.16 = (bf16[288,2048]{1,0:T(8,128)(2,1)S(1)}, bf16[288,2048]{1,0:T(8,128)(2,1)S(1)}, u32[]{:S(2)}, u32[]{:S(2)}) collective-permute-start(bf16[288,2048]{1,0:T(8,128)(2,1)S(1)} %copy-done), channel_id=1, source_target_pairs={{0,1},{1,0},{2,3},{3,2},{4,5},{5,4},{6,7},{7,6},{8,9},{9,8},{10,11... | collective-permute-start | bytes 3538952 | tf_op jit(solution)/shard_map/ppermute | solution.py:41
  62.8 14.9 %collective-permute-start.17 = (bf16[288,2048]{1,0:T(8,128)(2,1)}, bf16[288,2048]{1,0:T(8,128)(2,1)S(1)}, u32[]{:S(2)}, u32[]{:S(2)}) collective-permute-start(bf16[288,2048]{1,0:T(8,128)(2,1)} %get-tuple-element.125.picked_own), channel_id=1, source_target_pairs={{0,1},{1,0},{2,3},{3,2},{4,5},{5,4},{6,7},{7,6},{8,9},{9,8},{10,11... | collective-permute-start | bytes 3538952 | tf_op jit(solution)/shard_map/ppermute | solution.py:41
  63.3 11.8 %collective-permute-start.18 = (bf16[2,128,1024]{2,1,0:T(8,128)(2,1)}, bf16[2,128,1024]{2,1,0:T(8,128)(2,1)S(1)}, u32[]{:S(2)}, u32[]{:S(2)}) collective-permute-start(bf16[2,128,1024]{2,1,0:T(8,128)(2,1)} %pad_maximum_fusion.1), channel_id=1, source_target_pairs={{0,1},{1,0},{2,3},{3,2},{4,5},{5,4},{6,7},{7,6},{8,9},{9,8},{10,11... | collective-permute-start | bytes 1572872 | tf_op jit(solution)/shard_map/ppermute | solution.py:41
  63.4 14.3 %collective-permute-start.19 = (bf16[2,128,1024]{2,1,0:T(8,128)(2,1)}, bf16[2,128,1024]{2,1,0:T(8,128)(2,1)}, u32[]{:S(2)}, u32[]{:S(2)}) collective-permute-start(bf16[2,128,1024]{2,1,0:T(8,128)(2,1)} %collective-permute-done.11.refs_9_), channel_id=1, source_target_pairs={{33,0},{32,1},{65,32},{64,33},{97,64},{96,65},{129,96},{128,97},{1... | collective-permute-start | bytes 1572872 | tf_op jit(solution)/shard_map/ppermute | solution.py:57
  97.4 21.1 %collective-permute-start.21 = (bf16[3,128,1024]{2,1,0:T(8,128)(2,1)}, bf16[3,128,1024]{2,1,0:T(8,128)(2,1)S(1)}, u32[]{:S(2)}, u32[]{:S(2)}) collective-permute-start(bf16[3,128,1024]{2,1,0:T(8,128)(2,1)} %get-tuple-element.133), channel_id=1, source_target_pairs={{1,32},{0,33},{33,64},{32,65},{65,96},{64,97},{97,128},{96,129},{1... | collective-permute-start | bytes 2359304 | tf_op jit(solution)/shard_map/ppermute | solution.py:61
  97.5 21.2 %collective-permute-start.22 = (bf16[3,128,1024]{2,1,0:T(8,128)(2,1)}, bf16[3,128,1024]{2,1,0:T(8,128)(2,1)S(1)}, u32[]{:S(2)}, u32[]{:S(2)}) collective-permute-start(bf16[3,128,1024]{2,1,0:T(8,128)(2,1)} %get-tuple-element.134), channel_id=1, source_target_pairs={{33,0},{32,1},{65,32},{64,33},{97,64},{96,65},{129,96},{128,97},{1... | collective-permute-start | bytes 2359304 | tf_op jit(solution)/shard_map/ppermute | solution.py:57
  100.7 14.0 %collective-permute-start.23 = (bf16[2,128,1024]{2,1,0:T(8,128)(2,1)}, bf16[2,128,1024]{2,1,0:T(8,128)(2,1)S(1)}, u32[]{:S(2)}, u32[]{:S(2)}) collective-permute-start(bf16[2,128,1024]{2,1,0:T(8,128)(2,1)} %get-tuple-element.135), channel_id=1, source_target_pairs={{1,16},{0,17},{17,0},{16,1},{3,18},{2,19},{19,2},{18,3},{5,20},{4,... | collective-permute-start | bytes 1572872 | tf_op jit(solution)/shard_map/ppermute | solution.py:65
  125.0 32.3 %all-to-all-start = ((bf16[8,128,1024]{2,1,0:T(8,128)(2,1)}), bf16[8,128,1024]{2,1,0:T(8,128)(2,1)S(1)}, u32[]{:S(2)}, u32[]{:S(2)}) async-start(bf16[8,128,1024]{2,1,0:T(8,128)(2,1)} %shard_map.133), calls=%async_computation | async-start | bytes 4194304 | tf_op jit(solution)/shard_map/all_to_all | solution.py:501
  174.3 19.0 %all-to-all-start.2 = ((bf16[16,16,1024]{2,1,0:T(8,128)(2,1)}), bf16[16,16,1024]{2,1,0:T(8,128)(2,1)S(1)}, u32[]{:S(2)}, u32[]{:S(2)}) async-start(bf16[16,16,1024]{2,1,0:T(8,128)(2,1)} %broadcast_in_dim.2), calls=%async_computation.2 | async-start | bytes 1048576 | tf_op jit(solution)/shard_map/all_to_all | solution.py:510
  (21 other events, 218.4 us)

commit v6 on v5

--- a/solution.py
+++ b/solution.py
@@ -12,7 +12,7 @@
 PATCHES = 144
 EPS = 1e-06
 AXES = ("z", "xlo", "y", "xhi", "core")
-VMEM_LIMIT = 60 * 1024 * 1024
+VMEM_LIMIT = 32 * 1024 * 1024
 
 X_INDEX = (0, 2, 1, 3)
 CORE_SWAP = ((0, 1), (1, 0))

time: 201 us -> 191 us (0.950)
  Pallas kernels: 53 us -> 31.1 us
  waiting for transfers between devices: 77.8 us -> 82.7 us
  local copies, waits for them, and re-layouts: 11.5 us -> 15.7 us
  other arithmetic: 2.78 us -> 5.61 us
    unnamed x36 -> x38, local copies, waits for them, and re-layouts: 4.66 us -> 12.1 us
    pallas_call x1, Pallas kernels: 12.2 us -> 6.93 us  [prepare_rows(): pl.pallas_call(prepare_kernel, grid_spec=pltpu.PrefetchScalarGridSpec(num...]
    pallas_call x1, Pallas kernels: 7.91 us -> 3.98 us  [late_forward(): pl.pallas_call(late_kernel, grid_spec=pltpu.PrefetchScalarGridSpec(num_sc...]
    pallas_call x1, Pallas kernels: 5.56 us -> 2.78 us  [keep_grads(): pl.pallas_call(keep_kernel, grid=(columns // width,), in_specs=[pl.BlockS...]
    pallas_call x1, Pallas kernels: 9.78 us -> 7.04 us  [early_forward(): pl.pallas_call(early_kernel, grid=(columns // width,), in_specs=[whole, w...]
    pallas_call x1, Pallas kernels: 7.75 us -> 5.12 us  [send_grads(): pl.pallas_call(functools.partial(send_kernel, total_tokens), grid_spec=pl...]
    ppermute x2, waiting for transfers between devices: 8.42 us -> 11 us  [from_x_twin(): return lax.ppermute(value, ('xlo', 'core'), with_core_flip(CORE_SWAP))]
    ppermute x4, waiting for transfers between devices: 4.76 us -> 7.16 us  [from_z_next(): return lax.ppermute(value, ('z', 'core'), with_core_flip(from_next(8)))]
  transfers between devices with their start and end apart: 27 -> 27, of which waited for: 16 -> 14; matrix products, arithmetic and copies ran while one was open for 3% -> 3% of each run, Pallas kernels for 14% -> 9%
where the time goes in v6:
time: 191 us; the launch traced here: 190 us
  waiting for transfers between devices  82.7 us (43%)
  starting transfers between devices  37.9 us (20%)
  Pallas kernels  31.1 us (16%)
  blocking collectives  16.3 us (9%)
  local copies, waits for them, and re-layouts  15.7 us (8%)
  other arithmetic  5.61 us (3%)
    all_to_all x1, waiting for transfers between devices, shards(): lax.all_to_all(add_passed(kept, passed), ('xlo', 'y', 'xhi'), 0, 0, axis_...  21.8 us
    all_to_all x1, blocking collectives, shards(): lax.all_to_all(total.reshape(8, 16, half), ('z', 'xlo'), 0, 0, axis_index...  16.3 us
    all_to_all x1, waiting for transfers between devices, shards(): lax.all_to_all(jnp.broadcast_to(copy_rows[None], (16, 16, half)), ('z', '...  16 us
    unnamed x38, local copies, waits for them, and re-layouts  12.1 us
    ppermute x2, waiting for transfers between devices, from_x_twin(): return lax.ppermute(value, ('xlo', 'core'), with_core_flip(CORE_SWAP))  11 us
    ppermute x3, waiting for transfers between devices, from_x_near(): return lax.ppermute(value, ('xlo', 'xhi'), X_NEAR)  10.1 us
    ppermute x4, starting transfers between devices, from_z_next(): return lax.ppermute(value, ('z', 'core'), with_core_flip(from_next(8)))  9.35 us
    ppermute x4, waiting for transfers between devices, from_z_next(): return lax.ppermute(value, ('z', 'core'), with_core_flip(from_next(8)))  7.16 us
  transfers between devices with their start and end apart: 27, of which 14 were waited for; matrix products, arithmetic and copies ran while one was open for 3% of the time, Pallas kernels for 9%

profile of v6, /device:TPU:4, one launch (start us, length us, event | category | flops | bytes accessed | tf_op | source)
XLA Modules:
  0.0 190.2 jit_solution(17839036066659217558)
XLA Ops:
  8.4 8.4 %collective-permute-done.2.refs_3_ = bf16[2,128,1024]{2,1,0:T(8,128)(2,1)} collective-permute-done((bf16[2,128,1024]{2,1,0:T(8,128)(2,1)S(1)}, bf16[2,128,1024]{2,1,0:T(8,128)(2,1)}, u32[]{:S(2)}, u32[]{:S(2)}) %collective-permute-start.2) | collective-permute-done | bytes 524320 | tf_op jit(solution)/shard_map/ppermute | solution.py:53
  21.0 3.8 %collective-permute-start.9 = (bf16[2,128,1024]{2,1,0:T(8,128)(2,1)}, bf16[2,128,1024]{2,1,0:T(8,128)(2,1)}, u32[]{:S(2)}, u32[]{:S(2)}) collective-permute-start(bf16[2,128,1024]{2,1,0:T(8,128)(2,1)} %collective-permute-done.refs_1_), channel_id=1, source_target_pairs={{33,0},{32,1},{65,32},{64,33},{97,64},{96,65},{129,96},{128,97},{1... | collective-permute-start | bytes 1572872 | tf_op jit(solution)/shard_map/ppermute | solution.py:57
  26.3 2.0 %collective-permute-start.6 = (bf16[2,128,1024]{2,1,0:T(8,128)(2,1)}, bf16[2,128,1024]{2,1,0:T(8,128)(2,1)}, u32[]{:S(2)}, u32[]{:S(2)}) collective-permute-start(bf16[2,128,1024]{2,1,0:T(8,128)(2,1)} %collective-permute-done.refs_1_), channel_id=1, source_target_pairs={{4,0},{8,4},{12,8},{0,12},{5,1},{9,5},{13,9},{1,13},{6,2},{10,6},{... | collective-permute-start | bytes 1572872 | tf_op jit(solution)/shard_map/ppermute | solution.py:45
  29.4 4.3 %collective-permute-done.7.refs_5_ = bf16[2,128,1024]{2,1,0:T(8,128)(2,1)} collective-permute-done((bf16[2,128,1024]{2,1,0:T(8,128)(2,1)}, bf16[2,128,1024]{2,1,0:T(8,128)(2,1)}, u32[]{:S(2)}, u32[]{:S(2)}) %collective-permute-start.7) | collective-permute-done | bytes 524320 | tf_op jit(solution)/shard_map/ppermute | solution.py:49
  41.9 4.8 %collective-permute-start.15 = (bf16[2,128,1024]{2,1,0:T(8,128)(2,1)}, bf16[2,128,1024]{2,1,0:T(8,128)(2,1)}, u32[]{:S(2)}, u32[]{:S(2)}) collective-permute-start(bf16[2,128,1024]{2,1,0:T(8,128)(2,1)} %collective-permute-done.2.refs_3_), channel_id=1, source_target_pairs={{1,16},{0,17},{17,0},{16,1},{3,18},{2,19},{19,2},{18,3},{5,20},{4,... | collective-permute-start | bytes 1572872 | tf_op jit(solution)/shard_map/ppermute | solution.py:65
  46.7 2.6 %collective-permute-start.11 = (bf16[2,128,1024]{2,1,0:T(8,128)(2,1)}, bf16[2,128,1024]{2,1,0:T(8,128)(2,1)}, u32[]{:S(2)}, u32[]{:S(2)}) collective-permute-start(bf16[2,128,1024]{2,1,0:T(8,128)(2,1)} %collective-permute-done.8.refs_6_), channel_id=1, source_target_pairs={{4,0},{8,4},{12,8},{0,12},{5,1},{9,5},{13,9},{1,13},{6,2},{10,6},{... | collective-permute-start | bytes 1572872 | tf_op jit(solution)/shard_map/ppermute | solution.py:45
  56.4 6.9 %shard_map.128 = (bf16[576,1792]{1,0:T(8,128)(2,1)S(1)}, bf16[576,1792]{1,0:T(8,128)(2,1)S(1)}, bf16[576,256]{1,0:T(8,128)(2,1)S(1)}, bf16[576,256]{1,0:T(8,128)...) custom-call(s32[18]{0:T(128)S(1)} %stack.99.order, ...), custom_call_target="tpu_custom_call" | custom-call | flops 679477248 | bytes 16777216 | tf_op jit(solution)/shard_map/pallas_call | solution.py:126
  66.0 7.0 %shard_map.129 = (f32[576,1024]{1,0:T(8,128)S(1)}, f32[576,1024]{1,0:T(8,128)S(1)}) custom-call(bf16[576,1792]{1,0:T(8,128)(2,1)S(1)} %get-tuple-element.113.student_mix, bf16[576,1792]{1,0:T(8,128)(2,1)S(1)} %get-tuple-element.114.teacher_mix, bf16[2,128,1024]{2,1,0:T(8,128)(2,1)S(1)} %copy-done.13, bf16[2,128,1024]{2,1,0:T(8,128)(2,1)} %collective-permute-done.refs_1_, ...), custom_call_target="tpu_custom_call" | custom-call | flops 4227858432 | bytes 17825792 | tf_op jit(solution)/shard_map/pallas_call | solution.py:170
  73.0 5.3 %collective-permute-done.19.refs_1_ = bf16[2,128,1024]{2,1,0:T(8,128)(2,1)S(1)} collective-permute-done((bf16[2,128,1024]{2,1,0:T(8,128)(2,1)}, bf16[2,128,1024]{2,1,0:T(8,128)(2,1)S(1)}, u32[]{:S(2)}, u32[]{:S(2)}) %collective-permute-start.19) | collective-permute-done | bytes 524320 | tf_op jit(solution)/shard_map/ppermute | solution.py:57
  78.3 4.0 %shard_map.130 = (f32[576,1024]{1,0:T(8,128)S(1)}, f32[576,1024]{1,0:T(8,128)S(1)}, f32[576,128]{1,0:T(8,128)S(1)}) custom-call(s32[18]{0:T(128)S(1)} %stack.99.order, bf16[576,256]{1,0:T(8,128)(2,1)S(1)} %get-tuple-element.111.student_mix, bf16[576,256]{1,0:T(8,128)(2,1)S(1)} %get-tuple-element.112.teacher_mix, ...), custom_call_target="tpu_custom_call" | custom-call | flops 603979776 | bytes 13631488 | tf_op jit(solution)/shard_map/pallas_call | solution.py:226
  84.0 5.1 %shard_map.131 = (bf16[3,128,1024]{2,1,0:T(8,128)(2,1)S(1)}, bf16[3,128,1024]{2,1,0:T(8,128)(2,1)S(1)}, bf16[2,128,1024]{2,1,0:T(8,128)(2,1)S(1)}, bf16[576,1024...) custom-call(s32[18]{0:T(128)S(1)} %stack.99.order, ...), custom_call_target="tpu_custom_call" | custom-call | flops 1207959552 | bytes 12582912 | tf_op jit(solution)/shard_map/pallas_call | solution.py:294
  89.9 3.0 %collective-permute-start.22 = (bf16[3,128,1024]{2,1,0:T(8,128)(2,1)S(1)}, bf16[3,128,1024]{2,1,0:T(8,128)(2,1)S(1)}, u32[]{:S(2)}, u32[]{:S(2)}) collective-permute-start(bf16[3,128,1024]{2,1,0:T(8,128)(2,1)S(1)} %get-tuple-element.134), channel_id=1, source_target_pairs={{33,0},{32,1},{65,32},{64,33},{97,64},{96,65},{129,96},{128,97},{1... | collective-permute-start | bytes 2359304 | tf_op jit(solution)/shard_map/ppermute | solution.py:57
  93.0 2.8 %shard_map.132.kept = f32[8,128,1024]{2,1,0:T(8,128)S(1)} custom-call(bf16[576,1024]{1,0:T(8,128)(2,1)S(1)} %get-tuple-element.131.held, bf16[8,128,576]{2,1,0:T(8,128)(2,1)S(1)} %get-tuple-element.132.mix), custom_call_target="tpu_custom_call" | custom-call | flops 1207959552 | bytes 7340032 | tf_op jit(solution)/shard_map/pallas_call | solution.py:333
  95.8 11.0 %collective-permute-done.23.refs_2_ = bf16[2,128,1024]{2,1,0:T(8,128)(2,1)S(1)} collective-permute-done((bf16[2,128,1024]{2,1,0:T(8,128)(2,1)S(1)}, bf16[2,128,1024]{2,1,0:T(8,128)(2,1)S(1)}, u32[]{:S(2)}, u32[]{:S(2)}) %collective-permute-start.23) | collective-permute-done | bytes 524320 | tf_op jit(solution)/shard_map/ppermute | solution.py:65
  106.7 3.8 %collective-permute-done.21.refs_0_ = bf16[3,128,1024]{2,1,0:T(8,128)(2,1)S(1)} collective-permute-done((bf16[3,128,1024]{2,1,0:T(8,128)(2,1)S(1)}, bf16[3,128,1024]{2,1,0:T(8,128)(2,1)S(1)}, u32[]{:S(2)}, u32[]{:S(2)}) %collective-permute-start.21) | collective-permute-done | bytes 786464 | tf_op jit(solution)/shard_map/ppermute | solution.py:61
  110.6 2.5 %shard_map.133 = bf16[8,128,1024]{2,1,0:T(8,128)(2,1)} custom-call(f32[8,128,1024]{2,1,0:T(8,128)S(1)} %shard_map.132.kept, bf16[3,128,1024]{2,1,0:T(8,128)(2,1)S(1)} %collective-permute-done.21.refs_0_, bf16[3,128,1024]{2,1,0:T(8,128)(2,1)S(1)} %collective-permute-done.22.refs_1_, bf16[2,128,1024]{2,1,0:T(8,128)(2,1)S(1)} %collective-permute-done.23.refs_2_), custom_call_target="tpu_custom_call" | custom-call | tf_op jit(solution)/shard_map/pallas_call | solution.py:364
  113.1 6.5 %all-to-all-start = ((bf16[8,128,1024]{2,1,0:T(8,128)(2,1)}), bf16[8,128,1024]{2,1,0:T(8,128)(2,1)}, u32[]{:S(2)}, u32[]{:S(2)}) async-start(bf16[8,128,1024]{2,1,0:T(8,128)(2,1)} %shard_map.133), calls=%async_computation | async-start | bytes 4194304 | tf_op jit(solution)/shard_map/all_to_all | solution.py:501
  119.6 2.1 %collective-permute-done.24 = bf16[288,1024]{1,0:T(8,128)(2,1)} collective-permute-done((bf16[288,1024]{1,0:T(8,128)(2,1)S(1)}, bf16[288,1024]{1,0:T(8,128)(2,1)}, u32[]{:S(2)}, u32[]{:S(2)}) %collective-permute-start.24) | collective-permute-done | bytes 589856 | tf_op jit(solution)/shard_map/ppermute | solution.py:41
  121.8 2.7 %maximum_select_fusion = bf16[288,2048]{1,0:T(8,128)(2,1)} fusion(bf16[288,1024]{1,0:T(8,128)(2,1)} %collective-permute-done.24, bf16[288,1024]{1,0:T(8,128)(2,1)S(1)} %get-tuple-element.139, pred[]{:T(512)S(6)} %eq.3), kind=kLoop, calls=%fused_computation | loop fusion | flops 5308416 | bytes 2359297 | tf_op jit(solution)/shard_map/jit(_where)/select_n | solution.py:408
  124.5 21.8 %all-to-all-done = bf16[8,128,1024]{2,1,0:T(8,128)(2,1)} async-done(((bf16[8,128,1024]{2,1,0:T(8,128)(2,1)}), bf16[8,128,1024]{2,1,0:T(8,128)(2,1)}, u32[]{:S(2)}, u32[]{:S(2)}) %all-to-all-start) | async-done | bytes 2097184 | tf_op jit(solution)/shard_map/all_to_all | solution.py:501
  148.2 16.3 %all_to_all.15 = bf16[8,16,1024]{2,1,0:T(8,128)(2,1)S(1)} all-to-all(bf16[8,16,1024]{2,1,0:T(8,128)(2,1)S(1)} %bitcast.33), channel_id=1, replica_groups={{0,48,64,112,128,176,192,240},{16,32,80,96,144,160,208,224},{1,49,65,11..., dimensions={0} | all-to-all | bytes 524288 | tf_op jit(solution)/shard_map/all_to_all | solution.py:506
  165.4 3.6 %all-to-all-start.2 = ((bf16[16,16,1024]{2,1,0:T(8,128)(2,1)}), bf16[16,16,1024]{2,1,0:T(8,128)(2,1)S(1)}, u32[]{:S(2)}, u32[]{:S(2)}) async-start(bf16[16,16,1024]{2,1,0:T(8,128)(2,1)} %broadcast_in_dim.2), calls=%async_computation.2 | async-start | bytes 1048576 | tf_op jit(solution)/shard_map/all_to_all | solution.py:510
  169.0 16.0 %all-to-all-done.2 = bf16[16,16,1024]{2,1,0:T(8,128)(2,1)S(1)} async-done(((bf16[16,16,1024]{2,1,0:T(8,128)(2,1)}), bf16[16,16,1024]{2,1,0:T(8,128)(2,1)S(1)}, u32[]{:S(2)}, u32[]{:S(2)}) %all-to-all-start.2) | async-done | bytes 524320 | tf_op jit(solution)/shard_map/all_to_all | solution.py:510
  187.4 2.7 %shard_map.134 = (f32[128,2048]{1,0:T(8,128)}, f32[128,2048]{1,0:T(8,128)}, f32[128,2048]{1,0:T(8,128)}, f32[128,2048]{1,0:T(8,128)}) custom-call(s32[1]{0:T(128)} %bitcast.flip, bf16[8,2,16,1024]{3,2,1,0:T(8,128)(2,1)S(1)} %bitcast.30, f32[128,2048]{1,0:T(8,128)S(1)} %copy-done.1, f32[128,2048]{1,0:T(8,128)S(1)} %copy-done.2, f32[128,2048]{1,0:T(8,128)S(1)} %copy-done.9, ...), custom_call_target="tpu_custom_call" | custom-call | tf_op jit(solution)/shard_map/pallas_call | solution.py:394
  (90 shorter events, 40.0 us)
Async XLA Ops:
  2.3 16.1 %collective-permute-start.4 = (bf16[288,2048]{1,0:T(8,128)(2,1)}, bf16[288,2048]{1,0:T(8,128)(2,1)S(1)}, u32[]{:S(2)}, u32[]{:S(2)}) collective-permute-start(bf16[288,2048]{1,0:T(8,128)(2,1)} %teacher_own.1), channel_id=1, source_target_pairs={{0,1},{1,0},{2,3},{3,2},{4,5},{5,4},{6,7},{7,6},{8,9},{9,8},{10,11... | collective-permute-start | bytes 3538952 | tf_op jit(solution)/shard_map/ppermute | solution.py:41
  2.8 14.0 %collective-permute-start.2 = (bf16[2,128,1024]{2,1,0:T(8,128)(2,1)S(1)}, bf16[2,128,1024]{2,1,0:T(8,128)(2,1)}, u32[]{:S(2)}, u32[]{:S(2)}) collective-permute-start(bf16[2,128,1024]{2,1,0:T(8,128)(2,1)S(1)} %pad_maximum_fusion.refs_0_), channel_id=1, source_target_pairs={{16,2},{2,16},{0,18},{18,0},{17,3},{3,17},{1,19},{19,1},{20,6},{6,... | collective-permute-start | bytes 1572872 | tf_op jit(solution)/shard_map/ppermute | solution.py:53
  3.3 15.0 %collective-permute-start.1 = (bf16[2,128,1024]{2,1,0:T(8,128)(2,1)S(1)}, bf16[2,128,1024]{2,1,0:T(8,128)(2,1)}, u32[]{:S(2)}, u32[]{:S(2)}) collective-permute-start(bf16[2,128,1024]{2,1,0:T(8,128)(2,1)S(1)} %pad_maximum_fusion.refs_0_), channel_id=1, source_target_pairs={{0,4},{4,8},{8,12},{12,0},{1,5},{5,9},{9,13},{13,1},{2,6},{6,10},{... | collective-permute-start | bytes 1572872 | tf_op jit(solution)/shard_map/ppermute | solution.py:49
  4.9 13.5 %collective-permute-start = (bf16[2,128,1024]{2,1,0:T(8,128)(2,1)S(1)}, bf16[2,128,1024]{2,1,0:T(8,128)(2,1)}, u32[]{:S(2)}, u32[]{:S(2)}) collective-permute-start(bf16[2,128,1024]{2,1,0:T(8,128)(2,1)S(1)} %pad_maximum_fusion.refs_0_), channel_id=1, source_target_pairs={{4,0},{8,4},{12,8},{0,12},{5,1},{9,5},{13,9},{1,13},{6,2},{10,6},{... | collective-permute-start | bytes 1572872 | tf_op jit(solution)/shard_map/ppermute | solution.py:45
  8.4 11.1 %collective-permute-start.5 = (s32[2,144]{1,0:T(2,128)S(1)}, s32[2,144]{1,0:T(2,128)S(1)}, u32[]{:S(2)}, u32[]{:S(2)}) collective-permute-start(s32[2,144]{1,0:T(2,128)S(1)} %copy-done.18), channel_id=1, source_target_pairs={{0,1},{1,0},{2,3},{3,2},{4,5},{5,4},{6,7},{7,6},{8,9},{9,8},{10,11... | collective-permute-start | bytes 3464 | tf_op jit(solution)/shard_map/ppermute | solution.py:41
  19.4 14.3 %collective-permute-start.7 = (bf16[2,128,1024]{2,1,0:T(8,128)(2,1)}, bf16[2,128,1024]{2,1,0:T(8,128)(2,1)}, u32[]{:S(2)}, u32[]{:S(2)}) collective-permute-start(bf16[2,128,1024]{2,1,0:T(8,128)(2,1)} %collective-permute-done.2.refs_3_), channel_id=1, source_target_pairs={{0,4},{4,8},{8,12},{12,0},{1,5},{5,9},{9,13},{13,1},{2,6},{6,10},{... | collective-permute-start | bytes 1572872 | tf_op jit(solution)/shard_map/ppermute | solution.py:49
  21.0 14.2 %collective-permute-start.10 = (bf16[2,128,1024]{2,1,0:T(8,128)(2,1)}, bf16[2,128,1024]{2,1,0:T(8,128)(2,1)}, u32[]{:S(2)}, u32[]{:S(2)}) collective-permute-start(bf16[2,128,1024]{2,1,0:T(8,128)(2,1)} %collective-permute-done.1.refs_2_), channel_id=1, source_target_pairs={{1,32},{0,33},{33,64},{32,65},{65,96},{64,97},{97,128},{96,129},{1... | collective-permute-start | bytes 1572872 | tf_op jit(solution)/shard_map/ppermute | solution.py:61
  21.0 16.0 %collective-permute-start.9 = (bf16[2,128,1024]{2,1,0:T(8,128)(2,1)}, bf16[2,128,1024]{2,1,0:T(8,128)(2,1)}, u32[]{:S(2)}, u32[]{:S(2)}) collective-permute-start(bf16[2,128,1024]{2,1,0:T(8,128)(2,1)} %collective-permute-done.refs_1_), channel_id=1, source_target_pairs={{33,0},{32,1},{65,32},{64,33},{97,64},{96,65},{129,96},{128,97},{1... | collective-permute-start | bytes 1572872 | tf_op jit(solution)/shard_map/ppermute | solution.py:57
  24.8 13.9 %collective-permute-start.8 = (bf16[2,128,1024]{2,1,0:T(8,128)(2,1)}, bf16[2,128,1024]{2,1,0:T(8,128)(2,1)}, u32[]{:S(2)}, u32[]{:S(2)}) collective-permute-start(bf16[2,128,1024]{2,1,0:T(8,128)(2,1)} %collective-permute-done.refs_1_), channel_id=1, source_target_pairs={{16,2},{2,16},{0,18},{18,0},{17,3},{3,17},{1,19},{19,1},{20,6},{6,... | collective-permute-start | bytes 1572872 | tf_op jit(solution)/shard_map/ppermute | solution.py:53
  26.3 14.2 %collective-permute-start.6 = (bf16[2,128,1024]{2,1,0:T(8,128)(2,1)}, bf16[2,128,1024]{2,1,0:T(8,128)(2,1)}, u32[]{:S(2)}, u32[]{:S(2)}) collective-permute-start(bf16[2,128,1024]{2,1,0:T(8,128)(2,1)} %collective-permute-done.refs_1_), channel_id=1, source_target_pairs={{4,0},{8,4},{12,8},{0,12},{5,1},{9,5},{13,9},{1,13},{6,2},{10,6},{... | collective-permute-start | bytes 1572872 | tf_op jit(solution)/shard_map/ppermute | solution.py:45
  40.5 22.8 %collective-permute-start.12 = (bf16[2,128,1024]{2,1,0:T(8,128)(2,1)}, bf16[2,128,1024]{2,1,0:T(8,128)(2,1)}, u32[]{:S(2)}, u32[]{:S(2)}) collective-permute-start(bf16[2,128,1024]{2,1,0:T(8,128)(2,1)} %collective-permute-done.6.refs_4_), channel_id=1, source_target_pairs={{33,0},{32,1},{65,32},{64,33},{97,64},{96,65},{129,96},{128,97},{1... | collective-permute-start | bytes 1572872 | tf_op jit(solution)/shard_map/ppermute | solution.py:57
  41.1 22.2 %collective-permute-start.14 = (bf16[2,128,1024]{2,1,0:T(8,128)(2,1)}, bf16[2,128,1024]{2,1,0:T(8,128)(2,1)}, u32[]{:S(2)}, u32[]{:S(2)}) collective-permute-start(bf16[2,128,1024]{2,1,0:T(8,128)(2,1)} %collective-permute-done.10.refs_8_), channel_id=1, source_target_pairs={{16,2},{2,16},{0,18},{18,0},{17,3},{3,17},{1,19},{19,1},{20,6},{6,... | collective-permute-start | bytes 1572872 | tf_op jit(solution)/shard_map/ppermute | solution.py:53
  41.9 21.5 %collective-permute-start.15 = (bf16[2,128,1024]{2,1,0:T(8,128)(2,1)}, bf16[2,128,1024]{2,1,0:T(8,128)(2,1)}, u32[]{:S(2)}, u32[]{:S(2)}) collective-permute-start(bf16[2,128,1024]{2,1,0:T(8,128)(2,1)} %collective-permute-done.2.refs_3_), channel_id=1, source_target_pairs={{1,16},{0,17},{17,0},{16,1},{3,18},{2,19},{19,2},{18,3},{5,20},{4,... | collective-permute-start | bytes 1572872 | tf_op jit(solution)/shard_map/ppermute | solution.py:65
  46.7 16.7 %collective-permute-start.13 = (bf16[2,128,1024]{2,1,0:T(8,128)(2,1)}, bf16[2,128,1024]{2,1,0:T(8,128)(2,1)}, u32[]{:S(2)}, u32[]{:S(2)}) collective-permute-start(bf16[2,128,1024]{2,1,0:T(8,128)(2,1)} %collective-permute-done.8.refs_6_), channel_id=1, source_target_pairs={{1,32},{0,33},{33,64},{32,65},{65,96},{64,97},{97,128},{96,129},{1... | collective-permute-start | bytes 1572872 | tf_op jit(solution)/shard_map/ppermute | solution.py:61
  46.7 16.7 %collective-permute-start.11 = (bf16[2,128,1024]{2,1,0:T(8,128)(2,1)}, bf16[2,128,1024]{2,1,0:T(8,128)(2,1)}, u32[]{:S(2)}, u32[]{:S(2)}) collective-permute-start(bf16[2,128,1024]{2,1,0:T(8,128)(2,1)} %collective-permute-done.8.refs_6_), channel_id=1, source_target_pairs={{4,0},{8,4},{12,8},{0,12},{5,1},{9,5},{13,9},{1,13},{6,2},{10,6},{... | collective-permute-start | bytes 1572872 | tf_op jit(solution)/shard_map/ppermute | solution.py:45
  63.4 15.0 %collective-permute-start.16 = (bf16[288,2048]{1,0:T(8,128)(2,1)S(1)}, bf16[288,2048]{1,0:T(8,128)(2,1)S(1)}, u32[]{:S(2)}, u32[]{:S(2)}) collective-permute-start(bf16[288,2048]{1,0:T(8,128)(2,1)S(1)} %copy-done), channel_id=1, source_target_pairs={{0,1},{1,0},{2,3},{3,2},{4,5},{5,4},{6,7},{7,6},{8,9},{9,8},{10,11... | collective-permute-start | bytes 3538952 | tf_op jit(solution)/shard_map/ppermute | solution.py:41
  63.5 14.9 %collective-permute-start.17 = (bf16[288,2048]{1,0:T(8,128)(2,1)S(1)}, bf16[288,2048]{1,0:T(8,128)(2,1)S(1)}, u32[]{:S(2)}, u32[]{:S(2)}) collective-permute-start(bf16[288,2048]{1,0:T(8,128)(2,1)S(1)} %get-tuple-element.125.picked_own), channel_id=1, source_target_pairs={{0,1},{1,0},{2,3},{3,2},{4,5},{5,4},{6,7},{7,6},{8,9},{9,8},{10,11... | collective-permute-start | bytes 3538952 | tf_op jit(solution)/shard_map/ppermute | solution.py:41
  64.0 9.0 %collective-permute-start.18 = (bf16[2,128,1024]{2,1,0:T(8,128)(2,1)S(1)}, bf16[2,128,1024]{2,1,0:T(8,128)(2,1)S(1)}, u32[]{:S(2)}, u32[]{:S(2)}) collective-permute-start(bf16[2,128,1024]{2,1,0:T(8,128)(2,1)S(1)} %copy-done.17), channel_id=1, source_target_pairs={{0,1},{1,0},{2,3},{3,2},{4,5},{5,4},{6,7},{7,6},{8,9},{9,8},{10,11... | collective-permute-start | bytes 1572872 | tf_op jit(solution)/shard_map/ppermute | solution.py:41
  64.1 14.3 %collective-permute-start.19 = (bf16[2,128,1024]{2,1,0:T(8,128)(2,1)}, bf16[2,128,1024]{2,1,0:T(8,128)(2,1)S(1)}, u32[]{:S(2)}, u32[]{:S(2)}) collective-permute-start(bf16[2,128,1024]{2,1,0:T(8,128)(2,1)} %collective-permute-done.11.refs_9_), channel_id=1, source_target_pairs={{33,0},{32,1},{65,32},{64,33},{97,64},{96,65},{129,96},{128,97},{1... | collective-permute-start | bytes 1572872 | tf_op jit(solution)/shard_map/ppermute | solution.py:57
  89.9 20.6 %collective-permute-start.21 = (bf16[3,128,1024]{2,1,0:T(8,128)(2,1)S(1)}, bf16[3,128,1024]{2,1,0:T(8,128)(2,1)S(1)}, u32[]{:S(2)}, u32[]{:S(2)}) collective-permute-start(bf16[3,128,1024]{2,1,0:T(8,128)(2,1)S(1)} %get-tuple-element.133), channel_id=1, source_target_pairs={{1,32},{0,33},{33,64},{32,65},{65,96},{64,97},{97,128},{96,129},{1... | collective-permute-start | bytes 2359304 | tf_op jit(solution)/shard_map/ppermute | solution.py:61
  89.9 20.7 %collective-permute-start.22 = (bf16[3,128,1024]{2,1,0:T(8,128)(2,1)S(1)}, bf16[3,128,1024]{2,1,0:T(8,128)(2,1)S(1)}, u32[]{:S(2)}, u32[]{:S(2)}) collective-permute-start(bf16[3,128,1024]{2,1,0:T(8,128)(2,1)S(1)} %get-tuple-element.134), channel_id=1, source_target_pairs={{33,0},{32,1},{65,32},{64,33},{97,64},{96,65},{129,96},{128,97},{1... | collective-permute-start | bytes 2359304 | tf_op jit(solution)/shard_map/ppermute | solution.py:57
  93.0 13.8 %collective-permute-start.23 = (bf16[2,128,1024]{2,1,0:T(8,128)(2,1)S(1)}, bf16[2,128,1024]{2,1,0:T(8,128)(2,1)S(1)}, u32[]{:S(2)}, u32[]{:S(2)}) collective-permute-start(bf16[2,128,1024]{2,1,0:T(8,128)(2,1)S(1)} %get-tuple-element.135), channel_id=1, source_target_pairs={{1,16},{0,17},{17,0},{16,1},{3,18},{2,19},{19,2},{18,3},{5,20},{4,... | collective-permute-start | bytes 1572872 | tf_op jit(solution)/shard_map/ppermute | solution.py:65
  113.1 33.2 %all-to-all-start = ((bf16[8,128,1024]{2,1,0:T(8,128)(2,1)}), bf16[8,128,1024]{2,1,0:T(8,128)(2,1)}, u32[]{:S(2)}, u32[]{:S(2)}) async-start(bf16[8,128,1024]{2,1,0:T(8,128)(2,1)} %shard_map.133), calls=%async_computation | async-start | bytes 4194304 | tf_op jit(solution)/shard_map/all_to_all | solution.py:501
  165.4 19.5 %all-to-all-start.2 = ((bf16[16,16,1024]{2,1,0:T(8,128)(2,1)}), bf16[16,16,1024]{2,1,0:T(8,128)(2,1)S(1)}, u32[]{:S(2)}, u32[]{:S(2)}) async-start(bf16[16,16,1024]{2,1,0:T(8,128)(2,1)} %broadcast_in_dim.2), calls=%async_computation.2 | async-start | bytes 1048576 | tf_op jit(solution)/shard_map/all_to_all | solution.py:510
  (22 other events, 171.4 us)

commit v7 on v6

--- a/solution.py
+++ b/solution.py
@@ -74,82 +74,121 @@
 HALF_AT = len(ORDER)
 CORE_AT = HALF_AT + 1
 SENT = (3, 3, 2)
-
-
-def prepare_kernel(
-    order, student_own, student_other, teacher_own, teacher_other, residual, places_own, places_other, student_early,
-    teacher_early, student_late, teacher_late, picked_out, sent_out, kept_out, turned, packed, gathered
-):
-    own, step = student_own.shape[0], pl.program_id(0)
-    lane = lax.broadcasted_iota(jnp.int32, (PATCHES, PATCHES), 1)
-    for side, (teacher, places) in enumerate(((teacher_own, places_own), (teacher_other, places_other))):
-        for crop in range(own // PATCHES):
-            rows = slice(crop * PATCHES, (crop + 1) * PATCHES)
-            out_rows = slice(side * own + crop * PATCHES, side * own + (crop + 1) * PATCHES)
-            pick = (places[rows, :] == lane).astype(jnp.float32).astype(jnp.bfloat16)
-            gathered[out_rows, :] = jnp.dot(
-                pick, teacher[rows, :], preferred_element_type=jnp.float32
-            ).astype(jnp.bfloat16)
-            if side == 0:
-                picked_out[rows, :] = jnp.dot(
-                    pick, residual[rows, :], preferred_element_type=jnp.float32
-                ).astype(jnp.bfloat16)
-    packed[:own, :] = student_own[...]
-    packed[own:, :] = student_other[...]
-    turned[...] = packed[...].T
-    core = order[CORE_AT]
-    kept_out[0] = turned[pl.ds(pl.multiple_of(core * 128, 128), 128), :]
-    sent_out[0] = turned[pl.ds(pl.multiple_of((1 - core) * 128, 128), 128), :]
+PARTS = 2
+
+
+def place_blocks(order, step, packed, early, late):
     for part in range(2):
         columns = slice(part * 128, (part + 1) * 128)
         for block in range(len(ORDER)):
             @pl.when(order[block] == 2 * step + part)
             def _():
-                at = block if block < EARLY else block - EARLY
-                spot = slice(at * 128, (at + 1) * 128)
                 if block < EARLY:
-                    student_early[:, spot] = packed[:, columns]
-                    teacher_early[:, spot] = gathered[:, columns]
+                    early[:, block * 128 : (block + 1) * 128] = packed[:, columns]
                 else:
-                    student_late[:, spot] = packed[:, columns]
-                    teacher_late[:, spot] = gathered[:, columns]
-
-
-def prepare_rows(order, student_own, student_other, teacher_own, teacher_other, residual, places, places_other):
-    own, steps = student_own.shape[0], 8
+                    late[:, (block - EARLY) * 128 : (block - EARLY + 1) * 128] = packed[:, columns]
+
+
+def student_kernel(order, mix_own, mix_other, early, late, sent_out, kept_out, turned, packed):
+    own = mix_own.shape[0]
+    packed[:own, :] = mix_own[...]
+    packed[own:, :] = mix_other[...]
+    turned[...] = packed[...].T
+    core = order[CORE_AT]
+    kept_out[0] = turned[pl.ds(pl.multiple_of(core * 128, 128), 128), :]
+    sent_out[0] = turned[pl.ds(pl.multiple_of((1 - core) * 128, 128), 128), :]
+    place_blocks(order, pl.program_id(0), packed, early, late)
+
+
+def teacher_kernel(
+    order, mix_own, mix_other, residual, places_own, places_other, early, late, picked_out, packed, picks
+):
+    own, step = mix_own.shape[0], pl.program_id(0)
+    crops = own // PATCHES
+
+    @pl.when(step == 0)
+    def _():
+        lane = lax.broadcasted_iota(jnp.int32, (PATCHES, PATCHES), 1)
+        for side, places in enumerate((places_own, places_other)):
+            for crop in range(crops):
+                rows = slice(crop * PATCHES, (crop + 1) * PATCHES)
+                picks[side * crops + crop] = (places[rows, :] == lane).astype(jnp.float32).astype(jnp.bfloat16)
+
+    for side, mix in enumerate((mix_own, mix_other)):
+        for crop in range(crops):
+            rows = slice(crop * PATCHES, (crop + 1) * PATCHES)
+            at = side * crops + crop
+            packed[at * PATCHES : (at + 1) * PATCHES, :] = jnp.dot(
+                picks[at], mix[rows, :], preferred_element_type=jnp.float32
+            ).astype(jnp.bfloat16)
+            if side == 0:
+                picked_out[rows, :] = jnp.dot(
+                    picks[at], residual[rows, :], preferred_element_type=jnp.float32
+                ).astype(jnp.bfloat16)
+    place_blocks(order, step, packed, early, late)
+
+
+def prepare_student(order, mix_own, mix_other):
+    own, steps = mix_own.shape[0], 8
+    rows, width = 2 * own, KIN // steps
+    mix = pl.BlockSpec((own, width), lambda i, order: (0, i))
+    turned = pl.BlockSpec((1, 128, rows), lambda i, order: (i, 0, 0))
+    return pl.pallas_call(
+        student_kernel,
+        grid_spec=pltpu.PrefetchScalarGridSpec(
+            num_scalar_prefetch=1,
+            grid=(steps,),
+            in_specs=[mix] * 2,
+            out_specs=[
+                pl.BlockSpec((rows, EARLY * 128), lambda i, order: (0, 0)),
+                pl.BlockSpec((rows, LATE * 128), lambda i, order: (0, 0)),
+                turned,
+                turned,
+            ],
+            scratch_shapes=[pltpu.VMEM((width, rows), jnp.bfloat16), pltpu.VMEM((rows, width), jnp.bfloat16)],
+        ),
+        out_shape=[
+            jax.ShapeDtypeStruct((rows, EARLY * 128), jnp.bfloat16),
+            jax.ShapeDtypeStruct((rows, LATE * 128), jnp.bfloat16),
+            jax.ShapeDtypeStruct((8, 128, rows), jnp.bfloat16),
+            jax.ShapeDtypeStruct((8, 128, rows), jnp.bfloat16),
+        ],
+        compiler_params=pltpu.CompilerParams(vmem_limit_bytes=VMEM_LIMIT),
+        cost_estimate=pl.CostEstimate(flops=0, bytes_accessed=7 * 1024 * 1024, transcendentals=0),
+    )(order, mix_own, mix_other)
+
+
+def prepare_teacher(order, mix_own, mix_other, residual, places, places_other):
+    own, steps = mix_own.shape[0], 8
     rows, width = 2 * own, KIN // steps
     mix = pl.BlockSpec((own, width), lambda i, order: (0, i))
     place = pl.BlockSpec((own, 1), lambda i, order: (0, 0))
-    early = pl.BlockSpec((rows, EARLY * 128), lambda i, order: (0, 0))
-    late = pl.BlockSpec((rows, LATE * 128), lambda i, order: (0, 0))
-    turned = pl.BlockSpec((1, 128, rows), lambda i, order: (i, 0, 0))
-    return pl.pallas_call(
-        prepare_kernel,
+    return pl.pallas_call(
+        teacher_kernel,
         grid_spec=pltpu.PrefetchScalarGridSpec(
             num_scalar_prefetch=1,
             grid=(steps,),
-            in_specs=[mix] * 5 + [place] * 2,
-            out_specs=[early, early, late, late, mix, turned, turned],
+            in_specs=[mix] * 3 + [place] * 2,
+            out_specs=[
+                pl.BlockSpec((rows, EARLY * 128), lambda i, order: (0, 0)),
+                pl.BlockSpec((rows, LATE * 128), lambda i, order: (0, 0)),
+                mix,
+            ],
             scratch_shapes=[
-                pltpu.VMEM((width, rows), jnp.bfloat16),
                 pltpu.VMEM((rows, width), jnp.bfloat16),
-                pltpu.VMEM((rows, width), jnp.bfloat16),
+                pltpu.VMEM((rows // PATCHES, PATCHES, PATCHES), jnp.bfloat16),
             ],
         ),
         out_shape=[
             jax.ShapeDtypeStruct((rows, EARLY * 128), jnp.bfloat16),
-            jax.ShapeDtypeStruct((rows, EARLY * 128), jnp.bfloat16),
-            jax.ShapeDtypeStruct((rows, LATE * 128), jnp.bfloat16),
             jax.ShapeDtypeStruct((rows, LATE * 128), jnp.bfloat16),
             jax.ShapeDtypeStruct((own, DOUT), jnp.bfloat16),
-            jax.ShapeDtypeStruct((8, 128, rows), jnp.bfloat16),
-            jax.ShapeDtypeStruct((8, 128, rows), jnp.bfloat16),
         ],
         compiler_params=pltpu.CompilerParams(vmem_limit_bytes=VMEM_LIMIT),
         cost_estimate=pl.CostEstimate(
-            flops=4 * rows * PATCHES * KIN, bytes_accessed=16 * 1024 * 1024, transcendentals=0
-        ),
-    )(order, student_own, student_other, teacher_own, teacher_other, residual, places, places_other)
+            flops=3 * rows * PATCHES * KIN, bytes_accessed=9 * 1024 * 1024, transcendentals=0
+        ),
+    )(order, mix_own, mix_other, residual, places, places_other)
 
 
 def early_kernel(student_mix, teacher_mix, *refs):
@@ -281,42 +320,39 @@
         at += count
 
 
-def send_grads(total_tokens, order, student, matched, sums, more_sums, scale, turned):
+def send_grads(total_tokens, part, order, student, matched, sums, more_sums, scale, turned):
     (rows, columns), width = student.shape, 256
     steps = columns // width
-    column = pl.BlockSpec((rows, width), lambda j, order: (0, j))
+    count = steps // PARTS
+    column = pl.BlockSpec((rows, width), lambda j, order: (0, part * count + j))
     narrow = pl.BlockSpec((rows, 128), lambda j, order: (0, 0))
+    out = pl.BlockSpec((rows, width), lambda j, order: (0, j))
     half = pl.BlockSpec((rows // 2, width), lambda j, order: (0, j))
-
-    def blocks(count):
-        return pl.BlockSpec((count, 128, width), lambda j, order: (0, 0, j))
-
     return pl.pallas_call(
         functools.partial(send_kernel, total_tokens),
         grid_spec=pltpu.PrefetchScalarGridSpec(
             num_scalar_prefetch=1,
-            grid=(steps,),
+            grid=(count,),
             in_specs=[
                 column,
                 column,
                 narrow,
                 narrow,
-                pl.BlockSpec((1, width), lambda j, order: (0, order[HALF_AT] * steps + j)),
+                pl.BlockSpec((1, width), lambda j, order: (0, order[HALF_AT] * steps + part * count + j)),
                 pl.BlockSpec((8, 128, rows), lambda j, order: (0, 0, 0)),
             ],
-            out_specs=[blocks(count) for count in SENT] + [column, half, half],
-        ),
-        out_shape=[
-            jax.ShapeDtypeStruct((count, 128, columns), jnp.bfloat16) for count in SENT
-        ]
+            out_specs=[pl.BlockSpec((size, 128, width), lambda j, order: (0, 0, j)) for size in SENT]
+            + [out, half, half],
+        ),
+        out_shape=[jax.ShapeDtypeStruct((size, 128, columns // PARTS), jnp.bfloat16) for size in SENT]
         + [
-            jax.ShapeDtypeStruct((rows, columns), jnp.bfloat16),
-            jax.ShapeDtypeStruct((rows // 2, columns), jnp.bfloat16),
-            jax.ShapeDtypeStruct((rows // 2, columns), jnp.bfloat16),
+            jax.ShapeDtypeStruct((rows, columns // PARTS), jnp.bfloat16),
+            jax.ShapeDtypeStruct((rows // 2, columns // PARTS), jnp.bfloat16),
+            jax.ShapeDtypeStruct((rows // 2, columns // PARTS), jnp.bfloat16),
         ],
         compiler_params=pltpu.CompilerParams(vmem_limit_bytes=VMEM_LIMIT),
         cost_estimate=pl.CostEstimate(
-            flops=rows * KIN * columns, bytes_accessed=12 * 1024 * 1024, transcendentals=0
+            flops=rows * KIN * columns // PARTS, bytes_accessed=6 * 1024 * 1024, transcendentals=0
         ),
     )(order, student, matched, sums, more_sums, scale, turned)
 
@@ -456,19 +492,18 @@
     other_sent = jnp.stack(
         [columns_of(student_held, 1 - which), columns_of(teacher_held, 1 - which)]
     ).astype(jnp.bfloat16)
+    student_prepared = prepare_student(order, student_mix, student_other)
     (
-        up_two, across_down, across_up, passed_up, passed_down, across, other_sent, places, places_other, student_other,
-        teacher_other, residual,
+        up_two, across_down, across_up, passed_up, passed_down, across, other_sent, places, places_other,
+        student_prepared, teacher_other, residual,
     ) = lax.optimization_barrier(
         (
             from_y_next(up), from_y_previous(across), from_x_near(up), from_z_next(up), from_z_previous(down), across,
-            other_sent, places.reshape(token_count, 1), places_other.reshape(token_count, 1), student_other,
+            other_sent, places.reshape(token_count, 1), places_other.reshape(token_count, 1), student_prepared,
             teacher_other, residual,
         )
     )
-    prepared = prepare_rows(
-        order, student_mix, student_other, teacher_mix, teacher_other, residual, places, places_other
-    )
+    prepared = prepare_teacher(order, teacher_mix, teacher_other, residual, places, places_other)
     (
         across_two, passed_two, passed_across_up, passed_across_down, passed_across, prepared, other_sent, residual_sent
     ) = lax.optimization_barrier(
@@ -477,7 +512,8 @@
             from_x_twin(across), prepared, other_sent, residual,
         )
     )
-    student_early, teacher_early, student_late, teacher_late, picked, sent_mix, kept_mix = prepared
+    student_early, student_late, sent_mix, kept_mix = student_prepared
+    teacher_early, teacher_late, picked = prepared
     passed_across_two = from_z_next(across_two)
     residual_other, picked_other, other = swap_cores(residual_sent), swap_cores(picked), swap_cores(other_sent)
     student_part, teacher_part = early_forward(
@@ -492,17 +528,35 @@
         order, (other, passed_across_two), student_late, teacher_late, student_part, teacher_part, residual,
         residual_other, picked, picked_other, scale
     )
-    *sent, held, tokens_own, tokens_other = send_grads(
-        total_tokens, order, student_out, matched, sums, swap_cores(sums), scale, sent_mix
-    )
-    kept = keep_grads(held, kept_mix)
-    student_tokens = join_columns(which, tokens_own, swap_cores(tokens_other))
-    passed = lax.optimization_barrier((from_z_previous(sent[0]), from_z_next(sent[1]), from_x_twin(sent[2])))
-    by_chip = lax.all_to_all(
-        add_passed(kept, passed), ("xlo", "y", "xhi"), 0, 0, axis_index_groups=FSDP_GROUPS
-    )
-    by_chip, student_tokens = lax.optimization_barrier((by_chip, student_tokens))
-    total = jnp.sum(by_chip.astype(jnp.float32), axis=0).astype(jnp.bfloat16)
+    more_sums = swap_cores(sums)
+
+    def to_neighbours(part, after):
+        part_sums, after = lax.optimization_barrier((sums, after))
+        *sent, held, tokens_own, tokens_other = send_grads(
+            total_tokens, part, order, student_out, matched, part_sums, more_sums, scale, sent_mix
+        )
+        passed = (from_z_previous(sent[0]), from_z_next(sent[1]), from_x_twin(sent[2]))
+        return sent, held, tokens_own, tokens_other, passed
+
+    def over_fsdp(rows):
+        return lax.all_to_all(rows, ("xlo", "y", "xhi"), 0, 0, axis_index_groups=FSDP_GROUPS)
+
+    sent, first_held, first_own, first_other, first_passed = to_neighbours(0, more_sums)
+    _, last_held, last_own, last_other, last_passed = to_neighbours(1, sent)
+    first_kept, last_kept = keep_grads(first_held, kept_mix), keep_grads(last_held, kept_mix)
+    first_passed, last_kept, last_other = lax.optimization_barrier((first_passed, last_kept, last_other))
+    first_rows, last_kept, last_other = lax.optimization_barrier(
+        (add_passed(first_kept, first_passed), last_kept, last_other)
+    )
+    swapped = swap_cores(jnp.concatenate([first_other, last_other], axis=1))
+    tokens_own = jnp.concatenate([first_own, last_own], axis=1)
+    first_chip, last_rows = lax.optimization_barrier((over_fsdp(first_rows), add_passed(last_kept, last_passed)))
+    last_chip = over_fsdp(last_rows)
+    student_tokens = join_columns(which, tokens_own, swapped)
+    first_chip, last_chip, student_tokens = lax.optimization_barrier((first_chip, last_chip, student_tokens))
+    total = jnp.concatenate(
+        [jnp.sum(chip.astype(jnp.float32), axis=0).astype(jnp.bfloat16) for chip in (first_chip, last_chip)], axis=1
+    )
     by_copy = lax.all_to_all(
         total.reshape(8, 16, half), ("z", "xlo"), 0, 0, axis_index_groups=DP_GROUPS
     )

time: 191 us -> 187 us (0.979)
  waiting for transfers between devices: 82.7 us -> 60 us
  starting transfers between devices: 37.9 us -> 47.7 us
  Pallas kernels: 31.1 us -> 37.7 us
  local copies, waits for them, and re-layouts: 15.7 us -> 17.7 us
    all_to_all x1 -> x2, waiting for transfers between devices: 21.8 us -> 11.6 us  [over_fsdp(): lax.all_to_all(rows, ('xlo', 'y', 'xhi'), 0, 0, axis_index_groups=FSDP_GR...]
    all_to_all x1 -> x2, starting transfers between devices: 6.53 us -> 12.1 us  [over_fsdp(): lax.all_to_all(rows, ('xlo', 'y', 'xhi'), 0, 0, axis_index_groups=FSDP_GR...]
    pallas_call x1 -> x2, Pallas kernels: 6.93 us -> 12.4 us  [the longest x1 7.76 us: prepare_teacher(): pl.pallas_call(teacher_kernel, grid_spec=pltpu.PrefetchScalarGridSpec(num...]
    ppermute x2, waiting for transfers between devices: 5.86 us -> 1.53 us  [from_y_previous(): return lax.ppermute(value, 'y', from_previous(4))]
    ppermute x4 -> x5, starting transfers between devices: 9.35 us -> 12.1 us  [from_z_next(): return lax.ppermute(value, ('z', 'core'), with_core_flip(from_next(8)))]
    another operation x2, local copies, waits for them, and re-layouts: 0.07 us -> 2.26 us  [shards(): jnp.stack([columns_of(student_held, 1 - which), columns_of(teacher_held,...]
    ppermute x3 -> x4, waiting for transfers between devices: 5.26 us -> 3.49 us  [from_z_previous(): return lax.ppermute(value, ('z', 'core'), with_core_flip(from_previous(8)))]
    ppermute x2 -> x3, waiting for transfers between devices: 11 us -> 9.84 us  [from_x_twin(): return lax.ppermute(value, ('xlo', 'core'), with_core_flip(CORE_SWAP))]
  transfers between devices with their start and end apart: 27 -> 31, of which waited for: 14 -> 15; matrix products, arithmetic and copies ran while one was open for 3% -> 3% of each run, Pallas kernels for 9% -> 14%
where the time goes in v7:
time: 187 us; the launch traced here: 185 us
  waiting for transfers between devices  60 us (32%)
  starting transfers between devices  47.7 us (26%)
  Pallas kernels  37.7 us (20%)
  local copies, waits for them, and re-layouts  17.7 us (9%)
  blocking collectives  17.1 us (9%)
  other arithmetic  3.94 us (2%)
    all_to_all x1, blocking collectives, shards(): lax.all_to_all(total.reshape(8, 16, half), ('z', 'xlo'), 0, 0, axis_index...  17.1 us
    all_to_all x1, waiting for transfers between devices, shards(): lax.all_to_all(jnp.broadcast_to(copy_rows[None], (16, 16, half)), ('z', '...  15.4 us
    unnamed x68, local copies, waits for them, and re-layouts  12.6 us
    ppermute x5, starting transfers between devices, from_z_next(): return lax.ppermute(value, ('z', 'core'), with_core_flip(from_next(8)))  12.1 us
    all_to_all x2, starting transfers between devices, over_fsdp(): lax.all_to_all(rows, ('xlo', 'y', 'xhi'), 0, 0, axis_index_groups=FSDP_GR...  12.1 us
    all_to_all x2, waiting for transfers between devices, over_fsdp(): lax.all_to_all(rows, ('xlo', 'y', 'xhi'), 0, 0, axis_index_groups=FSDP_GR...  11.6 us
    ppermute x3, waiting for transfers between devices, from_x_twin(): return lax.ppermute(value, ('xlo', 'core'), with_core_flip(CORE_SWAP))  9.84 us
    ppermute x3, waiting for transfers between devices, from_x_near(): return lax.ppermute(value, ('xlo', 'xhi'), X_NEAR)  8.41 us
  transfers between devices with their start and end apart: 31, of which 15 were waited for; matrix products, arithmetic and copies ran while one was open for 3% of the time, Pallas kernels for 14%

profile of v7, /device:TPU:4, one launch (start us, length us, event | category | flops | bytes accessed | tf_op | source)
XLA Modules:
  0.0 185.1 jit_solution(7185697038607360736)
XLA Ops:
  8.3 8.4 %collective-permute-done.2.refs_3_ = bf16[2,128,1024]{2,1,0:T(8,128)(2,1)} collective-permute-done((bf16[2,128,1024]{2,1,0:T(8,128)(2,1)S(1)}, bf16[2,128,1024]{2,1,0:T(8,128)(2,1)}, u32[]{:S(2)}, u32[]{:S(2)}) %collective-permute-start.2) | collective-permute-done | bytes 524320 | tf_op jit(solution)/shard_map/ppermute | solution.py:53
  20.9 3.8 %collective-permute-start.9 = (bf16[2,128,1024]{2,1,0:T(8,128)(2,1)}, bf16[2,128,1024]{2,1,0:T(8,128)(2,1)}, u32[]{:S(2)}, u32[]{:S(2)}) collective-permute-start(bf16[2,128,1024]{2,1,0:T(8,128)(2,1)} %collective-permute-done.refs_1_), channel_id=1, source_target_pairs={{33,0},{32,1},{65,32},{64,33},{97,64},{96,65},{129,96},{128,97},{1... | collective-permute-start | bytes 1572872 | tf_op jit(solution)/shard_map/ppermute | solution.py:57
  26.2 2.0 %collective-permute-start.6 = (bf16[2,128,1024]{2,1,0:T(8,128)(2,1)}, bf16[2,128,1024]{2,1,0:T(8,128)(2,1)}, u32[]{:S(2)}, u32[]{:S(2)}) collective-permute-start(bf16[2,128,1024]{2,1,0:T(8,128)(2,1)} %collective-permute-done.refs_1_), channel_id=1, source_target_pairs={{4,0},{8,4},{12,8},{0,12},{5,1},{9,5},{13,9},{1,13},{6,2},{10,6},{... | collective-permute-start | bytes 1572872 | tf_op jit(solution)/shard_map/ppermute | solution.py:45
  31.0 4.6 %shard_map.128 = (bf16[576,1792]{1,0:T(8,128)(2,1)S(1)}, bf16[576,256]{1,0:T(8,128)(2,1)S(1)}, bf16[8,128,576]{2,1,0:T(8,128)(2,1)S(1)}, bf16[8,128,576]{2,1,0:T(8,128)(2,1)S(1)}) custom-call(s32[18]{0:T(128)S(1)} %stack.99.order, bf16[288,2048]{1,0:T(8,128)(2,1)S(1)} %copy-done.3, bf16[288,2048]{1,0:T(8,128)(2,1)S(1)} %copy-done.5), custom_call_target="tpu_custom_call" | custom-call | bytes 7340032 | tf_op jit(solution)/shard_map/pallas_call | solution.py:136
  42.6 4.0 %collective-permute-start.15 = (bf16[2,128,1024]{2,1,0:T(8,128)(2,1)}, bf16[2,128,1024]{2,1,0:T(8,128)(2,1)}, u32[]{:S(2)}, u32[]{:S(2)}) collective-permute-start(bf16[2,128,1024]{2,1,0:T(8,128)(2,1)} %collective-permute-done.2.refs_3_), channel_id=1, source_target_pairs={{1,16},{0,17},{17,0},{16,1},{3,18},{2,19},{19,2},{18,3},{5,20},{4,... | collective-permute-start | bytes 1572872 | tf_op jit(solution)/shard_map/ppermute | solution.py:65
  46.6 2.6 %collective-permute-start.11 = (bf16[2,128,1024]{2,1,0:T(8,128)(2,1)}, bf16[2,128,1024]{2,1,0:T(8,128)(2,1)}, u32[]{:S(2)}, u32[]{:S(2)}) collective-permute-start(bf16[2,128,1024]{2,1,0:T(8,128)(2,1)} %collective-permute-done.8.refs_6_), channel_id=1, source_target_pairs={{4,0},{8,4},{12,8},{0,12},{5,1},{9,5},{13,9},{1,13},{6,2},{10,6},{... | collective-permute-start | bytes 1572872 | tf_op jit(solution)/shard_map/ppermute | solution.py:45
  52.1 7.8 %shard_map.129 = (bf16[576,1792]{1,0:T(8,128)(2,1)S(1)}, bf16[576,256]{1,0:T(8,128)(2,1)S(1)}, bf16[288,2048]{1,0:T(8,128)(2,1)S(1)}) custom-call(s32[18]{0:T(128)S(1)} %stack.99.order, bf16[288,2048]{1,0:T(8,128)(2,1)S(1)} %copy-done.6, bf16[288,2048]{1,0:T(8,128)(2,1)S(1)} %copy-done.8, bf16[288,2048]{1,0:T(8,128)(2,1)} %residual_own, ...), custom_call_target="tpu_custom_call" | custom-call | flops 509607936 | bytes 9437184 | tf_op jit(solution)/shard_map/pallas_call | solution.py:166
  62.0 1.9 %collective-permute-start.19 = (bf16[2,128,1024]{2,1,0:T(8,128)(2,1)}, bf16[2,128,1024]{2,1,0:T(8,128)(2,1)S(1)}, u32[]{:S(2)}, u32[]{:S(2)}) collective-permute-start(bf16[2,128,1024]{2,1,0:T(8,128)(2,1)} %collective-permute-done.11.refs_9_), channel_id=1, source_target_pairs={{33,0},{32,1},{65,32},{64,33},{97,64},{96,65},{129,96},{128,97},{1... | collective-permute-start | bytes 1572872 | tf_op jit(solution)/shard_map/ppermute | solution.py:57
  63.9 7.0 %shard_map.130 = (f32[576,1024]{1,0:T(8,128)S(1)}, f32[576,1024]{1,0:T(8,128)S(1)}) custom-call(bf16[576,1792]{1,0:T(8,128)(2,1)S(1)} %copy-done.25, bf16[576,1792]{1,0:T(8,128)(2,1)S(1)} %get-tuple-element.128.teacher_mix, bf16[2,128,1024]{2,1,0:T(8,128)(2,1)S(1)} %copy-done.12, bf16[2,128,1024]{2,1,0:T(8,128)(2,1)} %collective-permute-done.refs_1_, ...), custom_call_target="tpu_custom_call" | custom-call | flops 4227858432 | bytes 17825792 | tf_op jit(solution)/shard_map/pallas_call | solution.py:209
  71.0 5.1 %collective-permute-done.19.refs_1_ = bf16[2,128,1024]{2,1,0:T(8,128)(2,1)S(1)} collective-permute-done((bf16[2,128,1024]{2,1,0:T(8,128)(2,1)}, bf16[2,128,1024]{2,1,0:T(8,128)(2,1)S(1)}, u32[]{:S(2)}, u32[]{:S(2)}) %collective-permute-start.19) | collective-permute-done | bytes 524320 | tf_op jit(solution)/shard_map/ppermute | solution.py:57
  76.1 4.7 %shard_map.131 = (f32[576,1024]{1,0:T(8,128)S(1)}, f32[576,1024]{1,0:T(8,128)S(1)}, f32[576,128]{1,0:T(8,128)S(1)}) custom-call(s32[18]{0:T(128)S(1)} %stack.99.order, bf16[576,256]{1,0:T(8,128)(2,1)S(1)} %copy-done.14, bf16[576,256]{1,0:T(8,128)(2,1)S(1)} %get-tuple-element.126.teacher_mix, f32[576,1024]{1,0:T(8,128)S(1)} %get-tuple-element.136.student_part, ...), custom_call_target="tpu_custom_call" | custom-call | flops 603979776 | bytes 13631488 | tf_op jit(solution)/shard_map/pallas_call | solution.py:265
  82.4 2.7 %shard_map.132 = (bf16[3,128,512]{2,1,0:T(8,128)(2,1)S(1)}, bf16[3,128,512]{2,1,0:T(8,128)(2,1)S(1)}, bf16[2,128,512]{2,1,0:T(8,128)(2,1)S(1)}, bf16[576,512]{1,...) custom-call(s32[18]{0:T(128)S(1)} %stack.99.order, ...), custom_call_target="tpu_custom_call" | custom-call | flops 603979776 | bytes 6291456 | tf_op jit(solution)/shard_map/pallas_call | solution.py:331
  85.9 3.0 %collective-permute-start.22 = (bf16[3,128,512]{2,1,0:T(8,128)(2,1)S(1)}, bf16[3,128,512]{2,1,0:T(8,128)(2,1)S(1)}, u32[]{:S(2)}, u32[]{:S(2)}) collective-permute-start(bf16[3,128,512]{2,1,0:T(8,128)(2,1)S(1)} %get-tuple-element.149), channel_id=1, source_target_pairs={{33,0},{32,1},{65,32},{64,33},{97,64},{96,65},{129,96},{128,97},{1... | collective-permute-start | bytes 1179656 | tf_op jit(solution)/shard_map/ppermute | solution.py:57
  88.9 2.8 %shard_map.134 = (bf16[3,128,512]{2,1,0:T(8,128)(2,1)S(1)}, bf16[3,128,512]{2,1,0:T(8,128)(2,1)S(1)}, bf16[2,128,512]{2,1,0:T(8,128)(2,1)S(1)}, bf16[576,512]{1,...) custom-call(s32[18]{0:T(128)S(1)} %stack.99.order, ...), custom_call_target="tpu_custom_call" | custom-call | flops 603979776 | bytes 6291456 | tf_op jit(solution)/shard_map/pallas_call | solution.py:331
  94.6 2.5 %collective-permute-done.23.refs_2_ = bf16[2,128,512]{2,1,0:T(8,128)(2,1)S(1)} collective-permute-done((bf16[2,128,512]{2,1,0:T(8,128)(2,1)S(1)}, bf16[2,128,512]{2,1,0:T(8,128)(2,1)S(1)}, u32[]{:S(2)}, u32[]{:S(2)}) %collective-permute-start.23) | collective-permute-done | bytes 262176 | tf_op jit(solution)/shard_map/ppermute | solution.py:65
  99.5 6.6 %all-to-all-start = ((bf16[8,128,512]{2,1,0:T(8,128)(2,1)}), bf16[8,128,512]{2,1,0:T(8,128)(2,1)}, u32[]{:S(2)}, u32[]{:S(2)}) async-start(bf16[8,128,512]{2,1,0:T(8,128)(2,1)} %shard_map.136), calls=%async_computation | async-start | bytes 2097152 | tf_op jit(solution)/shard_map/all_to_all | solution.py:542
  110.0 7.3 %collective-permute-done.26.refs_2_ = bf16[2,128,512]{2,1,0:T(8,128)(2,1)S(1)} collective-permute-done((bf16[2,128,512]{2,1,0:T(8,128)(2,1)S(1)}, bf16[2,128,512]{2,1,0:T(8,128)(2,1)S(1)}, u32[]{:S(2)}, u32[]{:S(2)}) %collective-permute-start.26) | collective-permute-done | bytes 262176 | tf_op jit(solution)/shard_map/ppermute | solution.py:65
  121.0 5.5 %all-to-all-start.1 = ((bf16[8,128,512]{2,1,0:T(8,128)(2,1)}), bf16[8,128,512]{2,1,0:T(8,128)(2,1)S(1)}, u32[]{:S(2)}, u32[]{:S(2)}) async-start(bf16[8,128,512]{2,1,0:T(8,128)(2,1)} %shard_map.137), calls=%async_computation.1 | async-start | bytes 2097152 | tf_op jit(solution)/shard_map/all_to_all | solution.py:542
  126.7 2.0 %collective-permute-done.27 = bf16[288,1024]{1,0:T(8,128)(2,1)S(1)} collective-permute-done((bf16[288,1024]{1,0:T(8,128)(2,1)S(1)}, bf16[288,1024]{1,0:T(8,128)(2,1)S(1)}, u32[]{:S(2)}, u32[]{:S(2)}) %collective-permute-start.27) | collective-permute-done | bytes 589856 | tf_op jit(solution)/shard_map/ppermute | solution.py:41
  130.1 11.2 %all-to-all-done.1 = bf16[8,128,512]{2,1,0:T(8,128)(2,1)S(1)} async-done(((bf16[8,128,512]{2,1,0:T(8,128)(2,1)}), bf16[8,128,512]{2,1,0:T(8,128)(2,1)S(1)}, u32[]{:S(2)}, u32[]{:S(2)}) %all-to-all-start.1) | async-done | bytes 1048608 | tf_op jit(solution)/shard_map/all_to_all | solution.py:542
  142.9 17.1 %all_to_all.20 = bf16[8,16,1024]{2,1,0:T(8,128)(2,1)S(1)} all-to-all(bf16[8,16,1024]{2,1,0:T(8,128)(2,1)S(1)} %bitcast.34), channel_id=1, replica_groups={{0,48,64,112,128,176,192,240},{16,32,80,96,144,160,208,224},{1,49,65,11..., dimensions={0} | all-to-all | bytes 524288 | tf_op jit(solution)/shard_map/all_to_all | solution.py:560
  160.9 3.6 %all-to-all-start.3 = ((bf16[16,16,1024]{2,1,0:T(8,128)(2,1)}), bf16[16,16,1024]{2,1,0:T(8,128)(2,1)S(1)}, u32[]{:S(2)}, u32[]{:S(2)}) async-start(bf16[16,16,1024]{2,1,0:T(8,128)(2,1)} %broadcast_in_dim.2), calls=%async_computation.3 | async-start | bytes 1048576 | tf_op jit(solution)/shard_map/all_to_all | solution.py:564
  164.5 15.4 %all-to-all-done.3 = bf16[16,16,1024]{2,1,0:T(8,128)(2,1)S(1)} async-done(((bf16[16,16,1024]{2,1,0:T(8,128)(2,1)}), bf16[16,16,1024]{2,1,0:T(8,128)(2,1)S(1)}, u32[]{:S(2)}, u32[]{:S(2)}) %all-to-all-start.3) | async-done | bytes 524320 | tf_op jit(solution)/shard_map/all_to_all | solution.py:564
  182.4 2.7 %shard_map.138 = (f32[128,2048]{1,0:T(8,128)}, f32[128,2048]{1,0:T(8,128)}, f32[128,2048]{1,0:T(8,128)}, f32[128,2048]{1,0:T(8,128)}) custom-call(s32[1]{0:T(128)} %bitcast.flip, bf16[8,2,16,1024]{3,2,1,0:T(8,128)(2,1)S(1)} %bitcast.30, f32[128,2048]{1,0:T(8,128)S(1)} %copy-done, f32[128,2048]{1,0:T(8,128)S(1)} %copy-done.1, f32[128,2048]{1,0:T(8,128)S(1)} %copy-done.9, ...), custom_call_target="tpu_custom_call" | custom-call | tf_op jit(solution)/shard_map/pallas_call | solution.py:430
  (135 shorter events, 49.6 us)
Async XLA Ops:
  2.2 16.1 %collective-permute-start.4 = (bf16[288,2048]{1,0:T(8,128)(2,1)}, bf16[288,2048]{1,0:T(8,128)(2,1)S(1)}, u32[]{:S(2)}, u32[]{:S(2)}) collective-permute-start(bf16[288,2048]{1,0:T(8,128)(2,1)} %mix_own.3), channel_id=1, source_target_pairs={{0,1},{1,0},{2,3},{3,2},{4,5},{5,4},{6,7},{7,6},{8,9},{9,8},{10,11... | collective-permute-start | bytes 3538952 | tf_op jit(solution)/shard_map/ppermute | solution.py:41
  2.7 14.0 %collective-permute-start.2 = (bf16[2,128,1024]{2,1,0:T(8,128)(2,1)S(1)}, bf16[2,128,1024]{2,1,0:T(8,128)(2,1)}, u32[]{:S(2)}, u32[]{:S(2)}) collective-permute-start(bf16[2,128,1024]{2,1,0:T(8,128)(2,1)S(1)} %pad_maximum_fusion.1.refs_0_), channel_id=1, source_target_pairs={{16,2},{2,16},{0,18},{18,0},{17,3},{3,17},{1,19},{19,1},{20,6},{6,... | collective-permute-start | bytes 1572872 | tf_op jit(solution)/shard_map/ppermute | solution.py:53
  3.3 15.0 %collective-permute-start.1 = (bf16[2,128,1024]{2,1,0:T(8,128)(2,1)S(1)}, bf16[2,128,1024]{2,1,0:T(8,128)(2,1)}, u32[]{:S(2)}, u32[]{:S(2)}) collective-permute-start(bf16[2,128,1024]{2,1,0:T(8,128)(2,1)S(1)} %pad_maximum_fusion.1.refs_0_), channel_id=1, source_target_pairs={{0,4},{4,8},{8,12},{12,0},{1,5},{5,9},{9,13},{13,1},{2,6},{6,10},{... | collective-permute-start | bytes 1572872 | tf_op jit(solution)/shard_map/ppermute | solution.py:49
  4.9 13.4 %collective-permute-start = (bf16[2,128,1024]{2,1,0:T(8,128)(2,1)S(1)}, bf16[2,128,1024]{2,1,0:T(8,128)(2,1)}, u32[]{:S(2)}, u32[]{:S(2)}) collective-permute-start(bf16[2,128,1024]{2,1,0:T(8,128)(2,1)S(1)} %pad_maximum_fusion.1.refs_0_), channel_id=1, source_target_pairs={{4,0},{8,4},{12,8},{0,12},{5,1},{9,5},{13,9},{1,13},{6,2},{10,6},{... | collective-permute-start | bytes 1572872 | tf_op jit(solution)/shard_map/ppermute | solution.py:45
  19.3 20.8 %collective-permute-start.7 = (bf16[2,128,1024]{2,1,0:T(8,128)(2,1)}, bf16[2,128,1024]{2,1,0:T(8,128)(2,1)}, u32[]{:S(2)}, u32[]{:S(2)}) collective-permute-start(bf16[2,128,1024]{2,1,0:T(8,128)(2,1)} %collective-permute-done.2.refs_3_), channel_id=1, source_target_pairs={{0,4},{4,8},{8,12},{12,0},{1,5},{5,9},{9,13},{13,1},{2,6},{6,10},{... | collective-permute-start | bytes 1572872 | tf_op jit(solution)/shard_map/ppermute | solution.py:49
  20.9 19.2 %collective-permute-start.10 = (bf16[2,128,1024]{2,1,0:T(8,128)(2,1)}, bf16[2,128,1024]{2,1,0:T(8,128)(2,1)}, u32[]{:S(2)}, u32[]{:S(2)}) collective-permute-start(bf16[2,128,1024]{2,1,0:T(8,128)(2,1)} %collective-permute-done.1.refs_2_), channel_id=1, source_target_pairs={{1,32},{0,33},{33,64},{32,65},{65,96},{64,97},{97,128},{96,129},{1... | collective-permute-start | bytes 1572872 | tf_op jit(solution)/shard_map/ppermute | solution.py:61
  20.9 19.2 %collective-permute-start.9 = (bf16[2,128,1024]{2,1,0:T(8,128)(2,1)}, bf16[2,128,1024]{2,1,0:T(8,128)(2,1)}, u32[]{:S(2)}, u32[]{:S(2)}) collective-permute-start(bf16[2,128,1024]{2,1,0:T(8,128)(2,1)} %collective-permute-done.refs_1_), channel_id=1, source_target_pairs={{33,0},{32,1},{65,32},{64,33},{97,64},{96,65},{129,96},{128,97},{1... | collective-permute-start | bytes 1572872 | tf_op jit(solution)/shard_map/ppermute | solution.py:57
  24.7 15.4 %collective-permute-start.8 = (bf16[2,128,1024]{2,1,0:T(8,128)(2,1)}, bf16[2,128,1024]{2,1,0:T(8,128)(2,1)}, u32[]{:S(2)}, u32[]{:S(2)}) collective-permute-start(bf16[2,128,1024]{2,1,0:T(8,128)(2,1)} %collective-permute-done.refs_1_), channel_id=1, source_target_pairs={{16,2},{2,16},{0,18},{18,0},{17,3},{3,17},{1,19},{19,1},{20,6},{6,... | collective-permute-start | bytes 1572872 | tf_op jit(solution)/shard_map/ppermute | solution.py:53
  26.2 14.2 %collective-permute-start.6 = (bf16[2,128,1024]{2,1,0:T(8,128)(2,1)}, bf16[2,128,1024]{2,1,0:T(8,128)(2,1)}, u32[]{:S(2)}, u32[]{:S(2)}) collective-permute-start(bf16[2,128,1024]{2,1,0:T(8,128)(2,1)} %collective-permute-done.refs_1_), channel_id=1, source_target_pairs={{4,0},{8,4},{12,8},{0,12},{5,1},{9,5},{13,9},{1,13},{6,2},{10,6},{... | collective-permute-start | bytes 1572872 | tf_op jit(solution)/shard_map/ppermute | solution.py:45
  40.3 19.5 %collective-permute-start.12 = (bf16[2,128,1024]{2,1,0:T(8,128)(2,1)}, bf16[2,128,1024]{2,1,0:T(8,128)(2,1)}, u32[]{:S(2)}, u32[]{:S(2)}) collective-permute-start(bf16[2,128,1024]{2,1,0:T(8,128)(2,1)} %collective-permute-done.6.refs_4_), channel_id=1, source_target_pairs={{33,0},{32,1},{65,32},{64,33},{97,64},{96,65},{129,96},{128,97},{1... | collective-permute-start | bytes 1572872 | tf_op jit(solution)/shard_map/ppermute | solution.py:57
  42.1 17.8 %collective-permute-start.14 = (bf16[2,128,1024]{2,1,0:T(8,128)(2,1)}, bf16[2,128,1024]{2,1,0:T(8,128)(2,1)}, u32[]{:S(2)}, u32[]{:S(2)}) collective-permute-start(bf16[2,128,1024]{2,1,0:T(8,128)(2,1)} %collective-permute-done.10.refs_8_), channel_id=1, source_target_pairs={{16,2},{2,16},{0,18},{18,0},{17,3},{3,17},{1,19},{19,1},{20,6},{6,... | collective-permute-start | bytes 1572872 | tf_op jit(solution)/shard_map/ppermute | solution.py:53
  42.6 17.3 %collective-permute-start.15 = (bf16[2,128,1024]{2,1,0:T(8,128)(2,1)}, bf16[2,128,1024]{2,1,0:T(8,128)(2,1)}, u32[]{:S(2)}, u32[]{:S(2)}) collective-permute-start(bf16[2,128,1024]{2,1,0:T(8,128)(2,1)} %collective-permute-done.2.refs_3_), channel_id=1, source_target_pairs={{1,16},{0,17},{17,0},{16,1},{3,18},{2,19},{19,2},{18,3},{5,20},{4,... | collective-permute-start | bytes 1572872 | tf_op jit(solution)/shard_map/ppermute | solution.py:65
  46.6 14.7 %collective-permute-start.13 = (bf16[2,128,1024]{2,1,0:T(8,128)(2,1)}, bf16[2,128,1024]{2,1,0:T(8,128)(2,1)}, u32[]{:S(2)}, u32[]{:S(2)}) collective-permute-start(bf16[2,128,1024]{2,1,0:T(8,128)(2,1)} %collective-permute-done.8.refs_6_), channel_id=1, source_target_pairs={{1,32},{0,33},{33,64},{32,65},{65,96},{64,97},{97,128},{96,129},{1... | collective-permute-start | bytes 1572872 | tf_op jit(solution)/shard_map/ppermute | solution.py:61
  46.6 14.7 %collective-permute-start.11 = (bf16[2,128,1024]{2,1,0:T(8,128)(2,1)}, bf16[2,128,1024]{2,1,0:T(8,128)(2,1)}, u32[]{:S(2)}, u32[]{:S(2)}) collective-permute-start(bf16[2,128,1024]{2,1,0:T(8,128)(2,1)} %collective-permute-done.8.refs_6_), channel_id=1, source_target_pairs={{4,0},{8,4},{12,8},{0,12},{5,1},{9,5},{13,9},{1,13},{6,2},{10,6},{... | collective-permute-start | bytes 1572872 | tf_op jit(solution)/shard_map/ppermute | solution.py:45
  61.3 14.8 %collective-permute-start.16 = (bf16[288,2048]{1,0:T(8,128)(2,1)}, bf16[288,2048]{1,0:T(8,128)(2,1)S(1)}, u32[]{:S(2)}, u32[]{:S(2)}) collective-permute-start(bf16[288,2048]{1,0:T(8,128)(2,1)} %residual_own), channel_id=1, source_target_pairs={{0,1},{1,0},{2,3},{3,2},{4,5},{5,4},{6,7},{7,6},{8,9},{9,8},{10,11... | collective-permute-start | bytes 3538952 | tf_op jit(solution)/shard_map/ppermute | solution.py:41
  61.4 14.7 %collective-permute-start.17 = (bf16[288,2048]{1,0:T(8,128)(2,1)S(1)}, bf16[288,2048]{1,0:T(8,128)(2,1)S(1)}, u32[]{:S(2)}, u32[]{:S(2)}) collective-permute-start(bf16[288,2048]{1,0:T(8,128)(2,1)S(1)} %get-tuple-element.139.picked_own), channel_id=1, source_target_pairs={{0,1},{1,0},{2,3},{3,2},{4,5},{5,4},{6,7},{7,6},{8,9},{9,8},{10,11... | collective-permute-start | bytes 3538952 | tf_op jit(solution)/shard_map/ppermute | solution.py:41
  62.0 14.1 %collective-permute-start.19 = (bf16[2,128,1024]{2,1,0:T(8,128)(2,1)}, bf16[2,128,1024]{2,1,0:T(8,128)(2,1)S(1)}, u32[]{:S(2)}, u32[]{:S(2)}) collective-permute-start(bf16[2,128,1024]{2,1,0:T(8,128)(2,1)} %collective-permute-done.11.refs_9_), channel_id=1, source_target_pairs={{33,0},{32,1},{65,32},{64,33},{97,64},{96,65},{129,96},{128,97},{1... | collective-permute-start | bytes 1572872 | tf_op jit(solution)/shard_map/ppermute | solution.py:57
  85.9 12.3 %collective-permute-start.21 = (bf16[3,128,512]{2,1,0:T(8,128)(2,1)S(1)}, bf16[3,128,512]{2,1,0:T(8,128)(2,1)S(1)}, u32[]{:S(2)}, u32[]{:S(2)}) collective-permute-start(bf16[3,128,512]{2,1,0:T(8,128)(2,1)S(1)} %get-tuple-element.148), channel_id=1, source_target_pairs={{1,32},{0,33},{33,64},{32,65},{65,96},{64,97},{97,128},{96,129},{1... | collective-permute-start | bytes 1179656 | tf_op jit(solution)/shard_map/ppermute | solution.py:61
  85.9 12.3 %collective-permute-start.22 = (bf16[3,128,512]{2,1,0:T(8,128)(2,1)S(1)}, bf16[3,128,512]{2,1,0:T(8,128)(2,1)S(1)}, u32[]{:S(2)}, u32[]{:S(2)}) collective-permute-start(bf16[3,128,512]{2,1,0:T(8,128)(2,1)S(1)} %get-tuple-element.149), channel_id=1, source_target_pairs={{33,0},{32,1},{65,32},{64,33},{97,64},{96,65},{129,96},{128,97},{1... | collective-permute-start | bytes 1179656 | tf_op jit(solution)/shard_map/ppermute | solution.py:57
  99.5 21.5 %all-to-all-start = ((bf16[8,128,512]{2,1,0:T(8,128)(2,1)}), bf16[8,128,512]{2,1,0:T(8,128)(2,1)}, u32[]{:S(2)}, u32[]{:S(2)}) async-start(bf16[8,128,512]{2,1,0:T(8,128)(2,1)} %shard_map.136), calls=%async_computation | async-start | bytes 2097152 | tf_op jit(solution)/shard_map/all_to_all | solution.py:542
  106.0 12.3 %collective-permute-start.24 = (bf16[3,128,512]{2,1,0:T(8,128)(2,1)S(1)}, bf16[3,128,512]{2,1,0:T(8,128)(2,1)S(1)}, u32[]{:S(2)}, u32[]{:S(2)}) collective-permute-start(bf16[3,128,512]{2,1,0:T(8,128)(2,1)S(1)} %copy-done.29), channel_id=1, source_target_pairs={{1,32},{0,33},{33,64},{32,65},{65,96},{64,97},{97,128},{96,129},{1... | collective-permute-start | bytes 1179656 | tf_op jit(solution)/shard_map/ppermute | solution.py:61
  107.4 12.0 %collective-permute-start.25 = (bf16[3,128,512]{2,1,0:T(8,128)(2,1)S(1)}, bf16[3,128,512]{2,1,0:T(8,128)(2,1)S(1)}, u32[]{:S(2)}, u32[]{:S(2)}) collective-permute-start(bf16[3,128,512]{2,1,0:T(8,128)(2,1)S(1)} %copy-done.27), channel_id=1, source_target_pairs={{33,0},{32,1},{65,32},{64,33},{97,64},{96,65},{129,96},{128,97},{1... | collective-permute-start | bytes 1179656 | tf_op jit(solution)/shard_map/ppermute | solution.py:57
  121.0 20.3 %all-to-all-start.1 = ((bf16[8,128,512]{2,1,0:T(8,128)(2,1)}), bf16[8,128,512]{2,1,0:T(8,128)(2,1)S(1)}, u32[]{:S(2)}, u32[]{:S(2)}) async-start(bf16[8,128,512]{2,1,0:T(8,128)(2,1)} %shard_map.137), calls=%async_computation.1 | async-start | bytes 2097152 | tf_op jit(solution)/shard_map/all_to_all | solution.py:542
  160.9 19.0 %all-to-all-start.3 = ((bf16[16,16,1024]{2,1,0:T(8,128)(2,1)}), bf16[16,16,1024]{2,1,0:T(8,128)(2,1)S(1)}, u32[]{:S(2)}, u32[]{:S(2)}) async-start(bf16[16,16,1024]{2,1,0:T(8,128)(2,1)} %broadcast_in_dim.2), calls=%async_computation.3 | async-start | bytes 1048576 | tf_op jit(solution)/shard_map/all_to_all | solution.py:564
  (41 other events, 278.8 us)

commit v8 on v7

--- a/solution.py
+++ b/solution.py
@@ -13,6 +13,7 @@
 EPS = 1e-06
 AXES = ("z", "xlo", "y", "xhi", "core")
 VMEM_LIMIT = 32 * 1024 * 1024
+SMALL_LIMIT = 16 * 1024 * 1024
 
 X_INDEX = (0, 2, 1, 3)
 CORE_SWAP = ((0, 1), (1, 0))
@@ -77,6 +78,31 @@
 PARTS = 2
 
 
+def split_kernel(order, student, teacher, out):
+    out[0] = student[...].astype(jnp.bfloat16)
+    out[1] = teacher[...].astype(jnp.bfloat16)
+
+
+def split_weights(order, student, teacher):
+    rows, width, steps = student.shape[0], 512, 2
+
+    def half(j, order):
+        return (0, (order[HALF_AT] ^ 1) * steps + j)
+
+    return pl.pallas_call(
+        split_kernel,
+        grid_spec=pltpu.PrefetchScalarGridSpec(
+            num_scalar_prefetch=1,
+            grid=(steps,),
+            in_specs=[pl.BlockSpec((rows, width), half)] * 2,
+            out_specs=pl.BlockSpec((2, rows, width), lambda j, order: (0, 0, j)),
+        ),
+        out_shape=jax.ShapeDtypeStruct((2, rows, width * steps), jnp.bfloat16),
+        compiler_params=pltpu.CompilerParams(vmem_limit_bytes=SMALL_LIMIT),
+        cost_estimate=pl.CostEstimate(flops=0, bytes_accessed=1536 * 1024, transcendentals=0),
+    )(order, student, teacher)
+
+
 def place_blocks(order, step, packed, early, late):
     for part in range(2):
         columns = slice(part * 128, (part + 1) * 128)
@@ -108,11 +134,11 @@
 
     @pl.when(step == 0)
     def _():
-        lane = lax.broadcasted_iota(jnp.int32, (PATCHES, PATCHES), 1)
+        source = lax.broadcasted_iota(jnp.int32, (PATCHES, PATCHES), 0)
         for side, places in enumerate((places_own, places_other)):
             for crop in range(crops):
-                rows = slice(crop * PATCHES, (crop + 1) * PATCHES)
-                picks[side * crops + crop] = (places[rows, :] == lane).astype(jnp.float32).astype(jnp.bfloat16)
+                chosen = jnp.where(places[crop : crop + 1, :] == source, 1.0, 0.0)
+                picks[side * crops + crop] = chosen.T.astype(jnp.bfloat16)
 
     for side, mix in enumerate((mix_own, mix_other)):
         for crop in range(crops):
@@ -162,7 +188,7 @@
     own, steps = mix_own.shape[0], 8
     rows, width = 2 * own, KIN // steps
     mix = pl.BlockSpec((own, width), lambda i, order: (0, i))
-    place = pl.BlockSpec((own, 1), lambda i, order: (0, 0))
+    place = pl.BlockSpec(places.shape, lambda i, order: (0, 0))
     return pl.pallas_call(
         teacher_kernel,
         grid_spec=pltpu.PrefetchScalarGridSpec(
@@ -407,6 +433,70 @@
     )(kept, *passed)
 
 
+def join_kernel(order, first_own, last_own, first_other, last_other, out):
+    step = pl.program_id(0)
+    for at, half in enumerate((first_own, last_own, first_other, last_other)):
+        @pl.when(step == (at ^ (2 * order[HALF_AT])))
+        def _():
+            out[...] = half[...]
+
+
+def join_tokens(order, *halves):
+    rows, width = halves[0].shape
+    return pl.pallas_call(
+        join_kernel,
+        grid_spec=pltpu.PrefetchScalarGridSpec(
+            num_scalar_prefetch=1,
+            grid=(4,),
+            in_specs=[pl.BlockSpec((rows, width), lambda j, order: (0, 0))] * 4,
+            out_specs=pl.BlockSpec((rows, width), lambda j, order: (0, j)),
+        ),
+        out_shape=jax.ShapeDtypeStruct((rows, 4 * width), jnp.bfloat16),
+        compiler_params=pltpu.CompilerParams(vmem_limit_bytes=SMALL_LIMIT),
+        cost_estimate=pl.CostEstimate(flops=0, bytes_accessed=2400 * 1024, transcendentals=0),
+    )(order, *halves)
+
+
+def total_kernel(first, last, out):
+    width = first.shape[-1]
+    for at, chips in enumerate((first, last)):
+        total = chips[0].astype(jnp.float32)
+        for chip in range(1, chips.shape[0]):
+            total = total + chips[chip].astype(jnp.float32)
+        out[:, at * width : (at + 1) * width] = total.astype(jnp.bfloat16)
+
+
+def total_rows(first, last):
+    chips, rows, width = first.shape
+    block = pl.BlockSpec((chips, rows // 2, width), lambda i: (0, i, 0))
+    return pl.pallas_call(
+        total_kernel,
+        grid=(2,),
+        in_specs=[block, block],
+        out_specs=pl.BlockSpec((rows // 2, 2 * width), lambda i: (i, 0)),
+        out_shape=jax.ShapeDtypeStruct((rows, 2 * width), jnp.bfloat16),
+        compiler_params=pltpu.CompilerParams(vmem_limit_bytes=SMALL_LIMIT),
+        cost_estimate=pl.CostEstimate(flops=0, bytes_accessed=2400 * 1024, transcendentals=0),
+    )(first, last)
+
+
+def spread_kernel(copies, out):
+    total = copies[0].astype(jnp.float32)
+    for copy in range(1, copies.shape[0]):
+        total = total + copies[copy].astype(jnp.float32)
+    out[...] = jnp.broadcast_to(total.astype(jnp.bfloat16)[None], out.shape)
+
+
+def spread_rows(copies, count):
+    _, rows, columns = copies.shape
+    return pl.pallas_call(
+        spread_kernel,
+        out_shape=jax.ShapeDtypeStruct((count, rows, columns), jnp.bfloat16),
+        compiler_params=pltpu.CompilerParams(vmem_limit_bytes=SMALL_LIMIT),
+        cost_estimate=pl.CostEstimate(flops=0, bytes_accessed=800 * 1024, transcendentals=0),
+    )(copies)
+
+
 def update_kernel(flip, grads, weight, teacher, first, squares, weight_out, teacher_out, first_out, squares_out):
     rows = []
     for index in range(grads.shape[0]):
@@ -440,12 +530,6 @@
     )(flip, grads, weight, teacher, first, squares)
 
 
-def join_columns(which, own, other):
-    return jnp.where(
-        which == 0, jnp.concatenate([own, other], axis=-1), jnp.concatenate([other, own], axis=-1)
-    )
-
-
 def shards(
     residual,
     student_mix,
@@ -463,17 +547,16 @@
     z, xlo, y, xhi, core = (lax.axis_index(name) for name in AXES)
     which = (core + z + xhi + xlo) & 1
 
-    def columns_of(value, index):
-        return lax.dynamic_slice_in_dim(value, index * half, half, axis=-1)
-
-    def both_weights(index):
-        return jnp.stack([columns_of(student_weight, index), columns_of(teacher_weight, index)]).astype(jnp.bfloat16)
-
-    own = both_weights(which)
     order = jnp.stack(
         [(((y + dy) & 3) * 2 + (xhi ^ dx)) * 2 + (core ^ side) for side, dy, dx in ORDER] + [which, core]
     ).astype(jnp.int32)
     scale = layer_scale.reshape(1, DOUT)
+    own = jnp.stack(
+        [
+            lax.dynamic_slice_in_dim(weight, which * half, half, axis=-1)
+            for weight in (student_weight, teacher_weight)
+        ]
+    ).astype(jnp.bfloat16)
 
     own, student_sent, teacher_sent, positions_sent, student_held, teacher_held, residual = lax.optimization_barrier(
         (own, student_mix, teacher_mix, positions, student_weight, teacher_weight, residual)
@@ -489,9 +572,7 @@
             )
         )
     )
-    other_sent = jnp.stack(
-        [columns_of(student_held, 1 - which), columns_of(teacher_held, 1 - which)]
-    ).astype(jnp.bfloat16)
+    other_sent = split_weights(order, student_held, teacher_held)
     student_prepared = prepare_student(order, student_mix, student_other)
     (
         up_two, across_down, across_up, passed_up, passed_down, across, other_sent, places, places_other,
@@ -499,7 +580,7 @@
     ) = lax.optimization_barrier(
         (
             from_y_next(up), from_y_previous(across), from_x_near(up), from_z_next(up), from_z_previous(down), across,
-            other_sent, places.reshape(token_count, 1), places_other.reshape(token_count, 1), student_prepared,
+            other_sent, places, places_other, student_prepared,
             teacher_other, residual,
         )
     )
@@ -548,20 +629,16 @@
     first_rows, last_kept, last_other = lax.optimization_barrier(
         (add_passed(first_kept, first_passed), last_kept, last_other)
     )
-    swapped = swap_cores(jnp.concatenate([first_other, last_other], axis=1))
-    tokens_own = jnp.concatenate([first_own, last_own], axis=1)
+    swapped = swap_cores(first_other), swap_cores(last_other)
     first_chip, last_rows = lax.optimization_barrier((over_fsdp(first_rows), add_passed(last_kept, last_passed)))
     last_chip = over_fsdp(last_rows)
-    student_tokens = join_columns(which, tokens_own, swapped)
+    student_tokens = join_tokens(order, first_own, last_own, *swapped)
     first_chip, last_chip, student_tokens = lax.optimization_barrier((first_chip, last_chip, student_tokens))
-    total = jnp.concatenate(
-        [jnp.sum(chip.astype(jnp.float32), axis=0).astype(jnp.bfloat16) for chip in (first_chip, last_chip)], axis=1
-    )
+    total = total_rows(first_chip, last_chip)
     by_copy = lax.all_to_all(
         total.reshape(8, 16, half), ("z", "xlo"), 0, 0, axis_index_groups=DP_GROUPS
     )
-    copy_rows = jnp.sum(by_copy.astype(jnp.float32), axis=0).astype(jnp.bfloat16)
-    full = lax.all_to_all(jnp.broadcast_to(copy_rows[None], (16, 16, half)), ("z", "xlo"), 0, 0)
+    full = lax.all_to_all(spread_rows(by_copy, 16), ("z", "xlo"), 0, 0)
     flip = ((core + xhi) & 1).astype(jnp.int32).reshape(1)
     weight_next, teacher_next, first_next, squares_next = adamw_update(
         flip, full.reshape(8, 2, 16, half), student_weight, teacher_weight, moment, second

time: 187 us -> 186 us (level)
  waiting for transfers between devices: 60 us -> 68.2 us
  local copies, waits for them, and re-layouts: 17.7 us -> 12 us
  other arithmetic: 3.94 us -> 0.05 us
    pallas_call x0 -> x4, Pallas kernels: none -> 5.2 us  [the longest x1 2.18 us: join_tokens(): pl.pallas_call(join_kernel, grid_spec=pltpu.PrefetchScalarGridSpec(num_sc...]
    ppermute x3, waiting for transfers between devices: 9.84 us -> 13.3 us  [from_x_twin(): return lax.ppermute(value, ('xlo', 'core'), with_core_flip(CORE_SWAP))]
    another operation x3 -> x1, local copies, waits for them, and re-layouts: 3.62 us -> 1.37 us  [shards(): jnp.stack([lax.dynamic_slice_in_dim(weight, which * half, half, axis=-1)...]
    unnamed x68 -> x58, local copies, waits for them, and re-layouts: 12.6 us -> 10.6 us
  transfers between devices with their start and end apart: 31 -> 32, of which waited for: 15 -> 18; matrix products, arithmetic and copies ran while one was open for 3% -> 0% of each run, Pallas kernels for 14% -> 14%
where the time goes in v8:
time: 186 us; the launch traced here: 185 us
  waiting for transfers between devices  68.2 us (37%)
  starting transfers between devices  48.3 us (26%)
  Pallas kernels  38.6 us (21%)
  blocking collectives  17.2 us (9%)
  local copies, waits for them, and re-layouts  12 us (6%)
    all_to_all x1, blocking collectives, shards(): lax.all_to_all(total.reshape(8, 16, half), ('z', 'xlo'), 0, 0, axis_index...  17.2 us
    all_to_all x1, waiting for transfers between devices, shards(): full = lax.all_to_all(spread_rows(by_copy, 16), ('z', 'xlo'), 0, 0)  16.4 us
    ppermute x3, waiting for transfers between devices, from_x_twin(): return lax.ppermute(value, ('xlo', 'core'), with_core_flip(CORE_SWAP))  13.3 us
    all_to_all x2, starting transfers between devices, over_fsdp(): lax.all_to_all(rows, ('xlo', 'y', 'xhi'), 0, 0, axis_index_groups=FSDP_GR...  12.2 us
    ppermute x5, starting transfers between devices, from_z_next(): return lax.ppermute(value, ('z', 'core'), with_core_flip(from_next(8)))  11.2 us
    all_to_all x2, waiting for transfers between devices, over_fsdp(): lax.all_to_all(rows, ('xlo', 'y', 'xhi'), 0, 0, axis_index_groups=FSDP_GR...  10.6 us
    unnamed x58, local copies, waits for them, and re-layouts  10.6 us
    ppermute x3, waiting for transfers between devices, from_x_near(): return lax.ppermute(value, ('xlo', 'xhi'), X_NEAR)  10.1 us
  transfers between devices with their start and end apart: 32, of which 18 were waited for; matrix products, arithmetic and copies ran while one was open for 0% of the time, Pallas kernels for 14%

profile of v8, /device:TPU:4, one launch (start us, length us, event | category | flops | bytes accessed | tf_op | source)
XLA Modules:
  0.0 185.5 jit_solution(9180942950116637483)
XLA Ops:
  8.3 8.5 %collective-permute-done.2.refs_3_ = bf16[2,128,1024]{2,1,0:T(8,128)(2,1)} collective-permute-done((bf16[2,128,1024]{2,1,0:T(8,128)(2,1)S(1)}, bf16[2,128,1024]{2,1,0:T(8,128)(2,1)}, u32[]{:S(2)}, u32[]{:S(2)}) %collective-permute-start.2) | collective-permute-done | bytes 524320 | tf_op jit(solution)/shard_map/ppermute | solution.py:54
  21.0 3.8 %collective-permute-start.9 = (bf16[2,128,1024]{2,1,0:T(8,128)(2,1)}, bf16[2,128,1024]{2,1,0:T(8,128)(2,1)}, u32[]{:S(2)}, u32[]{:S(2)}) collective-permute-start(bf16[2,128,1024]{2,1,0:T(8,128)(2,1)} %collective-permute-done.refs_1_), channel_id=1, source_target_pairs={{33,0},{32,1},{65,32},{64,33},{97,64},{96,65},{129,96},{128,97},{1... | collective-permute-start | bytes 1572872 | tf_op jit(solution)/shard_map/ppermute | solution.py:58
  30.9 4.6 %shard_map.129 = (bf16[576,1792]{1,0:T(8,128)(2,1)S(1)}, bf16[576,256]{1,0:T(8,128)(2,1)S(1)}, bf16[8,128,576]{2,1,0:T(8,128)(2,1)S(1)}, bf16[8,128,576]{2,1,0:T(8,128)(2,1)S(1)}) custom-call(s32[18]{0:T(128)S(1)} %stack.87.order, bf16[288,2048]{1,0:T(8,128)(2,1)S(1)} %copy-done.9, bf16[288,2048]{1,0:T(8,128)(2,1)S(1)} %copy-done.11), custom_call_target="tpu_custom_call" | custom-call | bytes 7340032 | tf_op jit(solution)/shard_map/pallas_call | solution.py:162
  41.9 4.8 %collective-permute-start.15 = (bf16[2,128,1024]{2,1,0:T(8,128)(2,1)}, bf16[2,128,1024]{2,1,0:T(8,128)(2,1)S(1)}, u32[]{:S(2)}, u32[]{:S(2)}) collective-permute-start(bf16[2,128,1024]{2,1,0:T(8,128)(2,1)} %collective-permute-done.2.refs_3_), channel_id=1, source_target_pairs={{1,16},{0,17},{17,0},{16,1},{3,18},{2,19},{19,2},{18,3},{5,20},{4,... | collective-permute-start | bytes 1572872 | tf_op jit(solution)/shard_map/ppermute | solution.py:66
  46.6 2.6 %collective-permute-start.11 = (bf16[2,128,1024]{2,1,0:T(8,128)(2,1)}, bf16[2,128,1024]{2,1,0:T(8,128)(2,1)S(1)}, u32[]{:S(2)}, u32[]{:S(2)}) collective-permute-start(bf16[2,128,1024]{2,1,0:T(8,128)(2,1)} %collective-permute-done.8.refs_6_), channel_id=1, source_target_pairs={{4,0},{8,4},{12,8},{0,12},{5,1},{9,5},{13,9},{1,13},{6,2},{10,6},{... | collective-permute-start | bytes 1572872 | tf_op jit(solution)/shard_map/ppermute | solution.py:46
  49.3 5.9 %shard_map.130 = (bf16[576,1792]{1,0:T(8,128)(2,1)S(1)}, bf16[576,256]{1,0:T(8,128)(2,1)S(1)}, bf16[288,2048]{1,0:T(8,128)(2,1)S(1)}) custom-call(s32[18]{0:T(128)S(1)} %stack.87.order, bf16[288,2048]{1,0:T(8,128)(2,1)S(1)} %copy-done.6, bf16[288,2048]{1,0:T(8,128)(2,1)S(1)} %copy-done.8, bf16[288,2048]{1,0:T(8,128)(2,1)S(1)} %copy-done.3, ...), custom_call_target="tpu_custom_call" | custom-call | flops 509607936 | bytes 9437184 | tf_op jit(solution)/shard_map/pallas_call | solution.py:192
  55.2 3.1 %collective-permute-done.15.refs_13_ = bf16[2,128,1024]{2,1,0:T(8,128)(2,1)S(1)} collective-permute-done((bf16[2,128,1024]{2,1,0:T(8,128)(2,1)}, bf16[2,128,1024]{2,1,0:T(8,128)(2,1)S(1)}, u32[]{:S(2)}, u32[]{:S(2)}) %collective-permute-start.15) | collective-permute-done | bytes 524320 | tf_op jit(solution)/shard_map/ppermute | solution.py:66
  58.3 2.9 %collective-permute-done.13.refs_11_ = bf16[2,128,1024]{2,1,0:T(8,128)(2,1)S(1)} collective-permute-done((bf16[2,128,1024]{2,1,0:T(8,128)(2,1)}, bf16[2,128,1024]{2,1,0:T(8,128)(2,1)S(1)}, u32[]{:S(2)}, u32[]{:S(2)}) %collective-permute-start.13) | collective-permute-done | bytes 524320 | tf_op jit(solution)/shard_map/ppermute | solution.py:62
  63.9 6.9 %shard_map.131 = (f32[576,1024]{1,0:T(8,128)S(1)}, f32[576,1024]{1,0:T(8,128)S(1)}) custom-call(bf16[576,1792]{1,0:T(8,128)(2,1)S(1)} %get-tuple-element.127.student_mix, bf16[576,1792]{1,0:T(8,128)(2,1)S(1)} %get-tuple-element.128.teacher_mix, bf16[2,128,1024]{2,1,0:T(8,128)(2,1)S(1)} %copy-done.15, bf16[2,128,1024]{2,1,0:T(8,128)(2,1)} %collective-permute-done.refs_1_, ...), custom_call_target="tpu_custom_call" | custom-call | flops 4227858432 | bytes 17825792 | tf_op jit(solution)/shard_map/pallas_call | solution.py:235
  70.9 4.9 %collective-permute-done.19.refs_1_ = bf16[2,128,1024]{2,1,0:T(8,128)(2,1)S(1)} collective-permute-done((bf16[2,128,1024]{2,1,0:T(8,128)(2,1)S(1)}, bf16[2,128,1024]{2,1,0:T(8,128)(2,1)S(1)}, u32[]{:S(2)}, u32[]{:S(2)}) %collective-permute-start.19) | collective-permute-done | bytes 524320 | tf_op jit(solution)/shard_map/ppermute | solution.py:58
  75.8 4.0 %shard_map.132 = (f32[576,1024]{1,0:T(8,128)S(1)}, f32[576,1024]{1,0:T(8,128)S(1)}, f32[576,128]{1,0:T(8,128)S(1)}) custom-call(s32[18]{0:T(128)S(1)} %stack.87.order, bf16[576,256]{1,0:T(8,128)(2,1)S(1)} %copy-done.17, bf16[576,256]{1,0:T(8,128)(2,1)S(1)} %get-tuple-element.126.teacher_mix, f32[576,1024]{1,0:T(8,128)S(1)} %get-tuple-element.136.student_part, ...), custom_call_target="tpu_custom_call" | custom-call | flops 603979776 | bytes 13631488 | tf_op jit(solution)/shard_map/pallas_call | solution.py:291
  81.4 2.7 %shard_map.133 = (bf16[3,128,512]{2,1,0:T(8,128)(2,1)S(1)}, bf16[3,128,512]{2,1,0:T(8,128)(2,1)S(1)}, bf16[2,128,512]{2,1,0:T(8,128)(2,1)S(1)}, bf16[576,512]{1,...) custom-call(s32[18]{0:T(128)S(1)} %stack.87.order, ...), custom_call_target="tpu_custom_call" | custom-call | flops 603979776 | bytes 6291456 | tf_op jit(solution)/shard_map/pallas_call | solution.py:357
  84.9 3.1 %collective-permute-start.22 = (bf16[3,128,512]{2,1,0:T(8,128)(2,1)S(1)}, bf16[3,128,512]{2,1,0:T(8,128)(2,1)S(1)}, u32[]{:S(2)}, u32[]{:S(2)}) collective-permute-start(bf16[3,128,512]{2,1,0:T(8,128)(2,1)S(1)} %get-tuple-element.149), channel_id=1, source_target_pairs={{33,0},{32,1},{65,32},{64,33},{97,64},{96,65},{129,96},{128,97},{1... | collective-permute-start | bytes 1179656 | tf_op jit(solution)/shard_map/ppermute | solution.py:58
  88.0 2.7 %shard_map.135 = (bf16[3,128,512]{2,1,0:T(8,128)(2,1)S(1)}, bf16[3,128,512]{2,1,0:T(8,128)(2,1)S(1)}, bf16[2,128,512]{2,1,0:T(8,128)(2,1)S(1)}, bf16[576,512]{1,...) custom-call(s32[18]{0:T(128)S(1)} %stack.87.order, ...), custom_call_target="tpu_custom_call" | custom-call | flops 603979776 | bytes 6291456 | tf_op jit(solution)/shard_map/pallas_call | solution.py:357
  93.6 2.6 %collective-permute-done.23.refs_2_ = bf16[2,128,512]{2,1,0:T(8,128)(2,1)S(1)} collective-permute-done((bf16[2,128,512]{2,1,0:T(8,128)(2,1)S(1)}, bf16[2,128,512]{2,1,0:T(8,128)(2,1)S(1)}, u32[]{:S(2)}, u32[]{:S(2)}) %collective-permute-start.23) | collective-permute-done | bytes 262176 | tf_op jit(solution)/shard_map/ppermute | solution.py:66
  98.8 6.3 %all-to-all-start = ((bf16[8,128,512]{2,1,0:T(8,128)(2,1)}), bf16[8,128,512]{2,1,0:T(8,128)(2,1)}, u32[]{:S(2)}, u32[]{:S(2)}) async-start(bf16[8,128,512]{2,1,0:T(8,128)(2,1)} %copy-done.4), calls=%async_computation | async-start | bytes 2097152 | tf_op jit(solution)/shard_map/all_to_all | solution.py:623
  109.0 7.6 %collective-permute-done.26.refs_2_ = bf16[2,128,512]{2,1,0:T(8,128)(2,1)S(1)} collective-permute-done((bf16[2,128,512]{2,1,0:T(8,128)(2,1)}, bf16[2,128,512]{2,1,0:T(8,128)(2,1)S(1)}, u32[]{:S(2)}, u32[]{:S(2)}) %collective-permute-start.26) | collective-permute-done | bytes 262176 | tf_op jit(solution)/shard_map/ppermute | solution.py:66
  120.1 5.8 %all-to-all-start.1 = ((bf16[8,128,512]{2,1,0:T(8,128)(2,1)}), bf16[8,128,512]{2,1,0:T(8,128)(2,1)S(1)}, u32[]{:S(2)}, u32[]{:S(2)}) async-start(bf16[8,128,512]{2,1,0:T(8,128)(2,1)} %copy-done.5), calls=%async_computation.1 | async-start | bytes 2097152 | tf_op jit(solution)/shard_map/all_to_all | solution.py:623
  128.0 2.2 %shard_map.139 = bf16[288,2048]{1,0:T(8,128)(2,1)} custom-call(s32[18]{0:T(128)S(1)} %stack.87.order, bf16[288,512]{1,0:T(8,128)(2,1)S(1)} %get-tuple-element.166.first_own, bf16[288,512]{1,0:T(8,128)(2,1)S(1)} %copy-done.19, bf16[288,512]{1,0:T(8,128)(2,1)S(1)} %collective-permute-done.27.first_other, bf16[288,512]{1,0:T(8,128)(2,1)S(1)} %collective-permute-done.28.last_other), custom_call_target="tpu_custom_call" | custom-call | bytes 2457600 | tf_op jit(solution)/shard_map/pallas_call | solution.py:446
  130.2 10.6 %all-to-all-done.1.last = bf16[8,128,512]{2,1,0:T(8,128)(2,1)S(1)} async-done(((bf16[8,128,512]{2,1,0:T(8,128)(2,1)}), bf16[8,128,512]{2,1,0:T(8,128)(2,1)S(1)}, u32[]{:S(2)}, u32[]{:S(2)}) %all-to-all-start.1) | async-done | bytes 1048608 | tf_op jit(solution)/shard_map/all_to_all | solution.py:623
  142.2 17.2 %all_to_all.20.copies = bf16[8,16,1024]{2,1,0:T(8,128)(2,1)S(1)} all-to-all(bf16[8,16,1024]{2,1,0:T(8,128)(2,1)S(1)} %bitcast.27), channel_id=1, replica_groups={{0,48,64,112,128,176,192,240},{16,32,80,96,144,160,208,224},{1,49,65,11..., dimensions={0} | all-to-all | bytes 524288 | tf_op jit(solution)/shard_map/all_to_all | solution.py:638
  160.3 3.6 %all-to-all-start.3 = ((bf16[16,16,1024]{2,1,0:T(8,128)(2,1)}), bf16[16,16,1024]{2,1,0:T(8,128)(2,1)S(1)}, u32[]{:S(2)}, u32[]{:S(2)}) async-start(bf16[16,16,1024]{2,1,0:T(8,128)(2,1)} %shard_map.141), calls=%async_computation.3 | async-start | bytes 1048576 | tf_op jit(solution)/shard_map/all_to_all | solution.py:641
  163.9 16.4 %all-to-all-done.3 = bf16[16,16,1024]{2,1,0:T(8,128)(2,1)S(1)} async-done(((bf16[16,16,1024]{2,1,0:T(8,128)(2,1)}), bf16[16,16,1024]{2,1,0:T(8,128)(2,1)S(1)}, u32[]{:S(2)}, u32[]{:S(2)}) %all-to-all-start.3) | async-done | bytes 524320 | tf_op jit(solution)/shard_map/all_to_all | solution.py:641
  182.7 2.7 %shard_map.142 = (f32[128,2048]{1,0:T(8,128)}, f32[128,2048]{1,0:T(8,128)}, f32[128,2048]{1,0:T(8,128)}, f32[128,2048]{1,0:T(8,128)}) custom-call(s32[1]{0:T(128)} %bitcast.flip, bf16[8,2,16,1024]{3,2,1,0:T(8,128)(2,1)S(1)} %bitcast.26, f32[128,2048]{1,0:T(8,128)S(1)} %copy-done, f32[128,2048]{1,0:T(8,128)S(1)} %copy-done.2, f32[128,2048]{1,0:T(8,128)S(1)} %copy-done.12, ...), custom_call_target="tpu_custom_call" | custom-call | tf_op jit(solution)/shard_map/pallas_call | solution.py:520
  (117 shorter events, 48.7 us)
Async XLA Ops:
  2.2 16.1 %collective-permute-start.4 = (bf16[288,2048]{1,0:T(8,128)(2,1)S(1)}, bf16[288,2048]{1,0:T(8,128)(2,1)S(1)}, u32[]{:S(2)}, u32[]{:S(2)}) collective-permute-start(bf16[288,2048]{1,0:T(8,128)(2,1)S(1)} %copy-done.6), channel_id=1, source_target_pairs={{0,1},{1,0},{2,3},{3,2},{4,5},{5,4},{6,7},{7,6},{8,9},{9,8},{10,11... | collective-permute-start | bytes 3538952 | tf_op jit(solution)/shard_map/ppermute | solution.py:42
  2.7 14.0 %collective-permute-start.2 = (bf16[2,128,1024]{2,1,0:T(8,128)(2,1)S(1)}, bf16[2,128,1024]{2,1,0:T(8,128)(2,1)}, u32[]{:S(2)}, u32[]{:S(2)}) collective-permute-start(bf16[2,128,1024]{2,1,0:T(8,128)(2,1)S(1)} %pad_maximum_fusion.refs_0_), channel_id=1, source_target_pairs={{16,2},{2,16},{0,18},{18,0},{17,3},{3,17},{1,19},{19,1},{20,6},{6,... | collective-permute-start | bytes 1572872 | tf_op jit(solution)/shard_map/ppermute | solution.py:54
  3.3 15.0 %collective-permute-start.1 = (bf16[2,128,1024]{2,1,0:T(8,128)(2,1)S(1)}, bf16[2,128,1024]{2,1,0:T(8,128)(2,1)}, u32[]{:S(2)}, u32[]{:S(2)}) collective-permute-start(bf16[2,128,1024]{2,1,0:T(8,128)(2,1)S(1)} %pad_maximum_fusion.refs_0_), channel_id=1, source_target_pairs={{0,4},{4,8},{8,12},{12,0},{1,5},{5,9},{9,13},{13,1},{2,6},{6,10},{... | collective-permute-start | bytes 1572872 | tf_op jit(solution)/shard_map/ppermute | solution.py:50
  4.8 13.5 %collective-permute-start = (bf16[2,128,1024]{2,1,0:T(8,128)(2,1)S(1)}, bf16[2,128,1024]{2,1,0:T(8,128)(2,1)}, u32[]{:S(2)}, u32[]{:S(2)}) collective-permute-start(bf16[2,128,1024]{2,1,0:T(8,128)(2,1)S(1)} %pad_maximum_fusion.refs_0_), channel_id=1, source_target_pairs={{4,0},{8,4},{12,8},{0,12},{5,1},{9,5},{13,9},{1,13},{6,2},{10,6},{... | collective-permute-start | bytes 1572872 | tf_op jit(solution)/shard_map/ppermute | solution.py:46
  19.4 17.1 %collective-permute-start.7 = (bf16[2,128,1024]{2,1,0:T(8,128)(2,1)}, bf16[2,128,1024]{2,1,0:T(8,128)(2,1)}, u32[]{:S(2)}, u32[]{:S(2)}) collective-permute-start(bf16[2,128,1024]{2,1,0:T(8,128)(2,1)} %collective-permute-done.2.refs_3_), channel_id=1, source_target_pairs={{0,4},{4,8},{8,12},{12,0},{1,5},{5,9},{9,13},{13,1},{2,6},{6,10},{... | collective-permute-start | bytes 1572872 | tf_op jit(solution)/shard_map/ppermute | solution.py:50
  21.0 15.5 %collective-permute-start.10 = (bf16[2,128,1024]{2,1,0:T(8,128)(2,1)}, bf16[2,128,1024]{2,1,0:T(8,128)(2,1)}, u32[]{:S(2)}, u32[]{:S(2)}) collective-permute-start(bf16[2,128,1024]{2,1,0:T(8,128)(2,1)} %collective-permute-done.1.refs_2_), channel_id=1, source_target_pairs={{1,32},{0,33},{33,64},{32,65},{65,96},{64,97},{97,128},{96,129},{1... | collective-permute-start | bytes 1572872 | tf_op jit(solution)/shard_map/ppermute | solution.py:62
  21.0 16.0 %collective-permute-start.9 = (bf16[2,128,1024]{2,1,0:T(8,128)(2,1)}, bf16[2,128,1024]{2,1,0:T(8,128)(2,1)}, u32[]{:S(2)}, u32[]{:S(2)}) collective-permute-start(bf16[2,128,1024]{2,1,0:T(8,128)(2,1)} %collective-permute-done.refs_1_), channel_id=1, source_target_pairs={{33,0},{32,1},{65,32},{64,33},{97,64},{96,65},{129,96},{128,97},{1... | collective-permute-start | bytes 1572872 | tf_op jit(solution)/shard_map/ppermute | solution.py:58
  24.8 13.9 %collective-permute-start.8 = (bf16[2,128,1024]{2,1,0:T(8,128)(2,1)}, bf16[2,128,1024]{2,1,0:T(8,128)(2,1)}, u32[]{:S(2)}, u32[]{:S(2)}) collective-permute-start(bf16[2,128,1024]{2,1,0:T(8,128)(2,1)} %collective-permute-done.refs_1_), channel_id=1, source_target_pairs={{16,2},{2,16},{0,18},{18,0},{17,3},{3,17},{1,19},{19,1},{20,6},{6,... | collective-permute-start | bytes 1572872 | tf_op jit(solution)/shard_map/ppermute | solution.py:54
  26.3 14.2 %collective-permute-start.6 = (bf16[2,128,1024]{2,1,0:T(8,128)(2,1)}, bf16[2,128,1024]{2,1,0:T(8,128)(2,1)}, u32[]{:S(2)}, u32[]{:S(2)}) collective-permute-start(bf16[2,128,1024]{2,1,0:T(8,128)(2,1)} %collective-permute-done.refs_1_), channel_id=1, source_target_pairs={{4,0},{8,4},{12,8},{0,12},{5,1},{9,5},{13,9},{1,13},{6,2},{10,6},{... | collective-permute-start | bytes 1572872 | tf_op jit(solution)/shard_map/ppermute | solution.py:46
  40.5 14.7 %collective-permute-start.12 = (bf16[2,128,1024]{2,1,0:T(8,128)(2,1)}, bf16[2,128,1024]{2,1,0:T(8,128)(2,1)S(1)}, u32[]{:S(2)}, u32[]{:S(2)}) collective-permute-start(bf16[2,128,1024]{2,1,0:T(8,128)(2,1)} %collective-permute-done.6.refs_4_), channel_id=1, source_target_pairs={{33,0},{32,1},{65,32},{64,33},{97,64},{96,65},{129,96},{128,97},{1... | collective-permute-start | bytes 1572872 | tf_op jit(solution)/shard_map/ppermute | solution.py:58
  41.1 14.1 %collective-permute-start.14 = (bf16[2,128,1024]{2,1,0:T(8,128)(2,1)}, bf16[2,128,1024]{2,1,0:T(8,128)(2,1)S(1)}, u32[]{:S(2)}, u32[]{:S(2)}) collective-permute-start(bf16[2,128,1024]{2,1,0:T(8,128)(2,1)} %collective-permute-done.10.refs_8_), channel_id=1, source_target_pairs={{16,2},{2,16},{0,18},{18,0},{17,3},{3,17},{1,19},{19,1},{20,6},{6,... | collective-permute-start | bytes 1572872 | tf_op jit(solution)/shard_map/ppermute | solution.py:54
  41.9 16.4 %collective-permute-start.15 = (bf16[2,128,1024]{2,1,0:T(8,128)(2,1)}, bf16[2,128,1024]{2,1,0:T(8,128)(2,1)S(1)}, u32[]{:S(2)}, u32[]{:S(2)}) collective-permute-start(bf16[2,128,1024]{2,1,0:T(8,128)(2,1)} %collective-permute-done.2.refs_3_), channel_id=1, source_target_pairs={{1,16},{0,17},{17,0},{16,1},{3,18},{2,19},{19,2},{18,3},{5,20},{4,... | collective-permute-start | bytes 1572872 | tf_op jit(solution)/shard_map/ppermute | solution.py:66
  46.6 14.6 %collective-permute-start.13 = (bf16[2,128,1024]{2,1,0:T(8,128)(2,1)}, bf16[2,128,1024]{2,1,0:T(8,128)(2,1)S(1)}, u32[]{:S(2)}, u32[]{:S(2)}) collective-permute-start(bf16[2,128,1024]{2,1,0:T(8,128)(2,1)} %collective-permute-done.8.refs_6_), channel_id=1, source_target_pairs={{1,32},{0,33},{33,64},{32,65},{65,96},{64,97},{97,128},{96,129},{1... | collective-permute-start | bytes 1572872 | tf_op jit(solution)/shard_map/ppermute | solution.py:62
  46.6 14.6 %collective-permute-start.11 = (bf16[2,128,1024]{2,1,0:T(8,128)(2,1)}, bf16[2,128,1024]{2,1,0:T(8,128)(2,1)S(1)}, u32[]{:S(2)}, u32[]{:S(2)}) collective-permute-start(bf16[2,128,1024]{2,1,0:T(8,128)(2,1)} %collective-permute-done.8.refs_6_), channel_id=1, source_target_pairs={{4,0},{8,4},{12,8},{0,12},{5,1},{9,5},{13,9},{1,13},{6,2},{10,6},{... | collective-permute-start | bytes 1572872 | tf_op jit(solution)/shard_map/ppermute | solution.py:46
  61.2 14.6 %collective-permute-start.16 = (bf16[288,2048]{1,0:T(8,128)(2,1)S(1)}, bf16[288,2048]{1,0:T(8,128)(2,1)S(1)}, u32[]{:S(2)}, u32[]{:S(2)}) collective-permute-start(bf16[288,2048]{1,0:T(8,128)(2,1)S(1)} %copy-done.3), channel_id=1, source_target_pairs={{0,1},{1,0},{2,3},{3,2},{4,5},{5,4},{6,7},{7,6},{8,9},{9,8},{10,11... | collective-permute-start | bytes 3538952 | tf_op jit(solution)/shard_map/ppermute | solution.py:42
  61.3 14.5 %collective-permute-start.17 = (bf16[288,2048]{1,0:T(8,128)(2,1)S(1)}, bf16[288,2048]{1,0:T(8,128)(2,1)S(1)}, u32[]{:S(2)}, u32[]{:S(2)}) collective-permute-start(bf16[288,2048]{1,0:T(8,128)(2,1)S(1)} %get-tuple-element.139.picked_own), channel_id=1, source_target_pairs={{0,1},{1,0},{2,3},{3,2},{4,5},{5,4},{6,7},{7,6},{8,9},{9,8},{10,11... | collective-permute-start | bytes 3538952 | tf_op jit(solution)/shard_map/ppermute | solution.py:42
  61.9 13.9 %collective-permute-start.19 = (bf16[2,128,1024]{2,1,0:T(8,128)(2,1)S(1)}, bf16[2,128,1024]{2,1,0:T(8,128)(2,1)S(1)}, u32[]{:S(2)}, u32[]{:S(2)}) collective-permute-start(bf16[2,128,1024]{2,1,0:T(8,128)(2,1)S(1)} %collective-permute-done.11.refs_9_), channel_id=1, source_target_pairs={{33,0},{32,1},{65,32},{64,33},{97,64},{96,65},{129,96},{128,97},{1... | collective-permute-start | bytes 1572872 | tf_op jit(solution)/shard_map/ppermute | solution.py:58
  84.9 12.4 %collective-permute-start.21 = (bf16[3,128,512]{2,1,0:T(8,128)(2,1)S(1)}, bf16[3,128,512]{2,1,0:T(8,128)(2,1)S(1)}, u32[]{:S(2)}, u32[]{:S(2)}) collective-permute-start(bf16[3,128,512]{2,1,0:T(8,128)(2,1)S(1)} %get-tuple-element.148), channel_id=1, source_target_pairs={{1,32},{0,33},{33,64},{32,65},{65,96},{64,97},{97,128},{96,129},{1... | collective-permute-start | bytes 1179656 | tf_op jit(solution)/shard_map/ppermute | solution.py:62
  84.9 12.4 %collective-permute-start.22 = (bf16[3,128,512]{2,1,0:T(8,128)(2,1)S(1)}, bf16[3,128,512]{2,1,0:T(8,128)(2,1)S(1)}, u32[]{:S(2)}, u32[]{:S(2)}) collective-permute-start(bf16[3,128,512]{2,1,0:T(8,128)(2,1)S(1)} %get-tuple-element.149), channel_id=1, source_target_pairs={{33,0},{32,1},{65,32},{64,33},{97,64},{96,65},{129,96},{128,97},{1... | collective-permute-start | bytes 1179656 | tf_op jit(solution)/shard_map/ppermute | solution.py:58
  98.8 21.4 %all-to-all-start = ((bf16[8,128,512]{2,1,0:T(8,128)(2,1)}), bf16[8,128,512]{2,1,0:T(8,128)(2,1)}, u32[]{:S(2)}, u32[]{:S(2)}) async-start(bf16[8,128,512]{2,1,0:T(8,128)(2,1)} %copy-done.4), calls=%async_computation | async-start | bytes 2097152 | tf_op jit(solution)/shard_map/all_to_all | solution.py:623
  105.1 12.5 %collective-permute-start.24 = (bf16[3,128,512]{2,1,0:T(8,128)(2,1)}, bf16[3,128,512]{2,1,0:T(8,128)(2,1)S(1)}, u32[]{:S(2)}, u32[]{:S(2)}) collective-permute-start(bf16[3,128,512]{2,1,0:T(8,128)(2,1)} %copy-done.23), channel_id=1, source_target_pairs={{1,32},{0,33},{33,64},{32,65},{65,96},{64,97},{97,128},{96,129},{1... | collective-permute-start | bytes 1179656 | tf_op jit(solution)/shard_map/ppermute | solution.py:62
  106.4 12.2 %collective-permute-start.25 = (bf16[3,128,512]{2,1,0:T(8,128)(2,1)}, bf16[3,128,512]{2,1,0:T(8,128)(2,1)S(1)}, u32[]{:S(2)}, u32[]{:S(2)}) collective-permute-start(bf16[3,128,512]{2,1,0:T(8,128)(2,1)} %copy-done.22), channel_id=1, source_target_pairs={{33,0},{32,1},{65,32},{64,33},{97,64},{96,65},{129,96},{128,97},{1... | collective-permute-start | bytes 1179656 | tf_op jit(solution)/shard_map/ppermute | solution.py:58
  120.1 20.7 %all-to-all-start.1 = ((bf16[8,128,512]{2,1,0:T(8,128)(2,1)}), bf16[8,128,512]{2,1,0:T(8,128)(2,1)S(1)}, u32[]{:S(2)}, u32[]{:S(2)}) async-start(bf16[8,128,512]{2,1,0:T(8,128)(2,1)} %copy-done.5), calls=%async_computation.1 | async-start | bytes 2097152 | tf_op jit(solution)/shard_map/all_to_all | solution.py:623
  160.3 20.0 %all-to-all-start.3 = ((bf16[16,16,1024]{2,1,0:T(8,128)(2,1)}), bf16[16,16,1024]{2,1,0:T(8,128)(2,1)S(1)}, u32[]{:S(2)}, u32[]{:S(2)}) async-start(bf16[16,16,1024]{2,1,0:T(8,128)(2,1)} %shard_map.141), calls=%async_computation.3 | async-start | bytes 1048576 | tf_op jit(solution)/shard_map/all_to_all | solution.py:641
  (37 other events, 281.2 us)

commit v9 on v8

--- a/solution.py
+++ b/solution.py
@@ -75,7 +75,8 @@
 HALF_AT = len(ORDER)
 CORE_AT = HALF_AT + 1
 SENT = (3, 3, 2)
-PARTS = 2
+TILE = 256
+PARTS = (3, 1)
 
 
 def split_kernel(order, student, teacher, out):
@@ -347,13 +348,12 @@
 
 
 def send_grads(total_tokens, part, order, student, matched, sums, more_sums, scale, turned):
-    (rows, columns), width = student.shape, 256
-    steps = columns // width
-    count = steps // PARTS
-    column = pl.BlockSpec((rows, width), lambda j, order: (0, part * count + j))
+    rows, columns = student.shape
+    steps, count, first = columns // TILE, PARTS[part], sum(PARTS[:part])
+    column = pl.BlockSpec((rows, TILE), lambda j, order: (0, first + j))
     narrow = pl.BlockSpec((rows, 128), lambda j, order: (0, 0))
-    out = pl.BlockSpec((rows, width), lambda j, order: (0, j))
-    half = pl.BlockSpec((rows // 2, width), lambda j, order: (0, j))
+    out = pl.BlockSpec((rows, TILE), lambda j, order: (0, j))
+    half = pl.BlockSpec((rows // 2, TILE), lambda j, order: (0, j))
     return pl.pallas_call(
         functools.partial(send_kernel, total_tokens),
         grid_spec=pltpu.PrefetchScalarGridSpec(
@@ -364,21 +364,21 @@
                 column,
                 narrow,
                 narrow,
-                pl.BlockSpec((1, width), lambda j, order: (0, order[HALF_AT] * steps + part * count + j)),
+                pl.BlockSpec((1, TILE), lambda j, order: (0, order[HALF_AT] * steps + first + j)),
                 pl.BlockSpec((8, 128, rows), lambda j, order: (0, 0, 0)),
             ],
-            out_specs=[pl.BlockSpec((size, 128, width), lambda j, order: (0, 0, j)) for size in SENT]
+            out_specs=[pl.BlockSpec((size, 128, TILE), lambda j, order: (0, 0, j)) for size in SENT]
             + [out, half, half],
         ),
-        out_shape=[jax.ShapeDtypeStruct((size, 128, columns // PARTS), jnp.bfloat16) for size in SENT]
+        out_shape=[jax.ShapeDtypeStruct((size, 128, count * TILE), jnp.bfloat16) for size in SENT]
         + [
-            jax.ShapeDtypeStruct((rows, columns // PARTS), jnp.bfloat16),
-            jax.ShapeDtypeStruct((rows // 2, columns // PARTS), jnp.bfloat16),
-            jax.ShapeDtypeStruct((rows // 2, columns // PARTS), jnp.bfloat16),
+            jax.ShapeDtypeStruct((rows, count * TILE), jnp.bfloat16),
+            jax.ShapeDtypeStruct((rows // 2, count * TILE), jnp.bfloat16),
+            jax.ShapeDtypeStruct((rows // 2, count * TILE), jnp.bfloat16),
         ],
         compiler_params=pltpu.CompilerParams(vmem_limit_bytes=VMEM_LIMIT),
         cost_estimate=pl.CostEstimate(
-            flops=rows * KIN * columns // PARTS, bytes_accessed=6 * 1024 * 1024, transcendentals=0
+            flops=rows * KIN * count * TILE, bytes_accessed=3 * count * 1024 * 1024, transcendentals=0
         ),
     )(order, student, matched, sums, more_sums, scale, turned)
 
@@ -434,47 +434,52 @@
 
 
 def join_kernel(order, first_own, last_own, first_other, last_other, out):
-    step = pl.program_id(0)
-    for at, half in enumerate((first_own, last_own, first_other, last_other)):
-        @pl.when(step == (at ^ (2 * order[HALF_AT])))
+    step, width = pl.program_id(0), first_own.shape[1]
+    for at, (first, last) in enumerate(((first_own, last_own), (first_other, last_other))):
+        @pl.when(step == (at ^ order[HALF_AT]))
         def _():
-            out[...] = half[...]
-
-
-def join_tokens(order, *halves):
-    rows, width = halves[0].shape
+            out[:, :width] = first[...]
+            out[:, width:] = last[...]
+
+
+def join_tokens(order, first_own, last_own, first_other, last_other):
+    rows, half = first_own.shape[0], first_own.shape[1] + last_own.shape[1]
+    first = pl.BlockSpec(first_own.shape, lambda j, order: (0, 0))
+    last = pl.BlockSpec(last_own.shape, lambda j, order: (0, 0))
     return pl.pallas_call(
         join_kernel,
         grid_spec=pltpu.PrefetchScalarGridSpec(
             num_scalar_prefetch=1,
-            grid=(4,),
-            in_specs=[pl.BlockSpec((rows, width), lambda j, order: (0, 0))] * 4,
-            out_specs=pl.BlockSpec((rows, width), lambda j, order: (0, j)),
-        ),
-        out_shape=jax.ShapeDtypeStruct((rows, 4 * width), jnp.bfloat16),
+            grid=(2,),
+            in_specs=[first, last, first, last],
+            out_specs=pl.BlockSpec((rows, half), lambda j, order: (0, j)),
+        ),
+        out_shape=jax.ShapeDtypeStruct((rows, 2 * half), jnp.bfloat16),
         compiler_params=pltpu.CompilerParams(vmem_limit_bytes=SMALL_LIMIT),
         cost_estimate=pl.CostEstimate(flops=0, bytes_accessed=2400 * 1024, transcendentals=0),
-    )(order, *halves)
+    )(order, first_own, last_own, first_other, last_other)
 
 
 def total_kernel(first, last, out):
-    width = first.shape[-1]
-    for at, chips in enumerate((first, last)):
+    at = 0
+    for chips in (first, last):
         total = chips[0].astype(jnp.float32)
         for chip in range(1, chips.shape[0]):
             total = total + chips[chip].astype(jnp.float32)
-        out[:, at * width : (at + 1) * width] = total.astype(jnp.bfloat16)
+        out[:, at : at + total.shape[1]] = total.astype(jnp.bfloat16)
+        at += total.shape[1]
 
 
 def total_rows(first, last):
-    chips, rows, width = first.shape
-    block = pl.BlockSpec((chips, rows // 2, width), lambda i: (0, i, 0))
+    chips, rows, _ = first.shape
+    parts = [pl.BlockSpec((chips, rows // 2, part.shape[-1]), lambda i: (0, i, 0)) for part in (first, last)]
+    columns = first.shape[-1] + last.shape[-1]
     return pl.pallas_call(
         total_kernel,
         grid=(2,),
-        in_specs=[block, block],
-        out_specs=pl.BlockSpec((rows // 2, 2 * width), lambda i: (i, 0)),
-        out_shape=jax.ShapeDtypeStruct((rows, 2 * width), jnp.bfloat16),
+        in_specs=parts,
+        out_specs=pl.BlockSpec((rows // 2, columns), lambda i: (i, 0)),
+        out_shape=jax.ShapeDtypeStruct((rows, columns), jnp.bfloat16),
         compiler_params=pltpu.CompilerParams(vmem_limit_bytes=SMALL_LIMIT),
         cost_estimate=pl.CostEstimate(flops=0, bytes_accessed=2400 * 1024, transcendentals=0),
     )(first, last)
@@ -495,6 +500,24 @@
         compiler_params=pltpu.CompilerParams(vmem_limit_bytes=SMALL_LIMIT),
         cost_estimate=pl.CostEstimate(flops=0, bytes_accessed=800 * 1024, transcendentals=0),
     )(copies)
+
+
+def moments_kernel(first, squares, first_out, squares_out):
+    first_out[...] = 0.9 * first[...]
+    squares_out[...] = 0.95 * squares[...]
+
+
+def scale_moments(first, squares):
+    rows = pl.BlockSpec((64, DOUT), lambda i: (i, 0))
+    return pl.pallas_call(
+        moments_kernel,
+        grid=(2,),
+        in_specs=[rows, rows],
+        out_specs=[rows, rows],
+        out_shape=[jax.ShapeDtypeStruct(first.shape, jnp.float32)] * 2,
+        compiler_params=pltpu.CompilerParams(vmem_limit_bytes=SMALL_LIMIT),
+        cost_estimate=pl.CostEstimate(flops=0, bytes_accessed=4 * 1024 * 1024, transcendentals=0),
+    )(first, squares)
 
 
 def update_kernel(flip, grads, weight, teacher, first, squares, weight_out, teacher_out, first_out, squares_out):
@@ -505,8 +528,8 @@
         right = jnp.where(swap, grads[index, 0], grads[index, 1])
         rows.append(jnp.concatenate([left, right], axis=1))
     grad = jnp.concatenate(rows, axis=0).astype(jnp.float32)
-    first_next = 0.9 * first[...] + 0.1 * grad
-    squares_next = 0.95 * squares[...] + 0.05 * grad * grad
+    first_next = first[...] + 0.1 * grad
+    squares_next = squares[...] + 0.05 * grad * grad
     held = weight[...]
     weight_next = held - 0.1 * (first_next / (jnp.sqrt(squares_next) + 1e-08) + 0.04 * held)
     weight_out[...] = weight_next
@@ -633,7 +656,11 @@
     first_chip, last_rows = lax.optimization_barrier((over_fsdp(first_rows), add_passed(last_kept, last_passed)))
     last_chip = over_fsdp(last_rows)
     student_tokens = join_tokens(order, first_own, last_own, *swapped)
-    first_chip, last_chip, student_tokens = lax.optimization_barrier((first_chip, last_chip, student_tokens))
+    moment_held, second_held, first_chip = lax.optimization_barrier((moment, second, first_chip))
+    moments = scale_moments(moment_held, second_held)
+    first_chip, last_chip, student_tokens, moments = lax.optimization_barrier(
+        (first_chip, last_chip, student_tokens, moments)
+    )
     total = total_rows(first_chip, last_chip)
     by_copy = lax.all_to_all(
         total.reshape(8, 16, half), ("z", "xlo"), 0, 0, axis_index_groups=DP_GROUPS
@@ -641,7 +668,7 @@
     full = lax.all_to_all(spread_rows(by_copy, 16), ("z", "xlo"), 0, 0)
     flip = ((core + xhi) & 1).astype(jnp.int32).reshape(1)
     weight_next, teacher_next, first_next, squares_next = adamw_update(
-        flip, full.reshape(8, 2, 16, half), student_weight, teacher_weight, moment, second
+        flip, full.reshape(8, 2, 16, half), student_weight, teacher_weight, *moments
     )
     return (weight_next, teacher_next, first_next, squares_next, student_tokens)
 

time: 186 us -> 190 us (1.022); the launches traced: 185 us -> 186 us
  local copies, waits for them, and re-layouts: 12 us -> 14.2 us
    unnamed x58 -> x60, local copies, waits for them, and re-layouts: 10.6 us -> 12.8 us
    pallas_call x2, Pallas kernels: 1.02 us -> 3 us  [add_passed(): pl.pallas_call(add_kernel, grid=(kept.shape[-1] // width,), in_specs=[blo...]
  transfers between devices with their start and end apart: 32 -> 32, of which waited for: 18 -> 17; matrix products, arithmetic and copies ran while one was open for 0% -> 0% of each run, Pallas kernels for 14% -> 13%
where the time goes in v9:
time: 190 us; the launch traced here: 186 us
  waiting for transfers between devices  67.3 us (35%)
  starting transfers between devices  47.2 us (25%)
  Pallas kernels  38.9 us (20%)
  blocking collectives  17.4 us (9%)
  local copies, waits for them, and re-layouts  14.2 us (7%)
    all_to_all x1, blocking collectives, shards(): lax.all_to_all(total.reshape(8, 16, half), ('z', 'xlo'), 0, 0, axis_index...  17.4 us
    all_to_all x1, waiting for transfers between devices, shards(): full = lax.all_to_all(spread_rows(by_copy, 16), ('z', 'xlo'), 0, 0)  14.6 us
    ppermute x3, waiting for transfers between devices, from_x_twin(): return lax.ppermute(value, ('xlo', 'core'), with_core_flip(CORE_SWAP))  13 us
    unnamed x60, local copies, waits for them, and re-layouts  12.8 us
    ppermute x5, starting transfers between devices, from_z_next(): return lax.ppermute(value, ('z', 'core'), with_core_flip(from_next(8)))  11.4 us
    all_to_all x2, starting transfers between devices, over_fsdp(): lax.all_to_all(rows, ('xlo', 'y', 'xhi'), 0, 0, axis_index_groups=FSDP_GR...  11.1 us
    ppermute x3, waiting for transfers between devices, from_x_near(): return lax.ppermute(value, ('xlo', 'xhi'), X_NEAR)  10.9 us
    all_to_all x2, waiting for transfers between devices, over_fsdp(): lax.all_to_all(rows, ('xlo', 'y', 'xhi'), 0, 0, axis_index_groups=FSDP_GR...  10.9 us
  transfers between devices with their start and end apart: 32, of which 17 were waited for; matrix products, arithmetic and copies ran while one was open for 0% of the time, Pallas kernels for 13%

profile of v9, /device:TPU:4, one launch (start us, length us, event | category | flops | bytes accessed | tf_op | source)
XLA Modules:
  0.0 186.1 jit_solution(12951087461403371400)
XLA Ops:
  7.5 9.2 %collective-permute-done.2.refs_3_ = bf16[2,128,1024]{2,1,0:T(8,128)(2,1)} collective-permute-done((bf16[2,128,1024]{2,1,0:T(8,128)(2,1)S(1)}, bf16[2,128,1024]{2,1,0:T(8,128)(2,1)}, u32[]{:S(2)}, u32[]{:S(2)}) %collective-permute-start.2) | collective-permute-done | bytes 524320 | tf_op jit(solution)/shard_map/ppermute | solution.py:54
  21.0 3.8 %collective-permute-start.9 = (bf16[2,128,1024]{2,1,0:T(8,128)(2,1)}, bf16[2,128,1024]{2,1,0:T(8,128)(2,1)}, u32[]{:S(2)}, u32[]{:S(2)}) collective-permute-start(bf16[2,128,1024]{2,1,0:T(8,128)(2,1)} %collective-permute-done.refs_1_), channel_id=1, source_target_pairs={{33,0},{32,1},{65,32},{64,33},{97,64},{96,65},{129,96},{128,97},{1... | collective-permute-start | bytes 1572872 | tf_op jit(solution)/shard_map/ppermute | solution.py:58
  30.9 4.6 %shard_map.129 = (bf16[576,1792]{1,0:T(8,128)(2,1)S(1)}, bf16[576,256]{1,0:T(8,128)(2,1)S(1)}, bf16[8,128,576]{2,1,0:T(8,128)(2,1)S(1)}, bf16[8,128,576]{2,1,0:T(8,128)(2,1)S(1)}) custom-call(s32[18]{0:T(128)S(1)} %stack.87.order, bf16[288,2048]{1,0:T(8,128)(2,1)S(1)} %copy-done.10, bf16[288,2048]{1,0:T(8,128)(2,1)S(1)} %copy-done.12), custom_call_target="tpu_custom_call" | custom-call | bytes 7340032 | tf_op jit(solution)/shard_map/pallas_call | solution.py:163
  41.9 4.8 %collective-permute-start.15 = (bf16[2,128,1024]{2,1,0:T(8,128)(2,1)}, bf16[2,128,1024]{2,1,0:T(8,128)(2,1)S(1)}, u32[]{:S(2)}, u32[]{:S(2)}) collective-permute-start(bf16[2,128,1024]{2,1,0:T(8,128)(2,1)} %collective-permute-done.2.refs_3_), channel_id=1, source_target_pairs={{1,16},{0,17},{17,0},{16,1},{3,18},{2,19},{19,2},{18,3},{5,20},{4,... | collective-permute-start | bytes 1572872 | tf_op jit(solution)/shard_map/ppermute | solution.py:66
  46.7 2.6 %collective-permute-start.11 = (bf16[2,128,1024]{2,1,0:T(8,128)(2,1)}, bf16[2,128,1024]{2,1,0:T(8,128)(2,1)S(1)}, u32[]{:S(2)}, u32[]{:S(2)}) collective-permute-start(bf16[2,128,1024]{2,1,0:T(8,128)(2,1)} %collective-permute-done.8.refs_6_), channel_id=1, source_target_pairs={{4,0},{8,4},{12,8},{0,12},{5,1},{9,5},{13,9},{1,13},{6,2},{10,6},{... | collective-permute-start | bytes 1572872 | tf_op jit(solution)/shard_map/ppermute | solution.py:46
  50.6 5.9 %shard_map.130 = (bf16[576,1792]{1,0:T(8,128)(2,1)S(1)}, bf16[576,256]{1,0:T(8,128)(2,1)S(1)}, bf16[288,2048]{1,0:T(8,128)(2,1)S(1)}) custom-call(s32[18]{0:T(128)S(1)} %stack.87.order, bf16[288,2048]{1,0:T(8,128)(2,1)S(1)} %copy-done.7, bf16[288,2048]{1,0:T(8,128)(2,1)S(1)} %copy-done.9, bf16[288,2048]{1,0:T(8,128)(2,1)S(1)} %copy-done.3, ...), custom_call_target="tpu_custom_call" | custom-call | flops 509607936 | bytes 9437184 | tf_op jit(solution)/shard_map/pallas_call | solution.py:193
  58.3 2.9 %collective-permute-done.13.refs_11_ = bf16[2,128,1024]{2,1,0:T(8,128)(2,1)S(1)} collective-permute-done((bf16[2,128,1024]{2,1,0:T(8,128)(2,1)}, bf16[2,128,1024]{2,1,0:T(8,128)(2,1)S(1)}, u32[]{:S(2)}, u32[]{:S(2)}) %collective-permute-start.13) | collective-permute-done | bytes 524320 | tf_op jit(solution)/shard_map/ppermute | solution.py:62
  61.8 2.1 %collective-permute-start.19 = (bf16[2,128,1024]{2,1,0:T(8,128)(2,1)S(1)}, bf16[2,128,1024]{2,1,0:T(8,128)(2,1)S(1)}, u32[]{:S(2)}, u32[]{:S(2)}) collective-permute-start(bf16[2,128,1024]{2,1,0:T(8,128)(2,1)S(1)} %collective-permute-done.11.refs_9_), channel_id=1, source_target_pairs={{33,0},{32,1},{65,32},{64,33},{97,64},{96,65},{129,96},{128,97},{1... | collective-permute-start | bytes 1572872 | tf_op jit(solution)/shard_map/ppermute | solution.py:58
  63.9 6.9 %shard_map.131 = (f32[576,1024]{1,0:T(8,128)S(1)}, f32[576,1024]{1,0:T(8,128)S(1)}) custom-call(bf16[576,1792]{1,0:T(8,128)(2,1)S(1)} %get-tuple-element.134.student_mix, bf16[576,1792]{1,0:T(8,128)(2,1)S(1)} %get-tuple-element.135.teacher_mix, bf16[2,128,1024]{2,1,0:T(8,128)(2,1)S(1)} %pad_maximum_fusion.refs_0_, ...), custom_call_target="tpu_custom_call" | custom-call | flops 4227858432 | bytes 17825792 | tf_op jit(solution)/shard_map/pallas_call | solution.py:236
  70.9 4.9 %collective-permute-done.19.refs_1_ = bf16[2,128,1024]{2,1,0:T(8,128)(2,1)S(1)} collective-permute-done((bf16[2,128,1024]{2,1,0:T(8,128)(2,1)S(1)}, bf16[2,128,1024]{2,1,0:T(8,128)(2,1)S(1)}, u32[]{:S(2)}, u32[]{:S(2)}) %collective-permute-start.19) | collective-permute-done | bytes 524320 | tf_op jit(solution)/shard_map/ppermute | solution.py:58
  75.8 4.0 %shard_map.132 = (f32[576,1024]{1,0:T(8,128)S(1)}, f32[576,1024]{1,0:T(8,128)S(1)}, f32[576,128]{1,0:T(8,128)S(1)}) custom-call(s32[18]{0:T(128)S(1)} %stack.87.order, bf16[576,256]{1,0:T(8,128)(2,1)S(1)} %get-tuple-element.120.student_mix, bf16[576,256]{1,0:T(8,128)(2,1)S(1)} %get-tuple-element.133.teacher_mix, ...), custom_call_target="tpu_custom_call" | custom-call | flops 603979776 | bytes 13631488 | tf_op jit(solution)/shard_map/pallas_call | solution.py:292
  81.5 3.8 %shard_map.133 = (bf16[3,128,768]{2,1,0:T(8,128)(2,1)S(1)}, bf16[3,128,768]{2,1,0:T(8,128)(2,1)S(1)}, bf16[2,128,768]{2,1,0:T(8,128)(2,1)S(1)}, bf16[576,768]{1,...) custom-call(s32[18]{0:T(128)S(1)} %stack.87.order, ...), custom_call_target="tpu_custom_call" | custom-call | flops 905969664 | bytes 9437184 | tf_op jit(solution)/shard_map/pallas_call | solution.py:357
  85.4 3.2 %collective-permute-start.22 = (bf16[3,128,768]{2,1,0:T(8,128)(2,1)S(1)}, bf16[3,128,768]{2,1,0:T(8,128)(2,1)S(1)}, u32[]{:S(2)}, u32[]{:S(2)}) collective-permute-start(bf16[3,128,768]{2,1,0:T(8,128)(2,1)S(1)} %get-tuple-element.156), channel_id=1, source_target_pairs={{33,0},{32,1},{65,32},{64,33},{97,64},{96,65},{129,96},{128,97},{1... | collective-permute-start | bytes 1769480 | tf_op jit(solution)/shard_map/ppermute | solution.py:58
  92.9 6.7 %collective-permute-done.23.refs_2_ = bf16[2,128,768]{2,1,0:T(8,128)(2,1)S(1)} collective-permute-done((bf16[2,128,768]{2,1,0:T(8,128)(2,1)S(1)}, bf16[2,128,768]{2,1,0:T(8,128)(2,1)S(1)}, u32[]{:S(2)}, u32[]{:S(2)}) %collective-permute-start.23) | collective-permute-done | bytes 393248 | tf_op jit(solution)/shard_map/ppermute | solution.py:66
  99.6 2.4 %collective-permute-done.21.refs_0_ = bf16[3,128,768]{2,1,0:T(8,128)(2,1)S(1)} collective-permute-done((bf16[3,128,768]{2,1,0:T(8,128)(2,1)S(1)}, bf16[3,128,768]{2,1,0:T(8,128)(2,1)S(1)}, u32[]{:S(2)}, u32[]{:S(2)}) %collective-permute-start.21) | collective-permute-done | bytes 589856 | tf_op jit(solution)/shard_map/ppermute | solution.py:62
  101.9 2.1 %shard_map.137 = bf16[8,128,768]{2,1,0:T(8,128)(2,1)} custom-call(f32[8,128,768]{2,1,0:T(8,128)S(1)} %shard_map.134.kept, bf16[3,128,768]{2,1,0:T(8,128)(2,1)S(1)} %collective-permute-done.21.refs_0_, bf16[3,128,768]{2,1,0:T(8,128)(2,1)S(1)} %collective-permute-done.22.refs_1_, bf16[2,128,768]{2,1,0:T(8,128)(2,1)S(1)} %collective-permute-done.23.refs_2_), custom_call_target="tpu_custom_call" | custom-call | tf_op jit(solution)/shard_map/pallas_call | solution.py:426
  104.1 6.5 %all-to-all-start = ((bf16[8,128,768]{2,1,0:T(8,128)(2,1)}), bf16[8,128,768]{2,1,0:T(8,128)(2,1)S(1)}, u32[]{:S(2)}, u32[]{:S(2)}) async-start(bf16[8,128,768]{2,1,0:T(8,128)(2,1)} %shard_map.137), calls=%async_computation | async-start | bytes 3145728 | tf_op jit(solution)/shard_map/all_to_all | solution.py:646
  114.4 4.5 %collective-permute-done.26.refs_2_ = bf16[2,128,256]{2,1,0:T(8,128)(2,1)S(1)} collective-permute-done((bf16[2,128,256]{2,1,0:T(8,128)(2,1)S(1)}, bf16[2,128,256]{2,1,0:T(8,128)(2,1)S(1)}, u32[]{:S(2)}, u32[]{:S(2)}) %collective-permute-start.26) | collective-permute-done | bytes 131104 | tf_op jit(solution)/shard_map/ppermute | solution.py:66
  121.7 9.3 %all-to-all-done.first = bf16[8,128,768]{2,1,0:T(8,128)(2,1)S(1)} async-done(((bf16[8,128,768]{2,1,0:T(8,128)(2,1)}), bf16[8,128,768]{2,1,0:T(8,128)(2,1)S(1)}, u32[]{:S(2)}, u32[]{:S(2)}) %all-to-all-start) | async-done | bytes 1572896 | tf_op jit(solution)/shard_map/all_to_all | solution.py:646
  131.0 4.6 %all-to-all-start.1 = ((bf16[8,128,256]{2,1,0:T(8,128)(2,1)}), bf16[8,128,256]{2,1,0:T(8,128)(2,1)S(1)}, u32[]{:S(2)}, u32[]{:S(2)}) async-start(bf16[8,128,256]{2,1,0:T(8,128)(2,1)} %shard_map.138), calls=%async_computation.1 | async-start | bytes 1048576 | tf_op jit(solution)/shard_map/all_to_all | solution.py:646
  144.5 17.4 %all_to_all.20.copies = bf16[8,16,1024]{2,1,0:T(8,128)(2,1)S(1)} all-to-all(bf16[8,16,1024]{2,1,0:T(8,128)(2,1)S(1)} %bitcast.27), channel_id=1, replica_groups={{0,48,64,112,128,176,192,240},{16,32,80,96,144,160,208,224},{1,49,65,11..., dimensions={0} | all-to-all | bytes 524288 | tf_op jit(solution)/shard_map/all_to_all | solution.py:665
  162.7 3.6 %all-to-all-start.3 = ((bf16[16,16,1024]{2,1,0:T(8,128)(2,1)}), bf16[16,16,1024]{2,1,0:T(8,128)(2,1)S(1)}, u32[]{:S(2)}, u32[]{:S(2)}) async-start(bf16[16,16,1024]{2,1,0:T(8,128)(2,1)} %shard_map.142), calls=%async_computation.3 | async-start | bytes 1048576 | tf_op jit(solution)/shard_map/all_to_all | solution.py:668
  166.3 14.6 %all-to-all-done.3 = bf16[16,16,1024]{2,1,0:T(8,128)(2,1)S(1)} async-done(((bf16[16,16,1024]{2,1,0:T(8,128)(2,1)}), bf16[16,16,1024]{2,1,0:T(8,128)(2,1)S(1)}, u32[]{:S(2)}, u32[]{:S(2)}) %all-to-all-start.3) | async-done | bytes 524320 | tf_op jit(solution)/shard_map/all_to_all | solution.py:668
  183.4 2.7 %shard_map.143 = (f32[128,2048]{1,0:T(8,128)}, f32[128,2048]{1,0:T(8,128)}, f32[128,2048]{1,0:T(8,128)}, f32[128,2048]{1,0:T(8,128)}) custom-call(s32[1]{0:T(128)} %bitcast.flip, bf16[8,2,16,1024]{3,2,1,0:T(8,128)(2,1)S(1)} %bitcast.26, f32[128,2048]{1,0:T(8,128)S(1)} %copy-done, f32[128,2048]{1,0:T(8,128)S(1)} %copy-done.2, f32[128,2048]{1,0:T(8,128)S(1)} %copy-done.14, ...), custom_call_target="tpu_custom_call" | custom-call | tf_op jit(solution)/shard_map/pallas_call | solution.py:543
  (120 shorter events, 51.8 us)
Async XLA Ops:
  2.2 16.1 %collective-permute-start.4 = (bf16[288,2048]{1,0:T(8,128)(2,1)S(1)}, bf16[288,2048]{1,0:T(8,128)(2,1)S(1)}, u32[]{:S(2)}, u32[]{:S(2)}) collective-permute-start(bf16[288,2048]{1,0:T(8,128)(2,1)S(1)} %copy-done.6), channel_id=1, source_target_pairs={{0,1},{1,0},{2,3},{3,2},{4,5},{5,4},{6,7},{7,6},{8,9},{9,8},{10,11... | collective-permute-start | bytes 3538952 | tf_op jit(solution)/shard_map/ppermute | solution.py:42
  2.7 14.0 %collective-permute-start.2 = (bf16[2,128,1024]{2,1,0:T(8,128)(2,1)S(1)}, bf16[2,128,1024]{2,1,0:T(8,128)(2,1)}, u32[]{:S(2)}, u32[]{:S(2)}) collective-permute-start(bf16[2,128,1024]{2,1,0:T(8,128)(2,1)S(1)} %pad_maximum_fusion.refs_0_), channel_id=1, source_target_pairs={{16,2},{2,16},{0,18},{18,0},{17,3},{3,17},{1,19},{19,1},{20,6},{6,... | collective-permute-start | bytes 1572872 | tf_op jit(solution)/shard_map/ppermute | solution.py:54
  3.3 15.0 %collective-permute-start.1 = (bf16[2,128,1024]{2,1,0:T(8,128)(2,1)S(1)}, bf16[2,128,1024]{2,1,0:T(8,128)(2,1)}, u32[]{:S(2)}, u32[]{:S(2)}) collective-permute-start(bf16[2,128,1024]{2,1,0:T(8,128)(2,1)S(1)} %pad_maximum_fusion.refs_0_), channel_id=1, source_target_pairs={{0,4},{4,8},{8,12},{12,0},{1,5},{5,9},{9,13},{13,1},{2,6},{6,10},{... | collective-permute-start | bytes 1572872 | tf_op jit(solution)/shard_map/ppermute | solution.py:50
  4.8 13.5 %collective-permute-start = (bf16[2,128,1024]{2,1,0:T(8,128)(2,1)S(1)}, bf16[2,128,1024]{2,1,0:T(8,128)(2,1)}, u32[]{:S(2)}, u32[]{:S(2)}) collective-permute-start(bf16[2,128,1024]{2,1,0:T(8,128)(2,1)S(1)} %pad_maximum_fusion.refs_0_), channel_id=1, source_target_pairs={{4,0},{8,4},{12,8},{0,12},{5,1},{9,5},{13,9},{1,13},{6,2},{10,6},{... | collective-permute-start | bytes 1572872 | tf_op jit(solution)/shard_map/ppermute | solution.py:46
  7.5 11.9 %collective-permute-start.5 = (s32[2,144]{1,0:T(2,128)S(1)}, s32[2,144]{1,0:T(2,128)S(1)}, u32[]{:S(2)}, u32[]{:S(2)}) collective-permute-start(s32[2,144]{1,0:T(2,128)S(1)} %copy-done.22), channel_id=1, source_target_pairs={{0,1},{1,0},{2,3},{3,2},{4,5},{5,4},{6,7},{7,6},{8,9},{9,8},{10,11... | collective-permute-start | bytes 3464 | tf_op jit(solution)/shard_map/ppermute | solution.py:42
  19.4 17.1 %collective-permute-start.7 = (bf16[2,128,1024]{2,1,0:T(8,128)(2,1)}, bf16[2,128,1024]{2,1,0:T(8,128)(2,1)}, u32[]{:S(2)}, u32[]{:S(2)}) collective-permute-start(bf16[2,128,1024]{2,1,0:T(8,128)(2,1)} %collective-permute-done.2.refs_3_), channel_id=1, source_target_pairs={{0,4},{4,8},{8,12},{12,0},{1,5},{5,9},{9,13},{13,1},{2,6},{6,10},{... | collective-permute-start | bytes 1572872 | tf_op jit(solution)/shard_map/ppermute | solution.py:50
  21.0 15.5 %collective-permute-start.10 = (bf16[2,128,1024]{2,1,0:T(8,128)(2,1)}, bf16[2,128,1024]{2,1,0:T(8,128)(2,1)}, u32[]{:S(2)}, u32[]{:S(2)}) collective-permute-start(bf16[2,128,1024]{2,1,0:T(8,128)(2,1)} %collective-permute-done.1.refs_2_), channel_id=1, source_target_pairs={{1,32},{0,33},{33,64},{32,65},{65,96},{64,97},{97,128},{96,129},{1... | collective-permute-start | bytes 1572872 | tf_op jit(solution)/shard_map/ppermute | solution.py:62
  21.0 16.0 %collective-permute-start.9 = (bf16[2,128,1024]{2,1,0:T(8,128)(2,1)}, bf16[2,128,1024]{2,1,0:T(8,128)(2,1)}, u32[]{:S(2)}, u32[]{:S(2)}) collective-permute-start(bf16[2,128,1024]{2,1,0:T(8,128)(2,1)} %collective-permute-done.refs_1_), channel_id=1, source_target_pairs={{33,0},{32,1},{65,32},{64,33},{97,64},{96,65},{129,96},{128,97},{1... | collective-permute-start | bytes 1572872 | tf_op jit(solution)/shard_map/ppermute | solution.py:58
  24.8 13.9 %collective-permute-start.8 = (bf16[2,128,1024]{2,1,0:T(8,128)(2,1)}, bf16[2,128,1024]{2,1,0:T(8,128)(2,1)}, u32[]{:S(2)}, u32[]{:S(2)}) collective-permute-start(bf16[2,128,1024]{2,1,0:T(8,128)(2,1)} %collective-permute-done.refs_1_), channel_id=1, source_target_pairs={{16,2},{2,16},{0,18},{18,0},{17,3},{3,17},{1,19},{19,1},{20,6},{6,... | collective-permute-start | bytes 1572872 | tf_op jit(solution)/shard_map/ppermute | solution.py:54
  26.3 14.2 %collective-permute-start.6 = (bf16[2,128,1024]{2,1,0:T(8,128)(2,1)}, bf16[2,128,1024]{2,1,0:T(8,128)(2,1)}, u32[]{:S(2)}, u32[]{:S(2)}) collective-permute-start(bf16[2,128,1024]{2,1,0:T(8,128)(2,1)} %collective-permute-done.refs_1_), channel_id=1, source_target_pairs={{4,0},{8,4},{12,8},{0,12},{5,1},{9,5},{13,9},{1,13},{6,2},{10,6},{... | collective-permute-start | bytes 1572872 | tf_op jit(solution)/shard_map/ppermute | solution.py:46
  40.5 16.0 %collective-permute-start.12 = (bf16[2,128,1024]{2,1,0:T(8,128)(2,1)}, bf16[2,128,1024]{2,1,0:T(8,128)(2,1)S(1)}, u32[]{:S(2)}, u32[]{:S(2)}) collective-permute-start(bf16[2,128,1024]{2,1,0:T(8,128)(2,1)} %collective-permute-done.6.refs_4_), channel_id=1, source_target_pairs={{33,0},{32,1},{65,32},{64,33},{97,64},{96,65},{129,96},{128,97},{1... | collective-permute-start | bytes 1572872 | tf_op jit(solution)/shard_map/ppermute | solution.py:58
  41.1 15.4 %collective-permute-start.14 = (bf16[2,128,1024]{2,1,0:T(8,128)(2,1)}, bf16[2,128,1024]{2,1,0:T(8,128)(2,1)S(1)}, u32[]{:S(2)}, u32[]{:S(2)}) collective-permute-start(bf16[2,128,1024]{2,1,0:T(8,128)(2,1)} %collective-permute-done.10.refs_8_), channel_id=1, source_target_pairs={{16,2},{2,16},{0,18},{18,0},{17,3},{3,17},{1,19},{19,1},{20,6},{6,... | collective-permute-start | bytes 1572872 | tf_op jit(solution)/shard_map/ppermute | solution.py:54
  41.9 16.4 %collective-permute-start.15 = (bf16[2,128,1024]{2,1,0:T(8,128)(2,1)}, bf16[2,128,1024]{2,1,0:T(8,128)(2,1)S(1)}, u32[]{:S(2)}, u32[]{:S(2)}) collective-permute-start(bf16[2,128,1024]{2,1,0:T(8,128)(2,1)} %collective-permute-done.2.refs_3_), channel_id=1, source_target_pairs={{1,16},{0,17},{17,0},{16,1},{3,18},{2,19},{19,2},{18,3},{5,20},{4,... | collective-permute-start | bytes 1572872 | tf_op jit(solution)/shard_map/ppermute | solution.py:66
  46.6 14.6 %collective-permute-start.13 = (bf16[2,128,1024]{2,1,0:T(8,128)(2,1)}, bf16[2,128,1024]{2,1,0:T(8,128)(2,1)S(1)}, u32[]{:S(2)}, u32[]{:S(2)}) collective-permute-start(bf16[2,128,1024]{2,1,0:T(8,128)(2,1)} %collective-permute-done.8.refs_6_), channel_id=1, source_target_pairs={{1,32},{0,33},{33,64},{32,65},{65,96},{64,97},{97,128},{96,129},{1... | collective-permute-start | bytes 1572872 | tf_op jit(solution)/shard_map/ppermute | solution.py:62
  46.7 14.6 %collective-permute-start.11 = (bf16[2,128,1024]{2,1,0:T(8,128)(2,1)}, bf16[2,128,1024]{2,1,0:T(8,128)(2,1)S(1)}, u32[]{:S(2)}, u32[]{:S(2)}) collective-permute-start(bf16[2,128,1024]{2,1,0:T(8,128)(2,1)} %collective-permute-done.8.refs_6_), channel_id=1, source_target_pairs={{4,0},{8,4},{12,8},{0,12},{5,1},{9,5},{13,9},{1,13},{6,2},{10,6},{... | collective-permute-start | bytes 1572872 | tf_op jit(solution)/shard_map/ppermute | solution.py:46
  61.2 14.6 %collective-permute-start.16 = (bf16[288,2048]{1,0:T(8,128)(2,1)S(1)}, bf16[288,2048]{1,0:T(8,128)(2,1)S(1)}, u32[]{:S(2)}, u32[]{:S(2)}) collective-permute-start(bf16[288,2048]{1,0:T(8,128)(2,1)S(1)} %copy-done.3), channel_id=1, source_target_pairs={{0,1},{1,0},{2,3},{3,2},{4,5},{5,4},{6,7},{7,6},{8,9},{9,8},{10,11... | collective-permute-start | bytes 3538952 | tf_op jit(solution)/shard_map/ppermute | solution.py:42
  61.2 14.6 %collective-permute-start.17 = (bf16[288,2048]{1,0:T(8,128)(2,1)S(1)}, bf16[288,2048]{1,0:T(8,128)(2,1)S(1)}, u32[]{:S(2)}, u32[]{:S(2)}) collective-permute-start(bf16[288,2048]{1,0:T(8,128)(2,1)S(1)} %get-tuple-element.146.picked_own), channel_id=1, source_target_pairs={{0,1},{1,0},{2,3},{3,2},{4,5},{5,4},{6,7},{7,6},{8,9},{9,8},{10,11... | collective-permute-start | bytes 3538952 | tf_op jit(solution)/shard_map/ppermute | solution.py:42
  61.8 14.0 %collective-permute-start.19 = (bf16[2,128,1024]{2,1,0:T(8,128)(2,1)S(1)}, bf16[2,128,1024]{2,1,0:T(8,128)(2,1)S(1)}, u32[]{:S(2)}, u32[]{:S(2)}) collective-permute-start(bf16[2,128,1024]{2,1,0:T(8,128)(2,1)S(1)} %collective-permute-done.11.refs_9_), channel_id=1, source_target_pairs={{33,0},{32,1},{65,32},{64,33},{97,64},{96,65},{129,96},{128,97},{1... | collective-permute-start | bytes 1572872 | tf_op jit(solution)/shard_map/ppermute | solution.py:58
  85.3 16.7 %collective-permute-start.21 = (bf16[3,128,768]{2,1,0:T(8,128)(2,1)S(1)}, bf16[3,128,768]{2,1,0:T(8,128)(2,1)S(1)}, u32[]{:S(2)}, u32[]{:S(2)}) collective-permute-start(bf16[3,128,768]{2,1,0:T(8,128)(2,1)S(1)} %get-tuple-element.155), channel_id=1, source_target_pairs={{1,32},{0,33},{33,64},{32,65},{65,96},{64,97},{97,128},{96,129},{1... | collective-permute-start | bytes 1769480 | tf_op jit(solution)/shard_map/ppermute | solution.py:62
  85.4 16.6 %collective-permute-start.22 = (bf16[3,128,768]{2,1,0:T(8,128)(2,1)S(1)}, bf16[3,128,768]{2,1,0:T(8,128)(2,1)S(1)}, u32[]{:S(2)}, u32[]{:S(2)}) collective-permute-start(bf16[3,128,768]{2,1,0:T(8,128)(2,1)S(1)} %get-tuple-element.156), channel_id=1, source_target_pairs={{33,0},{32,1},{65,32},{64,33},{97,64},{96,65},{129,96},{128,97},{1... | collective-permute-start | bytes 1769480 | tf_op jit(solution)/shard_map/ppermute | solution.py:58
  88.5 11.0 %collective-permute-start.23 = (bf16[2,128,768]{2,1,0:T(8,128)(2,1)S(1)}, bf16[2,128,768]{2,1,0:T(8,128)(2,1)S(1)}, u32[]{:S(2)}, u32[]{:S(2)}) collective-permute-start(bf16[2,128,768]{2,1,0:T(8,128)(2,1)S(1)} %get-tuple-element.157), channel_id=1, source_target_pairs={{1,16},{0,17},{17,0},{16,1},{3,18},{2,19},{19,2},{18,3},{5,20},{4,... | collective-permute-start | bytes 1179656 | tf_op jit(solution)/shard_map/ppermute | solution.py:66
  104.1 26.9 %all-to-all-start = ((bf16[8,128,768]{2,1,0:T(8,128)(2,1)}), bf16[8,128,768]{2,1,0:T(8,128)(2,1)S(1)}, u32[]{:S(2)}, u32[]{:S(2)}) async-start(bf16[8,128,768]{2,1,0:T(8,128)(2,1)} %shard_map.137), calls=%async_computation | async-start | bytes 3145728 | tf_op jit(solution)/shard_map/all_to_all | solution.py:646
  131.0 13.0 %all-to-all-start.1 = ((bf16[8,128,256]{2,1,0:T(8,128)(2,1)}), bf16[8,128,256]{2,1,0:T(8,128)(2,1)S(1)}, u32[]{:S(2)}, u32[]{:S(2)}) async-start(bf16[8,128,256]{2,1,0:T(8,128)(2,1)} %shard_map.138), calls=%async_computation.1 | async-start | bytes 1048576 | tf_op jit(solution)/shard_map/all_to_all | solution.py:646
  162.7 18.2 %all-to-all-start.3 = ((bf16[16,16,1024]{2,1,0:T(8,128)(2,1)}), bf16[16,16,1024]{2,1,0:T(8,128)(2,1)S(1)}, u32[]{:S(2)}, u32[]{:S(2)}) async-start(bf16[16,16,1024]{2,1,0:T(8,128)(2,1)} %shard_map.142), calls=%async_computation.3 | async-start | bytes 1048576 | tf_op jit(solution)/shard_map/all_to_all | solution.py:668
  (38 other events, 261.5 us)

commit v10 on v8

--- a/solution.py
+++ b/solution.py
@@ -101,6 +101,21 @@
         compiler_params=pltpu.CompilerParams(vmem_limit_bytes=SMALL_LIMIT),
         cost_estimate=pl.CostEstimate(flops=0, bytes_accessed=1536 * 1024, transcendentals=0),
     )(order, student, teacher)
+
+
+def halves_kernel(pair, first, second):
+    first[...] = pair[0]
+    second[...] = pair[1]
+
+
+def both_halves(pair):
+    _, rows, columns = pair.shape
+    return pl.pallas_call(
+        halves_kernel,
+        out_shape=[jax.ShapeDtypeStruct((rows, columns), pair.dtype)] * 2,
+        compiler_params=pltpu.CompilerParams(vmem_limit_bytes=SMALL_LIMIT),
+        cost_estimate=pl.CostEstimate(flops=0, bytes_accessed=1024 * 1024, transcendentals=0),
+    )(pair)
 
 
 def place_blocks(order, step, packed, early, late):
@@ -250,11 +265,10 @@
     order, student_mix, teacher_mix, student_part, teacher_part, residual_own, residual_other, picked_own, picked_other,
     scale, *refs
 ):
-    weights, (student_out, matched_out, sums_out, held) = refs[:LATE], refs[LATE:]
-    for block in range(LATE):
-        rows = slice(block * 128, (block + 1) * 128)
-        held[0, rows, :] = weights[block][0]
-        held[1, rows, :] = weights[block][1]
+    pair, student_weight, teacher_weight, student_out, matched_out, sums_out, held = refs
+    held[:, :128, :] = pair[...]
+    held[0, 128:, :] = student_weight[...]
+    held[1, 128:, :] = teacher_weight[...]
     factor = scale[...] * (KIN ** (-0.5))
     student_sum = student_part[...] + jnp.dot(student_mix[...], held[0], preferred_element_type=jnp.float32)
     teacher_sum = teacher_part[...] + jnp.dot(teacher_mix[...], held[1], preferred_element_type=jnp.float32)
@@ -296,7 +310,8 @@
             in_specs=[whole, whole, column, column]
             + [tokens] * 4
             + [pl.BlockSpec((1, width), lambda j, order: (0, order[HALF_AT] * steps + j))]
-            + [pl.BlockSpec((2, 128, width), lambda j, order: (0, 0, j))] * LATE,
+            + [pl.BlockSpec((2, 128, width), lambda j, order: (0, 0, j))]
+            + [pl.BlockSpec((128, width), lambda j, order: (0, j))] * 2,
             out_specs=[column, column, pl.BlockSpec((rows, 128), lambda j, order: (0, 0))],
             scratch_shapes=[pltpu.VMEM((2, LATE * 128, width), jnp.bfloat16)],
         ),
@@ -585,17 +600,19 @@
         )
     )
     prepared = prepare_teacher(order, teacher_mix, teacher_other, residual, places, places_other)
+    across_two = from_y_next(across_up)
     (
-        across_two, passed_two, passed_across_up, passed_across_down, passed_across, prepared, other_sent, residual_sent
+        (student_two, teacher_two), passed_two, passed_across_up, passed_across_down, passed_across, prepared,
+        other_sent, residual_sent,
     ) = lax.optimization_barrier(
         (
-            from_y_next(across_up), from_z_next(up_two), from_z_previous(across_up), from_x_near(passed_down),
+            both_halves(across_two), from_z_next(up_two), from_z_previous(across_up), from_x_near(passed_down),
             from_x_twin(across), prepared, other_sent, residual,
         )
     )
     student_early, student_late, sent_mix, kept_mix = student_prepared
     teacher_early, teacher_late, picked = prepared
-    passed_across_two = from_z_next(across_two)
+    student_two, teacher_two = from_z_next(student_two), from_z_previous(teacher_two)
     residual_other, picked_other, other = swap_cores(residual_sent), swap_cores(picked), swap_cores(other_sent)
     student_part, teacher_part = early_forward(
         (
@@ -606,7 +623,7 @@
         teacher_early,
     )
     student_out, matched, sums = late_forward(
-        order, (other, passed_across_two), student_late, teacher_late, student_part, teacher_part, residual,
+        order, (other, student_two, teacher_two), student_late, teacher_late, student_part, teacher_part, residual,
         residual_other, picked, picked_other, scale
     )
     more_sums = swap_cores(sums)

time: 186 us -> 185 us (level)
  waiting for transfers between devices: 68.2 us -> 66.2 us
    ppermute x5, waiting for transfers between devices: 6.44 us -> 0.56 us  [from_z_next(): return lax.ppermute(value, ('z', 'core'), with_core_flip(from_next(8)))]
    ppermute x3, waiting for transfers between devices: 10.1 us -> 12.8 us  [from_x_near(): return lax.ppermute(value, ('xlo', 'xhi'), X_NEAR)]
    ppermute x4 -> x5, starting transfers between devices: 1.32 us -> 3.83 us  [from_z_previous(): return lax.ppermute(value, ('z', 'core'), with_core_flip(from_previous(8)))]
    ppermute x5, starting transfers between devices: 11.2 us -> 9.32 us  [from_z_next(): return lax.ppermute(value, ('z', 'core'), with_core_flip(from_next(8)))]
    ppermute x4 -> x5, waiting for transfers between devices: 4.98 us -> 5.5 us  [from_z_previous(): return lax.ppermute(value, ('z', 'core'), with_core_flip(from_previous(8)))]
    unnamed x58 -> x54, local copies, waits for them, and re-layouts: 10.6 us -> 10.6 us
  transfers between devices with their start and end apart: 32 -> 33, of which waited for: 18 -> 20; matrix products, arithmetic and copies ran while one was open for 0% -> 0% of each run, Pallas kernels for 14% -> 14%
where the time goes in v10:
time: 185 us; the launch traced here: 183 us
  waiting for transfers between devices  66.2 us (36%)
  starting transfers between devices  47.3 us (26%)
  Pallas kernels  38.6 us (21%)
  blocking collectives  17.9 us (10%)
  local copies, waits for them, and re-layouts  12 us (6%)
    all_to_all x1, blocking collectives, shards(): lax.all_to_all(total.reshape(8, 16, half), ('z', 'xlo'), 0, 0, axis_index...  17.9 us
    all_to_all x1, waiting for transfers between devices, shards(): full = lax.all_to_all(spread_rows(by_copy, 16), ('z', 'xlo'), 0, 0)  16.4 us
    ppermute x3, waiting for transfers between devices, from_x_near(): return lax.ppermute(value, ('xlo', 'xhi'), X_NEAR)  12.8 us
    ppermute x3, waiting for transfers between devices, from_x_twin(): return lax.ppermute(value, ('xlo', 'core'), with_core_flip(CORE_SWAP))  12.6 us
    all_to_all x2, waiting for transfers between devices, over_fsdp(): lax.all_to_all(rows, ('xlo', 'y', 'xhi'), 0, 0, axis_index_groups=FSDP_GR...  11.9 us
    all_to_all x2, starting transfers between devices, over_fsdp(): lax.all_to_all(rows, ('xlo', 'y', 'xhi'), 0, 0, axis_index_groups=FSDP_GR...  11.3 us
    unnamed x54, local copies, waits for them, and re-layouts  10.6 us
    ppermute x5, starting transfers between devices, from_z_next(): return lax.ppermute(value, ('z', 'core'), with_core_flip(from_next(8)))  9.32 us
  transfers between devices with their start and end apart: 33, of which 20 were waited for; matrix products, arithmetic and copies ran while one was open for 0% of the time, Pallas kernels for 14%

profile of v10, /device:TPU:4, one launch (start us, length us, event | category | flops | bytes accessed | tf_op | source)
XLA Modules:
  0.0 183.2 jit_solution(11465689106235686613)
XLA Ops:
  8.3 8.5 %collective-permute-done.2.refs_3_ = bf16[2,128,1024]{2,1,0:T(8,128)(2,1)} collective-permute-done((bf16[2,128,1024]{2,1,0:T(8,128)(2,1)S(1)}, bf16[2,128,1024]{2,1,0:T(8,128)(2,1)}, u32[]{:S(2)}, u32[]{:S(2)}) %collective-permute-start.2) | collective-permute-done | bytes 524320 | tf_op jit(solution)/shard_map/ppermute | solution.py:54
  21.0 3.8 %collective-permute-start.9 = (bf16[2,128,1024]{2,1,0:T(8,128)(2,1)}, bf16[2,128,1024]{2,1,0:T(8,128)(2,1)}, u32[]{:S(2)}, u32[]{:S(2)}) collective-permute-start(bf16[2,128,1024]{2,1,0:T(8,128)(2,1)} %collective-permute-done.refs_1_), channel_id=1, source_target_pairs={{33,0},{32,1},{65,32},{64,33},{97,64},{96,65},{129,96},{128,97},{1... | collective-permute-start | bytes 1572872 | tf_op jit(solution)/shard_map/ppermute | solution.py:58
  26.3 2.0 %collective-permute-start.6 = (bf16[2,128,1024]{2,1,0:T(8,128)(2,1)}, bf16[2,128,1024]{2,1,0:T(8,128)(2,1)}, u32[]{:S(2)}, u32[]{:S(2)}) collective-permute-start(bf16[2,128,1024]{2,1,0:T(8,128)(2,1)} %collective-permute-done.refs_1_), channel_id=1, source_target_pairs={{4,0},{8,4},{12,8},{0,12},{5,1},{9,5},{13,9},{1,13},{6,2},{10,6},{... | collective-permute-start | bytes 1572872 | tf_op jit(solution)/shard_map/ppermute | solution.py:46
  30.9 4.6 %shard_map.129 = (bf16[576,1792]{1,0:T(8,128)(2,1)S(1)}, bf16[576,256]{1,0:T(8,128)(2,1)S(1)}, bf16[8,128,576]{2,1,0:T(8,128)(2,1)S(1)}, bf16[8,128,576]{2,1,0:T(8,128)(2,1)S(1)}) custom-call(s32[18]{0:T(128)S(1)} %stack.87.order, bf16[288,2048]{1,0:T(8,128)(2,1)S(1)} %copy-done.9, bf16[288,2048]{1,0:T(8,128)(2,1)S(1)} %copy-done.11), custom_call_target="tpu_custom_call" | custom-call | bytes 7340032 | tf_op jit(solution)/shard_map/pallas_call | solution.py:177
  41.1 3.1 %collective-permute-start.11 = (bf16[2,128,1024]{2,1,0:T(8,128)(2,1)}, bf16[2,128,1024]{2,1,0:T(8,128)(2,1)S(1)}, u32[]{:S(2)}, u32[]{:S(2)}) collective-permute-start(bf16[2,128,1024]{2,1,0:T(8,128)(2,1)} %collective-permute-done.8.refs_6_), channel_id=1, source_target_pairs={{4,0},{8,4},{12,8},{0,12},{5,1},{9,5},{13,9},{1,13},{6,2},{10,6},{... | collective-permute-start | bytes 1572872 | tf_op jit(solution)/shard_map/ppermute | solution.py:46
  44.7 3.5 %collective-permute-start.15 = (bf16[2,128,1024]{2,1,0:T(8,128)(2,1)}, bf16[2,128,1024]{2,1,0:T(8,128)(2,1)S(1)}, u32[]{:S(2)}, u32[]{:S(2)}) collective-permute-start(bf16[2,128,1024]{2,1,0:T(8,128)(2,1)} %collective-permute-done.2.refs_3_), channel_id=1, source_target_pairs={{1,16},{0,17},{17,0},{16,1},{3,18},{2,19},{19,2},{18,3},{5,20},{4,... | collective-permute-start | bytes 1572872 | tf_op jit(solution)/shard_map/ppermute | solution.py:66
  49.3 5.9 %shard_map.131 = (bf16[576,1792]{1,0:T(8,128)(2,1)S(1)}, bf16[576,256]{1,0:T(8,128)(2,1)S(1)}, bf16[288,2048]{1,0:T(8,128)(2,1)S(1)}) custom-call(s32[18]{0:T(128)S(1)} %stack.87.order, bf16[288,2048]{1,0:T(8,128)(2,1)S(1)} %copy-done.6, bf16[288,2048]{1,0:T(8,128)(2,1)S(1)} %copy-done.8, bf16[288,2048]{1,0:T(8,128)(2,1)S(1)} %copy-done.3, ...), custom_call_target="tpu_custom_call" | custom-call | flops 509607936 | bytes 9437184 | tf_op jit(solution)/shard_map/pallas_call | solution.py:207
  55.6 2.6 %collective-permute-done.14.refs_12_ = bf16[2,128,1024]{2,1,0:T(8,128)(2,1)S(1)} collective-permute-done((bf16[2,128,1024]{2,1,0:T(8,128)(2,1)}, bf16[2,128,1024]{2,1,0:T(8,128)(2,1)S(1)}, u32[]{:S(2)}, u32[]{:S(2)}) %collective-permute-start.14) | collective-permute-done | bytes 524320 | tf_op jit(solution)/shard_map/ppermute | solution.py:54
  58.3 2.6 %collective-permute-done.15.refs_13_ = bf16[2,128,1024]{2,1,0:T(8,128)(2,1)S(1)} collective-permute-done((bf16[2,128,1024]{2,1,0:T(8,128)(2,1)}, bf16[2,128,1024]{2,1,0:T(8,128)(2,1)S(1)}, u32[]{:S(2)}, u32[]{:S(2)}) %collective-permute-start.15) | collective-permute-done | bytes 524320 | tf_op jit(solution)/shard_map/ppermute | solution.py:66
  60.9 2.9 %collective-permute-done.13.refs_11_ = bf16[2,128,1024]{2,1,0:T(8,128)(2,1)S(1)} collective-permute-done((bf16[2,128,1024]{2,1,0:T(8,128)(2,1)}, bf16[2,128,1024]{2,1,0:T(8,128)(2,1)S(1)}, u32[]{:S(2)}, u32[]{:S(2)}) %collective-permute-start.13) | collective-permute-done | bytes 524320 | tf_op jit(solution)/shard_map/ppermute | solution.py:62
  66.0 6.9 %shard_map.132 = (f32[576,1024]{1,0:T(8,128)S(1)}, f32[576,1024]{1,0:T(8,128)S(1)}) custom-call(bf16[576,1792]{1,0:T(8,128)(2,1)S(1)} %get-tuple-element.132.student_mix, bf16[576,1792]{1,0:T(8,128)(2,1)S(1)} %get-tuple-element.133.teacher_mix, bf16[2,128,1024]{2,1,0:T(8,128)(2,1)S(1)} %copy-done.15, bf16[2,128,1024]{2,1,0:T(8,128)(2,1)} %collective-permute-done.refs_1_, ...), custom_call_target="tpu_custom_call" | custom-call | flops 4227858432 | bytes 17825792 | tf_op jit(solution)/shard_map/pallas_call | solution.py:250
  73.5 4.0 %shard_map.133 = (f32[576,1024]{1,0:T(8,128)S(1)}, f32[576,1024]{1,0:T(8,128)S(1)}, f32[576,128]{1,0:T(8,128)S(1)}) custom-call(s32[18]{0:T(128)S(1)} %stack.87.order, bf16[576,256]{1,0:T(8,128)(2,1)S(1)} %get-tuple-element.116.student_mix, bf16[576,256]{1,0:T(8,128)(2,1)S(1)} %get-tuple-element.131.teacher_mix, ...), custom_call_target="tpu_custom_call" | custom-call | flops 603979776 | bytes 13631488 | tf_op jit(solution)/shard_map/pallas_call | solution.py:305
  79.2 2.7 %shard_map.134 = (bf16[3,128,512]{2,1,0:T(8,128)(2,1)S(1)}, bf16[3,128,512]{2,1,0:T(8,128)(2,1)S(1)}, bf16[2,128,512]{2,1,0:T(8,128)(2,1)S(1)}, bf16[576,512]{1,...) custom-call(s32[18]{0:T(128)S(1)} %stack.87.order, ...), custom_call_target="tpu_custom_call" | custom-call | flops 603979776 | bytes 6291456 | tf_op jit(solution)/shard_map/pallas_call | solution.py:372
  86.8 2.7 %shard_map.136 = (bf16[3,128,512]{2,1,0:T(8,128)(2,1)S(1)}, bf16[3,128,512]{2,1,0:T(8,128)(2,1)S(1)}, bf16[2,128,512]{2,1,0:T(8,128)(2,1)S(1)}, bf16[576,512]{1,...) custom-call(s32[18]{0:T(128)S(1)} %stack.87.order, ...), custom_call_target="tpu_custom_call" | custom-call | flops 603979776 | bytes 6291456 | tf_op jit(solution)/shard_map/pallas_call | solution.py:372
  96.4 6.5 %all-to-all-start = ((bf16[8,128,512]{2,1,0:T(8,128)(2,1)}), bf16[8,128,512]{2,1,0:T(8,128)(2,1)}, u32[]{:S(2)}, u32[]{:S(2)}) async-start(bf16[8,128,512]{2,1,0:T(8,128)(2,1)} %copy-done.4), calls=%async_computation | async-start | bytes 2097152 | tf_op jit(solution)/shard_map/all_to_all | solution.py:640
  102.9 3.0 %collective-permute-start.26 = (bf16[3,128,512]{2,1,0:T(8,128)(2,1)}, bf16[3,128,512]{2,1,0:T(8,128)(2,1)S(1)}, u32[]{:S(2)}, u32[]{:S(2)}) collective-permute-start(bf16[3,128,512]{2,1,0:T(8,128)(2,1)} %copy-done.20), channel_id=1, source_target_pairs={{33,0},{32,1},{65,32},{64,33},{97,64},{96,65},{129,96},{128,97},{1... | collective-permute-start | bytes 1179656 | tf_op jit(solution)/shard_map/ppermute | solution.py:58
  105.8 8.6 %collective-permute-done.27.refs_2_ = bf16[2,128,512]{2,1,0:T(8,128)(2,1)S(1)} collective-permute-done((bf16[2,128,512]{2,1,0:T(8,128)(2,1)}, bf16[2,128,512]{2,1,0:T(8,128)(2,1)S(1)}, u32[]{:S(2)}, u32[]{:S(2)}) %collective-permute-start.27) | collective-permute-done | bytes 262176 | tf_op jit(solution)/shard_map/ppermute | solution.py:66
  118.1 4.7 %all-to-all-start.1 = ((bf16[8,128,512]{2,1,0:T(8,128)(2,1)}), bf16[8,128,512]{2,1,0:T(8,128)(2,1)S(1)}, u32[]{:S(2)}, u32[]{:S(2)}) async-start(bf16[8,128,512]{2,1,0:T(8,128)(2,1)} %copy-done.5), calls=%async_computation.1 | async-start | bytes 2097152 | tf_op jit(solution)/shard_map/all_to_all | solution.py:640
  124.9 2.2 %shard_map.140 = bf16[288,2048]{1,0:T(8,128)(2,1)} custom-call(s32[18]{0:T(128)S(1)} %stack.87.order, bf16[288,512]{1,0:T(8,128)(2,1)S(1)} %get-tuple-element.172.first_own, bf16[288,512]{1,0:T(8,128)(2,1)S(1)} %copy-done.17, bf16[288,512]{1,0:T(8,128)(2,1)S(1)} %collective-permute-done.28.first_other, bf16[288,512]{1,0:T(8,128)(2,1)S(1)} %collective-permute-done.29.last_other), custom_call_target="tpu_custom_call" | custom-call | bytes 2457600 | tf_op jit(solution)/shard_map/pallas_call | solution.py:461
  127.1 10.8 %all-to-all-done.1.last = bf16[8,128,512]{2,1,0:T(8,128)(2,1)S(1)} async-done(((bf16[8,128,512]{2,1,0:T(8,128)(2,1)}), bf16[8,128,512]{2,1,0:T(8,128)(2,1)S(1)}, u32[]{:S(2)}, u32[]{:S(2)}) %all-to-all-start.1) | async-done | bytes 1048608 | tf_op jit(solution)/shard_map/all_to_all | solution.py:640
  139.2 17.9 %all_to_all.20.copies = bf16[8,16,1024]{2,1,0:T(8,128)(2,1)S(1)} all-to-all(bf16[8,16,1024]{2,1,0:T(8,128)(2,1)S(1)} %bitcast.27), channel_id=1, replica_groups={{0,48,64,112,128,176,192,240},{16,32,80,96,144,160,208,224},{1,49,65,11..., dimensions={0} | all-to-all | bytes 524288 | tf_op jit(solution)/shard_map/all_to_all | solution.py:655
  158.0 3.6 %all-to-all-start.3 = ((bf16[16,16,1024]{2,1,0:T(8,128)(2,1)}), bf16[16,16,1024]{2,1,0:T(8,128)(2,1)S(1)}, u32[]{:S(2)}, u32[]{:S(2)}) async-start(bf16[16,16,1024]{2,1,0:T(8,128)(2,1)} %shard_map.142), calls=%async_computation.3 | async-start | bytes 1048576 | tf_op jit(solution)/shard_map/all_to_all | solution.py:658
  161.6 16.4 %all-to-all-done.3 = bf16[16,16,1024]{2,1,0:T(8,128)(2,1)S(1)} async-done(((bf16[16,16,1024]{2,1,0:T(8,128)(2,1)}), bf16[16,16,1024]{2,1,0:T(8,128)(2,1)S(1)}, u32[]{:S(2)}, u32[]{:S(2)}) %all-to-all-start.3) | async-done | bytes 524320 | tf_op jit(solution)/shard_map/all_to_all | solution.py:658
  180.5 2.7 %shard_map.143 = (f32[128,2048]{1,0:T(8,128)}, f32[128,2048]{1,0:T(8,128)}, f32[128,2048]{1,0:T(8,128)}, f32[128,2048]{1,0:T(8,128)}) custom-call(s32[1]{0:T(128)} %bitcast.flip, bf16[8,2,16,1024]{3,2,1,0:T(8,128)(2,1)S(1)} %bitcast.26, f32[128,2048]{1,0:T(8,128)S(1)} %copy-done, f32[128,2048]{1,0:T(8,128)S(1)} %copy-done.2, f32[128,2048]{1,0:T(8,128)S(1)} %copy-done.12, ...), custom_call_target="tpu_custom_call" | custom-call | tf_op jit(solution)/shard_map/pallas_call | solution.py:535
  (116 shorter events, 49.8 us)
Async XLA Ops:
  2.2 16.1 %collective-permute-start.4 = (bf16[288,2048]{1,0:T(8,128)(2,1)S(1)}, bf16[288,2048]{1,0:T(8,128)(2,1)S(1)}, u32[]{:S(2)}, u32[]{:S(2)}) collective-permute-start(bf16[288,2048]{1,0:T(8,128)(2,1)S(1)} %copy-done.6), channel_id=1, source_target_pairs={{0,1},{1,0},{2,3},{3,2},{4,5},{5,4},{6,7},{7,6},{8,9},{9,8},{10,11... | collective-permute-start | bytes 3538952 | tf_op jit(solution)/shard_map/ppermute | solution.py:42
  2.7 14.0 %collective-permute-start.2 = (bf16[2,128,1024]{2,1,0:T(8,128)(2,1)S(1)}, bf16[2,128,1024]{2,1,0:T(8,128)(2,1)}, u32[]{:S(2)}, u32[]{:S(2)}) collective-permute-start(bf16[2,128,1024]{2,1,0:T(8,128)(2,1)S(1)} %pad_maximum_fusion.refs_0_), channel_id=1, source_target_pairs={{16,2},{2,16},{0,18},{18,0},{17,3},{3,17},{1,19},{19,1},{20,6},{6,... | collective-permute-start | bytes 1572872 | tf_op jit(solution)/shard_map/ppermute | solution.py:54
  3.3 15.0 %collective-permute-start.1 = (bf16[2,128,1024]{2,1,0:T(8,128)(2,1)S(1)}, bf16[2,128,1024]{2,1,0:T(8,128)(2,1)}, u32[]{:S(2)}, u32[]{:S(2)}) collective-permute-start(bf16[2,128,1024]{2,1,0:T(8,128)(2,1)S(1)} %pad_maximum_fusion.refs_0_), channel_id=1, source_target_pairs={{0,4},{4,8},{8,12},{12,0},{1,5},{5,9},{9,13},{13,1},{2,6},{6,10},{... | collective-permute-start | bytes 1572872 | tf_op jit(solution)/shard_map/ppermute | solution.py:50
  4.8 13.5 %collective-permute-start = (bf16[2,128,1024]{2,1,0:T(8,128)(2,1)S(1)}, bf16[2,128,1024]{2,1,0:T(8,128)(2,1)}, u32[]{:S(2)}, u32[]{:S(2)}) collective-permute-start(bf16[2,128,1024]{2,1,0:T(8,128)(2,1)S(1)} %pad_maximum_fusion.refs_0_), channel_id=1, source_target_pairs={{4,0},{8,4},{12,8},{0,12},{5,1},{9,5},{13,9},{1,13},{6,2},{10,6},{... | collective-permute-start | bytes 1572872 | tf_op jit(solution)/shard_map/ppermute | solution.py:46
  8.3 11.1 %collective-permute-start.5 = (s32[2,144]{1,0:T(2,128)S(1)}, s32[2,144]{1,0:T(2,128)S(1)}, u32[]{:S(2)}, u32[]{:S(2)}) collective-permute-start(s32[2,144]{1,0:T(2,128)S(1)} %copy-done.19), channel_id=1, source_target_pairs={{0,1},{1,0},{2,3},{3,2},{4,5},{5,4},{6,7},{7,6},{8,9},{9,8},{10,11... | collective-permute-start | bytes 3464 | tf_op jit(solution)/shard_map/ppermute | solution.py:42
  19.4 17.0 %collective-permute-start.7 = (bf16[2,128,1024]{2,1,0:T(8,128)(2,1)}, bf16[2,128,1024]{2,1,0:T(8,128)(2,1)}, u32[]{:S(2)}, u32[]{:S(2)}) collective-permute-start(bf16[2,128,1024]{2,1,0:T(8,128)(2,1)} %collective-permute-done.2.refs_3_), channel_id=1, source_target_pairs={{0,4},{4,8},{8,12},{12,0},{1,5},{5,9},{9,13},{13,1},{2,6},{6,10},{... | collective-permute-start | bytes 1572872 | tf_op jit(solution)/shard_map/ppermute | solution.py:50
  21.0 15.5 %collective-permute-start.10 = (bf16[2,128,1024]{2,1,0:T(8,128)(2,1)}, bf16[2,128,1024]{2,1,0:T(8,128)(2,1)}, u32[]{:S(2)}, u32[]{:S(2)}) collective-permute-start(bf16[2,128,1024]{2,1,0:T(8,128)(2,1)} %collective-permute-done.1.refs_2_), channel_id=1, source_target_pairs={{1,32},{0,33},{33,64},{32,65},{65,96},{64,97},{97,128},{96,129},{1... | collective-permute-start | bytes 1572872 | tf_op jit(solution)/shard_map/ppermute | solution.py:62
  21.0 16.0 %collective-permute-start.9 = (bf16[2,128,1024]{2,1,0:T(8,128)(2,1)}, bf16[2,128,1024]{2,1,0:T(8,128)(2,1)}, u32[]{:S(2)}, u32[]{:S(2)}) collective-permute-start(bf16[2,128,1024]{2,1,0:T(8,128)(2,1)} %collective-permute-done.refs_1_), channel_id=1, source_target_pairs={{33,0},{32,1},{65,32},{64,33},{97,64},{96,65},{129,96},{128,97},{1... | collective-permute-start | bytes 1572872 | tf_op jit(solution)/shard_map/ppermute | solution.py:58
  24.8 13.9 %collective-permute-start.8 = (bf16[2,128,1024]{2,1,0:T(8,128)(2,1)}, bf16[2,128,1024]{2,1,0:T(8,128)(2,1)}, u32[]{:S(2)}, u32[]{:S(2)}) collective-permute-start(bf16[2,128,1024]{2,1,0:T(8,128)(2,1)} %collective-permute-done.refs_1_), channel_id=1, source_target_pairs={{16,2},{2,16},{0,18},{18,0},{17,3},{3,17},{1,19},{19,1},{20,6},{6,... | collective-permute-start | bytes 1572872 | tf_op jit(solution)/shard_map/ppermute | solution.py:54
  26.3 14.2 %collective-permute-start.6 = (bf16[2,128,1024]{2,1,0:T(8,128)(2,1)}, bf16[2,128,1024]{2,1,0:T(8,128)(2,1)}, u32[]{:S(2)}, u32[]{:S(2)}) collective-permute-start(bf16[2,128,1024]{2,1,0:T(8,128)(2,1)} %collective-permute-done.refs_1_), channel_id=1, source_target_pairs={{4,0},{8,4},{12,8},{0,12},{5,1},{9,5},{13,9},{1,13},{6,2},{10,6},{... | collective-permute-start | bytes 1572872 | tf_op jit(solution)/shard_map/ppermute | solution.py:46
  40.5 15.1 %collective-permute-start.12 = (bf16[2,128,1024]{2,1,0:T(8,128)(2,1)}, bf16[2,128,1024]{2,1,0:T(8,128)(2,1)S(1)}, u32[]{:S(2)}, u32[]{:S(2)}) collective-permute-start(bf16[2,128,1024]{2,1,0:T(8,128)(2,1)} %collective-permute-done.6.refs_4_), channel_id=1, source_target_pairs={{33,0},{32,1},{65,32},{64,33},{97,64},{96,65},{129,96},{128,97},{1... | collective-permute-start | bytes 1572872 | tf_op jit(solution)/shard_map/ppermute | solution.py:58
  41.1 14.5 %collective-permute-start.11 = (bf16[2,128,1024]{2,1,0:T(8,128)(2,1)}, bf16[2,128,1024]{2,1,0:T(8,128)(2,1)S(1)}, u32[]{:S(2)}, u32[]{:S(2)}) collective-permute-start(bf16[2,128,1024]{2,1,0:T(8,128)(2,1)} %collective-permute-done.8.refs_6_), channel_id=1, source_target_pairs={{4,0},{8,4},{12,8},{0,12},{5,1},{9,5},{13,9},{1,13},{6,2},{10,6},{... | collective-permute-start | bytes 1572872 | tf_op jit(solution)/shard_map/ppermute | solution.py:46
  44.1 14.1 %collective-permute-start.14 = (bf16[2,128,1024]{2,1,0:T(8,128)(2,1)}, bf16[2,128,1024]{2,1,0:T(8,128)(2,1)S(1)}, u32[]{:S(2)}, u32[]{:S(2)}) collective-permute-start(bf16[2,128,1024]{2,1,0:T(8,128)(2,1)} %collective-permute-done.10.refs_8_), channel_id=1, source_target_pairs={{16,2},{2,16},{0,18},{18,0},{17,3},{3,17},{1,19},{19,1},{20,6},{6,... | collective-permute-start | bytes 1572872 | tf_op jit(solution)/shard_map/ppermute | solution.py:54
  44.7 16.2 %collective-permute-start.15 = (bf16[2,128,1024]{2,1,0:T(8,128)(2,1)}, bf16[2,128,1024]{2,1,0:T(8,128)(2,1)S(1)}, u32[]{:S(2)}, u32[]{:S(2)}) collective-permute-start(bf16[2,128,1024]{2,1,0:T(8,128)(2,1)} %collective-permute-done.2.refs_3_), channel_id=1, source_target_pairs={{1,16},{0,17},{17,0},{16,1},{3,18},{2,19},{19,2},{18,3},{5,20},{4,... | collective-permute-start | bytes 1572872 | tf_op jit(solution)/shard_map/ppermute | solution.py:66
  48.2 15.5 %collective-permute-start.13 = (bf16[2,128,1024]{2,1,0:T(8,128)(2,1)}, bf16[2,128,1024]{2,1,0:T(8,128)(2,1)S(1)}, u32[]{:S(2)}, u32[]{:S(2)}) collective-permute-start(bf16[2,128,1024]{2,1,0:T(8,128)(2,1)} %collective-permute-done.8.refs_6_), channel_id=1, source_target_pairs={{1,32},{0,33},{33,64},{32,65},{65,96},{64,97},{97,128},{96,129},{1... | collective-permute-start | bytes 1572872 | tf_op jit(solution)/shard_map/ppermute | solution.py:62
  63.8 9.7 %collective-permute-start.16 = (bf16[288,2048]{1,0:T(8,128)(2,1)S(1)}, bf16[288,2048]{1,0:T(8,128)(2,1)S(1)}, u32[]{:S(2)}, u32[]{:S(2)}) collective-permute-start(bf16[288,2048]{1,0:T(8,128)(2,1)S(1)} %copy-done.3), channel_id=1, source_target_pairs={{0,1},{1,0},{2,3},{3,2},{4,5},{5,4},{6,7},{7,6},{8,9},{9,8},{10,11... | collective-permute-start | bytes 3538952 | tf_op jit(solution)/shard_map/ppermute | solution.py:42
  63.8 9.7 %collective-permute-start.17 = (bf16[288,2048]{1,0:T(8,128)(2,1)S(1)}, bf16[288,2048]{1,0:T(8,128)(2,1)S(1)}, u32[]{:S(2)}, u32[]{:S(2)}) collective-permute-start(bf16[288,2048]{1,0:T(8,128)(2,1)S(1)} %get-tuple-element.143.picked_own), channel_id=1, source_target_pairs={{0,1},{1,0},{2,3},{3,2},{4,5},{5,4},{6,7},{7,6},{8,9},{9,8},{10,11... | collective-permute-start | bytes 3538952 | tf_op jit(solution)/shard_map/ppermute | solution.py:42
  82.7 12.2 %collective-permute-start.22 = (bf16[3,128,512]{2,1,0:T(8,128)(2,1)S(1)}, bf16[3,128,512]{2,1,0:T(8,128)(2,1)S(1)}, u32[]{:S(2)}, u32[]{:S(2)}) collective-permute-start(bf16[3,128,512]{2,1,0:T(8,128)(2,1)S(1)} %get-tuple-element.154), channel_id=1, source_target_pairs={{1,32},{0,33},{33,64},{32,65},{65,96},{64,97},{97,128},{96,129},{1... | collective-permute-start | bytes 1179656 | tf_op jit(solution)/shard_map/ppermute | solution.py:62
  83.7 11.2 %collective-permute-start.23 = (bf16[3,128,512]{2,1,0:T(8,128)(2,1)S(1)}, bf16[3,128,512]{2,1,0:T(8,128)(2,1)S(1)}, u32[]{:S(2)}, u32[]{:S(2)}) collective-permute-start(bf16[3,128,512]{2,1,0:T(8,128)(2,1)S(1)} %get-tuple-element.155), channel_id=1, source_target_pairs={{33,0},{32,1},{65,32},{64,33},{97,64},{96,65},{129,96},{128,97},{1... | collective-permute-start | bytes 1179656 | tf_op jit(solution)/shard_map/ppermute | solution.py:58
  96.4 21.8 %all-to-all-start = ((bf16[8,128,512]{2,1,0:T(8,128)(2,1)}), bf16[8,128,512]{2,1,0:T(8,128)(2,1)}, u32[]{:S(2)}, u32[]{:S(2)}) async-start(bf16[8,128,512]{2,1,0:T(8,128)(2,1)} %copy-done.4), calls=%async_computation | async-start | bytes 2097152 | tf_op jit(solution)/shard_map/all_to_all | solution.py:640
  102.9 12.6 %collective-permute-start.25 = (bf16[3,128,512]{2,1,0:T(8,128)(2,1)}, bf16[3,128,512]{2,1,0:T(8,128)(2,1)S(1)}, u32[]{:S(2)}, u32[]{:S(2)}) collective-permute-start(bf16[3,128,512]{2,1,0:T(8,128)(2,1)} %copy-done.21), channel_id=1, source_target_pairs={{1,32},{0,33},{33,64},{32,65},{65,96},{64,97},{97,128},{96,129},{1... | collective-permute-start | bytes 1179656 | tf_op jit(solution)/shard_map/ppermute | solution.py:62
  102.9 12.6 %collective-permute-start.26 = (bf16[3,128,512]{2,1,0:T(8,128)(2,1)}, bf16[3,128,512]{2,1,0:T(8,128)(2,1)S(1)}, u32[]{:S(2)}, u32[]{:S(2)}) collective-permute-start(bf16[3,128,512]{2,1,0:T(8,128)(2,1)} %copy-done.20), channel_id=1, source_target_pairs={{33,0},{32,1},{65,32},{64,33},{97,64},{96,65},{129,96},{128,97},{1... | collective-permute-start | bytes 1179656 | tf_op jit(solution)/shard_map/ppermute | solution.py:58
  118.1 19.7 %all-to-all-start.1 = ((bf16[8,128,512]{2,1,0:T(8,128)(2,1)}), bf16[8,128,512]{2,1,0:T(8,128)(2,1)S(1)}, u32[]{:S(2)}, u32[]{:S(2)}) async-start(bf16[8,128,512]{2,1,0:T(8,128)(2,1)} %copy-done.5), calls=%async_computation.1 | async-start | bytes 2097152 | tf_op jit(solution)/shard_map/all_to_all | solution.py:640
  158.0 20.0 %all-to-all-start.3 = ((bf16[16,16,1024]{2,1,0:T(8,128)(2,1)}), bf16[16,16,1024]{2,1,0:T(8,128)(2,1)S(1)}, u32[]{:S(2)}, u32[]{:S(2)}) async-start(bf16[16,16,1024]{2,1,0:T(8,128)(2,1)} %shard_map.142), calls=%async_computation.3 | async-start | bytes 1048576 | tf_op jit(solution)/shard_map/all_to_all | solution.py:658
  (36 other events, 270.8 us)

commit v11 on v9

--- a/solution.py
+++ b/solution.py
@@ -76,7 +76,7 @@
 CORE_AT = HALF_AT + 1
 SENT = (3, 3, 2)
 TILE = 256
-PARTS = (3, 1)
+PARTS = (1, 3)
 
 
 def split_kernel(order, student, teacher, out):
@@ -102,6 +102,21 @@
         compiler_params=pltpu.CompilerParams(vmem_limit_bytes=SMALL_LIMIT),
         cost_estimate=pl.CostEstimate(flops=0, bytes_accessed=1536 * 1024, transcendentals=0),
     )(order, student, teacher)
+
+
+def halves_kernel(pair, first, second):
+    first[...] = pair[0]
+    second[...] = pair[1]
+
+
+def both_halves(pair):
+    _, rows, columns = pair.shape
+    return pl.pallas_call(
+        halves_kernel,
+        out_shape=[jax.ShapeDtypeStruct((rows, columns), pair.dtype)] * 2,
+        compiler_params=pltpu.CompilerParams(vmem_limit_bytes=SMALL_LIMIT),
+        cost_estimate=pl.CostEstimate(flops=0, bytes_accessed=1024 * 1024, transcendentals=0),
+    )(pair)
 
 
 def place_blocks(order, step, packed, early, late):
@@ -251,11 +266,10 @@
     order, student_mix, teacher_mix, student_part, teacher_part, residual_own, residual_other, picked_own, picked_other,
     scale, *refs
 ):
-    weights, (student_out, matched_out, sums_out, held) = refs[:LATE], refs[LATE:]
-    for block in range(LATE):
-        rows = slice(block * 128, (block + 1) * 128)
-        held[0, rows, :] = weights[block][0]
-        held[1, rows, :] = weights[block][1]
+    pair, student_weight, teacher_weight, student_out, matched_out, sums_out, held = refs
+    held[:, :128, :] = pair[...]
+    held[0, 128:, :] = student_weight[...]
+    held[1, 128:, :] = teacher_weight[...]
     factor = scale[...] * (KIN ** (-0.5))
     student_sum = student_part[...] + jnp.dot(student_mix[...], held[0], preferred_element_type=jnp.float32)
     teacher_sum = teacher_part[...] + jnp.dot(teacher_mix[...], held[1], preferred_element_type=jnp.float32)
@@ -297,7 +311,8 @@
             in_specs=[whole, whole, column, column]
             + [tokens] * 4
             + [pl.BlockSpec((1, width), lambda j, order: (0, order[HALF_AT] * steps + j))]
-            + [pl.BlockSpec((2, 128, width), lambda j, order: (0, 0, j))] * LATE,
+            + [pl.BlockSpec((2, 128, width), lambda j, order: (0, 0, j))]
+            + [pl.BlockSpec((128, width), lambda j, order: (0, j))] * 2,
             out_specs=[column, column, pl.BlockSpec((rows, 128), lambda j, order: (0, 0))],
             scratch_shapes=[pltpu.VMEM((2, LATE * 128, width), jnp.bfloat16)],
         ),
@@ -502,24 +517,6 @@
     )(copies)
 
 
-def moments_kernel(first, squares, first_out, squares_out):
-    first_out[...] = 0.9 * first[...]
-    squares_out[...] = 0.95 * squares[...]
-
-
-def scale_moments(first, squares):
-    rows = pl.BlockSpec((64, DOUT), lambda i: (i, 0))
-    return pl.pallas_call(
-        moments_kernel,
-        grid=(2,),
-        in_specs=[rows, rows],
-        out_specs=[rows, rows],
-        out_shape=[jax.ShapeDtypeStruct(first.shape, jnp.float32)] * 2,
-        compiler_params=pltpu.CompilerParams(vmem_limit_bytes=SMALL_LIMIT),
-        cost_estimate=pl.CostEstimate(flops=0, bytes_accessed=4 * 1024 * 1024, transcendentals=0),
-    )(first, squares)
-
-
 def update_kernel(flip, grads, weight, teacher, first, squares, weight_out, teacher_out, first_out, squares_out):
     rows = []
     for index in range(grads.shape[0]):
@@ -528,8 +525,8 @@
         right = jnp.where(swap, grads[index, 0], grads[index, 1])
         rows.append(jnp.concatenate([left, right], axis=1))
     grad = jnp.concatenate(rows, axis=0).astype(jnp.float32)
-    first_next = first[...] + 0.1 * grad
-    squares_next = squares[...] + 0.05 * grad * grad
+    first_next = 0.9 * first[...] + 0.1 * grad
+    squares_next = 0.95 * squares[...] + 0.05 * grad * grad
     held = weight[...]
     weight_next = held - 0.1 * (first_next / (jnp.sqrt(squares_next) + 1e-08) + 0.04 * held)
     weight_out[...] = weight_next
@@ -608,17 +605,19 @@
         )
     )
     prepared = prepare_teacher(order, teacher_mix, teacher_other, residual, places, places_other)
+    across_two = from_y_next(across_up)
     (
-        across_two, passed_two, passed_across_up, passed_across_down, passed_across, prepared, other_sent, residual_sent
+        (student_two, teacher_two), passed_two, passed_across_up, passed_across_down, passed_across, prepared,
+        other_sent, residual_sent,
     ) = lax.optimization_barrier(
         (
-            from_y_next(across_up), from_z_next(up_two), from_z_previous(across_up), from_x_near(passed_down),
+            both_halves(across_two), from_z_next(up_two), from_z_previous(across_up), from_x_near(passed_down),
             from_x_twin(across), prepared, other_sent, residual,
         )
     )
     student_early, student_late, sent_mix, kept_mix = student_prepared
     teacher_early, teacher_late, picked = prepared
-    passed_across_two = from_z_next(across_two)
+    student_two, teacher_two = from_z_next(student_two), from_z_previous(teacher_two)
     residual_other, picked_other, other = swap_cores(residual_sent), swap_cores(picked), swap_cores(other_sent)
     student_part, teacher_part = early_forward(
         (
@@ -629,7 +628,7 @@
         teacher_early,
     )
     student_out, matched, sums = late_forward(
-        order, (other, passed_across_two), student_late, teacher_late, student_part, teacher_part, residual,
+        order, (other, student_two, teacher_two), student_late, teacher_late, student_part, teacher_part, residual,
         residual_other, picked, picked_other, scale
     )
     more_sums = swap_cores(sums)
@@ -656,11 +655,7 @@
     first_chip, last_rows = lax.optimization_barrier((over_fsdp(first_rows), add_passed(last_kept, last_passed)))
     last_chip = over_fsdp(last_rows)
     student_tokens = join_tokens(order, first_own, last_own, *swapped)
-    moment_held, second_held, first_chip = lax.optimization_barrier((moment, second, first_chip))
-    moments = scale_moments(moment_held, second_held)
-    first_chip, last_chip, student_tokens, moments = lax.optimization_barrier(
-        (first_chip, last_chip, student_tokens, moments)
-    )
+    first_chip, last_chip, student_tokens = lax.optimization_barrier((first_chip, last_chip, student_tokens))
     total = total_rows(first_chip, last_chip)
     by_copy = lax.all_to_all(
         total.reshape(8, 16, half), ("z", "xlo"), 0, 0, axis_index_groups=DP_GROUPS
@@ -668,7 +663,7 @@
     full = lax.all_to_all(spread_rows(by_copy, 16), ("z", "xlo"), 0, 0)
     flip = ((core + xhi) & 1).astype(jnp.int32).reshape(1)
     weight_next, teacher_next, first_next, squares_next = adamw_update(
-        flip, full.reshape(8, 2, 16, half), student_weight, teacher_weight, *moments
+        flip, full.reshape(8, 2, 16, half), student_weight, teacher_weight, moment, second
     )
     return (weight_next, teacher_next, first_next, squares_next, student_tokens)
 

time: 190 us -> 187 us (0.984); the launches traced: 186 us -> 186 us
  starting transfers between devices: 47.2 us -> 50.4 us
  local copies, waits for them, and re-layouts: 14.2 us -> 11.3 us
    all_to_all x2, waiting for transfers between devices: 10.9 us -> 16.8 us  [over_fsdp(): lax.all_to_all(rows, ('xlo', 'y', 'xhi'), 0, 0, axis_index_groups=FSDP_GR...]
    ppermute x5, waiting for transfers between devices: 6.13 us -> 0.56 us  [from_z_next(): return lax.ppermute(value, ('z', 'core'), with_core_flip(from_next(8)))]
    unnamed x60 -> x48, local copies, waits for them, and re-layouts: 12.8 us -> 9.88 us
    ppermute x4 -> x5, waiting for transfers between devices: 5.31 us -> 3.37 us  [from_z_previous(): return lax.ppermute(value, ('z', 'core'), with_core_flip(from_previous(8)))]
  transfers between devices with their start and end apart: 32 -> 33, of which waited for: 17 -> 15; matrix products, arithmetic and copies ran while one was open for 0% -> 0% of each run, Pallas kernels for 13% -> 16%
where the time goes in v11:
time: 187 us; the launch traced here: 186 us
  waiting for transfers between devices  68 us (36%)
  starting transfers between devices  50.4 us (27%)
  Pallas kernels  39.8 us (21%)
  blocking collectives  15.7 us (8%)
  local copies, waits for them, and re-layouts  11.3 us (6%)
    all_to_all x2, waiting for transfers between devices, over_fsdp(): lax.all_to_all(rows, ('xlo', 'y', 'xhi'), 0, 0, axis_index_groups=FSDP_GR...  16.8 us
    all_to_all x1, waiting for transfers between devices, shards(): full = lax.all_to_all(spread_rows(by_copy, 16), ('z', 'xlo'), 0, 0)  15.9 us
    all_to_all x1, blocking collectives, shards(): lax.all_to_all(total.reshape(8, 16, half), ('z', 'xlo'), 0, 0, axis_index...  15.7 us
    ppermute x3, waiting for transfers between devices, from_x_near(): return lax.ppermute(value, ('xlo', 'xhi'), X_NEAR)  12.8 us
    ppermute x3, waiting for transfers between devices, from_x_twin(): return lax.ppermute(value, ('xlo', 'core'), with_core_flip(CORE_SWAP))  12.2 us
    all_to_all x2, starting transfers between devices, over_fsdp(): lax.all_to_all(rows, ('xlo', 'y', 'xhi'), 0, 0, axis_index_groups=FSDP_GR...  11.1 us
    ppermute x5, starting transfers between devices, from_z_next(): return lax.ppermute(value, ('z', 'core'), with_core_flip(from_next(8)))  10.3 us
    unnamed x48, local copies, waits for them, and re-layouts  9.88 us
  transfers between devices with their start and end apart: 33, of which 15 were waited for; matrix products, arithmetic and copies ran while one was open for 0% of the time, Pallas kernels for 16%

profile of v11, /device:TPU:4, one launch (start us, length us, event | category | flops | bytes accessed | tf_op | source)
XLA Modules:
  0.0 186.2 jit_solution(15057221787231470926)
XLA Ops:
  8.3 8.5 %collective-permute-done.2.refs_3_ = bf16[2,128,1024]{2,1,0:T(8,128)(2,1)} collective-permute-done((bf16[2,128,1024]{2,1,0:T(8,128)(2,1)S(1)}, bf16[2,128,1024]{2,1,0:T(8,128)(2,1)}, u32[]{:S(2)}, u32[]{:S(2)}) %collective-permute-start.2) | collective-permute-done | bytes 524320 | tf_op jit(solution)/shard_map/ppermute | solution.py:54
  21.0 3.8 %collective-permute-start.9 = (bf16[2,128,1024]{2,1,0:T(8,128)(2,1)}, bf16[2,128,1024]{2,1,0:T(8,128)(2,1)}, u32[]{:S(2)}, u32[]{:S(2)}) collective-permute-start(bf16[2,128,1024]{2,1,0:T(8,128)(2,1)} %collective-permute-done.refs_1_), channel_id=1, source_target_pairs={{33,0},{32,1},{65,32},{64,33},{97,64},{96,65},{129,96},{128,97},{1... | collective-permute-start | bytes 1572872 | tf_op jit(solution)/shard_map/ppermute | solution.py:58
  26.3 2.0 %collective-permute-start.6 = (bf16[2,128,1024]{2,1,0:T(8,128)(2,1)}, bf16[2,128,1024]{2,1,0:T(8,128)(2,1)}, u32[]{:S(2)}, u32[]{:S(2)}) collective-permute-start(bf16[2,128,1024]{2,1,0:T(8,128)(2,1)} %collective-permute-done.refs_1_), channel_id=1, source_target_pairs={{4,0},{8,4},{12,8},{0,12},{5,1},{9,5},{13,9},{1,13},{6,2},{10,6},{... | collective-permute-start | bytes 1572872 | tf_op jit(solution)/shard_map/ppermute | solution.py:46
  30.9 4.6 %shard_map.129 = (bf16[576,1792]{1,0:T(8,128)(2,1)S(1)}, bf16[576,256]{1,0:T(8,128)(2,1)S(1)}, bf16[8,128,576]{2,1,0:T(8,128)(2,1)S(1)}, bf16[8,128,576]{2,1,0:T(8,128)(2,1)S(1)}) custom-call(s32[18]{0:T(128)S(1)} %stack.87.order, bf16[288,2048]{1,0:T(8,128)(2,1)S(1)} %copy-done.10, bf16[288,2048]{1,0:T(8,128)(2,1)S(1)} %copy-done.12), custom_call_target="tpu_custom_call" | custom-call | bytes 7340032 | tf_op jit(solution)/shard_map/pallas_call | solution.py:178
  41.1 3.1 %collective-permute-start.11 = (bf16[2,128,1024]{2,1,0:T(8,128)(2,1)}, bf16[2,128,1024]{2,1,0:T(8,128)(2,1)S(1)}, u32[]{:S(2)}, u32[]{:S(2)}) collective-permute-start(bf16[2,128,1024]{2,1,0:T(8,128)(2,1)} %collective-permute-done.8.refs_6_), channel_id=1, source_target_pairs={{4,0},{8,4},{12,8},{0,12},{5,1},{9,5},{13,9},{1,13},{6,2},{10,6},{... | collective-permute-start | bytes 1572872 | tf_op jit(solution)/shard_map/ppermute | solution.py:46
  44.7 3.5 %collective-permute-start.15 = (bf16[2,128,1024]{2,1,0:T(8,128)(2,1)}, bf16[2,128,1024]{2,1,0:T(8,128)(2,1)S(1)}, u32[]{:S(2)}, u32[]{:S(2)}) collective-permute-start(bf16[2,128,1024]{2,1,0:T(8,128)(2,1)} %collective-permute-done.2.refs_3_), channel_id=1, source_target_pairs={{1,16},{0,17},{17,0},{16,1},{3,18},{2,19},{19,2},{18,3},{5,20},{4,... | collective-permute-start | bytes 1572872 | tf_op jit(solution)/shard_map/ppermute | solution.py:66
  49.3 5.9 %shard_map.131 = (bf16[576,1792]{1,0:T(8,128)(2,1)S(1)}, bf16[576,256]{1,0:T(8,128)(2,1)S(1)}, bf16[288,2048]{1,0:T(8,128)(2,1)S(1)}) custom-call(s32[18]{0:T(128)S(1)} %stack.87.order, bf16[288,2048]{1,0:T(8,128)(2,1)S(1)} %copy-done.7, bf16[288,2048]{1,0:T(8,128)(2,1)S(1)} %copy-done.9, bf16[288,2048]{1,0:T(8,128)(2,1)S(1)} %copy-done.5, ...), custom_call_target="tpu_custom_call" | custom-call | flops 509607936 | bytes 9437184 | tf_op jit(solution)/shard_map/pallas_call | solution.py:208
  55.6 2.6 %collective-permute-done.14.refs_12_ = bf16[2,128,1024]{2,1,0:T(8,128)(2,1)S(1)} collective-permute-done((bf16[2,128,1024]{2,1,0:T(8,128)(2,1)}, bf16[2,128,1024]{2,1,0:T(8,128)(2,1)S(1)}, u32[]{:S(2)}, u32[]{:S(2)}) %collective-permute-start.14) | collective-permute-done | bytes 524320 | tf_op jit(solution)/shard_map/ppermute | solution.py:54
  58.3 2.6 %collective-permute-done.15.refs_13_ = bf16[2,128,1024]{2,1,0:T(8,128)(2,1)S(1)} collective-permute-done((bf16[2,128,1024]{2,1,0:T(8,128)(2,1)}, bf16[2,128,1024]{2,1,0:T(8,128)(2,1)S(1)}, u32[]{:S(2)}, u32[]{:S(2)}) %collective-permute-start.15) | collective-permute-done | bytes 524320 | tf_op jit(solution)/shard_map/ppermute | solution.py:66
  60.9 2.9 %collective-permute-done.13.refs_11_ = bf16[2,128,1024]{2,1,0:T(8,128)(2,1)S(1)} collective-permute-done((bf16[2,128,1024]{2,1,0:T(8,128)(2,1)}, bf16[2,128,1024]{2,1,0:T(8,128)(2,1)S(1)}, u32[]{:S(2)}, u32[]{:S(2)}) %collective-permute-start.13) | collective-permute-done | bytes 524320 | tf_op jit(solution)/shard_map/ppermute | solution.py:62
  66.0 6.9 %shard_map.132 = (f32[576,1024]{1,0:T(8,128)S(1)}, f32[576,1024]{1,0:T(8,128)S(1)}) custom-call(bf16[576,1792]{1,0:T(8,128)(2,1)S(1)} %get-tuple-element.132.student_mix, bf16[576,1792]{1,0:T(8,128)(2,1)S(1)} %get-tuple-element.133.teacher_mix, bf16[2,128,1024]{2,1,0:T(8,128)(2,1)S(1)} %copy-done.16, bf16[2,128,1024]{2,1,0:T(8,128)(2,1)} %collective-permute-done.refs_1_, ...), custom_call_target="tpu_custom_call" | custom-call | flops 4227858432 | bytes 17825792 | tf_op jit(solution)/shard_map/pallas_call | solution.py:251
  73.5 4.0 %shard_map.133 = (f32[576,1024]{1,0:T(8,128)S(1)}, f32[576,1024]{1,0:T(8,128)S(1)}, f32[576,128]{1,0:T(8,128)S(1)}) custom-call(s32[18]{0:T(128)S(1)} %stack.87.order, bf16[576,256]{1,0:T(8,128)(2,1)S(1)} %get-tuple-element.116.student_mix, bf16[576,256]{1,0:T(8,128)(2,1)S(1)} %get-tuple-element.131.teacher_mix, ...), custom_call_target="tpu_custom_call" | custom-call | flops 603979776 | bytes 13631488 | tf_op jit(solution)/shard_map/pallas_call | solution.py:306
  81.9 3.0 %collective-permute-start.23 = (bf16[3,128,256]{2,1,0:T(8,128)(2,1)S(1)}, bf16[3,128,256]{2,1,0:T(8,128)(2,1)S(1)}, u32[]{:S(2)}, u32[]{:S(2)}) collective-permute-start(bf16[3,128,256]{2,1,0:T(8,128)(2,1)S(1)} %get-tuple-element.155), channel_id=1, source_target_pairs={{33,0},{32,1},{65,32},{64,33},{97,64},{96,65},{129,96},{128,97},{1... | collective-permute-start | bytes 589832 | tf_op jit(solution)/shard_map/ppermute | solution.py:58
  84.9 4.4 %shard_map.136 = (bf16[3,128,768]{2,1,0:T(8,128)(2,1)}, bf16[3,128,768]{2,1,0:T(8,128)(2,1)}, bf16[2,128,768]{2,1,0:T(8,128)(2,1)S(1)}, bf16[576,768]{1,0:T(8,12...) custom-call(s32[18]{0:T(128)S(1)} %stack.87.order, f32[576,1024]{1,0:T(8,128)S(1)} %get-tuple-element.147.student, ...), custom_call_target="tpu_custom_call" | custom-call | flops 905969664 | bytes 9437184 | tf_op jit(solution)/shard_map/pallas_call | solution.py:372
  89.4 3.0 %collective-permute-start.26 = (bf16[3,128,768]{2,1,0:T(8,128)(2,1)}, bf16[3,128,768]{2,1,0:T(8,128)(2,1)}, u32[]{:S(2)}, u32[]{:S(2)}) collective-permute-start(bf16[3,128,768]{2,1,0:T(8,128)(2,1)} %get-tuple-element.168), channel_id=1, source_target_pairs={{33,0},{32,1},{65,32},{64,33},{97,64},{96,65},{129,96},{128,97},{1... | collective-permute-start | bytes 1769480 | tf_op jit(solution)/shard_map/ppermute | solution.py:58
  95.9 5.2 %all-to-all-start = ((bf16[8,128,256]{2,1,0:T(8,128)(2,1)}), bf16[8,128,256]{2,1,0:T(8,128)(2,1)}, u32[]{:S(2)}, u32[]{:S(2)}) async-start(bf16[8,128,256]{2,1,0:T(8,128)(2,1)} %copy-done.6), calls=%async_computation | async-start | bytes 1048576 | tf_op jit(solution)/shard_map/all_to_all | solution.py:645
  103.1 9.6 %collective-permute-done.27.refs_2_ = bf16[2,128,768]{2,1,0:T(8,128)(2,1)S(1)} collective-permute-done((bf16[2,128,768]{2,1,0:T(8,128)(2,1)}, bf16[2,128,768]{2,1,0:T(8,128)(2,1)S(1)}, u32[]{:S(2)}, u32[]{:S(2)}) %collective-permute-start.27) | collective-permute-done | bytes 393248 | tf_op jit(solution)/shard_map/ppermute | solution.py:66
  112.7 2.5 %shard_map.139 = bf16[8,128,768]{2,1,0:T(8,128)(2,1)S(1)} custom-call(f32[8,128,768]{2,1,0:T(8,128)S(1)} %shard_map.137.kept, bf16[3,128,768]{2,1,0:T(8,128)(2,1)} %collective-permute-done.25.refs_0_, bf16[3,128,768]{2,1,0:T(8,128)(2,1)} %collective-permute-done.26.refs_1_, bf16[2,128,768]{2,1,0:T(8,128)(2,1)S(1)} %collective-permute-done.27.refs_2_), custom_call_target="tpu_custom_call" | custom-call | tf_op jit(solution)/shard_map/pallas_call | solution.py:441
  116.3 5.9 %all-to-all-start.1 = ((bf16[8,128,768]{2,1,0:T(8,128)(2,1)}), bf16[8,128,768]{2,1,0:T(8,128)(2,1)S(1)}, u32[]{:S(2)}, u32[]{:S(2)}) async-start(bf16[8,128,768]{2,1,0:T(8,128)(2,1)} %copy-done), calls=%async_computation.1 | async-start | bytes 3145728 | tf_op jit(solution)/shard_map/all_to_all | solution.py:645
  125.8 16.8 %all-to-all-done.1.last = bf16[8,128,768]{2,1,0:T(8,128)(2,1)S(1)} async-done(((bf16[8,128,768]{2,1,0:T(8,128)(2,1)}), bf16[8,128,768]{2,1,0:T(8,128)(2,1)S(1)}, u32[]{:S(2)}, u32[]{:S(2)}) %all-to-all-start.1) | async-done | bytes 1572896 | tf_op jit(solution)/shard_map/all_to_all | solution.py:645
  143.9 15.7 %all_to_all.20.copies = bf16[8,16,1024]{2,1,0:T(8,128)(2,1)S(1)} all-to-all(bf16[8,16,1024]{2,1,0:T(8,128)(2,1)S(1)} %bitcast.27), channel_id=1, replica_groups={{0,48,64,112,128,176,192,240},{16,32,80,96,144,160,208,224},{1,49,65,11..., dimensions={0} | all-to-all | bytes 524288 | tf_op jit(solution)/shard_map/all_to_all | solution.py:660
  160.5 4.7 %all-to-all-start.3 = ((bf16[16,16,1024]{2,1,0:T(8,128)(2,1)}), bf16[16,16,1024]{2,1,0:T(8,128)(2,1)S(1)}, u32[]{:S(2)}, u32[]{:S(2)}) async-start(bf16[16,16,1024]{2,1,0:T(8,128)(2,1)} %shard_map.142), calls=%async_computation.3 | async-start | bytes 1048576 | tf_op jit(solution)/shard_map/all_to_all | solution.py:663
  165.2 15.9 %all-to-all-done.3 = bf16[16,16,1024]{2,1,0:T(8,128)(2,1)S(1)} async-done(((bf16[16,16,1024]{2,1,0:T(8,128)(2,1)}), bf16[16,16,1024]{2,1,0:T(8,128)(2,1)S(1)}, u32[]{:S(2)}, u32[]{:S(2)}) %all-to-all-start.3) | async-done | bytes 524320 | tf_op jit(solution)/shard_map/all_to_all | solution.py:663
  183.5 2.7 %shard_map.143 = (f32[128,2048]{1,0:T(8,128)}, f32[128,2048]{1,0:T(8,128)}, f32[128,2048]{1,0:T(8,128)}, f32[128,2048]{1,0:T(8,128)}) custom-call(s32[1]{0:T(128)} %bitcast.flip, bf16[8,2,16,1024]{3,2,1,0:T(8,128)(2,1)S(1)} %bitcast.26, f32[128,2048]{1,0:T(8,128)S(1)} %copy-done.2, f32[128,2048]{1,0:T(8,128)S(1)} %copy-done.4, f32[128,2048]{1,0:T(8,128)S(1)} %copy-done.13, ...), custom_call_target="tpu_custom_call" | custom-call | tf_op jit(solution)/shard_map/pallas_call | solution.py:540
  (110 shorter events, 45.6 us)
Async XLA Ops:
  2.2 16.1 %collective-permute-start.4 = (bf16[288,2048]{1,0:T(8,128)(2,1)S(1)}, bf16[288,2048]{1,0:T(8,128)(2,1)S(1)}, u32[]{:S(2)}, u32[]{:S(2)}) collective-permute-start(bf16[288,2048]{1,0:T(8,128)(2,1)S(1)} %copy-done.7), channel_id=1, source_target_pairs={{0,1},{1,0},{2,3},{3,2},{4,5},{5,4},{6,7},{7,6},{8,9},{9,8},{10,11... | collective-permute-start | bytes 3538952 | tf_op jit(solution)/shard_map/ppermute | solution.py:42
  2.7 14.0 %collective-permute-start.2 = (bf16[2,128,1024]{2,1,0:T(8,128)(2,1)S(1)}, bf16[2,128,1024]{2,1,0:T(8,128)(2,1)}, u32[]{:S(2)}, u32[]{:S(2)}) collective-permute-start(bf16[2,128,1024]{2,1,0:T(8,128)(2,1)S(1)} %pad_maximum_fusion.refs_0_), channel_id=1, source_target_pairs={{16,2},{2,16},{0,18},{18,0},{17,3},{3,17},{1,19},{19,1},{20,6},{6,... | collective-permute-start | bytes 1572872 | tf_op jit(solution)/shard_map/ppermute | solution.py:54
  3.3 15.0 %collective-permute-start.1 = (bf16[2,128,1024]{2,1,0:T(8,128)(2,1)S(1)}, bf16[2,128,1024]{2,1,0:T(8,128)(2,1)}, u32[]{:S(2)}, u32[]{:S(2)}) collective-permute-start(bf16[2,128,1024]{2,1,0:T(8,128)(2,1)S(1)} %pad_maximum_fusion.refs_0_), channel_id=1, source_target_pairs={{0,4},{4,8},{8,12},{12,0},{1,5},{5,9},{9,13},{13,1},{2,6},{6,10},{... | collective-permute-start | bytes 1572872 | tf_op jit(solution)/shard_map/ppermute | solution.py:50
  4.8 13.5 %collective-permute-start = (bf16[2,128,1024]{2,1,0:T(8,128)(2,1)S(1)}, bf16[2,128,1024]{2,1,0:T(8,128)(2,1)}, u32[]{:S(2)}, u32[]{:S(2)}) collective-permute-start(bf16[2,128,1024]{2,1,0:T(8,128)(2,1)S(1)} %pad_maximum_fusion.refs_0_), channel_id=1, source_target_pairs={{4,0},{8,4},{12,8},{0,12},{5,1},{9,5},{13,9},{1,13},{6,2},{10,6},{... | collective-permute-start | bytes 1572872 | tf_op jit(solution)/shard_map/ppermute | solution.py:46
  8.3 11.1 %collective-permute-start.5 = (s32[2,144]{1,0:T(2,128)S(1)}, s32[2,144]{1,0:T(2,128)S(1)}, u32[]{:S(2)}, u32[]{:S(2)}) collective-permute-start(s32[2,144]{1,0:T(2,128)S(1)} %copy-done.20), channel_id=1, source_target_pairs={{0,1},{1,0},{2,3},{3,2},{4,5},{5,4},{6,7},{7,6},{8,9},{9,8},{10,11... | collective-permute-start | bytes 3464 | tf_op jit(solution)/shard_map/ppermute | solution.py:42
  19.4 17.0 %collective-permute-start.7 = (bf16[2,128,1024]{2,1,0:T(8,128)(2,1)}, bf16[2,128,1024]{2,1,0:T(8,128)(2,1)}, u32[]{:S(2)}, u32[]{:S(2)}) collective-permute-start(bf16[2,128,1024]{2,1,0:T(8,128)(2,1)} %collective-permute-done.2.refs_3_), channel_id=1, source_target_pairs={{0,4},{4,8},{8,12},{12,0},{1,5},{5,9},{9,13},{13,1},{2,6},{6,10},{... | collective-permute-start | bytes 1572872 | tf_op jit(solution)/shard_map/ppermute | solution.py:50
  21.0 15.5 %collective-permute-start.10 = (bf16[2,128,1024]{2,1,0:T(8,128)(2,1)}, bf16[2,128,1024]{2,1,0:T(8,128)(2,1)}, u32[]{:S(2)}, u32[]{:S(2)}) collective-permute-start(bf16[2,128,1024]{2,1,0:T(8,128)(2,1)} %collective-permute-done.1.refs_2_), channel_id=1, source_target_pairs={{1,32},{0,33},{33,64},{32,65},{65,96},{64,97},{97,128},{96,129},{1... | collective-permute-start | bytes 1572872 | tf_op jit(solution)/shard_map/ppermute | solution.py:62
  21.0 16.0 %collective-permute-start.9 = (bf16[2,128,1024]{2,1,0:T(8,128)(2,1)}, bf16[2,128,1024]{2,1,0:T(8,128)(2,1)}, u32[]{:S(2)}, u32[]{:S(2)}) collective-permute-start(bf16[2,128,1024]{2,1,0:T(8,128)(2,1)} %collective-permute-done.refs_1_), channel_id=1, source_target_pairs={{33,0},{32,1},{65,32},{64,33},{97,64},{96,65},{129,96},{128,97},{1... | collective-permute-start | bytes 1572872 | tf_op jit(solution)/shard_map/ppermute | solution.py:58
  24.8 13.9 %collective-permute-start.8 = (bf16[2,128,1024]{2,1,0:T(8,128)(2,1)}, bf16[2,128,1024]{2,1,0:T(8,128)(2,1)}, u32[]{:S(2)}, u32[]{:S(2)}) collective-permute-start(bf16[2,128,1024]{2,1,0:T(8,128)(2,1)} %collective-permute-done.refs_1_), channel_id=1, source_target_pairs={{16,2},{2,16},{0,18},{18,0},{17,3},{3,17},{1,19},{19,1},{20,6},{6,... | collective-permute-start | bytes 1572872 | tf_op jit(solution)/shard_map/ppermute | solution.py:54
  26.3 14.2 %collective-permute-start.6 = (bf16[2,128,1024]{2,1,0:T(8,128)(2,1)}, bf16[2,128,1024]{2,1,0:T(8,128)(2,1)}, u32[]{:S(2)}, u32[]{:S(2)}) collective-permute-start(bf16[2,128,1024]{2,1,0:T(8,128)(2,1)} %collective-permute-done.refs_1_), channel_id=1, source_target_pairs={{4,0},{8,4},{12,8},{0,12},{5,1},{9,5},{13,9},{1,13},{6,2},{10,6},{... | collective-permute-start | bytes 1572872 | tf_op jit(solution)/shard_map/ppermute | solution.py:46
  40.5 15.1 %collective-permute-start.12 = (bf16[2,128,1024]{2,1,0:T(8,128)(2,1)}, bf16[2,128,1024]{2,1,0:T(8,128)(2,1)S(1)}, u32[]{:S(2)}, u32[]{:S(2)}) collective-permute-start(bf16[2,128,1024]{2,1,0:T(8,128)(2,1)} %collective-permute-done.6.refs_4_), channel_id=1, source_target_pairs={{33,0},{32,1},{65,32},{64,33},{97,64},{96,65},{129,96},{128,97},{1... | collective-permute-start | bytes 1572872 | tf_op jit(solution)/shard_map/ppermute | solution.py:58
  41.1 14.5 %collective-permute-start.11 = (bf16[2,128,1024]{2,1,0:T(8,128)(2,1)}, bf16[2,128,1024]{2,1,0:T(8,128)(2,1)S(1)}, u32[]{:S(2)}, u32[]{:S(2)}) collective-permute-start(bf16[2,128,1024]{2,1,0:T(8,128)(2,1)} %collective-permute-done.8.refs_6_), channel_id=1, source_target_pairs={{4,0},{8,4},{12,8},{0,12},{5,1},{9,5},{13,9},{1,13},{6,2},{10,6},{... | collective-permute-start | bytes 1572872 | tf_op jit(solution)/shard_map/ppermute | solution.py:46
  44.2 14.1 %collective-permute-start.14 = (bf16[2,128,1024]{2,1,0:T(8,128)(2,1)}, bf16[2,128,1024]{2,1,0:T(8,128)(2,1)S(1)}, u32[]{:S(2)}, u32[]{:S(2)}) collective-permute-start(bf16[2,128,1024]{2,1,0:T(8,128)(2,1)} %collective-permute-done.10.refs_8_), channel_id=1, source_target_pairs={{16,2},{2,16},{0,18},{18,0},{17,3},{3,17},{1,19},{19,1},{20,6},{6,... | collective-permute-start | bytes 1572872 | tf_op jit(solution)/shard_map/ppermute | solution.py:54
  44.7 16.2 %collective-permute-start.15 = (bf16[2,128,1024]{2,1,0:T(8,128)(2,1)}, bf16[2,128,1024]{2,1,0:T(8,128)(2,1)S(1)}, u32[]{:S(2)}, u32[]{:S(2)}) collective-permute-start(bf16[2,128,1024]{2,1,0:T(8,128)(2,1)} %collective-permute-done.2.refs_3_), channel_id=1, source_target_pairs={{1,16},{0,17},{17,0},{16,1},{3,18},{2,19},{19,2},{18,3},{5,20},{4,... | collective-permute-start | bytes 1572872 | tf_op jit(solution)/shard_map/ppermute | solution.py:66
  48.2 15.5 %collective-permute-start.13 = (bf16[2,128,1024]{2,1,0:T(8,128)(2,1)}, bf16[2,128,1024]{2,1,0:T(8,128)(2,1)S(1)}, u32[]{:S(2)}, u32[]{:S(2)}) collective-permute-start(bf16[2,128,1024]{2,1,0:T(8,128)(2,1)} %collective-permute-done.8.refs_6_), channel_id=1, source_target_pairs={{1,32},{0,33},{33,64},{32,65},{65,96},{64,97},{97,128},{96,129},{1... | collective-permute-start | bytes 1572872 | tf_op jit(solution)/shard_map/ppermute | solution.py:62
  80.7 14.3 %collective-permute-start.24 = (bf16[2,128,256]{2,1,0:T(8,128)(2,1)S(1)}, bf16[2,128,256]{2,1,0:T(8,128)(2,1)S(1)}, u32[]{:S(2)}, u32[]{:S(2)}) collective-permute-start(bf16[2,128,256]{2,1,0:T(8,128)(2,1)S(1)} %get-tuple-element.156), channel_id=1, source_target_pairs={{1,16},{0,17},{17,0},{16,1},{3,18},{2,19},{19,2},{18,3},{5,20},{4,... | collective-permute-start | bytes 393224 | tf_op jit(solution)/shard_map/ppermute | solution.py:66
  81.9 13.1 %collective-permute-start.22 = (bf16[3,128,256]{2,1,0:T(8,128)(2,1)S(1)}, bf16[3,128,256]{2,1,0:T(8,128)(2,1)S(1)}, u32[]{:S(2)}, u32[]{:S(2)}) collective-permute-start(bf16[3,128,256]{2,1,0:T(8,128)(2,1)S(1)} %get-tuple-element.154), channel_id=1, source_target_pairs={{1,32},{0,33},{33,64},{32,65},{65,96},{64,97},{97,128},{96,129},{1... | collective-permute-start | bytes 589832 | tf_op jit(solution)/shard_map/ppermute | solution.py:62
  81.9 13.1 %collective-permute-start.23 = (bf16[3,128,256]{2,1,0:T(8,128)(2,1)S(1)}, bf16[3,128,256]{2,1,0:T(8,128)(2,1)S(1)}, u32[]{:S(2)}, u32[]{:S(2)}) collective-permute-start(bf16[3,128,256]{2,1,0:T(8,128)(2,1)S(1)} %get-tuple-element.155), channel_id=1, source_target_pairs={{33,0},{32,1},{65,32},{64,33},{97,64},{96,65},{129,96},{128,97},{1... | collective-permute-start | bytes 589832 | tf_op jit(solution)/shard_map/ppermute | solution.py:58
  89.3 23.4 %collective-permute-start.25 = (bf16[3,128,768]{2,1,0:T(8,128)(2,1)}, bf16[3,128,768]{2,1,0:T(8,128)(2,1)}, u32[]{:S(2)}, u32[]{:S(2)}) collective-permute-start(bf16[3,128,768]{2,1,0:T(8,128)(2,1)} %get-tuple-element.167), channel_id=1, source_target_pairs={{1,32},{0,33},{33,64},{32,65},{65,96},{64,97},{97,128},{96,129},{1... | collective-permute-start | bytes 1769480 | tf_op jit(solution)/shard_map/ppermute | solution.py:62
  89.4 23.3 %collective-permute-start.26 = (bf16[3,128,768]{2,1,0:T(8,128)(2,1)}, bf16[3,128,768]{2,1,0:T(8,128)(2,1)}, u32[]{:S(2)}, u32[]{:S(2)}) collective-permute-start(bf16[3,128,768]{2,1,0:T(8,128)(2,1)} %get-tuple-element.168), channel_id=1, source_target_pairs={{33,0},{32,1},{65,32},{64,33},{97,64},{96,65},{129,96},{128,97},{1... | collective-permute-start | bytes 1769480 | tf_op jit(solution)/shard_map/ppermute | solution.py:58
  95.9 20.4 %all-to-all-start = ((bf16[8,128,256]{2,1,0:T(8,128)(2,1)}), bf16[8,128,256]{2,1,0:T(8,128)(2,1)}, u32[]{:S(2)}, u32[]{:S(2)}) async-start(bf16[8,128,256]{2,1,0:T(8,128)(2,1)} %copy-done.6), calls=%async_computation | async-start | bytes 1048576 | tf_op jit(solution)/shard_map/all_to_all | solution.py:645
  101.1 11.5 %collective-permute-start.27 = (bf16[2,128,768]{2,1,0:T(8,128)(2,1)}, bf16[2,128,768]{2,1,0:T(8,128)(2,1)S(1)}, u32[]{:S(2)}, u32[]{:S(2)}) collective-permute-start(bf16[2,128,768]{2,1,0:T(8,128)(2,1)} %copy-done.23), channel_id=1, source_target_pairs={{1,16},{0,17},{17,0},{16,1},{3,18},{2,19},{19,2},{18,3},{5,20},{4,... | collective-permute-start | bytes 1179656 | tf_op jit(solution)/shard_map/ppermute | solution.py:66
  116.3 26.3 %all-to-all-start.1 = ((bf16[8,128,768]{2,1,0:T(8,128)(2,1)}), bf16[8,128,768]{2,1,0:T(8,128)(2,1)S(1)}, u32[]{:S(2)}, u32[]{:S(2)}) async-start(bf16[8,128,768]{2,1,0:T(8,128)(2,1)} %copy-done), calls=%async_computation.1 | async-start | bytes 3145728 | tf_op jit(solution)/shard_map/all_to_all | solution.py:645
  160.5 20.6 %all-to-all-start.3 = ((bf16[16,16,1024]{2,1,0:T(8,128)(2,1)}), bf16[16,16,1024]{2,1,0:T(8,128)(2,1)S(1)}, u32[]{:S(2)}, u32[]{:S(2)}) async-start(bf16[16,16,1024]{2,1,0:T(8,128)(2,1)} %shard_map.142), calls=%async_computation.3 | async-start | bytes 1048576 | tf_op jit(solution)/shard_map/all_to_all | solution.py:663
  (33 other events, 307.1 us)

commit v12 on v11

--- a/solution.py
+++ b/solution.py
@@ -75,6 +75,7 @@
 HALF_AT = len(ORDER)
 CORE_AT = HALF_AT + 1
 SENT = (3, 3, 2)
+PADDED = (SENT, (3, 3, 3))
 TILE = 256
 PARTS = (1, 3)
 
@@ -351,14 +352,15 @@
     factor = scale[...] * (KIN ** (-0.5))
     held_out[...] = (factor * (values * student_part - matched[...] * matched_part)).astype(jnp.bfloat16)
     at = 0
-    for out in (next_out, previous_out, twin_out):
-        count = out.shape[0]
+    for out, count in zip((next_out, previous_out, twin_out), SENT):
         grad = jnp.dot(
             mix[at : at + count].reshape(count * 128, mix.shape[-1]),
             held_out[...],
             preferred_element_type=jnp.float32,
         )
-        out[...] = grad.astype(jnp.bfloat16).reshape(out.shape)
+        out[:count] = grad.astype(jnp.bfloat16).reshape((count,) + out.shape[1:])
+        for spare in range(count, out.shape[0]):
+            out[spare] = out[count - 1]
         at += count
 
 
@@ -382,10 +384,10 @@
                 pl.BlockSpec((1, TILE), lambda j, order: (0, order[HALF_AT] * steps + first + j)),
                 pl.BlockSpec((8, 128, rows), lambda j, order: (0, 0, 0)),
             ],
-            out_specs=[pl.BlockSpec((size, 128, TILE), lambda j, order: (0, 0, j)) for size in SENT]
+            out_specs=[pl.BlockSpec((size, 128, TILE), lambda j, order: (0, 0, j)) for size in PADDED[part]]
             + [out, half, half],
         ),
-        out_shape=[jax.ShapeDtypeStruct((size, 128, count * TILE), jnp.bfloat16) for size in SENT]
+        out_shape=[jax.ShapeDtypeStruct((size, 128, count * TILE), jnp.bfloat16) for size in PADDED[part]]
         + [
             jax.ShapeDtypeStruct((rows, count * TILE), jnp.bfloat16),
             jax.ShapeDtypeStruct((rows // 2, count * TILE), jnp.bfloat16),
@@ -426,10 +428,10 @@
 def add_kernel(kept, *refs):
     passed, out = refs[:-1], refs[-1]
     at = 0
-    for part in passed:
-        spot = slice(at, at + part.shape[0])
+    for part, count in zip(passed, SENT):
+        spot = slice(at, at + count)
         out[spot] = (kept[spot] + part[...].astype(jnp.float32)).astype(jnp.bfloat16)
-        at += part.shape[0]
+        at += count
 
 
 def add_passed(kept, passed):

time: 187 us -> 182 us (0.973)
  waiting for transfers between devices: 68 us -> 64.3 us
  starting transfers between devices: 50.4 us -> 47.7 us
    ppermute x3, waiting for transfers between devices: 12.2 us -> 4.38 us  [from_x_twin(): return lax.ppermute(value, ('xlo', 'core'), with_core_flip(CORE_SWAP))]
    ppermute x5, waiting for transfers between devices: 3.37 us -> 6.69 us  [from_z_previous(): return lax.ppermute(value, ('z', 'core'), with_core_flip(from_previous(8)))]
    unnamed x48 -> x46, local copies, waits for them, and re-layouts: 9.88 us -> 9.87 us
  transfers between devices with their start and end apart: 33 -> 33, of which waited for: 15 -> 17; matrix products, arithmetic and copies ran while one was open for 0% -> 0% of each run, Pallas kernels for 16% -> 16%
where the time goes in v12:
time: 182 us; the launch traced here: 181 us
  waiting for transfers between devices  64.3 us (35%)
  starting transfers between devices  47.7 us (26%)
  Pallas kernels  40 us (22%)
  blocking collectives  16.6 us (9%)
  local copies, waits for them, and re-layouts  11.3 us (6%)
    all_to_all x2, waiting for transfers between devices, over_fsdp(): lax.all_to_all(rows, ('xlo', 'y', 'xhi'), 0, 0, axis_index_groups=FSDP_GR...  17.6 us
    all_to_all x1, blocking collectives, shards(): lax.all_to_all(total.reshape(8, 16, half), ('z', 'xlo'), 0, 0, axis_index...  16.6 us
    all_to_all x1, waiting for transfers between devices, shards(): full = lax.all_to_all(spread_rows(by_copy, 16), ('z', 'xlo'), 0, 0)  15.8 us
    ppermute x3, waiting for transfers between devices, from_x_near(): return lax.ppermute(value, ('xlo', 'xhi'), X_NEAR)  12.8 us
    all_to_all x2, starting transfers between devices, over_fsdp(): lax.all_to_all(rows, ('xlo', 'y', 'xhi'), 0, 0, axis_index_groups=FSDP_GR...  10.9 us
    ppermute x5, starting transfers between devices, from_z_next(): return lax.ppermute(value, ('z', 'core'), with_core_flip(from_next(8)))  10.3 us
    unnamed x46, local copies, waits for them, and re-layouts  9.87 us
    pallas_call x1, Pallas kernels, early_forward(): pl.pallas_call(early_kernel, grid=(columns // width,), in_specs=[whole, w...  6.94 us
  transfers between devices with their start and end apart: 33, of which 17 were waited for; matrix products, arithmetic and copies ran while one was open for 0% of the time, Pallas kernels for 16%

profile of v12, /device:TPU:4, one launch (start us, length us, event | category | flops | bytes accessed | tf_op | source)
XLA Modules:
  0.0 180.9 jit_solution(11353984809299876227)
XLA Ops:
  8.3 8.5 %collective-permute-done.2.refs_3_ = bf16[2,128,1024]{2,1,0:T(8,128)(2,1)} collective-permute-done((bf16[2,128,1024]{2,1,0:T(8,128)(2,1)S(1)}, bf16[2,128,1024]{2,1,0:T(8,128)(2,1)}, u32[]{:S(2)}, u32[]{:S(2)}) %collective-permute-start.2) | collective-permute-done | bytes 524320 | tf_op jit(solution)/shard_map/ppermute | solution.py:54
  21.0 3.8 %collective-permute-start.9 = (bf16[2,128,1024]{2,1,0:T(8,128)(2,1)}, bf16[2,128,1024]{2,1,0:T(8,128)(2,1)}, u32[]{:S(2)}, u32[]{:S(2)}) collective-permute-start(bf16[2,128,1024]{2,1,0:T(8,128)(2,1)} %collective-permute-done.refs_1_), channel_id=1, source_target_pairs={{33,0},{32,1},{65,32},{64,33},{97,64},{96,65},{129,96},{128,97},{1... | collective-permute-start | bytes 1572872 | tf_op jit(solution)/shard_map/ppermute | solution.py:58
  26.3 2.0 %collective-permute-start.6 = (bf16[2,128,1024]{2,1,0:T(8,128)(2,1)}, bf16[2,128,1024]{2,1,0:T(8,128)(2,1)}, u32[]{:S(2)}, u32[]{:S(2)}) collective-permute-start(bf16[2,128,1024]{2,1,0:T(8,128)(2,1)} %collective-permute-done.refs_1_), channel_id=1, source_target_pairs={{4,0},{8,4},{12,8},{0,12},{5,1},{9,5},{13,9},{1,13},{6,2},{10,6},{... | collective-permute-start | bytes 1572872 | tf_op jit(solution)/shard_map/ppermute | solution.py:46
  30.9 4.6 %shard_map.129 = (bf16[576,1792]{1,0:T(8,128)(2,1)S(1)}, bf16[576,256]{1,0:T(8,128)(2,1)S(1)}, bf16[8,128,576]{2,1,0:T(8,128)(2,1)S(1)}, bf16[8,128,576]{2,1,0:T(8,128)(2,1)S(1)}) custom-call(s32[18]{0:T(128)S(1)} %stack.87.order, bf16[288,2048]{1,0:T(8,128)(2,1)S(1)} %copy-done.10, bf16[288,2048]{1,0:T(8,128)(2,1)S(1)} %copy-done.12), custom_call_target="tpu_custom_call" | custom-call | bytes 7340032 | tf_op jit(solution)/shard_map/pallas_call | solution.py:179
  41.1 3.1 %collective-permute-start.11 = (bf16[2,128,1024]{2,1,0:T(8,128)(2,1)}, bf16[2,128,1024]{2,1,0:T(8,128)(2,1)S(1)}, u32[]{:S(2)}, u32[]{:S(2)}) collective-permute-start(bf16[2,128,1024]{2,1,0:T(8,128)(2,1)} %collective-permute-done.8.refs_6_), channel_id=1, source_target_pairs={{4,0},{8,4},{12,8},{0,12},{5,1},{9,5},{13,9},{1,13},{6,2},{10,6},{... | collective-permute-start | bytes 1572872 | tf_op jit(solution)/shard_map/ppermute | solution.py:46
  44.7 3.5 %collective-permute-start.15 = (bf16[2,128,1024]{2,1,0:T(8,128)(2,1)}, bf16[2,128,1024]{2,1,0:T(8,128)(2,1)S(1)}, u32[]{:S(2)}, u32[]{:S(2)}) collective-permute-start(bf16[2,128,1024]{2,1,0:T(8,128)(2,1)} %collective-permute-done.2.refs_3_), channel_id=1, source_target_pairs={{1,16},{0,17},{17,0},{16,1},{3,18},{2,19},{19,2},{18,3},{5,20},{4,... | collective-permute-start | bytes 1572872 | tf_op jit(solution)/shard_map/ppermute | solution.py:66
  49.3 5.9 %shard_map.131 = (bf16[576,1792]{1,0:T(8,128)(2,1)S(1)}, bf16[576,256]{1,0:T(8,128)(2,1)S(1)}, bf16[288,2048]{1,0:T(8,128)(2,1)S(1)}) custom-call(s32[18]{0:T(128)S(1)} %stack.87.order, bf16[288,2048]{1,0:T(8,128)(2,1)S(1)} %copy-done.7, bf16[288,2048]{1,0:T(8,128)(2,1)S(1)} %copy-done.9, bf16[288,2048]{1,0:T(8,128)(2,1)S(1)} %copy-done.5, ...), custom_call_target="tpu_custom_call" | custom-call | flops 509607936 | bytes 9437184 | tf_op jit(solution)/shard_map/pallas_call | solution.py:209
  55.6 2.6 %collective-permute-done.14.refs_12_ = bf16[2,128,1024]{2,1,0:T(8,128)(2,1)S(1)} collective-permute-done((bf16[2,128,1024]{2,1,0:T(8,128)(2,1)}, bf16[2,128,1024]{2,1,0:T(8,128)(2,1)S(1)}, u32[]{:S(2)}, u32[]{:S(2)}) %collective-permute-start.14) | collective-permute-done | bytes 524320 | tf_op jit(solution)/shard_map/ppermute | solution.py:54
  58.3 2.6 %collective-permute-done.15.refs_13_ = bf16[2,128,1024]{2,1,0:T(8,128)(2,1)S(1)} collective-permute-done((bf16[2,128,1024]{2,1,0:T(8,128)(2,1)}, bf16[2,128,1024]{2,1,0:T(8,128)(2,1)S(1)}, u32[]{:S(2)}, u32[]{:S(2)}) %collective-permute-start.15) | collective-permute-done | bytes 524320 | tf_op jit(solution)/shard_map/ppermute | solution.py:66
  60.9 2.9 %collective-permute-done.13.refs_11_ = bf16[2,128,1024]{2,1,0:T(8,128)(2,1)S(1)} collective-permute-done((bf16[2,128,1024]{2,1,0:T(8,128)(2,1)}, bf16[2,128,1024]{2,1,0:T(8,128)(2,1)S(1)}, u32[]{:S(2)}, u32[]{:S(2)}) %collective-permute-start.13) | collective-permute-done | bytes 524320 | tf_op jit(solution)/shard_map/ppermute | solution.py:62
  66.0 6.9 %shard_map.132 = (f32[576,1024]{1,0:T(8,128)S(1)}, f32[576,1024]{1,0:T(8,128)S(1)}) custom-call(bf16[576,1792]{1,0:T(8,128)(2,1)S(1)} %get-tuple-element.132.student_mix, bf16[576,1792]{1,0:T(8,128)(2,1)S(1)} %get-tuple-element.133.teacher_mix, bf16[2,128,1024]{2,1,0:T(8,128)(2,1)S(1)} %copy-done.16, bf16[2,128,1024]{2,1,0:T(8,128)(2,1)} %collective-permute-done.refs_1_, ...), custom_call_target="tpu_custom_call" | custom-call | flops 4227858432 | bytes 17825792 | tf_op jit(solution)/shard_map/pallas_call | solution.py:252
  73.5 4.0 %shard_map.133 = (f32[576,1024]{1,0:T(8,128)S(1)}, f32[576,1024]{1,0:T(8,128)S(1)}, f32[576,128]{1,0:T(8,128)S(1)}) custom-call(s32[18]{0:T(128)S(1)} %stack.87.order, bf16[576,256]{1,0:T(8,128)(2,1)S(1)} %get-tuple-element.116.student_mix, bf16[576,256]{1,0:T(8,128)(2,1)S(1)} %get-tuple-element.131.teacher_mix, ...), custom_call_target="tpu_custom_call" | custom-call | flops 603979776 | bytes 13631488 | tf_op jit(solution)/shard_map/pallas_call | solution.py:307
  81.9 3.0 %collective-permute-start.23 = (bf16[3,128,256]{2,1,0:T(8,128)(2,1)S(1)}, bf16[3,128,256]{2,1,0:T(8,128)(2,1)S(1)}, u32[]{:S(2)}, u32[]{:S(2)}) collective-permute-start(bf16[3,128,256]{2,1,0:T(8,128)(2,1)S(1)} %get-tuple-element.155), channel_id=1, source_target_pairs={{33,0},{32,1},{65,32},{64,33},{97,64},{96,65},{129,96},{128,97},{1... | collective-permute-start | bytes 589832 | tf_op jit(solution)/shard_map/ppermute | solution.py:58
  84.9 4.4 %shard_map.136 = (bf16[3,128,768]{2,1,0:T(8,128)(2,1)}, bf16[3,128,768]{2,1,0:T(8,128)(2,1)}, bf16[3,128,768]{2,1,0:T(8,128)(2,1)}, bf16[576,768]{1,0:T(8,128)(2...) custom-call(s32[18]{0:T(128)S(1)} %stack.87.order, f32[576,1024]{1,0:T(8,128)S(1)} %get-tuple-element.147.student, ...), custom_call_target="tpu_custom_call" | custom-call | flops 905969664 | bytes 9437184 | tf_op jit(solution)/shard_map/pallas_call | solution.py:374
  89.4 3.0 %collective-permute-start.26 = (bf16[3,128,768]{2,1,0:T(8,128)(2,1)}, bf16[3,128,768]{2,1,0:T(8,128)(2,1)}, u32[]{:S(2)}, u32[]{:S(2)}) collective-permute-start(bf16[3,128,768]{2,1,0:T(8,128)(2,1)} %get-tuple-element.168), channel_id=1, source_target_pairs={{33,0},{32,1},{65,32},{64,33},{97,64},{96,65},{129,96},{128,97},{1... | collective-permute-start | bytes 1769480 | tf_op jit(solution)/shard_map/ppermute | solution.py:58
  96.5 6.2 %all-to-all-start = ((bf16[8,128,256]{2,1,0:T(8,128)(2,1)}), bf16[8,128,256]{2,1,0:T(8,128)(2,1)}, u32[]{:S(2)}, u32[]{:S(2)}) async-start(bf16[8,128,256]{2,1,0:T(8,128)(2,1)} %copy-done.6), calls=%async_computation | async-start | bytes 1048576 | tf_op jit(solution)/shard_map/all_to_all | solution.py:647
  102.7 3.3 %collective-permute-done.25.refs_0_ = bf16[3,128,768]{2,1,0:T(8,128)(2,1)} collective-permute-done((bf16[3,128,768]{2,1,0:T(8,128)(2,1)}, bf16[3,128,768]{2,1,0:T(8,128)(2,1)}, u32[]{:S(2)}, u32[]{:S(2)}) %collective-permute-start.25) | collective-permute-done | bytes 589856 | tf_op jit(solution)/shard_map/ppermute | solution.py:62
  107.9 2.6 %shard_map.139 = bf16[8,128,768]{2,1,0:T(8,128)(2,1)S(1)} custom-call(f32[8,128,768]{2,1,0:T(8,128)S(1)} %shard_map.137.kept, bf16[3,128,768]{2,1,0:T(8,128)(2,1)} %collective-permute-done.25.refs_0_, bf16[3,128,768]{2,1,0:T(8,128)(2,1)} %collective-permute-done.26.refs_1_, bf16[3,128,768]{2,1,0:T(8,128)(2,1)} %collective-permute-done.27.refs_2_), custom_call_target="tpu_custom_call" | custom-call | tf_op jit(solution)/shard_map/pallas_call | solution.py:443
  112.4 4.7 %all-to-all-start.1 = ((bf16[8,128,768]{2,1,0:T(8,128)(2,1)}), bf16[8,128,768]{2,1,0:T(8,128)(2,1)S(1)}, u32[]{:S(2)}, u32[]{:S(2)}) async-start(bf16[8,128,768]{2,1,0:T(8,128)(2,1)} %copy-done), calls=%async_computation.1 | async-start | bytes 3145728 | tf_op jit(solution)/shard_map/all_to_all | solution.py:647
  120.7 16.9 %all-to-all-done.1.last = bf16[8,128,768]{2,1,0:T(8,128)(2,1)S(1)} async-done(((bf16[8,128,768]{2,1,0:T(8,128)(2,1)}), bf16[8,128,768]{2,1,0:T(8,128)(2,1)S(1)}, u32[]{:S(2)}, u32[]{:S(2)}) %all-to-all-start.1) | async-done | bytes 1572896 | tf_op jit(solution)/shard_map/all_to_all | solution.py:647
  138.9 16.6 %all_to_all.20.copies = bf16[8,16,1024]{2,1,0:T(8,128)(2,1)S(1)} all-to-all(bf16[8,16,1024]{2,1,0:T(8,128)(2,1)S(1)} %bitcast.27), channel_id=1, replica_groups={{0,48,64,112,128,176,192,240},{16,32,80,96,144,160,208,224},{1,49,65,11..., dimensions={0} | all-to-all | bytes 524288 | tf_op jit(solution)/shard_map/all_to_all | solution.py:662
  156.3 3.6 %all-to-all-start.3 = ((bf16[16,16,1024]{2,1,0:T(8,128)(2,1)}), bf16[16,16,1024]{2,1,0:T(8,128)(2,1)S(1)}, u32[]{:S(2)}, u32[]{:S(2)}) async-start(bf16[16,16,1024]{2,1,0:T(8,128)(2,1)} %shard_map.142), calls=%async_computation.3 | async-start | bytes 1048576 | tf_op jit(solution)/shard_map/all_to_all | solution.py:665
  159.9 15.8 %all-to-all-done.3 = bf16[16,16,1024]{2,1,0:T(8,128)(2,1)S(1)} async-done(((bf16[16,16,1024]{2,1,0:T(8,128)(2,1)}), bf16[16,16,1024]{2,1,0:T(8,128)(2,1)S(1)}, u32[]{:S(2)}, u32[]{:S(2)}) %all-to-all-start.3) | async-done | bytes 524320 | tf_op jit(solution)/shard_map/all_to_all | solution.py:665
  178.1 2.7 %shard_map.143 = (f32[128,2048]{1,0:T(8,128)}, f32[128,2048]{1,0:T(8,128)}, f32[128,2048]{1,0:T(8,128)}, f32[128,2048]{1,0:T(8,128)}) custom-call(s32[1]{0:T(128)} %bitcast.flip, bf16[8,2,16,1024]{3,2,1,0:T(8,128)(2,1)S(1)} %bitcast.26, f32[128,2048]{1,0:T(8,128)S(1)} %copy-done.2, f32[128,2048]{1,0:T(8,128)S(1)} %copy-done.4, f32[128,2048]{1,0:T(8,128)S(1)} %copy-done.13, ...), custom_call_target="tpu_custom_call" | custom-call | tf_op jit(solution)/shard_map/pallas_call | solution.py:542
  (108 shorter events, 46.6 us)
Async XLA Ops:
  2.2 16.1 %collective-permute-start.4 = (bf16[288,2048]{1,0:T(8,128)(2,1)S(1)}, bf16[288,2048]{1,0:T(8,128)(2,1)S(1)}, u32[]{:S(2)}, u32[]{:S(2)}) collective-permute-start(bf16[288,2048]{1,0:T(8,128)(2,1)S(1)} %copy-done.7), channel_id=1, source_target_pairs={{0,1},{1,0},{2,3},{3,2},{4,5},{5,4},{6,7},{7,6},{8,9},{9,8},{10,11... | collective-permute-start | bytes 3538952 | tf_op jit(solution)/shard_map/ppermute | solution.py:42
  2.7 14.0 %collective-permute-start.2 = (bf16[2,128,1024]{2,1,0:T(8,128)(2,1)S(1)}, bf16[2,128,1024]{2,1,0:T(8,128)(2,1)}, u32[]{:S(2)}, u32[]{:S(2)}) collective-permute-start(bf16[2,128,1024]{2,1,0:T(8,128)(2,1)S(1)} %pad_maximum_fusion.refs_0_), channel_id=1, source_target_pairs={{16,2},{2,16},{0,18},{18,0},{17,3},{3,17},{1,19},{19,1},{20,6},{6,... | collective-permute-start | bytes 1572872 | tf_op jit(solution)/shard_map/ppermute | solution.py:54
  3.3 15.0 %collective-permute-start.1 = (bf16[2,128,1024]{2,1,0:T(8,128)(2,1)S(1)}, bf16[2,128,1024]{2,1,0:T(8,128)(2,1)}, u32[]{:S(2)}, u32[]{:S(2)}) collective-permute-start(bf16[2,128,1024]{2,1,0:T(8,128)(2,1)S(1)} %pad_maximum_fusion.refs_0_), channel_id=1, source_target_pairs={{0,4},{4,8},{8,12},{12,0},{1,5},{5,9},{9,13},{13,1},{2,6},{6,10},{... | collective-permute-start | bytes 1572872 | tf_op jit(solution)/shard_map/ppermute | solution.py:50
  4.8 13.5 %collective-permute-start = (bf16[2,128,1024]{2,1,0:T(8,128)(2,1)S(1)}, bf16[2,128,1024]{2,1,0:T(8,128)(2,1)}, u32[]{:S(2)}, u32[]{:S(2)}) collective-permute-start(bf16[2,128,1024]{2,1,0:T(8,128)(2,1)S(1)} %pad_maximum_fusion.refs_0_), channel_id=1, source_target_pairs={{4,0},{8,4},{12,8},{0,12},{5,1},{9,5},{13,9},{1,13},{6,2},{10,6},{... | collective-permute-start | bytes 1572872 | tf_op jit(solution)/shard_map/ppermute | solution.py:46
  8.3 11.1 %collective-permute-start.5 = (s32[2,144]{1,0:T(2,128)S(1)}, s32[2,144]{1,0:T(2,128)S(1)}, u32[]{:S(2)}, u32[]{:S(2)}) collective-permute-start(s32[2,144]{1,0:T(2,128)S(1)} %copy-done.20), channel_id=1, source_target_pairs={{0,1},{1,0},{2,3},{3,2},{4,5},{5,4},{6,7},{7,6},{8,9},{9,8},{10,11... | collective-permute-start | bytes 3464 | tf_op jit(solution)/shard_map/ppermute | solution.py:42
  19.4 17.0 %collective-permute-start.7 = (bf16[2,128,1024]{2,1,0:T(8,128)(2,1)}, bf16[2,128,1024]{2,1,0:T(8,128)(2,1)}, u32[]{:S(2)}, u32[]{:S(2)}) collective-permute-start(bf16[2,128,1024]{2,1,0:T(8,128)(2,1)} %collective-permute-done.2.refs_3_), channel_id=1, source_target_pairs={{0,4},{4,8},{8,12},{12,0},{1,5},{5,9},{9,13},{13,1},{2,6},{6,10},{... | collective-permute-start | bytes 1572872 | tf_op jit(solution)/shard_map/ppermute | solution.py:50
  21.0 15.5 %collective-permute-start.10 = (bf16[2,128,1024]{2,1,0:T(8,128)(2,1)}, bf16[2,128,1024]{2,1,0:T(8,128)(2,1)}, u32[]{:S(2)}, u32[]{:S(2)}) collective-permute-start(bf16[2,128,1024]{2,1,0:T(8,128)(2,1)} %collective-permute-done.1.refs_2_), channel_id=1, source_target_pairs={{1,32},{0,33},{33,64},{32,65},{65,96},{64,97},{97,128},{96,129},{1... | collective-permute-start | bytes 1572872 | tf_op jit(solution)/shard_map/ppermute | solution.py:62
  21.0 16.0 %collective-permute-start.9 = (bf16[2,128,1024]{2,1,0:T(8,128)(2,1)}, bf16[2,128,1024]{2,1,0:T(8,128)(2,1)}, u32[]{:S(2)}, u32[]{:S(2)}) collective-permute-start(bf16[2,128,1024]{2,1,0:T(8,128)(2,1)} %collective-permute-done.refs_1_), channel_id=1, source_target_pairs={{33,0},{32,1},{65,32},{64,33},{97,64},{96,65},{129,96},{128,97},{1... | collective-permute-start | bytes 1572872 | tf_op jit(solution)/shard_map/ppermute | solution.py:58
  24.8 13.9 %collective-permute-start.8 = (bf16[2,128,1024]{2,1,0:T(8,128)(2,1)}, bf16[2,128,1024]{2,1,0:T(8,128)(2,1)}, u32[]{:S(2)}, u32[]{:S(2)}) collective-permute-start(bf16[2,128,1024]{2,1,0:T(8,128)(2,1)} %collective-permute-done.refs_1_), channel_id=1, source_target_pairs={{16,2},{2,16},{0,18},{18,0},{17,3},{3,17},{1,19},{19,1},{20,6},{6,... | collective-permute-start | bytes 1572872 | tf_op jit(solution)/shard_map/ppermute | solution.py:54
  26.3 14.2 %collective-permute-start.6 = (bf16[2,128,1024]{2,1,0:T(8,128)(2,1)}, bf16[2,128,1024]{2,1,0:T(8,128)(2,1)}, u32[]{:S(2)}, u32[]{:S(2)}) collective-permute-start(bf16[2,128,1024]{2,1,0:T(8,128)(2,1)} %collective-permute-done.refs_1_), channel_id=1, source_target_pairs={{4,0},{8,4},{12,8},{0,12},{5,1},{9,5},{13,9},{1,13},{6,2},{10,6},{... | collective-permute-start | bytes 1572872 | tf_op jit(solution)/shard_map/ppermute | solution.py:46
  40.5 15.1 %collective-permute-start.12 = (bf16[2,128,1024]{2,1,0:T(8,128)(2,1)}, bf16[2,128,1024]{2,1,0:T(8,128)(2,1)S(1)}, u32[]{:S(2)}, u32[]{:S(2)}) collective-permute-start(bf16[2,128,1024]{2,1,0:T(8,128)(2,1)} %collective-permute-done.6.refs_4_), channel_id=1, source_target_pairs={{33,0},{32,1},{65,32},{64,33},{97,64},{96,65},{129,96},{128,97},{1... | collective-permute-start | bytes 1572872 | tf_op jit(solution)/shard_map/ppermute | solution.py:58
  41.1 14.5 %collective-permute-start.11 = (bf16[2,128,1024]{2,1,0:T(8,128)(2,1)}, bf16[2,128,1024]{2,1,0:T(8,128)(2,1)S(1)}, u32[]{:S(2)}, u32[]{:S(2)}) collective-permute-start(bf16[2,128,1024]{2,1,0:T(8,128)(2,1)} %collective-permute-done.8.refs_6_), channel_id=1, source_target_pairs={{4,0},{8,4},{12,8},{0,12},{5,1},{9,5},{13,9},{1,13},{6,2},{10,6},{... | collective-permute-start | bytes 1572872 | tf_op jit(solution)/shard_map/ppermute | solution.py:46
  44.1 14.1 %collective-permute-start.14 = (bf16[2,128,1024]{2,1,0:T(8,128)(2,1)}, bf16[2,128,1024]{2,1,0:T(8,128)(2,1)S(1)}, u32[]{:S(2)}, u32[]{:S(2)}) collective-permute-start(bf16[2,128,1024]{2,1,0:T(8,128)(2,1)} %collective-permute-done.10.refs_8_), channel_id=1, source_target_pairs={{16,2},{2,16},{0,18},{18,0},{17,3},{3,17},{1,19},{19,1},{20,6},{6,... | collective-permute-start | bytes 1572872 | tf_op jit(solution)/shard_map/ppermute | solution.py:54
  44.7 16.2 %collective-permute-start.15 = (bf16[2,128,1024]{2,1,0:T(8,128)(2,1)}, bf16[2,128,1024]{2,1,0:T(8,128)(2,1)S(1)}, u32[]{:S(2)}, u32[]{:S(2)}) collective-permute-start(bf16[2,128,1024]{2,1,0:T(8,128)(2,1)} %collective-permute-done.2.refs_3_), channel_id=1, source_target_pairs={{1,16},{0,17},{17,0},{16,1},{3,18},{2,19},{19,2},{18,3},{5,20},{4,... | collective-permute-start | bytes 1572872 | tf_op jit(solution)/shard_map/ppermute | solution.py:66
  48.2 15.5 %collective-permute-start.13 = (bf16[2,128,1024]{2,1,0:T(8,128)(2,1)}, bf16[2,128,1024]{2,1,0:T(8,128)(2,1)S(1)}, u32[]{:S(2)}, u32[]{:S(2)}) collective-permute-start(bf16[2,128,1024]{2,1,0:T(8,128)(2,1)} %collective-permute-done.8.refs_6_), channel_id=1, source_target_pairs={{1,32},{0,33},{33,64},{32,65},{65,96},{64,97},{97,128},{96,129},{1... | collective-permute-start | bytes 1572872 | tf_op jit(solution)/shard_map/ppermute | solution.py:62
  80.7 11.6 %collective-permute-start.24 = (bf16[2,128,256]{2,1,0:T(8,128)(2,1)S(1)}, bf16[2,128,256]{2,1,0:T(8,128)(2,1)S(1)}, u32[]{:S(2)}, u32[]{:S(2)}) collective-permute-start(bf16[2,128,256]{2,1,0:T(8,128)(2,1)S(1)} %get-tuple-element.156), channel_id=1, source_target_pairs={{1,16},{0,17},{17,0},{16,1},{3,18},{2,19},{19,2},{18,3},{5,20},{4,... | collective-permute-start | bytes 393224 | tf_op jit(solution)/shard_map/ppermute | solution.py:66
  81.9 13.6 %collective-permute-start.22 = (bf16[3,128,256]{2,1,0:T(8,128)(2,1)S(1)}, bf16[3,128,256]{2,1,0:T(8,128)(2,1)S(1)}, u32[]{:S(2)}, u32[]{:S(2)}) collective-permute-start(bf16[3,128,256]{2,1,0:T(8,128)(2,1)S(1)} %get-tuple-element.154), channel_id=1, source_target_pairs={{1,32},{0,33},{33,64},{32,65},{65,96},{64,97},{97,128},{96,129},{1... | collective-permute-start | bytes 589832 | tf_op jit(solution)/shard_map/ppermute | solution.py:62
  81.9 13.6 %collective-permute-start.23 = (bf16[3,128,256]{2,1,0:T(8,128)(2,1)S(1)}, bf16[3,128,256]{2,1,0:T(8,128)(2,1)S(1)}, u32[]{:S(2)}, u32[]{:S(2)}) collective-permute-start(bf16[3,128,256]{2,1,0:T(8,128)(2,1)S(1)} %get-tuple-element.155), channel_id=1, source_target_pairs={{33,0},{32,1},{65,32},{64,33},{97,64},{96,65},{129,96},{128,97},{1... | collective-permute-start | bytes 589832 | tf_op jit(solution)/shard_map/ppermute | solution.py:58
  89.4 16.7 %collective-permute-start.25 = (bf16[3,128,768]{2,1,0:T(8,128)(2,1)}, bf16[3,128,768]{2,1,0:T(8,128)(2,1)}, u32[]{:S(2)}, u32[]{:S(2)}) collective-permute-start(bf16[3,128,768]{2,1,0:T(8,128)(2,1)} %get-tuple-element.167), channel_id=1, source_target_pairs={{1,32},{0,33},{33,64},{32,65},{65,96},{64,97},{97,128},{96,129},{1... | collective-permute-start | bytes 1769480 | tf_op jit(solution)/shard_map/ppermute | solution.py:62
  89.4 16.7 %collective-permute-start.26 = (bf16[3,128,768]{2,1,0:T(8,128)(2,1)}, bf16[3,128,768]{2,1,0:T(8,128)(2,1)}, u32[]{:S(2)}, u32[]{:S(2)}) collective-permute-start(bf16[3,128,768]{2,1,0:T(8,128)(2,1)} %get-tuple-element.168), channel_id=1, source_target_pairs={{33,0},{32,1},{65,32},{64,33},{97,64},{96,65},{129,96},{128,97},{1... | collective-permute-start | bytes 1769480 | tf_op jit(solution)/shard_map/ppermute | solution.py:58
  92.3 15.5 %collective-permute-start.27 = (bf16[3,128,768]{2,1,0:T(8,128)(2,1)}, bf16[3,128,768]{2,1,0:T(8,128)(2,1)}, u32[]{:S(2)}, u32[]{:S(2)}) collective-permute-start(bf16[3,128,768]{2,1,0:T(8,128)(2,1)} %get-tuple-element.169), channel_id=1, source_target_pairs={{1,16},{0,17},{17,0},{16,1},{3,18},{2,19},{19,2},{18,3},{5,20},{4,... | collective-permute-start | bytes 1769480 | tf_op jit(solution)/shard_map/ppermute | solution.py:66
  96.5 15.9 %all-to-all-start = ((bf16[8,128,256]{2,1,0:T(8,128)(2,1)}), bf16[8,128,256]{2,1,0:T(8,128)(2,1)}, u32[]{:S(2)}, u32[]{:S(2)}) async-start(bf16[8,128,256]{2,1,0:T(8,128)(2,1)} %copy-done.6), calls=%async_computation | async-start | bytes 1048576 | tf_op jit(solution)/shard_map/all_to_all | solution.py:647
  112.4 25.2 %all-to-all-start.1 = ((bf16[8,128,768]{2,1,0:T(8,128)(2,1)}), bf16[8,128,768]{2,1,0:T(8,128)(2,1)S(1)}, u32[]{:S(2)}, u32[]{:S(2)}) async-start(bf16[8,128,768]{2,1,0:T(8,128)(2,1)} %copy-done), calls=%async_computation.1 | async-start | bytes 3145728 | tf_op jit(solution)/shard_map/all_to_all | solution.py:647
  156.3 19.4 %all-to-all-start.3 = ((bf16[16,16,1024]{2,1,0:T(8,128)(2,1)}), bf16[16,16,1024]{2,1,0:T(8,128)(2,1)S(1)}, u32[]{:S(2)}, u32[]{:S(2)}) async-start(bf16[16,16,1024]{2,1,0:T(8,128)(2,1)} %shard_map.142), calls=%async_computation.3 | async-start | bytes 1048576 | tf_op jit(solution)/shard_map/all_to_all | solution.py:665
  (32 other events, 301.0 us)

commit v13 on v12

--- a/solution.py
+++ b/solution.py
@@ -445,7 +445,7 @@
         grid=(kept.shape[-1] // width,),
         in_specs=[blocks(8)] + [blocks(count) for count in SENT],
         out_specs=blocks(8),
-        out_shape=jax.ShapeDtypeStruct(kept.shape, jnp.bfloat16),
+        out_shape=pltpu.HBM(kept.shape, jnp.bfloat16),
         compiler_params=pltpu.CompilerParams(vmem_limit_bytes=VMEM_LIMIT),
     )(kept, *passed)
 
@@ -586,11 +586,11 @@
     student_weight, teacher_weight = student_held, teacher_held
     student_other, positions_sent = lax.optimization_barrier((swap_cores(student_sent), positions_sent))
     teacher_other, places_other = swap_cores(teacher_sent), swap_cores(positions_sent)
-    up, down, across, student_other, teacher_other, places, places_other, student_held, teacher_held = (
+    up, down, across, student_other, teacher_other, places, places_other, student_held, teacher_held, order = (
         lax.optimization_barrier(
             (
                 from_y_next(own), from_y_previous(own), from_x_near(own), student_other, teacher_other, positions,
-                places_other, student_held, teacher_held,
+                places_other, student_held, teacher_held, order,
             )
         )
     )

time: 182 us -> 182 us (level)
  local copies, waits for them, and re-layouts: 11.3 us -> 5.23 us
  Pallas kernels: 40 us -> 45.4 us
    unnamed x46 -> x30, local copies, waits for them, and re-layouts: 9.87 us -> 3.77 us
    pallas_call x1, Pallas kernels: 4.63 us -> 6.68 us  [prepare_student(): pl.pallas_call(student_kernel, grid_spec=pltpu.PrefetchScalarGridSpec(num...]
    pallas_call x2, Pallas kernels: 2.72 us -> 4.57 us  [add_passed(): pl.pallas_call(add_kernel, grid=(kept.shape[-1] // width,), in_specs=[blo...]
  transfers between devices with their start and end apart: 33 -> 33, of which waited for: 17 -> 15; matrix products, arithmetic and copies ran while one was open for 0% -> 0% of each run, Pallas kernels for 16% -> 19%
where the time goes in v13:
time: 182 us; the launch traced here: 181 us
  waiting for transfers between devices  64.1 us (35%)
  starting transfers between devices  47.5 us (26%)
  Pallas kernels  45.4 us (25%)
  blocking collectives  16.7 us (9%)
  local copies, waits for them, and re-layouts  5.23 us (3%)
    all_to_all x2, waiting for transfers between devices, over_fsdp(): lax.all_to_all(rows, ('xlo', 'y', 'xhi'), 0, 0, axis_index_groups=FSDP_GR...  17.6 us
    all_to_all x1, blocking collectives, shards(): lax.all_to_all(total.reshape(8, 16, half), ('z', 'xlo'), 0, 0, axis_index...  16.7 us
    all_to_all x1, waiting for transfers between devices, shards(): full = lax.all_to_all(spread_rows(by_copy, 16), ('z', 'xlo'), 0, 0)  16 us
    ppermute x3, waiting for transfers between devices, from_x_near(): return lax.ppermute(value, ('xlo', 'xhi'), X_NEAR)  13.1 us
    all_to_all x2, starting transfers between devices, over_fsdp(): lax.all_to_all(rows, ('xlo', 'y', 'xhi'), 0, 0, axis_index_groups=FSDP_GR...  10.9 us
    ppermute x5, starting transfers between devices, from_z_next(): return lax.ppermute(value, ('z', 'core'), with_core_flip(from_next(8)))  10.1 us
    pallas_call x1, Pallas kernels, prepare_teacher(): pl.pallas_call(teacher_kernel, grid_spec=pltpu.PrefetchScalarGridSpec(num...  7.45 us
    ppermute x3, starting transfers between devices, from_y_next(): return lax.ppermute(value, 'y', from_next(4))  7.07 us
  transfers between devices with their start and end apart: 33, of which 15 were waited for; matrix products, arithmetic and copies ran while one was open for 0% of the time, Pallas kernels for 19%

profile of v13, /device:TPU:4, one launch (start us, length us, event | category | flops | bytes accessed | tf_op | source)
XLA Modules:
  0.0 180.8 jit_solution(13850536216379471963)
XLA Ops:
  7.3 10.4 %collective-permute-done.2.refs_3_ = bf16[2,128,1024]{2,1,0:T(8,128)(2,1)} collective-permute-done((bf16[2,128,1024]{2,1,0:T(8,128)(2,1)}, bf16[2,128,1024]{2,1,0:T(8,128)(2,1)}, u32[]{:S(2)}, u32[]{:S(2)}) %collective-permute-start.2) | collective-permute-done | bytes 524320 | tf_op jit(solution)/shard_map/ppermute | solution.py:54
  20.8 3.8 %collective-permute-start.9 = (bf16[2,128,1024]{2,1,0:T(8,128)(2,1)}, bf16[2,128,1024]{2,1,0:T(8,128)(2,1)S(1)}, u32[]{:S(2)}, u32[]{:S(2)}) collective-permute-start(bf16[2,128,1024]{2,1,0:T(8,128)(2,1)} %collective-permute-done.refs_1_), channel_id=1, source_target_pairs={{33,0},{32,1},{65,32},{64,33},{97,64},{96,65},{129,96},{128,97},{1... | collective-permute-start | bytes 1572872 | tf_op jit(solution)/shard_map/ppermute | solution.py:58
  26.1 2.2 %collective-permute-start.6 = (bf16[2,128,1024]{2,1,0:T(8,128)(2,1)}, bf16[2,128,1024]{2,1,0:T(8,128)(2,1)S(1)}, u32[]{:S(2)}, u32[]{:S(2)}) collective-permute-start(bf16[2,128,1024]{2,1,0:T(8,128)(2,1)} %collective-permute-done.refs_1_), channel_id=1, source_target_pairs={{4,0},{8,4},{12,8},{0,12},{5,1},{9,5},{13,9},{1,13},{6,2},{10,6},{... | collective-permute-start | bytes 1572872 | tf_op jit(solution)/shard_map/ppermute | solution.py:46
  29.5 6.7 %shard_map.129 = (bf16[576,1792]{1,0:T(8,128)(2,1)S(1)}, bf16[576,256]{1,0:T(8,128)(2,1)S(1)}, bf16[8,128,576]{2,1,0:T(8,128)(2,1)S(1)}, bf16[8,128,576]{2,1,0:T(8,128)(2,1)S(1)}) custom-call(s32[18]{0:T(128)S(1)} %stack.90.order, bf16[288,2048]{1,0:T(8,128)(2,1)S(1)} %copy-done.6, bf16[288,2048]{1,0:T(8,128)(2,1)} %collective-permute-done.3.mix_other), custom_call_target="tpu_custom_call" | custom-call | bytes 7340032 | tf_op jit(solution)/shard_map/pallas_call | solution.py:179
  38.3 2.1 %collective-permute-done.6.refs_4_ = bf16[2,128,1024]{2,1,0:T(8,128)(2,1)S(1)} collective-permute-done((bf16[2,128,1024]{2,1,0:T(8,128)(2,1)}, bf16[2,128,1024]{2,1,0:T(8,128)(2,1)S(1)}, u32[]{:S(2)}, u32[]{:S(2)}) %collective-permute-start.6) | collective-permute-done | bytes 524320 | tf_op jit(solution)/shard_map/ppermute | solution.py:46
  40.8 3.2 %collective-permute-start.11 = (bf16[2,128,1024]{2,1,0:T(8,128)(2,1)S(1)}, bf16[2,128,1024]{2,1,0:T(8,128)(2,1)S(1)}, u32[]{:S(2)}, u32[]{:S(2)}) collective-permute-start(bf16[2,128,1024]{2,1,0:T(8,128)(2,1)S(1)} %collective-permute-done.8.refs_6_), channel_id=1, source_target_pairs={{4,0},{8,4},{12,8},{0,12},{5,1},{9,5},{13,9},{1,13},{6,2},{10,6},{... | collective-permute-start | bytes 1572872 | tf_op jit(solution)/shard_map/ppermute | solution.py:46
  44.6 3.5 %collective-permute-start.15 = (bf16[2,128,1024]{2,1,0:T(8,128)(2,1)}, bf16[2,128,1024]{2,1,0:T(8,128)(2,1)S(1)}, u32[]{:S(2)}, u32[]{:S(2)}) collective-permute-start(bf16[2,128,1024]{2,1,0:T(8,128)(2,1)} %collective-permute-done.2.refs_3_), channel_id=1, source_target_pairs={{1,16},{0,17},{17,0},{16,1},{3,18},{2,19},{19,2},{18,3},{5,20},{4,... | collective-permute-start | bytes 1572872 | tf_op jit(solution)/shard_map/ppermute | solution.py:66
  49.1 7.4 %shard_map.131 = (bf16[576,1792]{1,0:T(8,128)(2,1)S(1)}, bf16[576,256]{1,0:T(8,128)(2,1)S(1)}, bf16[288,2048]{1,0:T(8,128)(2,1)S(1)}) custom-call(s32[18]{0:T(128)S(1)} %stack.90.order, bf16[288,2048]{1,0:T(8,128)(2,1)S(1)} %copy-done.5, bf16[288,2048]{1,0:T(8,128)(2,1)} %collective-permute-done.4.mix_other, bf16[288,2048]{1,0:T(8,128)(2,1)S(1)} %copy-done.4, ...), custom_call_target="tpu_custom_call" | custom-call | flops 509607936 | bytes 9437184 | tf_op jit(solution)/shard_map/pallas_call | solution.py:209
  58.0 2.6 %collective-permute-done.15.refs_13_ = bf16[2,128,1024]{2,1,0:T(8,128)(2,1)S(1)} collective-permute-done((bf16[2,128,1024]{2,1,0:T(8,128)(2,1)}, bf16[2,128,1024]{2,1,0:T(8,128)(2,1)S(1)}, u32[]{:S(2)}, u32[]{:S(2)}) %collective-permute-start.15) | collective-permute-done | bytes 524320 | tf_op jit(solution)/shard_map/ppermute | solution.py:66
  60.7 2.7 %collective-permute-done.13.refs_11_ = bf16[2,128,1024]{2,1,0:T(8,128)(2,1)S(1)} collective-permute-done((bf16[2,128,1024]{2,1,0:T(8,128)(2,1)S(1)}, bf16[2,128,1024]{2,1,0:T(8,128)(2,1)S(1)}, u32[]{:S(2)}, u32[]{:S(2)}) %collective-permute-start.13) | collective-permute-done | bytes 524320 | tf_op jit(solution)/shard_map/ppermute | solution.py:62
  65.6 6.8 %shard_map.132 = (f32[576,1024]{1,0:T(8,128)S(1)}, f32[576,1024]{1,0:T(8,128)S(1)}) custom-call(bf16[576,1792]{1,0:T(8,128)(2,1)S(1)} %get-tuple-element.134.student_mix, bf16[576,1792]{1,0:T(8,128)(2,1)S(1)} %get-tuple-element.135.teacher_mix, bf16[2,128,1024]{2,1,0:T(8,128)(2,1)} %pad_maximum_fusion.refs_0_, ...), custom_call_target="tpu_custom_call" | custom-call | flops 4227858432 | bytes 17825792 | tf_op jit(solution)/shard_map/pallas_call | solution.py:252
  73.0 4.0 %shard_map.133 = (f32[576,1024]{1,0:T(8,128)S(1)}, f32[576,1024]{1,0:T(8,128)S(1)}, f32[576,128]{1,0:T(8,128)S(1)}) custom-call(s32[18]{0:T(128)S(1)} %stack.90.order, bf16[576,256]{1,0:T(8,128)(2,1)S(1)} %get-tuple-element.118.student_mix, bf16[576,256]{1,0:T(8,128)(2,1)S(1)} %get-tuple-element.133.teacher_mix, ...), custom_call_target="tpu_custom_call" | custom-call | flops 603979776 | bytes 13631488 | tf_op jit(solution)/shard_map/pallas_call | solution.py:307
  81.6 3.0 %collective-permute-start.23 = (bf16[3,128,256]{2,1,0:T(8,128)(2,1)S(1)}, bf16[3,128,256]{2,1,0:T(8,128)(2,1)S(1)}, u32[]{:S(2)}, u32[]{:S(2)}) collective-permute-start(bf16[3,128,256]{2,1,0:T(8,128)(2,1)S(1)} %get-tuple-element.157), channel_id=1, source_target_pairs={{33,0},{32,1},{65,32},{64,33},{97,64},{96,65},{129,96},{128,97},{1... | collective-permute-start | bytes 589832 | tf_op jit(solution)/shard_map/ppermute | solution.py:58
  84.6 4.4 %shard_map.136 = (bf16[3,128,768]{2,1,0:T(8,128)(2,1)}, bf16[3,128,768]{2,1,0:T(8,128)(2,1)}, bf16[3,128,768]{2,1,0:T(8,128)(2,1)}, bf16[576,768]{1,0:T(8,128)(2...) custom-call(s32[18]{0:T(128)S(1)} %stack.90.order, f32[576,1024]{1,0:T(8,128)S(1)} %get-tuple-element.149.student, ...), custom_call_target="tpu_custom_call" | custom-call | flops 905969664 | bytes 9437184 | tf_op jit(solution)/shard_map/pallas_call | solution.py:374
  89.0 3.0 %collective-permute-start.26 = (bf16[3,128,768]{2,1,0:T(8,128)(2,1)}, bf16[3,128,768]{2,1,0:T(8,128)(2,1)}, u32[]{:S(2)}, u32[]{:S(2)}) collective-permute-start(bf16[3,128,768]{2,1,0:T(8,128)(2,1)} %get-tuple-element.170), channel_id=1, source_target_pairs={{33,0},{32,1},{65,32},{64,33},{97,64},{96,65},{129,96},{128,97},{1... | collective-permute-start | bytes 1769480 | tf_op jit(solution)/shard_map/ppermute | solution.py:58
  96.1 6.3 %all-to-all-start = ((bf16[8,128,256]{2,1,0:T(8,128)(2,1)}), bf16[8,128,256]{2,1,0:T(8,128)(2,1)}, u32[]{:S(2)}, u32[]{:S(2)}) async-start(bf16[8,128,256]{2,1,0:T(8,128)(2,1)} %shard_map.138), calls=%async_computation | async-start | bytes 1048576 | tf_op jit(solution)/shard_map/all_to_all | solution.py:647
  102.4 3.3 %collective-permute-done.25.refs_0_ = bf16[3,128,768]{2,1,0:T(8,128)(2,1)} collective-permute-done((bf16[3,128,768]{2,1,0:T(8,128)(2,1)}, bf16[3,128,768]{2,1,0:T(8,128)(2,1)}, u32[]{:S(2)}, u32[]{:S(2)}) %collective-permute-start.25) | collective-permute-done | bytes 589856 | tf_op jit(solution)/shard_map/ppermute | solution.py:62
  107.5 3.7 %shard_map.139 = bf16[8,128,768]{2,1,0:T(8,128)(2,1)} custom-call(f32[8,128,768]{2,1,0:T(8,128)S(1)} %shard_map.137.kept, bf16[3,128,768]{2,1,0:T(8,128)(2,1)} %collective-permute-done.25.refs_0_, bf16[3,128,768]{2,1,0:T(8,128)(2,1)} %collective-permute-done.26.refs_1_, bf16[3,128,768]{2,1,0:T(8,128)(2,1)} %collective-permute-done.27.refs_2_), custom_call_target="tpu_custom_call" | custom-call | tf_op jit(solution)/shard_map/pallas_call | solution.py:443
  112.0 4.7 %all-to-all-start.1 = ((bf16[8,128,768]{2,1,0:T(8,128)(2,1)}), bf16[8,128,768]{2,1,0:T(8,128)(2,1)S(1)}, u32[]{:S(2)}, u32[]{:S(2)}) async-start(bf16[8,128,768]{2,1,0:T(8,128)(2,1)} %shard_map.139), calls=%async_computation.1 | async-start | bytes 3145728 | tf_op jit(solution)/shard_map/all_to_all | solution.py:647
  120.4 16.7 %all-to-all-done.1.last = bf16[8,128,768]{2,1,0:T(8,128)(2,1)S(1)} async-done(((bf16[8,128,768]{2,1,0:T(8,128)(2,1)}), bf16[8,128,768]{2,1,0:T(8,128)(2,1)S(1)}, u32[]{:S(2)}, u32[]{:S(2)}) %all-to-all-start.1) | async-done | bytes 1572896 | tf_op jit(solution)/shard_map/all_to_all | solution.py:647
  138.4 16.7 %all_to_all.20.copies = bf16[8,16,1024]{2,1,0:T(8,128)(2,1)S(1)} all-to-all(bf16[8,16,1024]{2,1,0:T(8,128)(2,1)S(1)} %bitcast.27), channel_id=1, replica_groups={{0,48,64,112,128,176,192,240},{16,32,80,96,144,160,208,224},{1,49,65,11..., dimensions={0} | all-to-all | bytes 524288 | tf_op jit(solution)/shard_map/all_to_all | solution.py:662
  155.9 3.6 %all-to-all-start.3 = ((bf16[16,16,1024]{2,1,0:T(8,128)(2,1)}), bf16[16,16,1024]{2,1,0:T(8,128)(2,1)S(1)}, u32[]{:S(2)}, u32[]{:S(2)}) async-start(bf16[16,16,1024]{2,1,0:T(8,128)(2,1)} %shard_map.142), calls=%async_computation.3 | async-start | bytes 1048576 | tf_op jit(solution)/shard_map/all_to_all | solution.py:665
  159.5 16.0 %all-to-all-done.3 = bf16[16,16,1024]{2,1,0:T(8,128)(2,1)S(1)} async-done(((bf16[16,16,1024]{2,1,0:T(8,128)(2,1)}), bf16[16,16,1024]{2,1,0:T(8,128)(2,1)S(1)}, u32[]{:S(2)}, u32[]{:S(2)}) %all-to-all-start.3) | async-done | bytes 524320 | tf_op jit(solution)/shard_map/all_to_all | solution.py:665
  178.0 2.7 %shard_map.143 = (f32[128,2048]{1,0:T(8,128)}, f32[128,2048]{1,0:T(8,128)}, f32[128,2048]{1,0:T(8,128)}, f32[128,2048]{1,0:T(8,128)}) custom-call(s32[1]{0:T(128)} %bitcast.flip, bf16[8,2,16,1024]{3,2,1,0:T(8,128)(2,1)S(1)} %bitcast.26, f32[128,2048]{1,0:T(8,128)S(1)} %copy-done.1, f32[128,2048]{1,0:T(8,128)S(1)} %copy-done.3, f32[128,2048]{1,0:T(8,128)S(1)} %copy-done.7, ...), custom_call_target="tpu_custom_call" | custom-call | tf_op jit(solution)/shard_map/pallas_call | solution.py:542
  (92 shorter events, 40.4 us)
Async XLA Ops:
  2.9 16.3 %collective-permute-start.4 = (bf16[288,2048]{1,0:T(8,128)(2,1)S(1)}, bf16[288,2048]{1,0:T(8,128)(2,1)}, u32[]{:S(2)}, u32[]{:S(2)}) collective-permute-start(bf16[288,2048]{1,0:T(8,128)(2,1)S(1)} %copy-done.5), channel_id=1, source_target_pairs={{0,1},{1,0},{2,3},{3,2},{4,5},{5,4},{6,7},{7,6},{8,9},{9,8},{10,11... | collective-permute-start | bytes 3538952 | tf_op jit(solution)/shard_map/ppermute | solution.py:42
  3.4 14.2 %collective-permute-start.2 = (bf16[2,128,1024]{2,1,0:T(8,128)(2,1)}, bf16[2,128,1024]{2,1,0:T(8,128)(2,1)}, u32[]{:S(2)}, u32[]{:S(2)}) collective-permute-start(bf16[2,128,1024]{2,1,0:T(8,128)(2,1)} %pad_maximum_fusion.refs_0_), channel_id=1, source_target_pairs={{16,2},{2,16},{0,18},{18,0},{17,3},{3,17},{1,19},{19,1},{20,6},{6,... | collective-permute-start | bytes 1572872 | tf_op jit(solution)/shard_map/ppermute | solution.py:54
  3.9 15.3 %collective-permute-start.1 = (bf16[2,128,1024]{2,1,0:T(8,128)(2,1)}, bf16[2,128,1024]{2,1,0:T(8,128)(2,1)}, u32[]{:S(2)}, u32[]{:S(2)}) collective-permute-start(bf16[2,128,1024]{2,1,0:T(8,128)(2,1)} %pad_maximum_fusion.refs_0_), channel_id=1, source_target_pairs={{0,4},{4,8},{8,12},{12,0},{1,5},{5,9},{9,13},{13,1},{2,6},{6,10},{... | collective-permute-start | bytes 1572872 | tf_op jit(solution)/shard_map/ppermute | solution.py:50
  5.5 13.7 %collective-permute-start = (bf16[2,128,1024]{2,1,0:T(8,128)(2,1)}, bf16[2,128,1024]{2,1,0:T(8,128)(2,1)}, u32[]{:S(2)}, u32[]{:S(2)}) collective-permute-start(bf16[2,128,1024]{2,1,0:T(8,128)(2,1)} %pad_maximum_fusion.refs_0_), channel_id=1, source_target_pairs={{4,0},{8,4},{12,8},{0,12},{5,1},{9,5},{13,9},{1,13},{6,2},{10,6},{... | collective-permute-start | bytes 1572872 | tf_op jit(solution)/shard_map/ppermute | solution.py:46
  7.2 12.0 %collective-permute-start.5 = (s32[2,144]{1,0:T(2,128)S(1)}, s32[2,144]{1,0:T(2,128)S(1)}, u32[]{:S(2)}, u32[]{:S(2)}) collective-permute-start(s32[2,144]{1,0:T(2,128)S(1)} %copy-done.12), channel_id=1, source_target_pairs={{0,1},{1,0},{2,3},{3,2},{4,5},{5,4},{6,7},{7,6},{8,9},{9,8},{10,11... | collective-permute-start | bytes 3464 | tf_op jit(solution)/shard_map/ppermute | solution.py:42
  19.2 17.8 %collective-permute-start.7 = (bf16[2,128,1024]{2,1,0:T(8,128)(2,1)}, bf16[2,128,1024]{2,1,0:T(8,128)(2,1)S(1)}, u32[]{:S(2)}, u32[]{:S(2)}) collective-permute-start(bf16[2,128,1024]{2,1,0:T(8,128)(2,1)} %collective-permute-done.2.refs_3_), channel_id=1, source_target_pairs={{0,4},{4,8},{8,12},{12,0},{1,5},{5,9},{9,13},{13,1},{2,6},{6,10},{... | collective-permute-start | bytes 1572872 | tf_op jit(solution)/shard_map/ppermute | solution.py:50
  20.8 16.3 %collective-permute-start.10 = (bf16[2,128,1024]{2,1,0:T(8,128)(2,1)}, bf16[2,128,1024]{2,1,0:T(8,128)(2,1)S(1)}, u32[]{:S(2)}, u32[]{:S(2)}) collective-permute-start(bf16[2,128,1024]{2,1,0:T(8,128)(2,1)} %collective-permute-done.1.refs_2_), channel_id=1, source_target_pairs={{1,32},{0,33},{33,64},{32,65},{65,96},{64,97},{97,128},{96,129},{1... | collective-permute-start | bytes 1572872 | tf_op jit(solution)/shard_map/ppermute | solution.py:62
  20.8 16.3 %collective-permute-start.9 = (bf16[2,128,1024]{2,1,0:T(8,128)(2,1)}, bf16[2,128,1024]{2,1,0:T(8,128)(2,1)S(1)}, u32[]{:S(2)}, u32[]{:S(2)}) collective-permute-start(bf16[2,128,1024]{2,1,0:T(8,128)(2,1)} %collective-permute-done.refs_1_), channel_id=1, source_target_pairs={{33,0},{32,1},{65,32},{64,33},{97,64},{96,65},{129,96},{128,97},{1... | collective-permute-start | bytes 1572872 | tf_op jit(solution)/shard_map/ppermute | solution.py:58
  24.6 13.8 %collective-permute-start.8 = (bf16[2,128,1024]{2,1,0:T(8,128)(2,1)}, bf16[2,128,1024]{2,1,0:T(8,128)(2,1)S(1)}, u32[]{:S(2)}, u32[]{:S(2)}) collective-permute-start(bf16[2,128,1024]{2,1,0:T(8,128)(2,1)} %collective-permute-done.refs_1_), channel_id=1, source_target_pairs={{16,2},{2,16},{0,18},{18,0},{17,3},{3,17},{1,19},{19,1},{20,6},{6,... | collective-permute-start | bytes 1572872 | tf_op jit(solution)/shard_map/ppermute | solution.py:54
  26.1 14.4 %collective-permute-start.6 = (bf16[2,128,1024]{2,1,0:T(8,128)(2,1)}, bf16[2,128,1024]{2,1,0:T(8,128)(2,1)S(1)}, u32[]{:S(2)}, u32[]{:S(2)}) collective-permute-start(bf16[2,128,1024]{2,1,0:T(8,128)(2,1)} %collective-permute-done.refs_1_), channel_id=1, source_target_pairs={{4,0},{8,4},{12,8},{0,12},{5,1},{9,5},{13,9},{1,13},{6,2},{10,6},{... | collective-permute-start | bytes 1572872 | tf_op jit(solution)/shard_map/ppermute | solution.py:46
  40.4 16.1 %collective-permute-start.12 = (bf16[2,128,1024]{2,1,0:T(8,128)(2,1)S(1)}, bf16[2,128,1024]{2,1,0:T(8,128)(2,1)S(1)}, u32[]{:S(2)}, u32[]{:S(2)}) collective-permute-start(bf16[2,128,1024]{2,1,0:T(8,128)(2,1)S(1)} %collective-permute-done.6.refs_4_), channel_id=1, source_target_pairs={{33,0},{32,1},{65,32},{64,33},{97,64},{96,65},{129,96},{128,97},{1... | collective-permute-start | bytes 1572872 | tf_op jit(solution)/shard_map/ppermute | solution.py:58
  40.8 15.7 %collective-permute-start.11 = (bf16[2,128,1024]{2,1,0:T(8,128)(2,1)S(1)}, bf16[2,128,1024]{2,1,0:T(8,128)(2,1)S(1)}, u32[]{:S(2)}, u32[]{:S(2)}) collective-permute-start(bf16[2,128,1024]{2,1,0:T(8,128)(2,1)S(1)} %collective-permute-done.8.refs_6_), channel_id=1, source_target_pairs={{4,0},{8,4},{12,8},{0,12},{5,1},{9,5},{13,9},{1,13},{6,2},{10,6},{... | collective-permute-start | bytes 1572872 | tf_op jit(solution)/shard_map/ppermute | solution.py:46
  44.0 14.0 %collective-permute-start.14 = (bf16[2,128,1024]{2,1,0:T(8,128)(2,1)S(1)}, bf16[2,128,1024]{2,1,0:T(8,128)(2,1)S(1)}, u32[]{:S(2)}, u32[]{:S(2)}) collective-permute-start(bf16[2,128,1024]{2,1,0:T(8,128)(2,1)S(1)} %collective-permute-done.10.refs_8_), channel_id=1, source_target_pairs={{16,2},{2,16},{0,18},{18,0},{17,3},{3,17},{1,19},{19,1},{20,6},{6,... | collective-permute-start | bytes 1572872 | tf_op jit(solution)/shard_map/ppermute | solution.py:54
  44.6 16.1 %collective-permute-start.15 = (bf16[2,128,1024]{2,1,0:T(8,128)(2,1)}, bf16[2,128,1024]{2,1,0:T(8,128)(2,1)S(1)}, u32[]{:S(2)}, u32[]{:S(2)}) collective-permute-start(bf16[2,128,1024]{2,1,0:T(8,128)(2,1)} %collective-permute-done.2.refs_3_), channel_id=1, source_target_pairs={{1,16},{0,17},{17,0},{16,1},{3,18},{2,19},{19,2},{18,3},{5,20},{4,... | collective-permute-start | bytes 1572872 | tf_op jit(solution)/shard_map/ppermute | solution.py:66
  48.0 15.3 %collective-permute-start.13 = (bf16[2,128,1024]{2,1,0:T(8,128)(2,1)S(1)}, bf16[2,128,1024]{2,1,0:T(8,128)(2,1)S(1)}, u32[]{:S(2)}, u32[]{:S(2)}) collective-permute-start(bf16[2,128,1024]{2,1,0:T(8,128)(2,1)S(1)} %collective-permute-done.8.refs_6_), channel_id=1, source_target_pairs={{1,32},{0,33},{33,64},{32,65},{65,96},{64,97},{97,128},{96,129},{1... | collective-permute-start | bytes 1572872 | tf_op jit(solution)/shard_map/ppermute | solution.py:62
  80.3 11.7 %collective-permute-start.24 = (bf16[2,128,256]{2,1,0:T(8,128)(2,1)S(1)}, bf16[2,128,256]{2,1,0:T(8,128)(2,1)S(1)}, u32[]{:S(2)}, u32[]{:S(2)}) collective-permute-start(bf16[2,128,256]{2,1,0:T(8,128)(2,1)S(1)} %get-tuple-element.158), channel_id=1, source_target_pairs={{1,16},{0,17},{17,0},{16,1},{3,18},{2,19},{19,2},{18,3},{5,20},{4,... | collective-permute-start | bytes 393224 | tf_op jit(solution)/shard_map/ppermute | solution.py:66
  81.6 13.6 %collective-permute-start.22 = (bf16[3,128,256]{2,1,0:T(8,128)(2,1)S(1)}, bf16[3,128,256]{2,1,0:T(8,128)(2,1)S(1)}, u32[]{:S(2)}, u32[]{:S(2)}) collective-permute-start(bf16[3,128,256]{2,1,0:T(8,128)(2,1)S(1)} %get-tuple-element.156), channel_id=1, source_target_pairs={{1,32},{0,33},{33,64},{32,65},{65,96},{64,97},{97,128},{96,129},{1... | collective-permute-start | bytes 589832 | tf_op jit(solution)/shard_map/ppermute | solution.py:62
  81.6 13.6 %collective-permute-start.23 = (bf16[3,128,256]{2,1,0:T(8,128)(2,1)S(1)}, bf16[3,128,256]{2,1,0:T(8,128)(2,1)S(1)}, u32[]{:S(2)}, u32[]{:S(2)}) collective-permute-start(bf16[3,128,256]{2,1,0:T(8,128)(2,1)S(1)} %get-tuple-element.157), channel_id=1, source_target_pairs={{33,0},{32,1},{65,32},{64,33},{97,64},{96,65},{129,96},{128,97},{1... | collective-permute-start | bytes 589832 | tf_op jit(solution)/shard_map/ppermute | solution.py:58
  89.0 16.7 %collective-permute-start.25 = (bf16[3,128,768]{2,1,0:T(8,128)(2,1)}, bf16[3,128,768]{2,1,0:T(8,128)(2,1)}, u32[]{:S(2)}, u32[]{:S(2)}) collective-permute-start(bf16[3,128,768]{2,1,0:T(8,128)(2,1)} %get-tuple-element.169), channel_id=1, source_target_pairs={{1,32},{0,33},{33,64},{32,65},{65,96},{64,97},{97,128},{96,129},{1... | collective-permute-start | bytes 1769480 | tf_op jit(solution)/shard_map/ppermute | solution.py:62
  89.0 16.7 %collective-permute-start.26 = (bf16[3,128,768]{2,1,0:T(8,128)(2,1)}, bf16[3,128,768]{2,1,0:T(8,128)(2,1)}, u32[]{:S(2)}, u32[]{:S(2)}) collective-permute-start(bf16[3,128,768]{2,1,0:T(8,128)(2,1)} %get-tuple-element.170), channel_id=1, source_target_pairs={{33,0},{32,1},{65,32},{64,33},{97,64},{96,65},{129,96},{128,97},{1... | collective-permute-start | bytes 1769480 | tf_op jit(solution)/shard_map/ppermute | solution.py:58
  92.0 15.5 %collective-permute-start.27 = (bf16[3,128,768]{2,1,0:T(8,128)(2,1)}, bf16[3,128,768]{2,1,0:T(8,128)(2,1)}, u32[]{:S(2)}, u32[]{:S(2)}) collective-permute-start(bf16[3,128,768]{2,1,0:T(8,128)(2,1)} %get-tuple-element.171), channel_id=1, source_target_pairs={{1,16},{0,17},{17,0},{16,1},{3,18},{2,19},{19,2},{18,3},{5,20},{4,... | collective-permute-start | bytes 1769480 | tf_op jit(solution)/shard_map/ppermute | solution.py:66
  96.1 15.9 %all-to-all-start = ((bf16[8,128,256]{2,1,0:T(8,128)(2,1)}), bf16[8,128,256]{2,1,0:T(8,128)(2,1)}, u32[]{:S(2)}, u32[]{:S(2)}) async-start(bf16[8,128,256]{2,1,0:T(8,128)(2,1)} %shard_map.138), calls=%async_computation | async-start | bytes 1048576 | tf_op jit(solution)/shard_map/all_to_all | solution.py:647
  112.0 25.0 %all-to-all-start.1 = ((bf16[8,128,768]{2,1,0:T(8,128)(2,1)}), bf16[8,128,768]{2,1,0:T(8,128)(2,1)S(1)}, u32[]{:S(2)}, u32[]{:S(2)}) async-start(bf16[8,128,768]{2,1,0:T(8,128)(2,1)} %shard_map.139), calls=%async_computation.1 | async-start | bytes 3145728 | tf_op jit(solution)/shard_map/all_to_all | solution.py:647
  155.9 19.6 %all-to-all-start.3 = ((bf16[16,16,1024]{2,1,0:T(8,128)(2,1)}), bf16[16,16,1024]{2,1,0:T(8,128)(2,1)S(1)}, u32[]{:S(2)}, u32[]{:S(2)}) async-start(bf16[16,16,1024]{2,1,0:T(8,128)(2,1)} %shard_map.142), calls=%async_computation.3 | async-start | bytes 1048576 | tf_op jit(solution)/shard_map/all_to_all | solution.py:665
  (24 other events, 254.0 us)

commit v14 on v13

--- a/solution.py
+++ b/solution.py
@@ -665,7 +665,8 @@
     full = lax.all_to_all(spread_rows(by_copy, 16), ("z", "xlo"), 0, 0)
     flip = ((core + xhi) & 1).astype(jnp.int32).reshape(1)
     weight_next, teacher_next, first_next, squares_next = adamw_update(
-        flip, full.reshape(8, 2, 16, half), student_weight, teacher_weight, moment, second
+        flip, full.reshape(8, 2, 16, half), student_weight, teacher_weight,
+        pltpu.with_memory_space_constraint(moment, pltpu.HBM), pltpu.with_memory_space_constraint(second, pltpu.HBM),
     )
     return (weight_next, teacher_next, first_next, squares_next, student_tokens)
 

time: 182 us -> 181 us (level)
  local copies, waits for them, and re-layouts: 5.23 us -> 2.78 us
    unnamed x30 -> x26, local copies, waits for them, and re-layouts: 3.77 us -> 1.32 us
where the time goes in v14:
time: 181 us; the launch traced here: 180 us
  waiting for transfers between devices  64.1 us (35%)
  starting transfers between devices  47.5 us (26%)
  Pallas kernels  47.1 us (26%)
  blocking collectives  16.7 us (9%)
  local copies, waits for them, and re-layouts  2.78 us (2%)
    all_to_all x2, waiting for transfers between devices, over_fsdp(): lax.all_to_all(rows, ('xlo', 'y', 'xhi'), 0, 0, axis_index_groups=FSDP_GR...  17.6 us
    all_to_all x1, blocking collectives, shards(): lax.all_to_all(total.reshape(8, 16, half), ('z', 'xlo'), 0, 0, axis_index...  16.7 us
    all_to_all x1, waiting for transfers between devices, shards(): full = lax.all_to_all(spread_rows(by_copy, 16), ('z', 'xlo'), 0, 0)  16 us
    ppermute x3, waiting for transfers between devices, from_x_near(): return lax.ppermute(value, ('xlo', 'xhi'), X_NEAR)  13.1 us
    all_to_all x2, starting transfers between devices, over_fsdp(): lax.all_to_all(rows, ('xlo', 'y', 'xhi'), 0, 0, axis_index_groups=FSDP_GR...  10.9 us
    ppermute x5, starting transfers between devices, from_z_next(): return lax.ppermute(value, ('z', 'core'), with_core_flip(from_next(8)))  10.1 us
    pallas_call x1, Pallas kernels, prepare_teacher(): pl.pallas_call(teacher_kernel, grid_spec=pltpu.PrefetchScalarGridSpec(num...  7.45 us
    ppermute x3, starting transfers between devices, from_y_next(): return lax.ppermute(value, 'y', from_next(4))  7.07 us
  transfers between devices with their start and end apart: 33, of which 15 were waited for; matrix products, arithmetic and copies ran while one was open for 0% of the time, Pallas kernels for 19%

profile of v14, /device:TPU:4, one launch (start us, length us, event | category | flops | bytes accessed | tf_op | source)
XLA Modules:
  0.0 180.1 jit_solution(1077202170275900712)
XLA Ops:
  7.3 10.4 %collective-permute-done.2.refs_3_ = bf16[2,128,1024]{2,1,0:T(8,128)(2,1)} collective-permute-done((bf16[2,128,1024]{2,1,0:T(8,128)(2,1)}, bf16[2,128,1024]{2,1,0:T(8,128)(2,1)}, u32[]{:S(2)}, u32[]{:S(2)}) %collective-permute-start.2) | collective-permute-done | bytes 524320 | tf_op jit(solution)/shard_map/ppermute | solution.py:54
  20.8 3.8 %collective-permute-start.9 = (bf16[2,128,1024]{2,1,0:T(8,128)(2,1)}, bf16[2,128,1024]{2,1,0:T(8,128)(2,1)S(1)}, u32[]{:S(2)}, u32[]{:S(2)}) collective-permute-start(bf16[2,128,1024]{2,1,0:T(8,128)(2,1)} %collective-permute-done.refs_1_), channel_id=1, source_target_pairs={{33,0},{32,1},{65,32},{64,33},{97,64},{96,65},{129,96},{128,97},{1... | collective-permute-start | bytes 1572872 | tf_op jit(solution)/shard_map/ppermute | solution.py:58
  26.1 2.2 %collective-permute-start.6 = (bf16[2,128,1024]{2,1,0:T(8,128)(2,1)}, bf16[2,128,1024]{2,1,0:T(8,128)(2,1)S(1)}, u32[]{:S(2)}, u32[]{:S(2)}) collective-permute-start(bf16[2,128,1024]{2,1,0:T(8,128)(2,1)} %collective-permute-done.refs_1_), channel_id=1, source_target_pairs={{4,0},{8,4},{12,8},{0,12},{5,1},{9,5},{13,9},{1,13},{6,2},{10,6},{... | collective-permute-start | bytes 1572872 | tf_op jit(solution)/shard_map/ppermute | solution.py:46
  29.5 6.7 %shard_map.129 = (bf16[576,1792]{1,0:T(8,128)(2,1)S(1)}, bf16[576,256]{1,0:T(8,128)(2,1)S(1)}, bf16[8,128,576]{2,1,0:T(8,128)(2,1)S(1)}, bf16[8,128,576]{2,1,0:T(8,128)(2,1)S(1)}) custom-call(s32[18]{0:T(128)S(1)} %stack.90.order, bf16[288,2048]{1,0:T(8,128)(2,1)S(1)} %copy-done.6, bf16[288,2048]{1,0:T(8,128)(2,1)} %collective-permute-done.3.mix_other), custom_call_target="tpu_custom_call" | custom-call | bytes 7340032 | tf_op jit(solution)/shard_map/pallas_call | solution.py:179
  38.3 2.1 %collective-permute-done.6.refs_4_ = bf16[2,128,1024]{2,1,0:T(8,128)(2,1)S(1)} collective-permute-done((bf16[2,128,1024]{2,1,0:T(8,128)(2,1)}, bf16[2,128,1024]{2,1,0:T(8,128)(2,1)S(1)}, u32[]{:S(2)}, u32[]{:S(2)}) %collective-permute-start.6) | collective-permute-done | bytes 524320 | tf_op jit(solution)/shard_map/ppermute | solution.py:46
  40.8 3.2 %collective-permute-start.11 = (bf16[2,128,1024]{2,1,0:T(8,128)(2,1)S(1)}, bf16[2,128,1024]{2,1,0:T(8,128)(2,1)S(1)}, u32[]{:S(2)}, u32[]{:S(2)}) collective-permute-start(bf16[2,128,1024]{2,1,0:T(8,128)(2,1)S(1)} %collective-permute-done.8.refs_6_), channel_id=1, source_target_pairs={{4,0},{8,4},{12,8},{0,12},{5,1},{9,5},{13,9},{1,13},{6,2},{10,6},{... | collective-permute-start | bytes 1572872 | tf_op jit(solution)/shard_map/ppermute | solution.py:46
  44.6 3.5 %collective-permute-start.15 = (bf16[2,128,1024]{2,1,0:T(8,128)(2,1)}, bf16[2,128,1024]{2,1,0:T(8,128)(2,1)S(1)}, u32[]{:S(2)}, u32[]{:S(2)}) collective-permute-start(bf16[2,128,1024]{2,1,0:T(8,128)(2,1)} %collective-permute-done.2.refs_3_), channel_id=1, source_target_pairs={{1,16},{0,17},{17,0},{16,1},{3,18},{2,19},{19,2},{18,3},{5,20},{4,... | collective-permute-start | bytes 1572872 | tf_op jit(solution)/shard_map/ppermute | solution.py:66
  49.1 7.4 %shard_map.131 = (bf16[576,1792]{1,0:T(8,128)(2,1)S(1)}, bf16[576,256]{1,0:T(8,128)(2,1)S(1)}, bf16[288,2048]{1,0:T(8,128)(2,1)S(1)}) custom-call(s32[18]{0:T(128)S(1)} %stack.90.order, bf16[288,2048]{1,0:T(8,128)(2,1)S(1)} %copy-done.5, bf16[288,2048]{1,0:T(8,128)(2,1)} %collective-permute-done.4.mix_other, bf16[288,2048]{1,0:T(8,128)(2,1)S(1)} %copy-done.4, ...), custom_call_target="tpu_custom_call" | custom-call | flops 509607936 | bytes 9437184 | tf_op jit(solution)/shard_map/pallas_call | solution.py:209
  58.0 2.6 %collective-permute-done.15.refs_13_ = bf16[2,128,1024]{2,1,0:T(8,128)(2,1)S(1)} collective-permute-done((bf16[2,128,1024]{2,1,0:T(8,128)(2,1)}, bf16[2,128,1024]{2,1,0:T(8,128)(2,1)S(1)}, u32[]{:S(2)}, u32[]{:S(2)}) %collective-permute-start.15) | collective-permute-done | bytes 524320 | tf_op jit(solution)/shard_map/ppermute | solution.py:66
  60.7 2.7 %collective-permute-done.13.refs_11_ = bf16[2,128,1024]{2,1,0:T(8,128)(2,1)S(1)} collective-permute-done((bf16[2,128,1024]{2,1,0:T(8,128)(2,1)S(1)}, bf16[2,128,1024]{2,1,0:T(8,128)(2,1)S(1)}, u32[]{:S(2)}, u32[]{:S(2)}) %collective-permute-start.13) | collective-permute-done | bytes 524320 | tf_op jit(solution)/shard_map/ppermute | solution.py:62
  65.6 6.8 %shard_map.132 = (f32[576,1024]{1,0:T(8,128)S(1)}, f32[576,1024]{1,0:T(8,128)S(1)}) custom-call(bf16[576,1792]{1,0:T(8,128)(2,1)S(1)} %get-tuple-element.134.student_mix, bf16[576,1792]{1,0:T(8,128)(2,1)S(1)} %get-tuple-element.135.teacher_mix, bf16[2,128,1024]{2,1,0:T(8,128)(2,1)} %pad_maximum_fusion.refs_0_, ...), custom_call_target="tpu_custom_call" | custom-call | flops 4227858432 | bytes 17825792 | tf_op jit(solution)/shard_map/pallas_call | solution.py:252
  73.0 4.0 %shard_map.133 = (f32[576,1024]{1,0:T(8,128)S(1)}, f32[576,1024]{1,0:T(8,128)S(1)}, f32[576,128]{1,0:T(8,128)S(1)}) custom-call(s32[18]{0:T(128)S(1)} %stack.90.order, bf16[576,256]{1,0:T(8,128)(2,1)S(1)} %get-tuple-element.118.student_mix, bf16[576,256]{1,0:T(8,128)(2,1)S(1)} %get-tuple-element.133.teacher_mix, ...), custom_call_target="tpu_custom_call" | custom-call | flops 603979776 | bytes 13631488 | tf_op jit(solution)/shard_map/pallas_call | solution.py:307
  81.6 3.0 %collective-permute-start.23 = (bf16[3,128,256]{2,1,0:T(8,128)(2,1)S(1)}, bf16[3,128,256]{2,1,0:T(8,128)(2,1)S(1)}, u32[]{:S(2)}, u32[]{:S(2)}) collective-permute-start(bf16[3,128,256]{2,1,0:T(8,128)(2,1)S(1)} %get-tuple-element.157), channel_id=1, source_target_pairs={{33,0},{32,1},{65,32},{64,33},{97,64},{96,65},{129,96},{128,97},{1... | collective-permute-start | bytes 589832 | tf_op jit(solution)/shard_map/ppermute | solution.py:58
  84.6 4.4 %shard_map.136 = (bf16[3,128,768]{2,1,0:T(8,128)(2,1)}, bf16[3,128,768]{2,1,0:T(8,128)(2,1)}, bf16[3,128,768]{2,1,0:T(8,128)(2,1)}, bf16[576,768]{1,0:T(8,128)(2...) custom-call(s32[18]{0:T(128)S(1)} %stack.90.order, f32[576,1024]{1,0:T(8,128)S(1)} %get-tuple-element.149.student, ...), custom_call_target="tpu_custom_call" | custom-call | flops 905969664 | bytes 9437184 | tf_op jit(solution)/shard_map/pallas_call | solution.py:374
  89.0 3.0 %collective-permute-start.26 = (bf16[3,128,768]{2,1,0:T(8,128)(2,1)}, bf16[3,128,768]{2,1,0:T(8,128)(2,1)}, u32[]{:S(2)}, u32[]{:S(2)}) collective-permute-start(bf16[3,128,768]{2,1,0:T(8,128)(2,1)} %get-tuple-element.170), channel_id=1, source_target_pairs={{33,0},{32,1},{65,32},{64,33},{97,64},{96,65},{129,96},{128,97},{1... | collective-permute-start | bytes 1769480 | tf_op jit(solution)/shard_map/ppermute | solution.py:58
  96.1 6.3 %all-to-all-start = ((bf16[8,128,256]{2,1,0:T(8,128)(2,1)}), bf16[8,128,256]{2,1,0:T(8,128)(2,1)}, u32[]{:S(2)}, u32[]{:S(2)}) async-start(bf16[8,128,256]{2,1,0:T(8,128)(2,1)} %shard_map.138), calls=%async_computation | async-start | bytes 1048576 | tf_op jit(solution)/shard_map/all_to_all | solution.py:647
  102.4 3.3 %collective-permute-done.25.refs_0_ = bf16[3,128,768]{2,1,0:T(8,128)(2,1)} collective-permute-done((bf16[3,128,768]{2,1,0:T(8,128)(2,1)}, bf16[3,128,768]{2,1,0:T(8,128)(2,1)}, u32[]{:S(2)}, u32[]{:S(2)}) %collective-permute-start.25) | collective-permute-done | bytes 589856 | tf_op jit(solution)/shard_map/ppermute | solution.py:62
  107.5 3.7 %shard_map.139 = bf16[8,128,768]{2,1,0:T(8,128)(2,1)} custom-call(f32[8,128,768]{2,1,0:T(8,128)S(1)} %shard_map.137.kept, bf16[3,128,768]{2,1,0:T(8,128)(2,1)} %collective-permute-done.25.refs_0_, bf16[3,128,768]{2,1,0:T(8,128)(2,1)} %collective-permute-done.26.refs_1_, bf16[3,128,768]{2,1,0:T(8,128)(2,1)} %collective-permute-done.27.refs_2_), custom_call_target="tpu_custom_call" | custom-call | tf_op jit(solution)/shard_map/pallas_call | solution.py:443
  112.0 4.7 %all-to-all-start.1 = ((bf16[8,128,768]{2,1,0:T(8,128)(2,1)}), bf16[8,128,768]{2,1,0:T(8,128)(2,1)S(1)}, u32[]{:S(2)}, u32[]{:S(2)}) async-start(bf16[8,128,768]{2,1,0:T(8,128)(2,1)} %shard_map.139), calls=%async_computation.1 | async-start | bytes 3145728 | tf_op jit(solution)/shard_map/all_to_all | solution.py:647
  120.3 16.7 %all-to-all-done.1.last = bf16[8,128,768]{2,1,0:T(8,128)(2,1)S(1)} async-done(((bf16[8,128,768]{2,1,0:T(8,128)(2,1)}), bf16[8,128,768]{2,1,0:T(8,128)(2,1)S(1)}, u32[]{:S(2)}, u32[]{:S(2)}) %all-to-all-start.1) | async-done | bytes 1572896 | tf_op jit(solution)/shard_map/all_to_all | solution.py:647
  138.4 16.7 %all_to_all.20.copies = bf16[8,16,1024]{2,1,0:T(8,128)(2,1)S(1)} all-to-all(bf16[8,16,1024]{2,1,0:T(8,128)(2,1)S(1)} %bitcast.27), channel_id=1, replica_groups={{0,48,64,112,128,176,192,240},{16,32,80,96,144,160,208,224},{1,49,65,11..., dimensions={0} | all-to-all | bytes 524288 | tf_op jit(solution)/shard_map/all_to_all | solution.py:662
  155.9 3.6 %all-to-all-start.3 = ((bf16[16,16,1024]{2,1,0:T(8,128)(2,1)}), bf16[16,16,1024]{2,1,0:T(8,128)(2,1)S(1)}, u32[]{:S(2)}, u32[]{:S(2)}) async-start(bf16[16,16,1024]{2,1,0:T(8,128)(2,1)} %shard_map.142), calls=%async_computation.3 | async-start | bytes 1048576 | tf_op jit(solution)/shard_map/all_to_all | solution.py:665
  159.5 16.0 %all-to-all-done.3 = bf16[16,16,1024]{2,1,0:T(8,128)(2,1)S(1)} async-done(((bf16[16,16,1024]{2,1,0:T(8,128)(2,1)}), bf16[16,16,1024]{2,1,0:T(8,128)(2,1)S(1)}, u32[]{:S(2)}, u32[]{:S(2)}) %all-to-all-start.3) | async-done | bytes 524320 | tf_op jit(solution)/shard_map/all_to_all | solution.py:665
  175.6 4.5 %shard_map.143 = (f32[128,2048]{1,0:T(8,128)}, f32[128,2048]{1,0:T(8,128)}, f32[128,2048]{1,0:T(8,128)}, f32[128,2048]{1,0:T(8,128)}) custom-call(s32[1]{0:T(128)} %bitcast.flip, bf16[8,2,16,1024]{3,2,1,0:T(8,128)(2,1)S(1)} %bitcast.26, f32[128,2048]{1,0:T(8,128)S(1)} %copy-done.1, f32[128,2048]{1,0:T(8,128)S(1)} %copy-done.3, f32[128,2048]{1,0:T(8,128)} %first.1, ...), custom_call_target="tpu_custom_call" | custom-call | tf_op jit(solution)/shard_map/pallas_call | solution.py:542
  (88 shorter events, 37.9 us)
Async XLA Ops:
  2.9 16.3 %collective-permute-start.4 = (bf16[288,2048]{1,0:T(8,128)(2,1)S(1)}, bf16[288,2048]{1,0:T(8,128)(2,1)}, u32[]{:S(2)}, u32[]{:S(2)}) collective-permute-start(bf16[288,2048]{1,0:T(8,128)(2,1)S(1)} %copy-done.5), channel_id=1, source_target_pairs={{0,1},{1,0},{2,3},{3,2},{4,5},{5,4},{6,7},{7,6},{8,9},{9,8},{10,11... | collective-permute-start | bytes 3538952 | tf_op jit(solution)/shard_map/ppermute | solution.py:42
  3.4 14.2 %collective-permute-start.2 = (bf16[2,128,1024]{2,1,0:T(8,128)(2,1)}, bf16[2,128,1024]{2,1,0:T(8,128)(2,1)}, u32[]{:S(2)}, u32[]{:S(2)}) collective-permute-start(bf16[2,128,1024]{2,1,0:T(8,128)(2,1)} %pad_maximum_fusion.refs_0_), channel_id=1, source_target_pairs={{16,2},{2,16},{0,18},{18,0},{17,3},{3,17},{1,19},{19,1},{20,6},{6,... | collective-permute-start | bytes 1572872 | tf_op jit(solution)/shard_map/ppermute | solution.py:54
  3.9 15.3 %collective-permute-start.1 = (bf16[2,128,1024]{2,1,0:T(8,128)(2,1)}, bf16[2,128,1024]{2,1,0:T(8,128)(2,1)}, u32[]{:S(2)}, u32[]{:S(2)}) collective-permute-start(bf16[2,128,1024]{2,1,0:T(8,128)(2,1)} %pad_maximum_fusion.refs_0_), channel_id=1, source_target_pairs={{0,4},{4,8},{8,12},{12,0},{1,5},{5,9},{9,13},{13,1},{2,6},{6,10},{... | collective-permute-start | bytes 1572872 | tf_op jit(solution)/shard_map/ppermute | solution.py:50
  5.5 13.7 %collective-permute-start = (bf16[2,128,1024]{2,1,0:T(8,128)(2,1)}, bf16[2,128,1024]{2,1,0:T(8,128)(2,1)}, u32[]{:S(2)}, u32[]{:S(2)}) collective-permute-start(bf16[2,128,1024]{2,1,0:T(8,128)(2,1)} %pad_maximum_fusion.refs_0_), channel_id=1, source_target_pairs={{4,0},{8,4},{12,8},{0,12},{5,1},{9,5},{13,9},{1,13},{6,2},{10,6},{... | collective-permute-start | bytes 1572872 | tf_op jit(solution)/shard_map/ppermute | solution.py:46
  7.2 12.0 %collective-permute-start.5 = (s32[2,144]{1,0:T(2,128)S(1)}, s32[2,144]{1,0:T(2,128)S(1)}, u32[]{:S(2)}, u32[]{:S(2)}) collective-permute-start(s32[2,144]{1,0:T(2,128)S(1)} %copy-done.10), channel_id=1, source_target_pairs={{0,1},{1,0},{2,3},{3,2},{4,5},{5,4},{6,7},{7,6},{8,9},{9,8},{10,11... | collective-permute-start | bytes 3464 | tf_op jit(solution)/shard_map/ppermute | solution.py:42
  19.2 17.8 %collective-permute-start.7 = (bf16[2,128,1024]{2,1,0:T(8,128)(2,1)}, bf16[2,128,1024]{2,1,0:T(8,128)(2,1)S(1)}, u32[]{:S(2)}, u32[]{:S(2)}) collective-permute-start(bf16[2,128,1024]{2,1,0:T(8,128)(2,1)} %collective-permute-done.2.refs_3_), channel_id=1, source_target_pairs={{0,4},{4,8},{8,12},{12,0},{1,5},{5,9},{9,13},{13,1},{2,6},{6,10},{... | collective-permute-start | bytes 1572872 | tf_op jit(solution)/shard_map/ppermute | solution.py:50
  20.8 16.3 %collective-permute-start.10 = (bf16[2,128,1024]{2,1,0:T(8,128)(2,1)}, bf16[2,128,1024]{2,1,0:T(8,128)(2,1)S(1)}, u32[]{:S(2)}, u32[]{:S(2)}) collective-permute-start(bf16[2,128,1024]{2,1,0:T(8,128)(2,1)} %collective-permute-done.1.refs_2_), channel_id=1, source_target_pairs={{1,32},{0,33},{33,64},{32,65},{65,96},{64,97},{97,128},{96,129},{1... | collective-permute-start | bytes 1572872 | tf_op jit(solution)/shard_map/ppermute | solution.py:62
  20.8 16.3 %collective-permute-start.9 = (bf16[2,128,1024]{2,1,0:T(8,128)(2,1)}, bf16[2,128,1024]{2,1,0:T(8,128)(2,1)S(1)}, u32[]{:S(2)}, u32[]{:S(2)}) collective-permute-start(bf16[2,128,1024]{2,1,0:T(8,128)(2,1)} %collective-permute-done.refs_1_), channel_id=1, source_target_pairs={{33,0},{32,1},{65,32},{64,33},{97,64},{96,65},{129,96},{128,97},{1... | collective-permute-start | bytes 1572872 | tf_op jit(solution)/shard_map/ppermute | solution.py:58
  24.6 13.8 %collective-permute-start.8 = (bf16[2,128,1024]{2,1,0:T(8,128)(2,1)}, bf16[2,128,1024]{2,1,0:T(8,128)(2,1)S(1)}, u32[]{:S(2)}, u32[]{:S(2)}) collective-permute-start(bf16[2,128,1024]{2,1,0:T(8,128)(2,1)} %collective-permute-done.refs_1_), channel_id=1, source_target_pairs={{16,2},{2,16},{0,18},{18,0},{17,3},{3,17},{1,19},{19,1},{20,6},{6,... | collective-permute-start | bytes 1572872 | tf_op jit(solution)/shard_map/ppermute | solution.py:54
  26.1 14.4 %collective-permute-start.6 = (bf16[2,128,1024]{2,1,0:T(8,128)(2,1)}, bf16[2,128,1024]{2,1,0:T(8,128)(2,1)S(1)}, u32[]{:S(2)}, u32[]{:S(2)}) collective-permute-start(bf16[2,128,1024]{2,1,0:T(8,128)(2,1)} %collective-permute-done.refs_1_), channel_id=1, source_target_pairs={{4,0},{8,4},{12,8},{0,12},{5,1},{9,5},{13,9},{1,13},{6,2},{10,6},{... | collective-permute-start | bytes 1572872 | tf_op jit(solution)/shard_map/ppermute | solution.py:46
  40.4 16.1 %collective-permute-start.12 = (bf16[2,128,1024]{2,1,0:T(8,128)(2,1)S(1)}, bf16[2,128,1024]{2,1,0:T(8,128)(2,1)S(1)}, u32[]{:S(2)}, u32[]{:S(2)}) collective-permute-start(bf16[2,128,1024]{2,1,0:T(8,128)(2,1)S(1)} %collective-permute-done.6.refs_4_), channel_id=1, source_target_pairs={{33,0},{32,1},{65,32},{64,33},{97,64},{96,65},{129,96},{128,97},{1... | collective-permute-start | bytes 1572872 | tf_op jit(solution)/shard_map/ppermute | solution.py:58
  40.8 15.7 %collective-permute-start.11 = (bf16[2,128,1024]{2,1,0:T(8,128)(2,1)S(1)}, bf16[2,128,1024]{2,1,0:T(8,128)(2,1)S(1)}, u32[]{:S(2)}, u32[]{:S(2)}) collective-permute-start(bf16[2,128,1024]{2,1,0:T(8,128)(2,1)S(1)} %collective-permute-done.8.refs_6_), channel_id=1, source_target_pairs={{4,0},{8,4},{12,8},{0,12},{5,1},{9,5},{13,9},{1,13},{6,2},{10,6},{... | collective-permute-start | bytes 1572872 | tf_op jit(solution)/shard_map/ppermute | solution.py:46
  44.0 14.0 %collective-permute-start.14 = (bf16[2,128,1024]{2,1,0:T(8,128)(2,1)S(1)}, bf16[2,128,1024]{2,1,0:T(8,128)(2,1)S(1)}, u32[]{:S(2)}, u32[]{:S(2)}) collective-permute-start(bf16[2,128,1024]{2,1,0:T(8,128)(2,1)S(1)} %collective-permute-done.10.refs_8_), channel_id=1, source_target_pairs={{16,2},{2,16},{0,18},{18,0},{17,3},{3,17},{1,19},{19,1},{20,6},{6,... | collective-permute-start | bytes 1572872 | tf_op jit(solution)/shard_map/ppermute | solution.py:54
  44.6 16.1 %collective-permute-start.15 = (bf16[2,128,1024]{2,1,0:T(8,128)(2,1)}, bf16[2,128,1024]{2,1,0:T(8,128)(2,1)S(1)}, u32[]{:S(2)}, u32[]{:S(2)}) collective-permute-start(bf16[2,128,1024]{2,1,0:T(8,128)(2,1)} %collective-permute-done.2.refs_3_), channel_id=1, source_target_pairs={{1,16},{0,17},{17,0},{16,1},{3,18},{2,19},{19,2},{18,3},{5,20},{4,... | collective-permute-start | bytes 1572872 | tf_op jit(solution)/shard_map/ppermute | solution.py:66
  48.0 15.3 %collective-permute-start.13 = (bf16[2,128,1024]{2,1,0:T(8,128)(2,1)S(1)}, bf16[2,128,1024]{2,1,0:T(8,128)(2,1)S(1)}, u32[]{:S(2)}, u32[]{:S(2)}) collective-permute-start(bf16[2,128,1024]{2,1,0:T(8,128)(2,1)S(1)} %collective-permute-done.8.refs_6_), channel_id=1, source_target_pairs={{1,32},{0,33},{33,64},{32,65},{65,96},{64,97},{97,128},{96,129},{1... | collective-permute-start | bytes 1572872 | tf_op jit(solution)/shard_map/ppermute | solution.py:62
  80.3 11.7 %collective-permute-start.24 = (bf16[2,128,256]{2,1,0:T(8,128)(2,1)S(1)}, bf16[2,128,256]{2,1,0:T(8,128)(2,1)S(1)}, u32[]{:S(2)}, u32[]{:S(2)}) collective-permute-start(bf16[2,128,256]{2,1,0:T(8,128)(2,1)S(1)} %get-tuple-element.158), channel_id=1, source_target_pairs={{1,16},{0,17},{17,0},{16,1},{3,18},{2,19},{19,2},{18,3},{5,20},{4,... | collective-permute-start | bytes 393224 | tf_op jit(solution)/shard_map/ppermute | solution.py:66
  81.6 13.6 %collective-permute-start.22 = (bf16[3,128,256]{2,1,0:T(8,128)(2,1)S(1)}, bf16[3,128,256]{2,1,0:T(8,128)(2,1)S(1)}, u32[]{:S(2)}, u32[]{:S(2)}) collective-permute-start(bf16[3,128,256]{2,1,0:T(8,128)(2,1)S(1)} %get-tuple-element.156), channel_id=1, source_target_pairs={{1,32},{0,33},{33,64},{32,65},{65,96},{64,97},{97,128},{96,129},{1... | collective-permute-start | bytes 589832 | tf_op jit(solution)/shard_map/ppermute | solution.py:62
  81.6 13.6 %collective-permute-start.23 = (bf16[3,128,256]{2,1,0:T(8,128)(2,1)S(1)}, bf16[3,128,256]{2,1,0:T(8,128)(2,1)S(1)}, u32[]{:S(2)}, u32[]{:S(2)}) collective-permute-start(bf16[3,128,256]{2,1,0:T(8,128)(2,1)S(1)} %get-tuple-element.157), channel_id=1, source_target_pairs={{33,0},{32,1},{65,32},{64,33},{97,64},{96,65},{129,96},{128,97},{1... | collective-permute-start | bytes 589832 | tf_op jit(solution)/shard_map/ppermute | solution.py:58
  89.0 16.7 %collective-permute-start.25 = (bf16[3,128,768]{2,1,0:T(8,128)(2,1)}, bf16[3,128,768]{2,1,0:T(8,128)(2,1)}, u32[]{:S(2)}, u32[]{:S(2)}) collective-permute-start(bf16[3,128,768]{2,1,0:T(8,128)(2,1)} %get-tuple-element.169), channel_id=1, source_target_pairs={{1,32},{0,33},{33,64},{32,65},{65,96},{64,97},{97,128},{96,129},{1... | collective-permute-start | bytes 1769480 | tf_op jit(solution)/shard_map/ppermute | solution.py:62
  89.0 16.7 %collective-permute-start.26 = (bf16[3,128,768]{2,1,0:T(8,128)(2,1)}, bf16[3,128,768]{2,1,0:T(8,128)(2,1)}, u32[]{:S(2)}, u32[]{:S(2)}) collective-permute-start(bf16[3,128,768]{2,1,0:T(8,128)(2,1)} %get-tuple-element.170), channel_id=1, source_target_pairs={{33,0},{32,1},{65,32},{64,33},{97,64},{96,65},{129,96},{128,97},{1... | collective-permute-start | bytes 1769480 | tf_op jit(solution)/shard_map/ppermute | solution.py:58
  92.0 15.5 %collective-permute-start.27 = (bf16[3,128,768]{2,1,0:T(8,128)(2,1)}, bf16[3,128,768]{2,1,0:T(8,128)(2,1)}, u32[]{:S(2)}, u32[]{:S(2)}) collective-permute-start(bf16[3,128,768]{2,1,0:T(8,128)(2,1)} %get-tuple-element.171), channel_id=1, source_target_pairs={{1,16},{0,17},{17,0},{16,1},{3,18},{2,19},{19,2},{18,3},{5,20},{4,... | collective-permute-start | bytes 1769480 | tf_op jit(solution)/shard_map/ppermute | solution.py:66
  96.1 15.9 %all-to-all-start = ((bf16[8,128,256]{2,1,0:T(8,128)(2,1)}), bf16[8,128,256]{2,1,0:T(8,128)(2,1)}, u32[]{:S(2)}, u32[]{:S(2)}) async-start(bf16[8,128,256]{2,1,0:T(8,128)(2,1)} %shard_map.138), calls=%async_computation | async-start | bytes 1048576 | tf_op jit(solution)/shard_map/all_to_all | solution.py:647
  112.0 25.0 %all-to-all-start.1 = ((bf16[8,128,768]{2,1,0:T(8,128)(2,1)}), bf16[8,128,768]{2,1,0:T(8,128)(2,1)S(1)}, u32[]{:S(2)}, u32[]{:S(2)}) async-start(bf16[8,128,768]{2,1,0:T(8,128)(2,1)} %shard_map.139), calls=%async_computation.1 | async-start | bytes 3145728 | tf_op jit(solution)/shard_map/all_to_all | solution.py:647
  155.9 19.6 %all-to-all-start.3 = ((bf16[16,16,1024]{2,1,0:T(8,128)(2,1)}), bf16[16,16,1024]{2,1,0:T(8,128)(2,1)S(1)}, u32[]{:S(2)}, u32[]{:S(2)}) async-start(bf16[16,16,1024]{2,1,0:T(8,128)(2,1)} %shard_map.142), calls=%async_computation.3 | async-start | bytes 1048576 | tf_op jit(solution)/shard_map/all_to_all | solution.py:665
  (22 other events, 251.4 us)
